TPU v7x, 32 devices: a whole 2x2x4 slice. The times are simulated.
32 devices in a mesh: row: 2 (over x), col: 16 (over z, y, core).
Axes of the slice: x: 2, y: 2, z: 4, core: 2. Of those that a mesh axis runs over, the one named last changes fastest.
Arguments:
- features: float32 [8192, 128], P(('row', 'col')), may hold values from -6 to 6
- weight: float32 [128, 256], replicated, may hold values from -0.5 to 0.5
- out_bias: float32 [256], replicated, may hold values from -3 to 3
- cotangent: float32 [8192, 256], P(('row', 'col')), may hold values from -6 to 6
- drop_keep: int32 [8192, 256], P(('row', 'col')), may hold values 0 or 1
- tile_cols: int32 [2, 16, 32, 4], P('row', 'col'), may hold values from 0 to 3, as said below
- tile_edge_counts: int32 [2, 16, 32, 4], P('row', 'col'), may hold values from 1 to 64, as said below
- edge_pos: int32 [2, 16, 32, 256], P('row', 'col'), may hold values from 0 to 16383
- edge_keep_bits: int32 [2, 16, 32, 256], P('row', 'col'), may hold values 0 or 1
Outputs:
- hidden_out: float32 [8192, 256], P(('row', 'col'))
- grad_features: float32 [8192, 128], P(('row', 'col'))
- grad_weight: float32 [128, 256], replicated
Inputs may be any that keep to these rules, and one draw needn't show every extreme that they name: `tile_cols`: the 4 source tile columns of one tile-row of a device block are distinct. A tile's edges are its first tile_edge_counts slots; the slots at and after the count are unused.
All inputs are finite; a program needn't handle non-finite values. No bound on the sum of `drop_keep` or of `edge_keep_bits` on one device may be relied on, other than what follows from the above.
Results may differ from a plain program's by a relative error of at most 0.000071.
Values sent between devices are 32-bit elements; how exact they have to be, the bound alone decides.
No kernel may reach another device: no remote copies, remote signals or barrier semaphores. Data moves between devices by JAX's collectives and lax.ppermute only.
A program may use at most 64 MiB of HBM per device.

v0:
```python
import math

import jax
import jax.numpy as jnp
from jax import lax
from jax.sharding import PartitionSpec as P

TILE_SIDE = 128
TPR = 4
EPT = 64


keep_rate = 0.9
highest = lax.Precision.HIGHEST


def gelu_exact(values):
    return 0.5 * values * (1.0 + lax.erf(values * 0.7071067811865476))


def gelu_slope(values):
    return (
        0.5 * (1.0 + lax.erf(values * 0.7071067811865476))
        + values * jnp.exp(-0.5 * values * values) * 0.3989422804014327
    )


def surviving_slots(counts_here, edge_positions, keep_here):
    slot_ids = jnp.arange(edge_positions.shape[1], dtype=jnp.int32)
    tile_of = slot_ids // EPT
    slot_place = slot_ids % EPT
    count_slot = counts_here[:, tile_of]
    return jnp.where((slot_place[None, :] < count_slot) & (keep_here == 1), 1.0, 0.0).astype(
        jnp.float32
    )


def assemble_tiles(edge_positions, surviving_mask, leading_row, block_row_list):
    picked = lax.dynamic_slice_in_dim(edge_positions, leading_row, block_row_list, 0).reshape(
        block_row_list, TPR, EPT
    )
    surviving_part = lax.dynamic_slice_in_dim(
        surviving_mask, leading_row, block_row_list, 0
    ).reshape(block_row_list, TPR, EPT)
    within = jnp.arange(TILE_SIDE, dtype=jnp.int32)
    row_hot = jnp.where((picked // TILE_SIDE)[..., None] == within, surviving_part[..., None], 0.0)
    col_hot = jnp.where((picked % TILE_SIDE)[..., None] == within, 1.0, 0.0).astype(jnp.float32)
    return jnp.einsum("bkea,bkes->bkas", row_hot, col_hot, precision=highest)


def forward_row_block(
    feature_panels, edge_positions, surviving_mask, column_indices, count_of_rows
):
    feat_width = feature_panels.shape[1]
    source_tiles = feature_panels.shape[0] // TILE_SIDE
    panel_tiles = feature_panels.reshape(source_tiles, TILE_SIDE, feat_width)
    rows_per_tile = count_of_rows // TILE_SIDE
    block_row_list = math.gcd(rows_per_tile, 4)

    def forward_one_block(number):
        leading_row = number * block_row_list
        tile_entries = assemble_tiles(edge_positions, surviving_mask, leading_row, block_row_list)
        chosen = lax.dynamic_slice_in_dim(column_indices, leading_row, block_row_list, 0)
        source_nodes = panel_tiles[chosen]
        result = jnp.einsum("bkas,bksf->baf", tile_entries, source_nodes, precision=highest)
        return result.reshape(block_row_list * TILE_SIDE, feat_width)

    blocks = lax.map(
        forward_one_block, jnp.arange(rows_per_tile // block_row_list, dtype=jnp.int32)
    )
    return blocks.reshape(count_of_rows, feat_width)


def backward_row_block(
    collected_rows, edge_positions, surviving_mask, column_indices, source_tiles
):
    feat_width = collected_rows.shape[1]
    rows_per_tile = edge_positions.shape[0]
    block_row_list = math.gcd(rows_per_tile, 4)
    target_nodes = jnp.arange(source_tiles, dtype=jnp.int32)

    def backward_one_block(running_total, number):
        leading_row = number * block_row_list
        tile_entries = assemble_tiles(edge_positions, surviving_mask, leading_row, block_row_list)
        chosen = lax.dynamic_slice_in_dim(column_indices, leading_row, block_row_list, 0)
        grad_rows = lax.dynamic_slice_in_dim(
            collected_rows, leading_row * TILE_SIDE, block_row_list * TILE_SIDE, 0
        ).reshape(block_row_list, TILE_SIDE, feat_width)
        carried = jnp.einsum("bkas,baf->bksf", tile_entries, grad_rows, precision=highest)
        placing = jnp.where(chosen[..., None] == target_nodes, 1.0, 0.0).astype(jnp.float32)
        return (
            running_total + jnp.einsum("bkt,bksf->tsf", placing, carried, precision=highest),
            None,
        )

    running_total, _ = lax.scan(
        backward_one_block,
        jnp.zeros((source_tiles, TILE_SIDE, feat_width), jnp.float32),
        jnp.arange(rows_per_tile // block_row_list, dtype=jnp.int32),
    )
    return running_total.reshape(source_tiles * TILE_SIDE, feat_width)


def shards(
    features,
    weight,
    out_bias,
    cotangent,
    drop_keep,
    tile_cols,
    tile_edge_counts,
    edge_pos,
    edge_keep_bits,
):
    column_indices = tile_cols[0, 0]
    edge_positions = edge_pos[0, 0]
    surviving_mask = surviving_slots(tile_edge_counts[0, 0], edge_positions, edge_keep_bits[0, 0])
    local_nodes = features.shape[0]
    rows_per_tile = edge_positions.shape[0]
    source_tiles = local_nodes * lax.axis_size("row") // TILE_SIDE
    row_lookup = (
        jnp.arange(rows_per_tile, dtype=jnp.int32)[:, None] * TILE_SIDE
        + edge_positions // TILE_SIDE
    )
    degree_part = jax.ops.segment_sum(
        surviving_mask.ravel(), row_lookup.ravel(), num_segments=rows_per_tile * TILE_SIDE
    )
    degree = 1.0 + lax.psum_scatter(degree_part, "col", scatter_dimension=0, tiled=True)
    inv_root = lax.rsqrt(degree)[:, None]
    dropout = drop_keep.astype(jnp.float32) / keep_rate
    transformed = jnp.dot(features, weight, precision=highest, preferred_element_type=jnp.float32)
    scaled_rows = inv_root * transformed
    feature_panels = lax.all_gather(scaled_rows, "row", axis=0, tiled=True)
    summed = lax.psum_scatter(
        forward_row_block(
            feature_panels,
            edge_positions,
            surviving_mask,
            column_indices,
            local_nodes * lax.axis_size("col"),
        ),
        "col",
        scatter_dimension=0,
        tiled=True,
    )
    pre_act = inv_root * (summed + scaled_rows) + out_bias[None, :]
    hidden_out = gelu_exact(pre_act) * dropout
    grad_pre = cotangent * dropout * gelu_slope(pre_act)
    backward_scaled_rows = inv_root * grad_pre
    collected_rows = lax.all_gather(backward_scaled_rows, "col", axis=0, tiled=True)
    returned = lax.psum_scatter(
        backward_row_block(
            collected_rows, edge_positions, surviving_mask, column_indices, source_tiles
        ),
        "row",
        scatter_dimension=0,
        tiled=True,
    )
    grad_z = inv_root * (returned + backward_scaled_rows)
    grad_features = jnp.dot(grad_z, weight.T, precision=highest, preferred_element_type=jnp.float32)
    weight_term = jnp.dot(features.T, grad_z, precision=highest, preferred_element_type=jnp.float32)
    grad_weight = lax.psum(weight_term, ("row", "col"))
    return (hidden_out, grad_features, grad_weight)


def solution(mesh):
    in_specs = (
        P(("row", "col"), None),
        P(),
        P(),
        P(("row", "col"), None),
        P(("row", "col"), None),
        P("row", "col", None, None),
        P("row", "col", None, None),
        P("row", "col", None, None),
        P("row", "col", None, None),
    )
    out_specs = (P(("row", "col"), None), P(("row", "col"), None), P())
    return jax.shard_map(shards, mesh=mesh, in_specs=in_specs, out_specs=out_specs, check_vma=False)
```

profile of v0, /device:TPU:0, one launch (start us, length us, event | category | flops | bytes accessed | tf_op | source)
XLA Modules:
  0.0 620.2 jit_solution(15981580567076055196)
XLA Ops:
  11.3 57.0 %scatter_custom_fusion = f32[4096]{0:T(1024)S(1)} fusion(s32[8192]{0:T(1024)S(1)} %bitcast.91, f32[8192]{0:T(1024)S(1)} %and_select_fusion.1, f32[]{:T(128)} %constant.211.clone.1), kind=kCustom, calls=%fused_computation.91 | custom fusion | flops 8192 | bytes 16388 | tf_op jit(solution)/shard_map/scatter-add | solution.py:125
  68.3 63.0 %all-reduce = f32[4096]{0:T(1024)S(1)} all-reduce(f32[4096]{0:T(1024)S(1)} %scatter_custom_fusion), channel_id=2, replica_groups=mesh['row'=2,'col'=16] {'col'}, use_global_device_ids=true, to_apply=%region_1.2.clone | all-reduce | flops 4096 | bytes 32768
  134.5 7.0 %all_gather.6 = f32[512,256]{1,0:T(8,128)S(1)} all-gather(f32[256,256]{1,0:T(8,128)S(1)} %convolution_multiply_fusion), channel_id=1, replica_groups=mesh['row'=2,'col'=16] {'row'}, dimensions={0}, use_global_device_ids=true | all-gather | bytes 786432 | tf_op jit(solution)/shard_map/all_gather | solution.py:133
  141.7 83.9 %while.25 = (s32[]{:T(128)}, f32[8,512,256]{2,1,0:T(8,128)}, s32[8]{0:T(128)S(1)}, s32[32,256]{1,0:T(8,128)}, f32[32,256]{1,0:T(8,128)}, /*index=5*/s32[32,4]{1,...) while((s32[]{:T(128)}, f32[8,512,256]{2,1,0:T(8,128)}, ...), condition=%wide.region_3.4_spmd, body=%wide.region_2.3_spmd.sunk | while | flops 1007177792 | bytes 10023987 | solution.py:68
  144.7 3.3 fusion.80
  155.1 3.3 fusion.80
  165.6 3.3 fusion.80
  176.1 3.3 fusion.80
  186.6 3.3 fusion.80
  197.1 3.3 fusion.80
  207.6 3.3 fusion.80
  225.7 70.1 %reduce-scatter.3.cloned.1.call-done = f32[256,256]{1,0:T(8,128)} async-done(((f32[4096,256]{1,0:T(8,128)}), f32[256,256]{1,0:T(8,128)}) %reduce-scatter.3.cloned.1.call-update) | async-done | bytes 262160 | tf_op jit(solution)/shard_map/reduce_scatter | solution.py:134
  298.1 49.7 %all-gather.2.cloned.1.call-done = f32[4096,256]{1,0:T(8,128)} async-done(((f32[256,256]{1,0:T(8,128)}), f32[4096,256]{1,0:T(8,128)}) %all-gather.2.cloned.1.call-update) | async-done | bytes 4194320 | tf_op jit(solution)/shard_map/all_gather | solution.py:150
  348.3 120.1 %while.26 = (s32[]{:T(128)}, f32[4,128,256]{2,0,1:T(4,128)}, s32[8]{0:T(128)}, s32[32,4]{1,0:T(8,128)S(1)}, s32[32,256]{1,0:T(8,128)}, /*index=5*/f32[32,256]{1,...) while((s32[]{:T(128)}, f32[4,128,256]{2,0,1:T(4,128)}, ...), condition=%wide.region_6.7_spmd.clone, body=%wide.region_5.6_spmd.clone.sunk | while | flops 1032604800 | bytes 8970687 | solution.py:96
  357.4 5.1 fusion.90
  371.5 6.1 fusion.90
  386.6 6.1 fusion.90
  401.8 6.1 fusion.90
  416.9 6.1 fusion.90
  432.0 6.1 fusion.90
  447.2 6.1 fusion.90
  462.3 6.1 fusion.90
  470.5 13.2 %reduce-scatter.5.cloned.1.call-done = f32[256,256]{1,0:T(8,128)} async-done(((f32[512,256]{1,0:T(8,128)}), f32[256,256]{1,0:T(8,128)}) %reduce-scatter.5.cloned.1.call-update) | async-done | bytes 262160 | tf_op jit(solution)/shard_map/reduce_scatter | solution.py:151
  488.0 124.1 %all-reduce.3.cloned.1.call-done = f32[128,256]{0,1:T(8,128)} async-done(((f32[128,256]{0,1:T(8,128)}), f32[128,256]{0,1:T(8,128)}) %all-reduce.3.cloned.1.call-update) | async-done | bytes 131088 | tf_op jit(solution)/shard_map/psum | solution.py:162
  (230 shorter events, 134.6 us)
Async XLA Ops:
  7.2 126.1 %copy-start = (f32[256,128]{1,0:T(8,128)S(1)}, f32[256,128]{1,0:T(8,128)}, u32[]{:S(2)}) copy-start(f32[256,128]{1,0:T(8,128)} %param.13) | copy-start | bytes 393220
  7.2 134.4 %copy-start.7 = (s32[1,1,32,4]{2,3,1,0:T(4,128)S(1)}, s32[1,1,32,4]{2,3,1,0:T(4,128)}, u32[]{:S(2)}) copy-start(s32[1,1,32,4]{2,3,1,0:T(4,128)} %param.18) | copy-start | bytes 1540
  7.2 288.6 %reduce-scatter.3.cloned.1.call-start = ((), (), s32[]{:S(2)}) async-start(), calls=%async_computation.2 | async-start | bytes 4456448 | tf_op jit(solution)/shard_map/reduce_scatter | solution.py:134
  133.3 162.5 %copy-start.5 = (f32[256]{0:T(256)}, f32[256]{0:T(256)S(1)}, u32[]{:S(2)}) copy-start(f32[256]{0:T(256)S(1)} %fusion.50) | copy-start | bytes 3076
  225.6 70.2 %copy-start.3 = (f32[256,256]{1,0:T(8,128)S(1)}, f32[256,256]{1,0:T(8,128)}, u32[]{:S(2)}) copy-start(f32[256,256]{1,0:T(8,128)} %param.16) | copy-start | bytes 786436
  225.6 70.2 %copy-start.4 = (s32[256,256]{1,0:T(8,128)S(1)}, s32[256,256]{1,0:T(8,128)}, u32[]{:S(2)}) copy-start(s32[256,256]{1,0:T(8,128)} %param.17) | copy-start | bytes 786436
  225.6 70.2 %copy-start.8 = (f32[256]{0:T(256)S(1)}, f32[256]{0:T(256)}, u32[]{:S(2)}) copy-start(f32[256]{0:T(256)} %param.15) | copy-start | bytes 3076
  225.7 122.1 %all-gather.2.cloned.1.call-start = ((), (), s32[]{:S(2)}) async-start(), calls=%async_computation.3 | async-start | bytes 4456448 | tf_op jit(solution)/shard_map/all_gather | solution.py:150
  297.8 185.8 %reduce-scatter.5.cloned.1.call-start = ((), (), s32[]{:S(2)}) async-start(), calls=%async_computation.4 | async-start | bytes 786432 | tf_op jit(solution)/shard_map/reduce_scatter | solution.py:151
  348.3 135.3 %copy-start.1 = (f32[256,256]{1,0:T(8,128)S(1)}, f32[256,256]{1,0:T(8,128)}, u32[]{:S(2)}) copy-start(f32[256,256]{1,0:T(8,128)} %get-tuple-element.331) | copy-start | bytes 786436
  468.4 17.5 %copy-start.2 = (f32[128,256]{1,0:T(8,128)S(1)}, f32[128,256]{1,0:T(8,128)}, u32[]{:S(2)}) copy-start(f32[128,256]{1,0:T(8,128)} %param.14) | copy-start | bytes 393220
  468.4 17.5 %copy-start.6 = (f32[256]{0:T(256)S(1)}, f32[256]{0:T(256)}, u32[]{:S(2)}) copy-start(f32[256]{0:T(256)} %copy-done.5) | copy-start | bytes 3076
  470.4 141.6 %all-reduce.3.cloned.1.call-start = ((), (), s32[]{:S(2)}) async-start(), calls=%async_computation.5 | async-start | bytes 262144 | tf_op jit(solution)/shard_map/psum | solution.py:162
Sparse Core Ops, SparseCore 0:
  225.8 69.9 reduce-scatter.2
  298.2 49.5 all-gather.1
  470.5 13.0 reduce-scatter.4
  489.6 122.4 all-reduce.2
where the time goes:
time: 623 us; the launch traced here: 620 us
  waiting for transfers between devices  257 us (41%)
  matrix products  130 us (21%)
  local copies, waits for them, and re-layouts  70.8 us (11%)
  blocking collectives  70 us (11%)
  other arithmetic  61.2 us (10%)
  loops' own time  16.3 us (3%)
  between operations  14.6 us (2%)
    psum x1, waiting for transfers between devices, shards(): grad_weight = lax.psum(weight_term, ('row', 'col'))  124 us
    reduce_scatter x1, waiting for transfers between devices, shards(): lax.psum_scatter(forward_row_block(feature_panels, edge_positions, surviv...  70.1 us
    unnamed x1, blocking collectives  63 us
    scatter-add x1, other arithmetic, shards(): jax.ops.segment_sum(surviving_mask.ravel(), row_lookup.ravel(), num_segme...  57 us
    all_gather x1, waiting for transfers between devices, shards(): lax.all_gather(backward_scaled_rows, 'col', axis=0, tiled=True)  49.7 us
    dot_general x8, matrix products, backward_one_block(): jnp.einsum('bkt,bksf->tsf', placing, carried, precision=highest)  47.8 us
    dot_general x16, matrix products, assemble_tiles(): return jnp.einsum('bkea,bkes->bkas', row_hot, col_hot, precision=highest)  41.6 us
    dot_general x8, matrix products, forward_one_block(): jnp.einsum('bkas,bksf->baf', tile_entries, source_nodes, precision=highest)  20.7 us
  transfers between devices with their start and end apart: 4, of which 4 were waited for; matrix products, arithmetic and copies ran while one was open for 0% of the time, Pallas kernels for 0%

commit v1 on v0

v1 whole, which is shorter than its diff:
```python
import functools

import jax
import jax.numpy as jnp
from jax import lax
from jax.experimental import pallas as pl
from jax.experimental.pallas import tpu as pltpu
from jax.sharding import PartitionSpec as P

TILE_SIDE = 128
TPR = 4
EPT = 64
KEEP_RATE = 0.9

f32 = jnp.float32
bf16 = jnp.bfloat16
i32 = jnp.int32
highest = lax.Precision.HIGHEST
NT = (((1,), (1,)), ((), ()))
TN = (((0,), (0,)), ((), ()))
MIB = 1 << 20


def gelu_exact(values):
    return 0.5 * values * (1.0 + lax.erf(values * 0.7071067811865476))


def gelu_slope(values):
    return (
        0.5 * (1.0 + lax.erf(values * 0.7071067811865476))
        + values * jnp.exp(-0.5 * values * values) * 0.3989422804014327
    )


def one_hot(index_row, size):
    places = lax.broadcasted_iota(i32, (size, index_row.shape[1]), 0)
    return jnp.where(places == index_row, 1.0, 0.0).astype(bf16)


def pack_kernel(cols_ref, counts_ref, pos_ref, keep_ref, packed_ref, degree_ref):
    rows, slots = pos_ref.shape
    slot = lax.broadcasted_iota(i32, (rows, slots), 1)
    tile = lax.shift_right_arithmetic(slot, 6)
    count = jnp.zeros((rows, slots), i32)
    col = jnp.zeros((rows, slots), i32)
    for k in range(TPR):
        count = jnp.where(tile == k, counts_ref[:, k : k + 1], count)
        col = jnp.where(tile == k, cols_ref[:, k : k + 1], col)
    live = ((slot & (EPT - 1)) < count) & (keep_ref[...] == 1)
    pos = pos_ref[...]
    source = col * TILE_SIDE + (pos & (TILE_SIDE - 1))
    target = jnp.where(live, lax.shift_right_arithmetic(pos, 7), -1)
    packed = jnp.where(live, source * TILE_SIDE + target, -1)
    packed_ref[...] = packed
    ones = jnp.ones((8, slots), bf16)
    for t in range(rows):
        hot = one_hot(target[t : t + 1, :], TILE_SIDE)
        sums = lax.dot_general(ones, hot, NT, preferred_element_type=f32)
        degree_ref[t : t + 1, :] = sums[0:1, :]


def own_block_kernel(group, me_ref, packed_ref, block_ref):
    c = pl.program_id(0)
    sources = block_ref.shape[1]
    per_group = group // TILE_SIDE
    for s in range(per_group):
        row = packed_ref[pl.ds(c * per_group + s, 1), :]
        source = lax.shift_right_arithmetic(row, 7) - me_ref[0] * group
        source = jnp.where(source < 0, source + sources, source)
        target = jnp.where(row >= 0, row & (TILE_SIDE - 1), -1)
        hot = lax.dot_general(
            one_hot(source, sources), one_hot(target, TILE_SIDE), NT, preferred_element_type=f32
        )
        block_ref[0, :, s * TILE_SIDE : (s + 1) * TILE_SIDE] = hot.astype(bf16)


def turned_block_kernel(group, grid_rows, grid_cols, me_ref, edges_ref, block_ref):
    c = pl.program_id(0)
    per_group = group // TILE_SIDE
    slots = edges_ref.shape[1] // per_group
    for k in range(grid_rows):
        r = lax.rem(me_ref[0] + k, grid_rows)
        for s in range(per_group):
            row = edges_ref[pl.ds(r * grid_cols + c, 1), s * slots : (s + 1) * slots]
            source = lax.shift_right_arithmetic(row, 7) - me_ref[0] * group
            target = row & (TILE_SIDE - 1)
            hot = lax.dot_general(
                one_hot(target, TILE_SIDE), one_hot(source, group), NT, preferred_element_type=f32
            )
            at = (k * per_group + s) * TILE_SIDE
            block_ref[0, at : at + TILE_SIDE, :] = hot.astype(bf16)


def spread_down(row):
    return jnp.broadcast_to(row, (TILE_SIDE, TILE_SIDE)).T


def halves(values):
    high = values.astype(bf16)
    low = (values - high.astype(f32)).astype(bf16)
    return high, low


def sum_kernel(scaled, *refs):
    if scaled:
        degree_ref, block_ref, value_ref, own_ref, other_ref, total_ref = refs
    else:
        block_ref, value_ref, own_ref, other_ref, total_ref = refs
    c = pl.program_id(0)
    group, width = value_ref.shape
    values = value_ref[...]
    if scaled:
        per_group = group // TILE_SIDE
        scale = jnp.concatenate(
            [
                spread_down(lax.rsqrt(1.0 + degree_ref[pl.ds(c * per_group + s, 1), :]))
                for s in range(per_group)
            ],
            axis=0,
        )
        values = values * scale[:, :1] if width != TILE_SIDE else values * scale
    both = jnp.concatenate(halves(values), axis=1)
    part = jnp.dot(block_ref[0], both, preferred_element_type=f32)

    @pl.when(c == 0)
    def _():
        total_ref[...] = part

    @pl.when(c > 0)
    def _():
        total_ref[...] += part

    @pl.when(c == pl.num_programs(0) - 1)
    def _():
        total = total_ref[...]
        total = total[:, :width] + total[:, width:]
        own_ref[...] = total[:group]
        other_ref[...] = total[group:]


def middle_kernel(
    me_ref,
    own_ref,
    got_ref,
    degree_ref,
    features_ref,
    weight_ref,
    bias_ref,
    cotangent_ref,
    drop_ref,
    hidden_ref,
    sent_ref,
    scale_ref,
    weight_grad_ref,
):
    group, width = features_ref.shape
    per_group = group // TILE_SIDE
    scale = jnp.concatenate(
        [
            spread_down(lax.rsqrt(1.0 + degree_ref[pl.ds(me_ref[0] * per_group + s, 1), :]))
            for s in range(per_group)
        ],
        axis=0,
    )[:, :width]
    scale_ref[...] = scale
    total = own_ref[...]
    for k in range(got_ref.shape[0] // group):
        total = total + got_ref[k * group : (k + 1) * group, :]
    mixed = scale * (total + scale * features_ref[...])
    weight = weight_ref[...]
    pre_act = jnp.dot(mixed, weight, precision=highest, preferred_element_type=f32) + bias_ref[...]
    dropout = drop_ref[...].astype(f32) / KEEP_RATE
    hidden_ref[...] = gelu_exact(pre_act) * dropout
    grad_pre = cotangent_ref[...] * dropout * gelu_slope(pre_act)
    sent_ref[...] = scale * lax.dot_general(
        grad_pre, weight, NT, precision=highest, preferred_element_type=f32
    )
    weight_grad_ref[...] = lax.dot_general(
        mixed, grad_pre, TN, precision=highest, preferred_element_type=f32
    )


def shards(
    features,
    weight,
    out_bias,
    cotangent,
    drop_keep,
    tile_cols,
    tile_edge_counts,
    edge_pos,
    edge_keep_bits,
):
    grid_rows, grid_cols = lax.axis_size("row"), lax.axis_size("col")
    my_row, my_col = lax.axis_index("row"), lax.axis_index("col")
    group, width = features.shape
    hidden = weight.shape[1]
    rows, slots = edge_pos.shape[2:]
    per_group = group // TILE_SIDE
    block_side = grid_rows * group
    row_id, col_id = my_row[None].astype(i32), my_col[None].astype(i32)
    smem = pl.BlockSpec(memory_space=pltpu.SMEM)
    limit = pltpu.CompilerParams(vmem_limit_bytes=48 * MIB)

    packed, degree = pl.pallas_call(
        pack_kernel,
        out_shape=(
            jax.ShapeDtypeStruct((rows, slots), i32),
            jax.ShapeDtypeStruct((rows, TILE_SIDE), f32),
        ),
        compiler_params=limit,
        cost_estimate=pl.CostEstimate(flops=2**21, bytes_accessed=2**17, transcendentals=0),
        name="pack",
    )(tile_cols[0, 0], tile_edge_counts[0, 0], edge_pos[0, 0], edge_keep_bits[0, 0])

    gathered = lax.all_gather(features, "col", axis=0, tiled=True)

    pieces = packed.reshape(1, grid_cols, per_group * slots)
    pieces = jnp.broadcast_to(pieces, (grid_rows, grid_cols, per_group * slots))
    edges = lax.all_to_all(
        pieces.reshape(grid_rows * grid_cols, per_group * slots), ("row", "col"), 0, 0, tiled=True
    )

    bit = 1
    while bit < grid_cols:
        degree = degree + lax.ppermute(degree, "col", [(p, p ^ bit) for p in range(grid_cols)])
        bit *= 2

    formation = pl.CostEstimate(
        flops=2 * rows * slots * TILE_SIDE * block_side,
        bytes_accessed=2 * rows * TILE_SIDE * block_side,
        transcendentals=0,
    )
    block_shape = jax.ShapeDtypeStruct((grid_cols, block_side, group), bf16)
    block_spec = pl.BlockSpec((1, block_side, group), lambda c: (c, 0, 0))
    own_block = pl.pallas_call(
        functools.partial(own_block_kernel, group),
        grid=(grid_cols,),
        in_specs=[smem, pl.BlockSpec((rows, slots), lambda c: (0, 0))],
        out_specs=block_spec,
        out_shape=block_shape,
        compiler_params=limit,
        cost_estimate=formation,
        name="own_block",
    )(row_id, packed)
    turned_block = pl.pallas_call(
        functools.partial(turned_block_kernel, group, grid_rows, grid_cols),
        grid=(grid_cols,),
        in_specs=[smem, pl.BlockSpec(edges.shape, lambda c: (0, 0))],
        out_specs=block_spec,
        out_shape=block_shape,
        compiler_params=limit,
        cost_estimate=formation,
        name="turned_block",
    )(row_id, edges)

    def block_sum(block, values, node_degree=None):
        scaled = node_degree is not None
        return pl.pallas_call(
            functools.partial(sum_kernel, scaled),
            grid=(grid_cols,),
            in_specs=([pl.BlockSpec((rows, TILE_SIDE), lambda c: (0, 0))] if scaled else [])
            + [block_spec, pl.BlockSpec((group, width), lambda c: (c, 0))],
            out_specs=(
                pl.BlockSpec((group, width), lambda c: (0, 0)),
                pl.BlockSpec((block_side - group, width), lambda c: (0, 0)),
            ),
            out_shape=(
                jax.ShapeDtypeStruct((group, width), f32),
                jax.ShapeDtypeStruct((block_side - group, width), f32),
            ),
            scratch_shapes=[pltpu.VMEM((block_side, 2 * width), f32)],
            compiler_params=limit,
            cost_estimate=pl.CostEstimate(
                flops=4 * rows * TILE_SIDE * block_side * width,
                bytes_accessed=2 * rows * TILE_SIDE * block_side,
                transcendentals=0,
            ),
            name="forward_sum" if scaled else "backward_sum",
        )(*([node_degree] if scaled else []), block, values)

    def to_owners(others):
        got = [
            lax.ppermute(
                others[k * group : (k + 1) * group],
                "row",
                [(p, (p + k + 1) % grid_rows) for p in range(grid_rows)],
            )
            for k in range(grid_rows - 1)
        ]
        return got[0] if len(got) == 1 else jnp.concatenate(got, axis=0)

    own, others = block_sum(turned_block, gathered, degree)
    got = to_owners(others)

    hidden_out, sent, scale, weight_grad = pl.pallas_call(
        middle_kernel,
        in_specs=[smem] + [pl.BlockSpec(memory_space=pltpu.VMEM)] * 8,
        out_shape=(
            jax.ShapeDtypeStruct((group, hidden), f32),
            jax.ShapeDtypeStruct((group, width), f32),
            jax.ShapeDtypeStruct((group, width), f32),
            jax.ShapeDtypeStruct((width, hidden), f32),
        ),
        compiler_params=limit,
        cost_estimate=pl.CostEstimate(
            flops=36 * group * width * hidden, bytes_accessed=2**20, transcendentals=2**18
        ),
        name="middle",
    )(
        col_id,
        own,
        got,
        degree,
        features,
        weight,
        out_bias.reshape(1, hidden),
        cotangent,
        drop_keep,
    )

    collected = lax.all_gather(sent, "col", axis=0, tiled=True)
    for axis, size in (("col", grid_cols), ("row", grid_rows)):
        bit = 1
        while bit < size:
            weight_grad = weight_grad + lax.ppermute(
                weight_grad, axis, [(p, p ^ bit) for p in range(size)]
            )
            bit *= 2
    own, others = block_sum(own_block, collected)
    got = to_owners(others)
    total = own
    for k in range(grid_rows - 1):
        total = total + got[k * group : (k + 1) * group]
    grad_features = scale * (total + sent)
    return (hidden_out, grad_features, weight_grad)


def solution(mesh):
    in_specs = (
        P(("row", "col"), None),
        P(),
        P(),
        P(("row", "col"), None),
        P(("row", "col"), None),
        P("row", "col", None, None),
        P("row", "col", None, None),
        P("row", "col", None, None),
        P("row", "col", None, None),
    )
    out_specs = (P(("row", "col"), None), P(("row", "col"), None), P())
    return jax.shard_map(shards, mesh=mesh, in_specs=in_specs, out_specs=out_specs, check_vma=False)
```

time: 623 us -> 144 us (0.23)
  waiting for transfers between devices: 257 us -> 60.2 us
  matrix products: 130 us -> 0 us
  blocking collectives: 70 us -> 0 us
  local copies, waits for them, and re-layouts: 70.8 us -> 10.9 us
  other arithmetic: 61.2 us -> 2.34 us
  Pallas kernels: 0 us -> 34.6 us
  starting transfers between devices: 0.34 us -> 20.9 us
  loops' own time: 16.3 us -> 0 us
    dot_general x43 -> x0, matrix products: 130 us -> none  [the longest x8 47.8 us: backward_one_block(): jnp.einsum('bkt,bksf->tsf', placing, carried, precision=highest)]
    psum x1 -> x0, waiting for transfers between devices: 124 us -> none  [shards(): grad_weight = lax.psum(weight_term, ('row', 'col'))]
    reduce_scatter x2 -> x0, waiting for transfers between devices: 83.3 us -> none  [the longest x1 70.1 us: shards(): lax.psum_scatter(forward_row_block(feature_panels, edge_positions, surviv...]
    unnamed x1 -> x0, blocking collectives: 63 us -> none
    scatter-add x1 -> x0, other arithmetic: 57 us -> none  [shards(): jax.ops.segment_sum(surviving_mask.ravel(), row_lookup.ravel(), num_segme...]
    dynamic_slice x64 -> x0, local copies, waits for them, and re-layouts: 47.2 us -> none  [the longest x16 15.8 us: forward_row_block(): lax.map(forward_one_block, jnp.arange(rows_per_tile // block_row_list, dt...]
    pallas_call x0 -> x6, Pallas kernels: none -> 34.6 us  [the longest x2 21.7 us: block_sum(): pl.pallas_call(functools.partial(sum_kernel, scaled), grid=(grid_cols,),...]
    ppermute x0 -> x11, waiting for transfers between devices: none -> 28.8 us  [the longest x5 13.8 us: shards(): lax.ppermute(weight_grad, axis, [(p, p ^ bit) for p in range(size)])]
  transfers between devices with their start and end apart: 4 -> 14, of which waited for: 4 -> 12; matrix products, arithmetic and copies ran while one was open for 0% -> 2% of each run, Pallas kernels for 0% -> 15%
where the time goes in v1:
time: 144 us; the launch traced here: 143 us
  waiting for transfers between devices  60.2 us (42%)
  Pallas kernels  34.6 us (24%)
  starting transfers between devices  20.9 us (15%)
  between operations  14.2 us (10%)
  local copies, waits for them, and re-layouts  10.9 us (8%)
  other arithmetic  2.34 us (2%)
    pallas_call x2, Pallas kernels, block_sum(): pl.pallas_call(functools.partial(sum_kernel, scaled), grid=(grid_cols,),...  21.7 us
    all_gather x1, waiting for transfers between devices, shards(): collected = lax.all_gather(sent, 'col', axis=0, tiled=True)  17.1 us
    ppermute x5, waiting for transfers between devices, shards(): lax.ppermute(weight_grad, axis, [(p, p ^ bit) for p in range(size)])  13.8 us
    all_gather x1, waiting for transfers between devices, shards(): gathered = lax.all_gather(features, 'col', axis=0, tiled=True)  13.7 us
    unnamed x23, local copies, waits for them, and re-layouts  8.62 us
    ppermute x2, waiting for transfers between devices, to_owners(): lax.ppermute(others[k * group:(k + 1) * group], 'row', [(p, (p + k + 1) %...  7.7 us
    all_to_all x1, starting transfers between devices, shards(): lax.all_to_all(pieces.reshape(grid_rows * grid_cols, per_group * slots),...  7.3 us
    ppermute x4, waiting for transfers between devices, shards(): lax.ppermute(degree, 'col', [(p, p ^ bit) for p in range(grid_cols)])  7.29 us
  transfers between devices with their start and end apart: 14, of which 12 were waited for; matrix products, arithmetic and copies ran while one was open for 2% of the time, Pallas kernels for 15%

profile of v1, /device:TPU:0, one launch (start us, length us, event | category | flops | bytes accessed | tf_op | source)
XLA Modules:
  0.0 143.1 jit_solution(10611009022588279133)
XLA Ops:
  12.4 7.3 %all-to-all-start = ((s32[32,1,512]{2,1,0:T(1,128)}), s32[32,1,512]{2,1,0:T(1,128)S(1)}, u32[]{:S(2)}, u32[]{:S(2)}) async-start(s32[32,1,512]{2,1,0:T(1,128)} %all_to_all.7), calls=%async_computation | async-start | bytes 131072 | tf_op jit(solution)/shard_map/all_to_all | solution.py:220
  21.0 1.8 %collective-permute-start.1 = (f32[32,128]{1,0:T(8,128)S(1)}, f32[32,128]{1,0:T(8,128)S(1)}, u32[]{:S(2)}, u32[]{:S(2)}) collective-permute-start(f32[32,128]{1,0:T(8,128)S(1)} %add.33), channel_id=1, source_target_pairs={{0,2},{1,3},{2,0},{3,1},{4,6},{5,7},{6,4},{7,5},{8,10},{9,11},{10,... | collective-permute-start | bytes 49160 | tf_op jit(solution)/shard_map/ppermute | solution.py:226
  22.8 2.1 %collective-permute-done.1 = f32[32,128]{1,0:T(8,128)S(1)} collective-permute-done((f32[32,128]{1,0:T(8,128)S(1)}, f32[32,128]{1,0:T(8,128)S(1)}, u32[]{:S(2)}, u32[]{:S(2)}) %collective-permute-start.1) | collective-permute-done | bytes 16416 | tf_op jit(solution)/shard_map/ppermute | solution.py:226
  24.9 1.9 %collective-permute-start.2 = (f32[32,128]{1,0:T(8,128)S(1)}, f32[32,128]{1,0:T(8,128)S(1)}, u32[]{:S(2)}, u32[]{:S(2)}) collective-permute-start(f32[32,128]{1,0:T(8,128)S(1)} %add.34), channel_id=1, source_target_pairs={{0,4},{1,5},{2,6},{3,7},{4,0},{5,1},{6,2},{7,3},{8,12},{9,13},{10,... | collective-permute-start | bytes 49160 | tf_op jit(solution)/shard_map/ppermute | solution.py:226
  26.8 2.1 %collective-permute-done.2 = f32[32,128]{1,0:T(8,128)S(1)} collective-permute-done((f32[32,128]{1,0:T(8,128)S(1)}, f32[32,128]{1,0:T(8,128)S(1)}, u32[]{:S(2)}, u32[]{:S(2)}) %collective-permute-start.2) | collective-permute-done | bytes 16416 | tf_op jit(solution)/shard_map/ppermute | solution.py:226
  28.9 2.7 %collective-permute-start.3 = (f32[32,128]{1,0:T(8,128)S(1)}, f32[32,128]{1,0:T(8,128)S(1)}, u32[]{:S(2)}, u32[]{:S(2)}) collective-permute-start(f32[32,128]{1,0:T(8,128)S(1)} %add.35), channel_id=1, source_target_pairs={{0,8},{1,9},{2,10},{3,11},{4,12},{5,13},{6,14},{7,15},{8,0},{9,1},... | collective-permute-start | bytes 49160 | tf_op jit(solution)/shard_map/ppermute | solution.py:226
  31.6 2.2 %collective-permute-done.3 = f32[32,128]{1,0:T(8,128)S(1)} collective-permute-done((f32[32,128]{1,0:T(8,128)S(1)}, f32[32,128]{1,0:T(8,128)S(1)}, u32[]{:S(2)}, u32[]{:S(2)}) %collective-permute-start.3) | collective-permute-done | bytes 16416 | tf_op jit(solution)/shard_map/ppermute | solution.py:226
  33.8 5.3 %turned_block.1.refs_1_ = bf16[16,512,256]{2,1,0:T(8,128)(2,1)S(1)} custom-call(s32[1]{0:T(128)} %bitcast.5.me_ref, s32[32,512]{1,0:T(8,128)S(1)} %bitcast.10), custom_call_target="tpu_custom_call" | custom-call | flops 1073741824 | bytes 4194304 | tf_op jit(solution)/shard_map/turned_block/pallas_call | solution.py:246
  39.1 1.9 %copy-done.1 = bf16[16,512,256]{2,1,0:T(8,128)(2,1)} copy-done((bf16[16,512,256]{2,1,0:T(8,128)(2,1)}, bf16[16,512,256]{2,1,0:T(8,128)(2,1)S(1)}, u32[]{:S(2)}) %copy-start.1) | copy-done | bytes 4194328
  41.0 13.7 %all-gather.3.cloned.1.call-done.refs_2_ = f32[4096,128]{1,0:T(8,128)} async-done(((f32[256,128]{1,0:T(8,128)}), f32[4096,128]{1,0:T(8,128)}) %all-gather.3.cloned.1.call-update) | async-done | bytes 2097168 | tf_op jit(solution)/shard_map/all_gather | solution.py:216
  54.7 1.6 %copy-done.2 = f32[4096,128]{1,0:T(8,128)S(1)} copy-done((f32[4096,128]{1,0:T(8,128)S(1)}, f32[4096,128]{1,0:T(8,128)}, u32[]{:S(2)}) %copy-start.2) | copy-done | bytes 2097176
  56.3 11.3 %forward_sum.1 = (f32[256,128]{1,0:T(8,128)S(1)}, f32[256,128]{1,0:T(8,128)S(1)}) custom-call(f32[32,128]{1,0:T(8,128)S(1)} %add.36.refs_0_.degree_ref, bf16[16,512,256]{2,1,0:T(8,128)(2,1)} %copy-done.1, f32[4096,128]{1,0:T(8,128)S(1)} %copy-done.2), custom_call_target="tpu_custom_call" | custom-call | flops 1073741824 | bytes 4194304 | tf_op jit(solution)/shard_map/forward_sum/pallas_call | solution.py:259
  69.2 4.2 %collective-permute-done.4.got_ref = f32[256,128]{1,0:T(8,128)S(1)} collective-permute-done((f32[256,128]{1,0:T(8,128)S(1)}, f32[256,128]{1,0:T(8,128)S(1)}, u32[]{:S(2)}, u32[]{:S(2)}) %collective-permute-start.4) | collective-permute-done | bytes 131104 | tf_op jit(solution)/shard_map/ppermute | solution.py:284
  73.4 1.8 %middle.1 = (f32[256,256]{1,0:T(8,128)}, f32[256,128]{1,0:T(8,128)}, f32[256,128]{1,0:T(8,128)S(1)}, f32[128,256]{1,0:T(8,128)S(1)}) custom-call(s32[1]{0:T(128)} %bitcast.me_ref, f32[256,128]{1,0:T(8,128)S(1)} %get-tuple-element.15.own_ref, f32[256,128]{1,0:T(8,128)S(1)} %collective-permute-done.4.got_ref, f32[32,128]{1,0:T(8,128)S(1)} %add.36.refs_0_.degree_ref, ...), custom_call_target="tpu_custom_call" | custom-call | flops 301989888 | bytes 1048576 | tf_op jit(solution)/shard_map/middle/pallas_call | solution.py:296
  77.3 5.0 %collective-permute-done.7 = f32[128,256]{1,0:T(8,128)S(1)} collective-permute-done((f32[128,256]{1,0:T(8,128)S(1)}, f32[128,256]{1,0:T(8,128)S(1)}, u32[]{:S(2)}, u32[]{:S(2)}) %collective-permute-start.7) | collective-permute-done | bytes 131104 | tf_op jit(solution)/shard_map/ppermute | solution.py:326
  82.8 5.8 %collective-permute-done.8 = f32[128,256]{1,0:T(8,128)S(1)} collective-permute-done((f32[128,256]{1,0:T(8,128)S(1)}, f32[128,256]{1,0:T(8,128)S(1)}, u32[]{:S(2)}, u32[]{:S(2)}) %collective-permute-start.8) | collective-permute-done | bytes 131104 | tf_op jit(solution)/shard_map/ppermute | solution.py:326
  89.6 5.1 %own_block.1.refs_0_ = bf16[16,512,256]{2,1,0:T(8,128)(2,1)S(1)} custom-call(s32[1]{0:T(128)} %bitcast.5.me_ref, s32[32,256]{1,0:T(8,128)S(1)} %get-tuple-element.14.packed_ref), custom_call_target="tpu_custom_call" | custom-call | flops 1073741824 | bytes 4194304 | tf_op jit(solution)/shard_map/own_block/pallas_call | solution.py:236
  94.7 1.9 %copy-done = bf16[16,512,256]{2,1,0:T(8,128)(2,1)} copy-done((bf16[16,512,256]{2,1,0:T(8,128)(2,1)}, bf16[16,512,256]{2,1,0:T(8,128)(2,1)S(1)}, u32[]{:S(2)}) %copy-start) | copy-done | bytes 4194328
  96.7 1.7 %collective-permute-done.9 = f32[128,256]{1,0:T(8,128)S(1)} collective-permute-done((f32[128,256]{1,0:T(8,128)S(1)}, f32[128,256]{1,0:T(8,128)S(1)}, u32[]{:S(2)}, u32[]{:S(2)}) %collective-permute-start.9) | collective-permute-done | bytes 131104 | tf_op jit(solution)/shard_map/ppermute | solution.py:326
  99.9 17.1 %all-gather.5.cloned.1.call-done.refs_1_ = f32[4096,128]{1,0:T(8,128)} async-done(((f32[256,128]{1,0:T(8,128)}), f32[4096,128]{1,0:T(8,128)}) %all-gather.5.cloned.1.call-update) | async-done | bytes 2097168 | tf_op jit(solution)/shard_map/all_gather | solution.py:322
  117.0 1.6 %copy-done.3 = f32[4096,128]{1,0:T(8,128)S(1)} copy-done((f32[4096,128]{1,0:T(8,128)S(1)}, f32[4096,128]{1,0:T(8,128)}, u32[]{:S(2)}) %copy-start.3) | copy-done | bytes 2097176
  118.6 10.4 %backward_sum.1 = (f32[256,128]{1,0:T(8,128)S(1)}, f32[256,128]{1,0:T(8,128)S(1)}) custom-call(bf16[16,512,256]{2,1,0:T(8,128)(2,1)} %copy-done, f32[4096,128]{1,0:T(8,128)S(1)} %copy-done.3), custom_call_target="tpu_custom_call" | custom-call | flops 1073741824 | bytes 4194304 | tf_op jit(solution)/shard_map/backward_sum/pallas_call | solution.py:259
  131.2 3.5 %collective-permute-done.5 = f32[256,128]{1,0:T(8,128)S(1)} collective-permute-done((f32[256,128]{1,0:T(8,128)S(1)}, f32[256,128]{1,0:T(8,128)S(1)}, u32[]{:S(2)}, u32[]{:S(2)}) %collective-permute-start.5) | collective-permute-done | bytes 131104 | tf_op jit(solution)/shard_map/ppermute | solution.py:284
  134.7 1.6 %add_multiply_fusion = f32[256,128]{1,0:T(8,128)} fusion(f32[256,128]{1,0:T(8,128)S(1)} %get-tuple-element.18, f32[256,128]{1,0:T(8,128)} %get-tuple-element.19, f32[256,128]{1,0:T(8,128)S(1)} %get-tuple-element.20, f32[256,128]{1,0:T(8,128)S(1)} %collective-permute-done.5), kind=kLoop, calls=%fused_computation | loop fusion | flops 98304 | bytes 655360 | tf_op jit(solution)/shard_map/mul | solution.py:335
  (50 shorter events, 15.5 us)
Async XLA Ops:
  7.2 47.5 %all-gather.3.cloned.1.call-start = ((), (), s32[]{:S(2)}) async-start(), calls=%async_computation.1 | async-start | bytes 2228224 | tf_op jit(solution)/shard_map/all_gather | solution.py:216
  9.4 0.8 copy-start.5
  12.4 21.3 %all-to-all-start = ((s32[32,1,512]{2,1,0:T(1,128)}), s32[32,1,512]{2,1,0:T(1,128)S(1)}, u32[]{:S(2)}, u32[]{:S(2)}) async-start(s32[32,1,512]{2,1,0:T(1,128)} %all_to_all.7), calls=%async_computation | async-start | bytes 131072 | tf_op jit(solution)/shard_map/all_to_all | solution.py:220
  19.7 97.2 %all-gather.5.cloned.1.call-start = ((), (), s32[]{:S(2)}) async-start(), calls=%async_computation.2 | async-start | bytes 2228224 | tf_op jit(solution)/shard_map/all_gather | solution.py:322
  19.8 1.2 collective-permute-start
  21.0 3.8 %collective-permute-start.1 = (f32[32,128]{1,0:T(8,128)S(1)}, f32[32,128]{1,0:T(8,128)S(1)}, u32[]{:S(2)}, u32[]{:S(2)}) collective-permute-start(f32[32,128]{1,0:T(8,128)S(1)} %add.33), channel_id=1, source_target_pairs={{0,2},{1,3},{2,0},{3,1},{4,6},{5,7},{6,4},{7,5},{8,10},{9,11},{10,... | collective-permute-start | bytes 49160 | tf_op jit(solution)/shard_map/ppermute | solution.py:226
  24.9 4.0 %collective-permute-start.2 = (f32[32,128]{1,0:T(8,128)S(1)}, f32[32,128]{1,0:T(8,128)S(1)}, u32[]{:S(2)}, u32[]{:S(2)}) collective-permute-start(f32[32,128]{1,0:T(8,128)S(1)} %add.34), channel_id=1, source_target_pairs={{0,4},{1,5},{2,6},{3,7},{4,0},{5,1},{6,2},{7,3},{8,12},{9,13},{10,... | collective-permute-start | bytes 49160 | tf_op jit(solution)/shard_map/ppermute | solution.py:226
  28.9 4.9 %collective-permute-start.3 = (f32[32,128]{1,0:T(8,128)S(1)}, f32[32,128]{1,0:T(8,128)S(1)}, u32[]{:S(2)}, u32[]{:S(2)}) collective-permute-start(f32[32,128]{1,0:T(8,128)S(1)} %add.35), channel_id=1, source_target_pairs={{0,8},{1,9},{2,10},{3,11},{4,12},{5,13},{6,14},{7,15},{8,0},{9,1},... | collective-permute-start | bytes 49160 | tf_op jit(solution)/shard_map/ppermute | solution.py:226
  39.1 2.0 %copy-start.1 = (bf16[16,512,256]{2,1,0:T(8,128)(2,1)}, bf16[16,512,256]{2,1,0:T(8,128)(2,1)S(1)}, u32[]{:S(2)}) copy-start(bf16[16,512,256]{2,1,0:T(8,128)(2,1)S(1)} %turned_block.1.refs_1_) | copy-start | bytes 12582916
  54.7 1.6 %copy-start.2 = (f32[4096,128]{1,0:T(8,128)S(1)}, f32[4096,128]{1,0:T(8,128)}, u32[]{:S(2)}) copy-start(f32[4096,128]{1,0:T(8,128)} %all-gather.3.cloned.1.call-done.refs_2_) | copy-start | bytes 6291460
  56.3 17.1 %copy-start.4 = (f32[256,128]{1,0:T(8,128)S(1)}, f32[256,128]{1,0:T(8,128)}, u32[]{:S(2)}) copy-start(f32[256,128]{1,0:T(8,128)} %features_ref.1) | copy-start | bytes 393220
  56.3 17.1 %copy-start.7 = (f32[256,256]{1,0:T(8,128)S(1)}, f32[256,256]{1,0:T(8,128)}, u32[]{:S(2)}) copy-start(f32[256,256]{1,0:T(8,128)} %cotangent_ref.1) | copy-start | bytes 786436
  56.3 17.1 %copy-start.8 = (s32[256,256]{1,0:T(8,128)S(1)}, s32[256,256]{1,0:T(8,128)}, u32[]{:S(2)}) copy-start(s32[256,256]{1,0:T(8,128)} %drop_ref.1) | copy-start | bytes 786436
  56.3 17.1 %copy-start.9 = (f32[128,256]{1,0:T(8,128)S(1)}, f32[128,256]{1,0:T(8,128)}, u32[]{:S(2)}) copy-start(f32[128,256]{1,0:T(8,128)} %weight_ref.1) | copy-start | bytes 393220
  56.3 17.1 %copy-start.10 = (f32[256]{0:T(256)S(1)}, f32[256]{0:T(256)}, u32[]{:S(2)}) copy-start(f32[256]{0:T(256)} %param.11) | copy-start | bytes 3076
  67.6 5.7 %collective-permute-start.4 = (f32[256,128]{1,0:T(8,128)S(1)}, f32[256,128]{1,0:T(8,128)S(1)}, u32[]{:S(2)}, u32[]{:S(2)}) collective-permute-start(f32[256,128]{1,0:T(8,128)S(1)} %get-tuple-element.16), channel_id=1, source_target_pairs={{0,16},{16,0},{1,17},{17,1},{2,18},{18,2},{3,19},{19,3},{4,20},{20... | collective-permute-start | bytes 393224 | tf_op jit(solution)/shard_map/ppermute | solution.py:284
  75.2 1.4 collective-permute-start.6
  76.6 5.6 %collective-permute-start.7 = (f32[128,256]{1,0:T(8,128)S(1)}, f32[128,256]{1,0:T(8,128)S(1)}, u32[]{:S(2)}, u32[]{:S(2)}) collective-permute-start(f32[128,256]{1,0:T(8,128)S(1)} %add.39), channel_id=1, source_target_pairs={{0,2},{1,3},{2,0},{3,1},{4,6},{5,7},{6,4},{7,5},{8,10},{9,11},{10,... | collective-permute-start | bytes 393224 | tf_op jit(solution)/shard_map/ppermute | solution.py:326
  82.3 6.3 %collective-permute-start.8 = (f32[128,256]{1,0:T(8,128)S(1)}, f32[128,256]{1,0:T(8,128)S(1)}, u32[]{:S(2)}, u32[]{:S(2)}) collective-permute-start(f32[128,256]{1,0:T(8,128)S(1)} %add.40), channel_id=1, source_target_pairs={{0,4},{1,5},{2,6},{3,7},{4,0},{5,1},{6,2},{7,3},{8,12},{9,13},{10,... | collective-permute-start | bytes 393224 | tf_op jit(solution)/shard_map/ppermute | solution.py:326
  88.6 9.8 %collective-permute-start.9 = (f32[128,256]{1,0:T(8,128)S(1)}, f32[128,256]{1,0:T(8,128)S(1)}, u32[]{:S(2)}, u32[]{:S(2)}) collective-permute-start(f32[128,256]{1,0:T(8,128)S(1)} %add.41), channel_id=1, source_target_pairs={{0,8},{1,9},{2,10},{3,11},{4,12},{5,13},{6,14},{7,15},{8,0},{9,1},... | collective-permute-start | bytes 393224 | tf_op jit(solution)/shard_map/ppermute | solution.py:326
  94.7 2.0 %copy-start = (bf16[16,512,256]{2,1,0:T(8,128)(2,1)}, bf16[16,512,256]{2,1,0:T(8,128)(2,1)S(1)}, u32[]{:S(2)}) copy-start(bf16[16,512,256]{2,1,0:T(8,128)(2,1)S(1)} %own_block.1.refs_0_) | copy-start | bytes 12582916
  98.4 32.1 %collective-permute-start.10 = (f32[128,256]{1,0:T(8,128)S(1)}, f32[128,256]{1,0:T(8,128)S(1)}, u32[]{:S(2)}, u32[]{:S(2)}) collective-permute-start(f32[128,256]{1,0:T(8,128)S(1)} %add.42), channel_id=1, source_target_pairs={{0,16},{16,0},{1,17},{17,1},{2,18},{18,2},{3,19},{19,3},{4,20},{20... | collective-permute-start | bytes 393224 | tf_op jit(solution)/shard_map/ppermute | solution.py:326
  117.0 1.6 %copy-start.3 = (f32[4096,128]{1,0:T(8,128)S(1)}, f32[4096,128]{1,0:T(8,128)}, u32[]{:S(2)}) copy-start(f32[4096,128]{1,0:T(8,128)} %all-gather.5.cloned.1.call-done.refs_1_) | copy-start | bytes 6291460
  128.9 5.7 %collective-permute-start.5 = (f32[256,128]{1,0:T(8,128)S(1)}, f32[256,128]{1,0:T(8,128)S(1)}, u32[]{:S(2)}, u32[]{:S(2)}) collective-permute-start(f32[256,128]{1,0:T(8,128)S(1)} %get-tuple-element.21), channel_id=1, source_target_pairs={{0,16},{16,0},{1,17},{17,1},{2,18},{18,2},{3,19},{19,3},{4,20},{20... | collective-permute-start | bytes 393224 | tf_op jit(solution)/shard_map/ppermute | solution.py:284
  (1 other events, 0.8 us)
Sparse Core Ops, SparseCore 0:
  10.2 44.4 all-gather.2
  75.3 41.6 all-gather.4

commit v2 on v0

v2 whole, which is shorter than its diff:
```python
import functools

import jax
import jax.numpy as jnp
from jax import lax
from jax.experimental import pallas as pl
from jax.experimental.pallas import tpu as pltpu
from jax.sharding import PartitionSpec as P

TILE_SIDE = 128
TPR = 4
EPT = 64
KEEP_RATE = 0.9
CORES = 2
DEPTH = 4

f32 = jnp.float32
bf16 = jnp.bfloat16
i32 = jnp.int32
highest = lax.Precision.HIGHEST
NT = (((1,), (1,)), ((), ()))
TN = (((0,), (0,)), ((), ()))
MIB = 1 << 20


class Grid:
    def __init__(self, rows, cols, group):
        self.rows, self.cols, self.group = rows, cols, group
        self.wide = cols // (DEPTH * CORES)
        self.count = rows * cols
        self.per = group // TILE_SIDE
        self.gathered = DEPTH * CORES
        self.summed = rows * self.wide

    def place(self, me):
        col = lax.rem(me, self.cols)
        core = lax.rem(col, CORES)
        rest = lax.div(col, CORES)
        return lax.div(me, self.cols), lax.rem(rest, self.wide), lax.div(rest, self.wide), core

    def col(self, z, y, core):
        return (z * self.wide + y) * CORES + core

    def number(self, x, y, z, core):
        return x * self.cols + self.col(z, y, core)

    def all_places(self):
        return [
            (x, y, z, core)
            for x in range(self.rows)
            for z in range(DEPTH)
            for y in range(self.wide)
            for core in range(CORES)
        ]

    def pairs(self, move):
        return [(self.number(*p), self.number(*move(*p))) for p in self.all_places()]


def gelu_exact(values):
    return 0.5 * values * (1.0 + lax.erf(values * 0.7071067811865476))


def gelu_slope(values):
    return (
        0.5 * (1.0 + lax.erf(values * 0.7071067811865476))
        + values * jnp.exp(-0.5 * values * values) * 0.3989422804014327
    )


def one_hot(index_row, size):
    places = lax.broadcasted_iota(i32, (size, index_row.shape[1]), 0)
    return jnp.where(places == index_row, 1.0, 0.0).astype(bf16)


def turned_times(values, table):
    return lax.dot_general(
        values.astype(f32).astype(bf16), table, TN, preferred_element_type=f32
    ).astype(i32)


def pack_kernel(grid, cols_ref, counts_ref, pos_ref, keep_ref, lists_ref, pieces_ref):
    rows, slots = pos_ref.shape
    slot = lax.broadcasted_iota(i32, (rows, slots), 1)
    tile_of = lax.broadcasted_iota(i32, (TPR, slots), 1) // EPT
    spread = jnp.where(tile_of == lax.broadcasted_iota(i32, (TPR, slots), 0), 1.0, 0.0)
    count = turned_times(counts_ref[...], spread.astype(bf16))
    live = ((slot & (EPT - 1)) < count) & (keep_ref[...] == 1)
    pos = jnp.where(live, pos_ref[...], -1)
    lists_ref[:, :slots] = pos
    lane = lax.broadcasted_iota(i32, (TPR, TILE_SIDE), 1)
    k = lax.broadcasted_iota(i32, (TPR, TILE_SIDE), 0)
    placed = [
        turned_times(cols_ref[...], jnp.where(lane == u * TPR + k, 1.0, 0.0).astype(bf16))
        for u in range(grid.wide * grid.per)
    ]
    lists_ref[:, slots:] = placed[0]
    target = lax.shift_right_arithmetic(pos, 7)
    ones = jnp.ones((8, slots), bf16)
    degrees = []
    for t in range(rows):
        hot = one_hot(target[t : t + 1, :], TILE_SIDE)
        sums = lax.dot_general(ones, hot, NT, preferred_element_type=f32)
        degrees.append(sums[0:1, :].astype(i32))
    at_cols = grid.wide * grid.per * slots
    at_degrees = at_cols + TILE_SIDE
    for z in range(DEPTH):
        for core in range(CORES):
            parts = []
            columns = 0
            for y in range(grid.wide):
                for s in range(grid.per):
                    t = grid.col(z, y, core) * grid.per + s
                    parts.append(pos[t : t + 1, :])
                    columns = columns + placed[y * grid.per + s][t : t + 1, :]
            parts.append(columns)
            shared = jnp.concatenate(parts, axis=1)
            for y in range(grid.wide):
                t = grid.col(z, y, core) * grid.per
                own = jnp.concatenate(degrees[t : t + grid.per], axis=1)
                for x in range(grid.rows):
                    n = grid.number(x, y, z, core)
                    pieces_ref[n, :, :at_degrees] = shared
                    pieces_ref[n, :, at_degrees:] = own


def roots_kernel(grid, me_ref, edges_ref, roots_ref):
    x = lax.div(me_ref[0], grid.cols)
    at = edges_ref.shape[2] - grid.group
    counts = edges_ref[pl.ds(x * grid.cols, grid.cols), :, at:]
    root = lax.rsqrt(1.0 + jnp.sum(counts, axis=0).astype(f32))
    for g in range(grid.gathered):
        roots_ref[g] = root


def slot_columns(columns, first, slots):
    tile = lax.broadcasted_iota(i32, (1, slots), 1) // EPT
    spread = jnp.broadcast_to(columns[:, first : first + 1], (1, slots))
    for k in range(1, TPR):
        spread = jnp.where(tile == k, columns[:, first + k : first + k + 1], spread)
    return spread


def forward_block_kernel(grid, slots, me_ref, edges_ref, block_ref):
    g = pl.program_id(0)
    x, y, z, core = grid.place(me_ref[0])
    from_z = z ^ lax.div(g, CORES)
    from_core = core ^ lax.rem(g, CORES)
    at_cols = grid.wide * grid.per * slots
    for to_y in range(grid.wide):
        for to_x in range(grid.rows):
            n = grid.number(to_x, y, from_z, from_core)
            columns = edges_ref[n, :, at_cols : at_cols + TILE_SIDE]
            for s in range(grid.per):
                u = to_y * grid.per + s
                pos = edges_ref[n, :, u * slots : (u + 1) * slots]
                target = lax.shift_right_arithmetic(pos, 7)
                source = slot_columns(columns, u * TPR, slots) * TILE_SIDE + (pos & (TILE_SIDE - 1))
                hot = lax.dot_general(
                    one_hot(target, TILE_SIDE),
                    one_hot(source - x * grid.group, grid.group),
                    NT,
                    preferred_element_type=f32,
                )
                at = ((to_y * grid.rows + to_x) * grid.per + s) * TILE_SIDE
                block_ref[at : at + TILE_SIDE, :] = hot.astype(bf16)


def backward_block_kernel(grid, slots, me_ref, *refs):
    lists, block_ref = refs[:-1], refs[-1]
    g = pl.program_id(0)
    x, y, z, core = grid.place(me_ref[0])
    col = grid.col(z ^ lax.div(g, CORES), y, core ^ lax.rem(g, CORES))
    side = grid.rows * grid.group
    for k, list_ref in enumerate(lists):
        for s in range(grid.per):
            row = list_ref[pl.ds(col * grid.per + s, 1), :]
            pos = row[:, :slots]
            target = lax.shift_right_arithmetic(pos, 7)
            source = slot_columns(row[:, slots:], 0, slots) * TILE_SIDE + (pos & (TILE_SIDE - 1))
            hot = lax.dot_general(
                one_hot(source, side), one_hot(target, TILE_SIDE), NT, preferred_element_type=f32
            )
            block_ref[k * side : (k + 1) * side, s * TILE_SIDE : (s + 1) * TILE_SIDE] = hot.astype(
                bf16
            )


def spread_down(row):
    return jnp.concatenate(
        [
            jnp.broadcast_to(row[:, a : a + TILE_SIDE], (TILE_SIDE, TILE_SIDE)).T
            for a in range(0, row.shape[1], TILE_SIDE)
        ],
        axis=0,
    )


def sum_kernel(grid, scaled, me_ref, *refs):
    if scaled:
        roots_ref, refs = refs[0], refs[1:]
    block_ref, refs = refs[0], refs[1:]
    values, refs = refs[: grid.gathered], refs[grid.gathered :]
    outs, both_ref = refs[:-1], refs[-1]
    width = values[0].shape[1]
    step = pl.program_id(0)

    @pl.when(step == 0)
    def _():
        x, y, z, core = grid.place(me_ref[0])
        for g, ref in enumerate(values):
            value = ref[...]
            if scaled:
                n = (z ^ (g // CORES)) * CORES + (core ^ (g % CORES))
                value = value * spread_down(roots_ref[n])
            high = value.astype(bf16)
            rows = slice(g * grid.group, (g + 1) * grid.group)
            both_ref[rows, :width] = high
            both_ref[rows, width:] = (value - high.astype(f32)).astype(bf16)

    part = jnp.dot(block_ref[...], both_ref[...], preferred_element_type=f32)
    total = part[:, :width] + part[:, width:]
    for k, out_ref in enumerate(outs):

        @pl.when(step == k)
        def _(out_ref=out_ref):
            out_ref[...] = total


def middle_kernel(
    roots_ref,
    features_ref,
    weight_ref,
    bias_ref,
    cotangent_ref,
    drop_ref,
    *refs,
):
    sums, (hidden_ref, sent_ref, scale_ref, weight_grad_ref) = refs[:-4], refs[-4:]
    scale = spread_down(roots_ref[0])
    scale_ref[...] = scale
    total = scale * features_ref[...]
    for ref in sums:
        total = total + ref[...]
    mixed = scale * total
    weight = weight_ref[...]
    pre_act = jnp.dot(mixed, weight, precision=highest, preferred_element_type=f32) + bias_ref[...]
    dropout = drop_ref[...].astype(f32) / KEEP_RATE
    hidden_ref[...] = gelu_exact(pre_act) * dropout
    grad_pre = cotangent_ref[...] * dropout * gelu_slope(pre_act)
    sent_ref[...] = scale * lax.dot_general(
        grad_pre, weight, NT, precision=highest, preferred_element_type=f32
    )
    weight_grad_ref[...] = lax.dot_general(
        mixed, grad_pre, TN, precision=highest, preferred_element_type=f32
    )


def shards(
    features,
    weight,
    out_bias,
    cotangent,
    drop_keep,
    tile_cols,
    tile_edge_counts,
    edge_pos,
    edge_keep_bits,
):
    group, width = features.shape
    hidden = weight.shape[1]
    rows, slots = edge_pos.shape[2:]
    grid = Grid(lax.axis_size("row"), lax.axis_size("col"), group)
    both_axes = ("row", "col")
    me = lax.axis_index(both_axes).astype(i32)[None]
    smem = pl.BlockSpec(memory_space=pltpu.SMEM)
    vmem = pl.BlockSpec(memory_space=pltpu.VMEM)
    limit = pltpu.CompilerParams(vmem_limit_bytes=24 * MIB)

    def gather(values):
        blocks = []
        for dz in range(DEPTH):
            block = values
            if dz:
                block = lax.ppermute(
                    values, both_axes, grid.pairs(lambda x, y, z, c, dz=dz: (x, y, z ^ dz, c))
                )
            blocks.append(block)
        others = [
            lax.ppermute(block, both_axes, grid.pairs(lambda x, y, z, c: (x, y, z, c ^ 1)))
            for block in blocks
        ]
        return [block for pair in zip(blocks, others) for block in pair]

    sum_order = [(dx, dy) for dy in range(grid.wide) for dx in range(grid.rows)]

    def to_owners(sums):
        got = [sums[0]]
        for part, (dx, dy) in list(zip(sums, sum_order))[1:]:
            got.append(
                lax.ppermute(
                    part,
                    both_axes,
                    grid.pairs(
                        lambda x, y, z, c, dx=dx, dy=dy: (
                            (x + dx) % grid.rows,
                            (y + dy) % grid.wide,
                            z,
                            c,
                        )
                    ),
                )
            )
        return got

    piece = grid.wide * grid.per * slots + TILE_SIDE + group
    lists, pieces = pl.pallas_call(
        functools.partial(pack_kernel, grid),
        out_shape=(
            jax.ShapeDtypeStruct((rows, slots + TILE_SIDE), i32),
            jax.ShapeDtypeStruct((grid.count, 1, piece), i32),
        ),
        compiler_params=limit,
        cost_estimate=pl.CostEstimate(flops=2**21, bytes_accessed=2**17, transcendentals=0),
        name="pack",
    )(tile_cols[0, 0].T, tile_edge_counts[0, 0].T, edge_pos[0, 0], edge_keep_bits[0, 0])

    gathered = gather(features)
    edges = lax.all_to_all(pieces, both_axes, 0, 0, tiled=True)
    peer_lists = [lists] + [
        lax.ppermute(
            lists,
            both_axes,
            grid.pairs(lambda x, y, z, c, dy=dy: (x, (y - dy) % grid.wide, z, c)),
        )
        for dy in range(1, grid.wide)
    ]

    own_roots = pl.pallas_call(
        functools.partial(roots_kernel, grid),
        in_specs=[smem, vmem],
        out_shape=jax.ShapeDtypeStruct((grid.gathered, 1, group), f32),
        compiler_params=limit,
        cost_estimate=pl.CostEstimate(flops=2**14, bytes_accessed=2**16, transcendentals=0),
        name="roots",
    )(me, edges)
    roots = lax.all_to_all(
        own_roots,
        "col",
        0,
        0,
        tiled=True,
        axis_index_groups=[
            [grid.col(z, y, c) for z in range(DEPTH) for c in range(CORES)]
            for y in range(grid.wide)
        ],
    )

    side, depth = grid.summed * group, grid.gathered * group
    formation = pl.CostEstimate(
        flops=2 * rows * slots * TILE_SIDE * grid.rows * group,
        bytes_accessed=2 * side * depth,
        transcendentals=0,
    )

    def block_of(kernel, name, *operands):
        return pl.pallas_call(
            functools.partial(kernel, grid, slots),
            grid=(grid.gathered,),
            in_specs=[smem]
            + [pl.BlockSpec(a.shape, lambda g, a=a: (0,) * a.ndim) for a in operands],
            out_specs=pl.BlockSpec((side, group), lambda g: (0, g)),
            out_shape=jax.ShapeDtypeStruct((side, depth), bf16),
            compiler_params=limit,
            cost_estimate=formation,
            name=name,
        )(me, *operands)

    def block_sum(name, row_block, block, values, roots=None):
        scaled = roots is not None
        whole = pl.BlockSpec((group, width), lambda k, me_ref: (0, 0))
        return pl.pallas_call(
            functools.partial(sum_kernel, grid, scaled),
            grid_spec=pltpu.PrefetchScalarGridSpec(
                num_scalar_prefetch=1,
                grid=(grid.summed,),
                in_specs=([pl.BlockSpec(roots.shape, lambda k, me_ref: (0, 0, 0))] if scaled else [])
                + [pl.BlockSpec((group, depth), lambda k, me_ref: (row_block(k, me_ref), 0))]
                + [whole] * grid.gathered,
                out_specs=(whole,) * grid.summed,
                scratch_shapes=[pltpu.VMEM((depth, 2 * width), bf16)],
            ),
            out_shape=(jax.ShapeDtypeStruct((group, width), f32),) * grid.summed,
            compiler_params=limit,
            cost_estimate=pl.CostEstimate(
                flops=4 * side * depth * width, bytes_accessed=2 * side * depth, transcendentals=0
            ),
            name=name,
        )(me, *([roots] if scaled else []), block, *values)

    def forward_row(k, me_ref):
        x, y, _, _ = grid.place(me_ref[0])
        to_x = lax.rem(x + lax.rem(k, grid.rows), grid.rows)
        to_y = lax.rem(y + lax.div(k, grid.rows), grid.wide)
        return to_y * grid.rows + to_x

    def backward_row(k, me_ref):
        x, _, _, _ = grid.place(me_ref[0])
        to_x = lax.rem(x + lax.rem(k, grid.rows), grid.rows)
        return lax.div(k, grid.rows) * grid.rows + to_x

    forward_block = block_of(forward_block_kernel, "forward_block", edges)
    sums = to_owners(block_sum("forward_sum", forward_row, forward_block, gathered, roots))

    hidden_out, sent, scale, weight_grad = pl.pallas_call(
        middle_kernel,
        out_shape=(
            jax.ShapeDtypeStruct((group, hidden), f32),
            jax.ShapeDtypeStruct((group, width), f32),
            jax.ShapeDtypeStruct((group, width), f32),
            jax.ShapeDtypeStruct((width, hidden), f32),
        ),
        compiler_params=limit,
        cost_estimate=pl.CostEstimate(
            flops=36 * group * width * hidden, bytes_accessed=2**20, transcendentals=2**18
        ),
        name="middle",
    )(own_roots, features, weight, out_bias.reshape(1, hidden), cotangent, drop_keep, *sums)

    collected = gather(sent)
    shares = lax.all_to_all(
        weight_grad.reshape(grid.count, 1, -1), both_axes, 0, 0, tiled=True
    )
    share = jnp.sum(shares, axis=0, keepdims=True)
    weight_grad = lax.all_to_all(
        jnp.broadcast_to(share, shares.shape), both_axes, 0, 0, tiled=True
    ).reshape(width, hidden)

    if side * depth * 4 > 24 * MIB:
        peer_lists = list(lax.optimization_barrier((*peer_lists, sent))[:-1])
    backward_block = block_of(backward_block_kernel, "backward_block", *peer_lists)
    sums = to_owners(block_sum("backward_sum", backward_row, backward_block, collected))
    total = sent
    for part in sums:
        total = total + part
    return (hidden_out, scale * total, weight_grad)


def solution(mesh):
    in_specs = (
        P(("row", "col"), None),
        P(),
        P(),
        P(("row", "col"), None),
        P(("row", "col"), None),
        P("row", "col", None, None),
        P("row", "col", None, None),
        P("row", "col", None, None),
        P("row", "col", None, None),
    )
    out_specs = (P(("row", "col"), None), P(("row", "col"), None), P())
    return jax.shard_map(shards, mesh=mesh, in_specs=in_specs, out_specs=out_specs, check_vma=False)
```

time: 623 us -> 105 us (0.17)
  waiting for transfers between devices: 257 us -> 36.1 us
  matrix products: 130 us -> 0 us
  blocking collectives: 70 us -> 0 us
  local copies, waits for them, and re-layouts: 70.8 us -> 9.29 us
  other arithmetic: 61.2 us -> 1.1 us
  starting transfers between devices: 0.34 us -> 38.8 us
  Pallas kernels: 0 us -> 18.5 us
  loops' own time: 16.3 us -> 0 us
  between operations: 14.6 us -> 0.9 us
    dot_general x43 -> x0, matrix products: 130 us -> none  [the longest x8 47.8 us: backward_one_block(): jnp.einsum('bkt,bksf->tsf', placing, carried, precision=highest)]
    psum x1 -> x0, waiting for transfers between devices: 124 us -> none  [shards(): grad_weight = lax.psum(weight_term, ('row', 'col'))]
    reduce_scatter x2 -> x0, waiting for transfers between devices: 83.3 us -> none  [the longest x1 70.1 us: shards(): lax.psum_scatter(forward_row_block(feature_panels, edge_positions, surviv...]
    unnamed x1 -> x0, blocking collectives: 63 us -> none
    scatter-add x1 -> x0, other arithmetic: 57 us -> none  [shards(): jax.ops.segment_sum(surviving_mask.ravel(), row_lookup.ravel(), num_segme...]
    all_gather x1 -> x0, waiting for transfers between devices: 49.7 us -> none  [shards(): lax.all_gather(backward_scaled_rows, 'col', axis=0, tiled=True)]
    dynamic_slice x64 -> x0, local copies, waits for them, and re-layouts: 47.2 us -> none  [the longest x16 15.8 us: forward_row_block(): lax.map(forward_one_block, jnp.arange(rows_per_tile // block_row_list, dt...]
    ppermute x0 -> x21, waiting for transfers between devices: none -> 28.6 us  [the longest x6 22.3 us: gather(): lax.ppermute(values, both_axes, grid.pairs(lambda x, y, z, c, dz=dz: (x,...]
  transfers between devices with their start and end apart: 4 -> 25, of which waited for: 4 -> 7; matrix products, arithmetic and copies ran while one was open for 0% -> 2% of each run, Pallas kernels for 0% -> 12%
where the time goes in v2:
time: 105 us
  starting transfers between devices  38.8 us (37%)
  waiting for transfers between devices  36.1 us (34%)
  Pallas kernels  18.5 us (18%)
  local copies, waits for them, and re-layouts  9.29 us (9%)
  other arithmetic  1.1 us (1%)
    ppermute x6, waiting for transfers between devices, gather(): lax.ppermute(values, both_axes, grid.pairs(lambda x, y, z, c, dz=dz: (x,...  22.3 us
    pallas_call x2, Pallas kernels, block_of(): pl.pallas_call(functools.partial(kernel, grid, slots), grid=(grid.gathere...  9.56 us
    ppermute x6, starting transfers between devices, gather(): lax.ppermute(values, both_axes, grid.pairs(lambda x, y, z, c, dz=dz: (x,...  8.84 us
    all_to_all x1, waiting for transfers between devices, shards(): lax.all_to_all(jnp.broadcast_to(share, shares.shape), both_axes, 0, 0, ti...  7.5 us
    all_to_all x1, starting transfers between devices, shards(): edges = lax.all_to_all(pieces, both_axes, 0, 0, tiled=True)  7.3 us
    ppermute x6, starting transfers between devices, to_owners(): lax.ppermute(part, both_axes, grid.pairs(lambda x, y, z, c, dx=dx, dy=dy:...  7.12 us
    unnamed x22, local copies, waits for them, and re-layouts  7.08 us
    ppermute x6, waiting for transfers between devices, to_owners(): lax.ppermute(part, both_axes, grid.pairs(lambda x, y, z, c, dx=dx, dy=dy:...  6.28 us
  transfers between devices with their start and end apart: 25, of which 7 were waited for; matrix products, arithmetic and copies ran while one was open for 2% of the time, Pallas kernels for 12%

profile of v2, /device:TPU:0, one launch (start us, length us, event | category | flops | bytes accessed | tf_op | source)
XLA Modules:
  0.0 104.7 jit_solution(3723364303682750195)
XLA Ops:
  3.6 1.5 %pack.1 = (s32[32,384]{1,0:T(8,128)S(1)}, s32[32,1,1408]{2,1,0:T(1,128)}) custom-call(s32[4,32]{1,0:T(4,128)S(1)} %bitcast.12, s32[4,32]{1,0:T(4,128)S(1)} %bitcast.13, s32[32,256]{1,0:T(8,128)S(1)} %bitcast.10, s32[32,256]{1,0:T(8,128)S(1)} %bitcast.11), custom_call_target="tpu_custom_call" | custom-call | flops 2097152 | bytes 131072 | tf_op jit(solution)/shard_map/pack/pallas_call | solution.py:317
  5.1 7.3 %all-to-all-start = ((s32[32,1,1408]{2,1,0:T(1,128)}), s32[32,1,1408]{2,1,0:T(1,128)S(1)}, u32[]{:S(2)}, u32[]{:S(2)}) async-start(s32[32,1,1408]{2,1,0:T(1,128)} %get-tuple-element.17), calls=%async_computation | async-start | bytes 360448 | tf_op jit(solution)/shard_map/all_to_all | solution.py:329
  12.4 3.7 %collective-permute-start.5 = (f32[256,128]{1,0:T(8,128)}, f32[256,128]{1,0:T(8,128)S(1)}, u32[]{:S(2)}, u32[]{:S(2)}) collective-permute-start(f32[256,128]{1,0:T(8,128)} %features_ref.1), channel_id=1, source_target_pairs={{0,12},{1,13},{2,14},{3,15},{4,8},{5,9},{6,10},{7,11},{8,4},{9,5},... | collective-permute-start | bytes 393224 | tf_op jit(solution)/shard_map/ppermute | solution.py:285
  16.8 6.4 %collective-permute-done.5.refs_8_ = f32[256,128]{1,0:T(8,128)S(1)} collective-permute-done((f32[256,128]{1,0:T(8,128)}, f32[256,128]{1,0:T(8,128)S(1)}, u32[]{:S(2)}, u32[]{:S(2)}) %collective-permute-start.5) | collective-permute-done | bytes 131104 | tf_op jit(solution)/shard_map/ppermute | solution.py:285
  23.3 8.0 %collective-permute-done.3.refs_6_ = f32[256,128]{1,0:T(8,128)S(1)} collective-permute-done((f32[256,128]{1,0:T(8,128)}, f32[256,128]{1,0:T(8,128)S(1)}, u32[]{:S(2)}, u32[]{:S(2)}) %collective-permute-start.3) | collective-permute-done | bytes 131104 | tf_op jit(solution)/shard_map/ppermute | solution.py:285
  32.4 3.3 %all-to-all-start.1 = ((f32[8,1,256]{2,1,0:T(1,128)}), f32[8,1,256]{2,1,0:T(1,128)S(1)}, u32[]{:S(2)}, u32[]{:S(2)}) async-start(f32[8,1,256]{2,1,0:T(1,128)} %roots.1.roots_ref), calls=%async_computation.1 | async-start | bytes 16384 | tf_op jit(solution)/shard_map/all_to_all | solution.py:347
  35.8 5.1 %forward_block.1.refs_1_ = bf16[1024,2048]{1,0:T(8,128)(2,1)S(1)} custom-call(s32[1]{0:T(128)} %bitcast.me_ref, s32[32,1,1408]{2,1,0:T(1,128)S(1)} %all-to-all-done.edges_ref), custom_call_target="tpu_custom_call" | custom-call | flops 1073741824 | bytes 4194304 | tf_op jit(solution)/shard_map/forward_block/pallas_call | solution.py:367
  40.9 2.0 %copy-done = bf16[1024,2048]{1,0:T(8,128)(2,1)} copy-done((bf16[1024,2048]{1,0:T(8,128)(2,1)}, bf16[1024,2048]{1,0:T(8,128)(2,1)S(1)}, u32[]{:S(2)}) %copy-start) | copy-done | bytes 4194328
  42.9 2.2 %copy-done.1 = bf16[1024,2048]{1,0:T(8,128)(2,1)S(1)} copy-done((bf16[1024,2048]{1,0:T(8,128)(2,1)S(1)}, bf16[1024,2048]{1,0:T(8,128)(2,1)}, u32[]{:S(2)}) %copy-start.1) | copy-done | bytes 4194328
  45.1 2.3 %forward_sum.1 = (f32[256,128]{1,0:T(8,128)S(1)}, f32[256,128]{1,0:T(8,128)S(1)}, f32[256,128]{1,0:T(8,128)S(1)}, f32[256,128]{1,0:T(8,128)S(1)}) custom-call(s32[1]{0:T(128)} %bitcast.me_ref, f32[8,1,256]{2,1,0:T(1,128)S(1)} %all-to-all-done.1.refs_0_, bf16[1024,2048]{1,0:T(8,128)(2,1)S(1)} %copy-done.1, f32[256,128]{1,0:T(8,128)S(1)} %copy-done.2, ...), custom_call_target="tpu_custom_call" | custom-call | flops 1073741824 | bytes 4194304 | tf_op jit(solution)/shard_map/forward_sum/pallas_call | solution.py:382
  47.4 1.5 %collective-permute-start.7 = (f32[256,128]{1,0:T(8,128)S(1)}, f32[256,128]{1,0:T(8,128)S(1)}, u32[]{:S(2)}, u32[]{:S(2)}) collective-permute-start(f32[256,128]{1,0:T(8,128)S(1)} %get-tuple-element.19), channel_id=1, source_target_pairs={{0,16},{1,17},{2,18},{3,19},{4,20},{5,21},{6,22},{7,23},{8,24},{9,... | collective-permute-start | bytes 393224 | tf_op jit(solution)/shard_map/ppermute | solution.py:301
  48.9 1.5 %collective-permute-start.8 = (f32[256,128]{1,0:T(8,128)S(1)}, f32[256,128]{1,0:T(8,128)S(1)}, u32[]{:S(2)}, u32[]{:S(2)}) collective-permute-start(f32[256,128]{1,0:T(8,128)S(1)} %get-tuple-element.20), channel_id=1, source_target_pairs={{0,2},{1,3},{2,0},{3,1},{4,6},{5,7},{6,4},{7,5},{8,10},{9,11},{10,... | collective-permute-start | bytes 393224 | tf_op jit(solution)/shard_map/ppermute | solution.py:301
  51.0 2.6 %collective-permute-done.7.refs_1_ = f32[256,128]{1,0:T(8,128)S(1)} collective-permute-done((f32[256,128]{1,0:T(8,128)S(1)}, f32[256,128]{1,0:T(8,128)S(1)}, u32[]{:S(2)}, u32[]{:S(2)}) %collective-permute-start.7) | collective-permute-done | bytes 131104 | tf_op jit(solution)/shard_map/ppermute | solution.py:301
  53.6 3.6 %collective-permute-done.8.refs_2_ = f32[256,128]{1,0:T(8,128)S(1)} collective-permute-done((f32[256,128]{1,0:T(8,128)S(1)}, f32[256,128]{1,0:T(8,128)S(1)}, u32[]{:S(2)}, u32[]{:S(2)}) %collective-permute-start.8) | collective-permute-done | bytes 131104 | tf_op jit(solution)/shard_map/ppermute | solution.py:301
  57.3 2.4 %middle.1 = (f32[256,256]{1,0:T(8,128)}, f32[256,128]{1,0:T(8,128)S(1)}, f32[256,128]{1,0:T(8,128)S(1)}, f32[128,256]{1,0:T(8,128)S(1)}) custom-call(f32[8,1,256]{2,1,0:T(1,128)} %roots.1.roots_ref, f32[256,128]{1,0:T(8,128)S(1)} %copy-done.2, f32[128,256]{1,0:T(8,128)S(1)} %copy-done.5, f32[1,256]{1,0:T(1,128)S(1)} %bitcast.14, f32[256,256]{1,0:T(8,128)S(1)} %copy-done.3, ...), custom_call_target="tpu_custom_call" | custom-call | flops 301989888 | bytes 1048576 | tf_op jit(solution)/shard_map/middle/pallas_call | solution.py:415
  59.6 3.5 %collective-permute-start.16 = (f32[256,128]{1,0:T(8,128)S(1)}, f32[256,128]{1,0:T(8,128)S(1)}, u32[]{:S(2)}, u32[]{:S(2)}) collective-permute-start(f32[256,128]{1,0:T(8,128)S(1)} %get-tuple-element.24.refs_1_), channel_id=1, source_target_pairs={{0,12},{1,13},{2,14},{3,15},{4,8},{5,9},{6,10},{7,11},{8,4},{9,5},... | collective-permute-start | bytes 393224 | tf_op jit(solution)/shard_map/ppermute | solution.py:285
  65.5 2.4 %collective-permute-done.16.refs_7_ = f32[256,128]{1,0:T(8,128)S(1)} collective-permute-done((f32[256,128]{1,0:T(8,128)S(1)}, f32[256,128]{1,0:T(8,128)S(1)}, u32[]{:S(2)}, u32[]{:S(2)}) %collective-permute-start.16) | collective-permute-done | bytes 131104 | tf_op jit(solution)/shard_map/ppermute | solution.py:285
  67.9 5.6 %collective-permute-done.14.refs_5_ = f32[256,128]{1,0:T(8,128)S(1)} collective-permute-done((f32[256,128]{1,0:T(8,128)S(1)}, f32[256,128]{1,0:T(8,128)S(1)}, u32[]{:S(2)}, u32[]{:S(2)}) %collective-permute-start.14) | collective-permute-done | bytes 131104 | tf_op jit(solution)/shard_map/ppermute | solution.py:285
  74.7 3.8 %all-to-all-start.2 = ((f32[32,1,1024]{2,1,0:T(1,128)}), f32[32,1,1024]{2,1,0:T(1,128)S(1)}, u32[]{:S(2)}, u32[]{:S(2)}) async-start(f32[32,1,1024]{2,1,0:T(1,128)} %reshape.23), calls=%async_computation.2 | async-start | bytes 262144 | tf_op jit(solution)/shard_map/all_to_all | solution.py:431
  78.6 4.5 %backward_block.1.refs_0_ = bf16[1024,2048]{1,0:T(8,128)(2,1)S(1)} custom-call(s32[1]{0:T(128)} %bitcast.me_ref, s32[32,384]{1,0:T(8,128)S(1)} %get-tuple-element.25.refs_0_, s32[32,384]{1,0:T(8,128)S(1)} %collective-permute-done.10.refs_1_), custom_call_target="tpu_custom_call" | custom-call | flops 1073741824 | bytes 4194304 | tf_op jit(solution)/shard_map/backward_block/pallas_call | solution.py:367
  83.1 2.1 %backward_sum.1 = (f32[256,128]{1,0:T(8,128)S(1)}, f32[256,128]{1,0:T(8,128)S(1)}, f32[256,128]{1,0:T(8,128)S(1)}, f32[256,128]{1,0:T(8,128)S(1)}) custom-call(s32[1]{0:T(128)} %bitcast.me_ref, bf16[1024,2048]{1,0:T(8,128)(2,1)S(1)} %backward_block.1.refs_0_, f32[256,128]{1,0:T(8,128)S(1)} %get-tuple-element.24.refs_1_, ...), custom_call_target="tpu_custom_call" | custom-call | flops 1073741824 | bytes 4194304 | tf_op jit(solution)/shard_map/backward_sum/pallas_call | solution.py:382
  85.3 1.8 %collective-permute-start.18 = (f32[256,128]{1,0:T(8,128)S(1)}, f32[256,128]{1,0:T(8,128)S(1)}, u32[]{:S(2)}, u32[]{:S(2)}) collective-permute-start(f32[256,128]{1,0:T(8,128)S(1)} %get-tuple-element.27), channel_id=1, source_target_pairs={{0,16},{1,17},{2,18},{3,19},{4,20},{5,21},{6,22},{7,23},{8,24},{9,... | collective-permute-start | bytes 393224 | tf_op jit(solution)/shard_map/ppermute | solution.py:301
  89.7 5.8 %all-to-all-start.3 = ((f32[32,1,1024]{2,1,0:T(1,128)}), f32[32,1,1024]{2,1,0:T(1,128)S(1)}, u32[]{:S(2)}, u32[]{:S(2)}) async-start(f32[32,1,1024]{2,1,0:T(1,128)} %broadcast_in_dim.10), calls=%async_computation.3 | async-start | bytes 262144 | tf_op jit(solution)/shard_map/all_to_all | solution.py:435
  96.2 7.5 %all-to-all-done.3 = f32[32,1,1024]{2,1,0:T(1,128)S(1)} async-done(((f32[32,1,1024]{2,1,0:T(1,128)}), f32[32,1,1024]{2,1,0:T(1,128)S(1)}, u32[]{:S(2)}, u32[]{:S(2)}) %all-to-all-start.3) | async-done | bytes 131104 | tf_op jit(solution)/shard_map/all_to_all | solution.py:435
  (61 shorter events, 13.3 us)
Async XLA Ops:
  5.1 26.7 %all-to-all-start = ((s32[32,1,1408]{2,1,0:T(1,128)}), s32[32,1,1408]{2,1,0:T(1,128)S(1)}, u32[]{:S(2)}, u32[]{:S(2)}) async-start(s32[32,1,1408]{2,1,0:T(1,128)} %get-tuple-element.17), calls=%async_computation | async-start | bytes 360448 | tf_op jit(solution)/shard_map/all_to_all | solution.py:329
  12.4 10.9 %collective-permute-start.5 = (f32[256,128]{1,0:T(8,128)}, f32[256,128]{1,0:T(8,128)S(1)}, u32[]{:S(2)}, u32[]{:S(2)}) collective-permute-start(f32[256,128]{1,0:T(8,128)} %features_ref.1), channel_id=1, source_target_pairs={{0,12},{1,13},{2,14},{3,15},{4,8},{5,9},{6,10},{7,11},{8,4},{9,5},... | collective-permute-start | bytes 393224 | tf_op jit(solution)/shard_map/ppermute | solution.py:285
  16.1 15.2 %collective-permute-start.3 = (f32[256,128]{1,0:T(8,128)}, f32[256,128]{1,0:T(8,128)S(1)}, u32[]{:S(2)}, u32[]{:S(2)}) collective-permute-start(f32[256,128]{1,0:T(8,128)} %features_ref.1), channel_id=1, source_target_pairs={{0,8},{1,9},{2,10},{3,11},{4,12},{5,13},{6,14},{7,15},{8,0},{9,1},... | collective-permute-start | bytes 393224 | tf_op jit(solution)/shard_map/ppermute | solution.py:285
  16.1 15.2 %collective-permute-start.1 = (f32[256,128]{1,0:T(8,128)}, f32[256,128]{1,0:T(8,128)S(1)}, u32[]{:S(2)}, u32[]{:S(2)}) collective-permute-start(f32[256,128]{1,0:T(8,128)} %features_ref.1), channel_id=1, source_target_pairs={{0,4},{1,5},{2,6},{3,7},{4,0},{5,1},{6,2},{7,3},{8,12},{9,13},{10,... | collective-permute-start | bytes 393224 | tf_op jit(solution)/shard_map/ppermute | solution.py:285
  16.8 26.0 %collective-permute-start = (f32[256,128]{1,0:T(8,128)}, f32[256,128]{1,0:T(8,128)S(1)}, u32[]{:S(2)}, u32[]{:S(2)}) collective-permute-start(f32[256,128]{1,0:T(8,128)} %features_ref.1), channel_id=1, source_target_pairs={{0,1},{1,0},{2,3},{3,2},{4,5},{5,4},{6,7},{7,6},{8,9},{9,8},{10,11... | collective-permute-start | bytes 393224 | tf_op jit(solution)/shard_map/ppermute | solution.py:290
  23.3 19.6 %collective-permute-start.6 = (f32[256,128]{1,0:T(8,128)S(1)}, f32[256,128]{1,0:T(8,128)S(1)}, u32[]{:S(2)}, u32[]{:S(2)}) collective-permute-start(f32[256,128]{1,0:T(8,128)S(1)} %collective-permute-done.5.refs_8_), channel_id=1, source_target_pairs={{0,1},{1,0},{2,3},{3,2},{4,5},{5,4},{6,7},{7,6},{8,9},{9,8},{10,11... | collective-permute-start | bytes 393224 | tf_op jit(solution)/shard_map/ppermute | solution.py:290
  31.2 11.6 %collective-permute-start.4 = (f32[256,128]{1,0:T(8,128)S(1)}, f32[256,128]{1,0:T(8,128)S(1)}, u32[]{:S(2)}, u32[]{:S(2)}) collective-permute-start(f32[256,128]{1,0:T(8,128)S(1)} %collective-permute-done.3.refs_6_), channel_id=1, source_target_pairs={{0,1},{1,0},{2,3},{3,2},{4,5},{5,4},{6,7},{7,6},{8,9},{9,8},{10,11... | collective-permute-start | bytes 393224 | tf_op jit(solution)/shard_map/ppermute | solution.py:290
  31.3 11.6 %collective-permute-start.2 = (f32[256,128]{1,0:T(8,128)S(1)}, f32[256,128]{1,0:T(8,128)S(1)}, u32[]{:S(2)}, u32[]{:S(2)}) collective-permute-start(f32[256,128]{1,0:T(8,128)S(1)} %collective-permute-done.1.refs_4_), channel_id=1, source_target_pairs={{0,1},{1,0},{2,3},{3,2},{4,5},{5,4},{6,7},{7,6},{8,9},{9,8},{10,11... | collective-permute-start | bytes 393224 | tf_op jit(solution)/shard_map/ppermute | solution.py:290
  32.4 10.5 %all-to-all-start.1 = ((f32[8,1,256]{2,1,0:T(1,128)}), f32[8,1,256]{2,1,0:T(1,128)S(1)}, u32[]{:S(2)}, u32[]{:S(2)}) async-start(f32[8,1,256]{2,1,0:T(1,128)} %roots.1.roots_ref), calls=%async_computation.1 | async-start | bytes 16384 | tf_op jit(solution)/shard_map/all_to_all | solution.py:347
  48.9 8.3 %collective-permute-start.8 = (f32[256,128]{1,0:T(8,128)S(1)}, f32[256,128]{1,0:T(8,128)S(1)}, u32[]{:S(2)}, u32[]{:S(2)}) collective-permute-start(f32[256,128]{1,0:T(8,128)S(1)} %get-tuple-element.20), channel_id=1, source_target_pairs={{0,2},{1,3},{2,0},{3,1},{4,6},{5,7},{6,4},{7,5},{8,10},{9,11},{10,... | collective-permute-start | bytes 393224 | tf_op jit(solution)/shard_map/ppermute | solution.py:301
  50.4 6.8 %collective-permute-start.9 = (f32[256,128]{1,0:T(8,128)S(1)}, f32[256,128]{1,0:T(8,128)S(1)}, u32[]{:S(2)}, u32[]{:S(2)}) collective-permute-start(f32[256,128]{1,0:T(8,128)S(1)} %get-tuple-element.21), channel_id=1, source_target_pairs={{0,18},{1,19},{2,16},{3,17},{4,22},{5,23},{6,20},{7,21},{8,26},{9,... | collective-permute-start | bytes 393224 | tf_op jit(solution)/shard_map/ppermute | solution.py:301
  59.6 8.2 %collective-permute-start.16 = (f32[256,128]{1,0:T(8,128)S(1)}, f32[256,128]{1,0:T(8,128)S(1)}, u32[]{:S(2)}, u32[]{:S(2)}) collective-permute-start(f32[256,128]{1,0:T(8,128)S(1)} %get-tuple-element.24.refs_1_), channel_id=1, source_target_pairs={{0,12},{1,13},{2,14},{3,15},{4,8},{5,9},{6,10},{7,11},{8,4},{9,5},... | collective-permute-start | bytes 393224 | tf_op jit(solution)/shard_map/ppermute | solution.py:285
  63.1 10.3 %collective-permute-start.14 = (f32[256,128]{1,0:T(8,128)S(1)}, f32[256,128]{1,0:T(8,128)S(1)}, u32[]{:S(2)}, u32[]{:S(2)}) collective-permute-start(f32[256,128]{1,0:T(8,128)S(1)} %get-tuple-element.24.refs_1_), channel_id=1, source_target_pairs={{0,8},{1,9},{2,10},{3,11},{4,12},{5,13},{6,14},{7,15},{8,0},{9,1},... | collective-permute-start | bytes 393224 | tf_op jit(solution)/shard_map/ppermute | solution.py:285
  63.1 10.3 %collective-permute-start.12 = (f32[256,128]{1,0:T(8,128)S(1)}, f32[256,128]{1,0:T(8,128)S(1)}, u32[]{:S(2)}, u32[]{:S(2)}) collective-permute-start(f32[256,128]{1,0:T(8,128)S(1)} %get-tuple-element.24.refs_1_), channel_id=1, source_target_pairs={{0,4},{1,5},{2,6},{3,7},{4,0},{5,1},{6,2},{7,3},{8,12},{9,13},{10,... | collective-permute-start | bytes 393224 | tf_op jit(solution)/shard_map/ppermute | solution.py:285
  64.0 14.6 %collective-permute-start.10 = (s32[32,384]{1,0:T(8,128)S(1)}, s32[32,384]{1,0:T(8,128)S(1)}, u32[]{:S(2)}, u32[]{:S(2)}) collective-permute-start(s32[32,384]{1,0:T(8,128)S(1)} %get-tuple-element.25.refs_0_), channel_id=1, source_target_pairs={{0,2},{1,3},{2,0},{3,1},{4,6},{5,7},{6,4},{7,5},{8,10},{9,11},{10,... | collective-permute-start | bytes 147464 | tf_op jit(solution)/shard_map/ppermute | solution.py:331
  65.5 17.6 %collective-permute-start.11 = (f32[256,128]{1,0:T(8,128)S(1)}, f32[256,128]{1,0:T(8,128)S(1)}, u32[]{:S(2)}, u32[]{:S(2)}) collective-permute-start(f32[256,128]{1,0:T(8,128)S(1)} %get-tuple-element.24.refs_1_), channel_id=1, source_target_pairs={{0,1},{1,0},{2,3},{3,2},{4,5},{5,4},{6,7},{7,6},{8,9},{9,8},{10,11... | collective-permute-start | bytes 393224 | tf_op jit(solution)/shard_map/ppermute | solution.py:290
  67.9 15.2 %collective-permute-start.17 = (f32[256,128]{1,0:T(8,128)S(1)}, f32[256,128]{1,0:T(8,128)S(1)}, u32[]{:S(2)}, u32[]{:S(2)}) collective-permute-start(f32[256,128]{1,0:T(8,128)S(1)} %collective-permute-done.16.refs_7_), channel_id=1, source_target_pairs={{0,1},{1,0},{2,3},{3,2},{4,5},{5,4},{6,7},{7,6},{8,9},{9,8},{10,11... | collective-permute-start | bytes 393224 | tf_op jit(solution)/shard_map/ppermute | solution.py:290
  73.4 9.7 %collective-permute-start.15 = (f32[256,128]{1,0:T(8,128)S(1)}, f32[256,128]{1,0:T(8,128)S(1)}, u32[]{:S(2)}, u32[]{:S(2)}) collective-permute-start(f32[256,128]{1,0:T(8,128)S(1)} %collective-permute-done.14.refs_5_), channel_id=1, source_target_pairs={{0,1},{1,0},{2,3},{3,2},{4,5},{5,4},{6,7},{7,6},{8,9},{9,8},{10,11... | collective-permute-start | bytes 393224 | tf_op jit(solution)/shard_map/ppermute | solution.py:290
  73.4 9.7 %collective-permute-start.13 = (f32[256,128]{1,0:T(8,128)S(1)}, f32[256,128]{1,0:T(8,128)S(1)}, u32[]{:S(2)}, u32[]{:S(2)}) collective-permute-start(f32[256,128]{1,0:T(8,128)S(1)} %collective-permute-done.12.refs_3_), channel_id=1, source_target_pairs={{0,1},{1,0},{2,3},{3,2},{4,5},{5,4},{6,7},{7,6},{8,9},{9,8},{10,11... | collective-permute-start | bytes 393224 | tf_op jit(solution)/shard_map/ppermute | solution.py:290
  74.7 14.1 %all-to-all-start.2 = ((f32[32,1,1024]{2,1,0:T(1,128)}), f32[32,1,1024]{2,1,0:T(1,128)S(1)}, u32[]{:S(2)}, u32[]{:S(2)}) async-start(f32[32,1,1024]{2,1,0:T(1,128)} %reshape.23), calls=%async_computation.2 | async-start | bytes 262144 | tf_op jit(solution)/shard_map/all_to_all | solution.py:431
  85.3 10.2 %collective-permute-start.18 = (f32[256,128]{1,0:T(8,128)S(1)}, f32[256,128]{1,0:T(8,128)S(1)}, u32[]{:S(2)}, u32[]{:S(2)}) collective-permute-start(f32[256,128]{1,0:T(8,128)S(1)} %get-tuple-element.27), channel_id=1, source_target_pairs={{0,16},{1,17},{2,18},{3,19},{4,20},{5,21},{6,22},{7,23},{8,24},{9,... | collective-permute-start | bytes 393224 | tf_op jit(solution)/shard_map/ppermute | solution.py:301
  87.1 8.4 %collective-permute-start.19 = (f32[256,128]{1,0:T(8,128)S(1)}, f32[256,128]{1,0:T(8,128)S(1)}, u32[]{:S(2)}, u32[]{:S(2)}) collective-permute-start(f32[256,128]{1,0:T(8,128)S(1)} %get-tuple-element.28), channel_id=1, source_target_pairs={{0,2},{1,3},{2,0},{3,1},{4,6},{5,7},{6,4},{7,5},{8,10},{9,11},{10,... | collective-permute-start | bytes 393224 | tf_op jit(solution)/shard_map/ppermute | solution.py:301
  88.6 6.9 %collective-permute-start.20 = (f32[256,128]{1,0:T(8,128)S(1)}, f32[256,128]{1,0:T(8,128)S(1)}, u32[]{:S(2)}, u32[]{:S(2)}) collective-permute-start(f32[256,128]{1,0:T(8,128)S(1)} %get-tuple-element.29), channel_id=1, source_target_pairs={{0,18},{1,19},{2,16},{3,17},{4,22},{5,23},{6,20},{7,21},{8,26},{9,... | collective-permute-start | bytes 393224 | tf_op jit(solution)/shard_map/ppermute | solution.py:301
  89.7 14.1 %all-to-all-start.3 = ((f32[32,1,1024]{2,1,0:T(1,128)}), f32[32,1,1024]{2,1,0:T(1,128)S(1)}, u32[]{:S(2)}, u32[]{:S(2)}) async-start(f32[32,1,1024]{2,1,0:T(1,128)} %broadcast_in_dim.10), calls=%async_computation.3 | async-start | bytes 262144 | tf_op jit(solution)/shard_map/all_to_all | solution.py:435
  (12 other events, 141.5 us)

commit v3 on v2

--- a/solution.py
+++ b/solution.py
@@ -92,7 +92,7 @@
     k = lax.broadcasted_iota(i32, (TPR, TILE_SIDE), 0)
     placed = [
         turned_times(cols_ref[...], jnp.where(lane == u * TPR + k, 1.0, 0.0).astype(bf16))
-        for u in range(grid.wide * grid.per)
+        for u in range(grid.per)
     ]
     lists_ref[:, slots:] = placed[0]
     target = lax.shift_right_arithmetic(pos, 7)
@@ -103,18 +103,15 @@
         sums = lax.dot_general(ones, hot, NT, preferred_element_type=f32)
         degrees.append(sums[0:1, :].astype(i32))
     at_cols = grid.wide * grid.per * slots
-    at_degrees = at_cols + TILE_SIDE
+    at_degrees = at_cols + grid.wide * TILE_SIDE
     for z in range(DEPTH):
         for core in range(CORES):
-            parts = []
-            columns = 0
+            parts, columns = [], []
             for y in range(grid.wide):
-                for s in range(grid.per):
-                    t = grid.col(z, y, core) * grid.per + s
-                    parts.append(pos[t : t + 1, :])
-                    columns = columns + placed[y * grid.per + s][t : t + 1, :]
-            parts.append(columns)
-            shared = jnp.concatenate(parts, axis=1)
+                t = grid.col(z, y, core) * grid.per
+                parts += [pos[t + s : t + s + 1, :] for s in range(grid.per)]
+                columns.append(sum(placed[s][t + s : t + s + 1, :] for s in range(grid.per)))
+            shared = jnp.concatenate(parts + columns, axis=1)
             for y in range(grid.wide):
                 t = grid.col(z, y, core) * grid.per
                 own = jnp.concatenate(degrees[t : t + grid.per], axis=1)
@@ -141,29 +138,63 @@
     return spread
 
 
-def forward_block_kernel(grid, slots, me_ref, edges_ref, block_ref):
-    g = pl.program_id(0)
+def split_values(grid, values, both_ref, scale_of=None):
+    width = values[0].shape[1]
+    for g, ref in enumerate(values):
+        value = ref[: grid.group, :]
+        if scale_of is not None:
+            value = value * spread_down(scale_of(g))
+        high = value.astype(bf16)
+        rows = slice(g * grid.group, (g + 1) * grid.group)
+        both_ref[rows, :width] = high
+        both_ref[rows, width:] = (value - high.astype(f32)).astype(bf16)
+
+
+def forward_kernel(grid, slots, me_ref, roots_ref, edges_ref, *refs):
+    values, outs, both_ref = refs[: grid.gathered], refs[grid.gathered : -1], refs[-1]
+    width = values[0].shape[1]
+    step = pl.program_id(0)
     x, y, z, core = grid.place(me_ref[0])
-    from_z = z ^ lax.div(g, CORES)
-    from_core = core ^ lax.rem(g, CORES)
-    at_cols = grid.wide * grid.per * slots
-    for to_y in range(grid.wide):
-        for to_x in range(grid.rows):
-            n = grid.number(to_x, y, from_z, from_core)
-            columns = edges_ref[n, :, at_cols : at_cols + TILE_SIDE]
-            for s in range(grid.per):
-                u = to_y * grid.per + s
-                pos = edges_ref[n, :, u * slots : (u + 1) * slots]
-                target = lax.shift_right_arithmetic(pos, 7)
-                source = slot_columns(columns, u * TPR, slots) * TILE_SIDE + (pos & (TILE_SIDE - 1))
-                hot = lax.dot_general(
+
+    @pl.when(step == 0)
+    def _():
+        split_values(
+            grid,
+            values,
+            both_ref,
+            lambda g: roots_ref[(z ^ (g // CORES)) * CORES + (core ^ (g % CORES))],
+        )
+
+    to_x = lax.rem(x + lax.rem(step, grid.rows), grid.rows)
+    to_y = lax.rem(y + lax.div(step, grid.rows), grid.wide)
+    at_cols = grid.wide * grid.per * slots + to_y * TILE_SIDE
+    total = jnp.zeros((grid.group, 2 * width), f32)
+    for g in range(grid.gathered):
+        n = grid.number(to_x, y, z ^ (g // CORES), core ^ (g % CORES))
+        columns = edges_ref[n, :, pl.ds(pl.multiple_of(at_cols, TILE_SIDE), TILE_SIDE)]
+        hots = []
+        for s in range(grid.per):
+            at = pl.multiple_of((to_y * grid.per + s) * slots, TILE_SIDE)
+            pos = edges_ref[n, :, pl.ds(at, slots)]
+            target = lax.shift_right_arithmetic(pos, 7)
+            source = slot_columns(columns, s * TPR, slots) * TILE_SIDE + (pos & (TILE_SIDE - 1))
+            hots.append(
+                lax.dot_general(
                     one_hot(target, TILE_SIDE),
                     one_hot(source - x * grid.group, grid.group),
                     NT,
                     preferred_element_type=f32,
                 )
-                at = ((to_y * grid.rows + to_x) * grid.per + s) * TILE_SIDE
-                block_ref[at : at + TILE_SIDE, :] = hot.astype(bf16)
+            )
+        block = jnp.concatenate(hots, axis=0).astype(bf16)
+        rows = slice(g * grid.group, (g + 1) * grid.group)
+        total = total + jnp.dot(block, both_ref[rows, :], preferred_element_type=f32)
+    total = total[:, :width] + total[:, width:]
+    for k, out_ref in enumerate(outs):
+
+        @pl.when(step == k)
+        def _(out_ref=out_ref):
+            out_ref[...] = total
 
 
 def backward_block_kernel(grid, slots, me_ref, *refs):
@@ -196,27 +227,24 @@
     )
 
 
-def sum_kernel(grid, scaled, me_ref, *refs):
-    if scaled:
-        roots_ref, refs = refs[0], refs[1:]
-    block_ref, refs = refs[0], refs[1:]
-    values, refs = refs[: grid.gathered], refs[grid.gathered :]
-    outs, both_ref = refs[:-1], refs[-1]
+def backward_sum_kernel(grid, me_ref, block_ref, *refs):
+    values, outs = refs[: grid.gathered], refs[grid.gathered : -2]
+    shares_ref, both_ref = refs[-2:]
     width = values[0].shape[1]
     step = pl.program_id(0)
 
     @pl.when(step == 0)
     def _():
         x, y, z, core = grid.place(me_ref[0])
+        split_values(grid, values, both_ref)
         for g, ref in enumerate(values):
-            value = ref[...]
-            if scaled:
-                n = (z ^ (g // CORES)) * CORES + (core ^ (g % CORES))
-                value = value * spread_down(roots_ref[n])
-            high = value.astype(bf16)
-            rows = slice(g * grid.group, (g + 1) * grid.group)
-            both_ref[rows, :width] = high
-            both_ref[rows, width:] = (value - high.astype(f32)).astype(bf16)
+            n = (z ^ (g // CORES)) * CORES + (core ^ (g % CORES))
+            shares_ref[n] = ref[grid.group :, :]
+        share = shares_ref[0]
+        for n in range(1, grid.gathered):
+            share = share + shares_ref[n]
+        for out_ref in outs:
+            out_ref[grid.group :, :] = share
 
     part = jnp.dot(block_ref[...], both_ref[...], preferred_element_type=f32)
     total = part[:, :width] + part[:, width:]
@@ -224,10 +252,37 @@
 
         @pl.when(step == k)
         def _(out_ref=out_ref):
-            out_ref[...] = total
+            out_ref[: grid.group, :] = total
+
+
+def finish_kernel(grid, me_ref, scale_ref, sent_ref, *refs):
+    sums, (features_grad_ref, share_ref, shares_ref) = refs[:-3], refs[-3:]
+    x, y, z, core = grid.place(me_ref[0])
+    total = sent_ref[: grid.group, :]
+    for k, ref in enumerate(sums):
+        total = total + ref[: grid.group, :]
+        from_x = lax.rem(x + grid.rows - k % grid.rows, grid.rows)
+        from_y = lax.rem(y + grid.wide - k // grid.rows, grid.wide)
+        shares_ref[from_y * grid.rows + from_x] = ref[grid.group :, :]
+    features_grad_ref[...] = scale_ref[...] * total
+    share = shares_ref[0]
+    for n in range(1, grid.summed):
+        share = share + shares_ref[n]
+    share_ref[...] = share
+
+
+def join_kernel(grid, me_ref, *refs):
+    quarters, out_ref = refs[:-1], refs[-1]
+    _, _, z, _ = grid.place(me_ref[0])
+    half = quarters[0].shape[0] // 2
+    for dz, ref in enumerate(quarters):
+        rows = pl.ds(pl.multiple_of((z ^ dz) * half, 8), half)
+        out_ref[rows, :] = jnp.concatenate([ref[:half, :], ref[half:, :]], axis=1)
 
 
 def middle_kernel(
+    grid,
+    me_ref,
     roots_ref,
     features_ref,
     weight_ref,
@@ -236,7 +291,9 @@
     drop_ref,
     *refs,
 ):
-    sums, (hidden_ref, sent_ref, scale_ref, weight_grad_ref) = refs[:-4], refs[-4:]
+    sums, refs = refs[: grid.summed], refs[grid.summed :]
+    (hidden_ref, scale_ref), sent_refs, weight_grad_ref = refs[:2], refs[2:-1], refs[-1]
+    _, _, z, _ = grid.place(me_ref[0])
     scale = spread_down(roots_ref[0])
     scale_ref[...] = scale
     total = scale * features_ref[...]
@@ -248,12 +305,19 @@
     dropout = drop_ref[...].astype(f32) / KEEP_RATE
     hidden_ref[...] = gelu_exact(pre_act) * dropout
     grad_pre = cotangent_ref[...] * dropout * gelu_slope(pre_act)
-    sent_ref[...] = scale * lax.dot_general(
+    sent = scale * lax.dot_general(
         grad_pre, weight, NT, precision=highest, preferred_element_type=f32
     )
     weight_grad_ref[...] = lax.dot_general(
         mixed, grad_pre, TN, precision=highest, preferred_element_type=f32
     )
+    width = features_ref.shape[1]
+    quarter = width // DEPTH
+    for dz, sent_ref in enumerate(sent_refs):
+        share = weight_grad_ref[pl.ds(pl.multiple_of((z ^ dz) * quarter, 8), quarter), :]
+        sent_ref[: grid.group, :] = sent
+        sent_ref[grid.group : grid.group + quarter, :] = share[:, :width]
+        sent_ref[grid.group + quarter :, :] = share[:, width:]
 
 
 def shards(
@@ -277,20 +341,25 @@
     vmem = pl.BlockSpec(memory_space=pltpu.VMEM)
     limit = pltpu.CompilerParams(vmem_limit_bytes=24 * MIB)
 
-    def gather(values):
-        blocks = []
-        for dz in range(DEPTH):
-            block = values
-            if dz:
-                block = lax.ppermute(
-                    values, both_axes, grid.pairs(lambda x, y, z, c, dz=dz: (x, y, z ^ dz, c))
-                )
-            blocks.append(block)
+    def along_z(blocks):
+        return [blocks[0]] + [
+            lax.ppermute(
+                blocks[dz], both_axes, grid.pairs(lambda x, y, z, c, dz=dz: (x, y, z ^ dz, c))
+            )
+            for dz in range(1, DEPTH)
+        ]
+
+    def to_cores(blocks):
         others = [
             lax.ppermute(block, both_axes, grid.pairs(lambda x, y, z, c: (x, y, z, c ^ 1)))
             for block in blocks
         ]
         return [block for pair in zip(blocks, others) for block in pair]
+
+    def backward_row(k, me_ref):
+        x, _, _, _ = grid.place(me_ref[0])
+        to_x = lax.rem(x + lax.rem(k, grid.rows), grid.rows)
+        return lax.div(k, grid.rows) * grid.rows + to_x
 
     sum_order = [(dx, dy) for dy in range(grid.wide) for dx in range(grid.rows)]
 
@@ -313,7 +382,7 @@
             )
         return got
 
-    piece = grid.wide * grid.per * slots + TILE_SIDE + group
+    piece = grid.wide * grid.per * slots + grid.wide * TILE_SIDE + group
     lists, pieces = pl.pallas_call(
         functools.partial(pack_kernel, grid),
         out_shape=(
@@ -321,12 +390,11 @@
             jax.ShapeDtypeStruct((grid.count, 1, piece), i32),
         ),
         compiler_params=limit,
-        cost_estimate=pl.CostEstimate(flops=2**21, bytes_accessed=2**17, transcendentals=0),
+        cost_estimate=pl.CostEstimate(flops=2**31, bytes_accessed=2**23, transcendentals=0),
         name="pack",
     )(tile_cols[0, 0].T, tile_edge_counts[0, 0].T, edge_pos[0, 0], edge_keep_bits[0, 0])
 
-    gathered = gather(features)
-    edges = lax.all_to_all(pieces, both_axes, 0, 0, tiled=True)
+    along = along_z([features] * DEPTH)
     peer_lists = [lists] + [
         lax.ppermute(
             lists,
@@ -335,6 +403,20 @@
         )
         for dy in range(1, grid.wide)
     ]
+    side, depth = grid.summed * group, grid.gathered * group
+    backward_block = pl.pallas_call(
+        functools.partial(backward_block_kernel, grid, slots),
+        grid=(grid.gathered,),
+        in_specs=[smem] + [pl.BlockSpec(lists.shape, lambda g: (0, 0))] * grid.wide,
+        out_specs=pl.BlockSpec((side, group), lambda g: (0, g)),
+        out_shape=jax.ShapeDtypeStruct((side, depth), bf16),
+        compiler_params=limit,
+        cost_estimate=pl.CostEstimate(flops=2**16, bytes_accessed=2**16, transcendentals=0),
+        name="backward_block",
+    )(me, *peer_lists)
+    *along, pieces, backward_block = lax.optimization_barrier((*along, pieces, backward_block))
+    edges = lax.all_to_all(pieces, both_axes, 0, 0, tiled=True)
+    gathered = to_cores(along)
 
     own_roots = pl.pallas_call(
         functools.partial(roots_kernel, grid),
@@ -356,94 +438,86 @@
         ],
     )
 
-    side, depth = grid.summed * group, grid.gathered * group
-    formation = pl.CostEstimate(
-        flops=2 * rows * slots * TILE_SIDE * grid.rows * group,
-        bytes_accessed=2 * side * depth,
-        transcendentals=0,
-    )
-
-    def block_of(kernel, name, *operands):
-        return pl.pallas_call(
-            functools.partial(kernel, grid, slots),
-            grid=(grid.gathered,),
-            in_specs=[smem]
-            + [pl.BlockSpec(a.shape, lambda g, a=a: (0,) * a.ndim) for a in operands],
-            out_specs=pl.BlockSpec((side, group), lambda g: (0, g)),
-            out_shape=jax.ShapeDtypeStruct((side, depth), bf16),
-            compiler_params=limit,
-            cost_estimate=formation,
-            name=name,
-        )(me, *operands)
-
-    def block_sum(name, row_block, block, values, roots=None):
-        scaled = roots is not None
-        whole = pl.BlockSpec((group, width), lambda k, me_ref: (0, 0))
-        return pl.pallas_call(
-            functools.partial(sum_kernel, grid, scaled),
-            grid_spec=pltpu.PrefetchScalarGridSpec(
-                num_scalar_prefetch=1,
-                grid=(grid.summed,),
-                in_specs=([pl.BlockSpec(roots.shape, lambda k, me_ref: (0, 0, 0))] if scaled else [])
-                + [pl.BlockSpec((group, depth), lambda k, me_ref: (row_block(k, me_ref), 0))]
-                + [whole] * grid.gathered,
-                out_specs=(whole,) * grid.summed,
-                scratch_shapes=[pltpu.VMEM((depth, 2 * width), bf16)],
-            ),
-            out_shape=(jax.ShapeDtypeStruct((group, width), f32),) * grid.summed,
-            compiler_params=limit,
-            cost_estimate=pl.CostEstimate(
-                flops=4 * side * depth * width, bytes_accessed=2 * side * depth, transcendentals=0
-            ),
-            name=name,
-        )(me, *([roots] if scaled else []), block, *values)
-
-    def forward_row(k, me_ref):
-        x, y, _, _ = grid.place(me_ref[0])
-        to_x = lax.rem(x + lax.rem(k, grid.rows), grid.rows)
-        to_y = lax.rem(y + lax.div(k, grid.rows), grid.wide)
-        return to_y * grid.rows + to_x
-
-    def backward_row(k, me_ref):
-        x, _, _, _ = grid.place(me_ref[0])
-        to_x = lax.rem(x + lax.rem(k, grid.rows), grid.rows)
-        return lax.div(k, grid.rows) * grid.rows + to_x
-
-    forward_block = block_of(forward_block_kernel, "forward_block", edges)
-    sums = to_owners(block_sum("forward_sum", forward_row, forward_block, gathered, roots))
-
-    hidden_out, sent, scale, weight_grad = pl.pallas_call(
-        middle_kernel,
+    def whole(*shape):
+        return pl.BlockSpec(shape, lambda k: (0,) * len(shape))
+
+    sums = pl.pallas_call(
+        functools.partial(forward_kernel, grid, slots),
+        grid=(grid.summed,),
+        in_specs=[smem, whole(*roots.shape), whole(*edges.shape)]
+        + [whole(group, width)] * grid.gathered,
+        out_specs=(whole(group, width),) * grid.summed,
+        out_shape=(jax.ShapeDtypeStruct((group, width), f32),) * grid.summed,
+        scratch_shapes=[pltpu.VMEM((depth, 2 * width), bf16)],
+        compiler_params=limit,
+        cost_estimate=pl.CostEstimate(
+            flops=8 * side * depth * width, bytes_accessed=depth * width * 4, transcendentals=0
+        ),
+        name="forward",
+    )(me, roots, edges, *gathered)
+    sums = to_owners(sums)
+
+    tall = group + hidden // DEPTH
+    tall_shape = jax.ShapeDtypeStruct((tall, width), f32)
+    hidden_out, scale, *sent = pl.pallas_call(
+        functools.partial(middle_kernel, grid),
+        in_specs=[smem] + [vmem] * (6 + grid.summed),
         out_shape=(
             jax.ShapeDtypeStruct((group, hidden), f32),
             jax.ShapeDtypeStruct((group, width), f32),
-            jax.ShapeDtypeStruct((group, width), f32),
-            jax.ShapeDtypeStruct((width, hidden), f32),
-        ),
+        )
+        + (tall_shape,) * DEPTH,
+        scratch_shapes=[pltpu.VMEM((width, hidden), f32)],
         compiler_params=limit,
         cost_estimate=pl.CostEstimate(
             flops=36 * group * width * hidden, bytes_accessed=2**20, transcendentals=2**18
         ),
         name="middle",
-    )(own_roots, features, weight, out_bias.reshape(1, hidden), cotangent, drop_keep, *sums)
-
-    collected = gather(sent)
-    shares = lax.all_to_all(
-        weight_grad.reshape(grid.count, 1, -1), both_axes, 0, 0, tiled=True
-    )
-    share = jnp.sum(shares, axis=0, keepdims=True)
-    weight_grad = lax.all_to_all(
-        jnp.broadcast_to(share, shares.shape), both_axes, 0, 0, tiled=True
-    ).reshape(width, hidden)
-
-    if side * depth * 4 > 24 * MIB:
-        peer_lists = list(lax.optimization_barrier((*peer_lists, sent))[:-1])
-    backward_block = block_of(backward_block_kernel, "backward_block", *peer_lists)
-    sums = to_owners(block_sum("backward_sum", backward_row, backward_block, collected))
-    total = sent
-    for part in sums:
-        total = total + part
-    return (hidden_out, scale * total, weight_grad)
+    )(me, own_roots, features, weight, out_bias.reshape(1, hidden), cotangent, drop_keep, *sums)
+
+    collected = to_cores(along_z(sent))
+    sums = pl.pallas_call(
+        functools.partial(backward_sum_kernel, grid),
+        grid_spec=pltpu.PrefetchScalarGridSpec(
+            num_scalar_prefetch=1,
+            grid=(grid.summed,),
+            in_specs=[pl.BlockSpec((group, depth), lambda k, me_ref: (backward_row(k, me_ref), 0))]
+            + [pl.BlockSpec((tall, width), lambda k, me_ref: (0, 0))] * grid.gathered,
+            out_specs=(pl.BlockSpec((tall, width), lambda k, me_ref: (0, 0)),) * grid.summed,
+            scratch_shapes=[
+                pltpu.VMEM((grid.gathered, tall - group, width), f32),
+                pltpu.VMEM((depth, 2 * width), bf16),
+            ],
+        ),
+        out_shape=(tall_shape,) * grid.summed,
+        compiler_params=limit,
+        cost_estimate=pl.CostEstimate(
+            flops=4 * side * depth * width, bytes_accessed=2 * side * depth, transcendentals=0
+        ),
+        name="backward_sum",
+    )(me, backward_block, *collected)
+    sums = to_owners(sums)
+    grad_features, share = pl.pallas_call(
+        functools.partial(finish_kernel, grid),
+        in_specs=[smem] + [vmem] * (2 + grid.summed),
+        out_shape=(
+            jax.ShapeDtypeStruct((group, width), f32),
+            jax.ShapeDtypeStruct((tall - group, width), f32),
+        ),
+        scratch_shapes=[pltpu.VMEM((grid.summed, tall - group, width), f32)],
+        compiler_params=limit,
+        cost_estimate=pl.CostEstimate(flops=2**18, bytes_accessed=2**19, transcendentals=0),
+        name="finish",
+    )(me, scale, sent[0], *sums)
+    grad_weight = pl.pallas_call(
+        functools.partial(join_kernel, grid),
+        in_specs=[smem] + [vmem] * DEPTH,
+        out_shape=jax.ShapeDtypeStruct((width, hidden), f32),
+        compiler_params=limit,
+        cost_estimate=pl.CostEstimate(flops=0, bytes_accessed=2**18, transcendentals=0),
+        name="join",
+    )(me, *along_z([share] * DEPTH))
+    return (hidden_out, grad_features, grad_weight)
 
 
 def solution(mesh):

time: 105 us -> 102 us (0.971)
  waiting for transfers between devices: 36.1 us -> 42.5 us
  starting transfers between devices: 38.8 us -> 34.3 us
  local copies, waits for them, and re-layouts: 9.29 us -> 4.88 us
  other arithmetic: 1.1 us -> 0 us
    all_to_all x2 -> x0, starting transfers between devices: 9.67 us -> none  [the longest x1 5.83 us: shards(): lax.all_to_all(jnp.broadcast_to(share, shares.shape), both_axes, 0, 0, ti...]
    all_to_all x1, waiting for transfers between devices: 0.01 us -> 7.78 us  [shards(): edges = lax.all_to_all(pieces, both_axes, 0, 0, tiled=True)]
    ppermute x14 -> x17, waiting for transfers between devices: 22.3 us -> 14.7 us  [the longest x9 13.6 us: along_z(): lax.ppermute(blocks[dz], both_axes, grid.pairs(lambda x, y, z, c, dz=dz:...]
    all_to_all x2 -> x0, waiting for transfers between devices: 7.5 us -> none  [the longest x1 7.5 us: shards(): lax.all_to_all(jnp.broadcast_to(share, shares.shape), both_axes, 0, 0, ti...]
    ppermute x14 -> x17, starting transfers between devices: 9.87 us -> 16.1 us  [the longest x9 14.5 us: along_z(): lax.ppermute(blocks[dz], both_axes, grid.pairs(lambda x, y, z, c, dz=dz:...]
    ppermute x6, waiting for transfers between devices: 6.28 us -> 12.1 us  [to_owners(): lax.ppermute(part, both_axes, grid.pairs(lambda x, y, z, c, dx=dx, dy=dy:...]
    all_to_all x1, waiting for transfers between devices: 0.01 us -> 5.57 us  [shards(): lax.all_to_all(own_roots, 'col', 0, 0, tiled=True, axis_index_groups=[[gr...]
    ppermute x1, waiting for transfers between devices: 0.01 us -> 2.43 us  [shards(): lax.ppermute(lists, both_axes, grid.pairs(lambda x, y, z, c, dy=dy: (x, (...]
  transfers between devices with their start and end apart: 25 -> 26, of which waited for: 7 -> 16; matrix products, arithmetic and copies ran while one was open for 2% -> 0% of each run, Pallas kernels for 12% -> 7%
where the time goes in v3:
time: 102 us; the launch traced here: 101 us
  waiting for transfers between devices  42.5 us (42%)
  starting transfers between devices  34.3 us (34%)
  Pallas kernels  18.7 us (18%)
  local copies, waits for them, and re-layouts  4.88 us (5%)
    ppermute x9, starting transfers between devices, along_z(): lax.ppermute(blocks[dz], both_axes, grid.pairs(lambda x, y, z, c, dz=dz:...  14.5 us
    ppermute x9, waiting for transfers between devices, along_z(): lax.ppermute(blocks[dz], both_axes, grid.pairs(lambda x, y, z, c, dz=dz:...  13.6 us
    ppermute x6, waiting for transfers between devices, to_owners(): lax.ppermute(part, both_axes, grid.pairs(lambda x, y, z, c, dx=dx, dy=dy:...  12.1 us
    all_to_all x1, waiting for transfers between devices, shards(): edges = lax.all_to_all(pieces, both_axes, 0, 0, tiled=True)  7.78 us
    ppermute x6, starting transfers between devices, to_owners(): lax.ppermute(part, both_axes, grid.pairs(lambda x, y, z, c, dx=dx, dy=dy:...  7.11 us
    pallas_call x1, Pallas kernels, shards(): pl.pallas_call(functools.partial(forward_kernel, grid, slots), grid=(grid...  6.18 us
    all_to_all x1, starting transfers between devices, shards(): edges = lax.all_to_all(pieces, both_axes, 0, 0, tiled=True)  6 us
    all_to_all x1, waiting for transfers between devices, shards(): lax.all_to_all(own_roots, 'col', 0, 0, tiled=True, axis_index_groups=[[gr...  5.57 us
  transfers between devices with their start and end apart: 26, of which 16 were waited for; matrix products, arithmetic and copies ran while one was open for 0% of the time, Pallas kernels for 7%

profile of v3, /device:TPU:0, one launch (start us, length us, event | category | flops | bytes accessed | tf_op | source)
XLA Modules:
  0.0 101.1 jit_solution(438767078051724849)
XLA Ops:
  0.6 5.1 %collective-permute-start.2 = (f32[256,128]{1,0:T(8,128)}, f32[256,128]{1,0:T(8,128)S(1)}, u32[]{:S(2)}, u32[]{:S(2)}) collective-permute-start(f32[256,128]{1,0:T(8,128)} %features_ref.1), channel_id=1, source_target_pairs={{0,12},{1,13},{2,14},{3,15},{4,8},{5,9},{6,10},{7,11},{8,4},{9,5},... | collective-permute-start | bytes 393224 | tf_op jit(solution)/shard_map/ppermute | solution.py:346
  10.8 1.7 %collective-permute-start.3 = (s32[32,384]{1,0:T(8,128)S(1)}, s32[32,384]{1,0:T(8,128)S(1)}, u32[]{:S(2)}, u32[]{:S(2)}) collective-permute-start(s32[32,384]{1,0:T(8,128)S(1)} %get-tuple-element.28.refs_0_), channel_id=1, source_target_pairs={{0,2},{1,3},{2,0},{3,1},{4,6},{5,7},{6,4},{7,5},{8,10},{9,11},{10,... | collective-permute-start | bytes 147464 | tf_op jit(solution)/shard_map/ppermute | solution.py:399
  12.5 2.4 %collective-permute-done.3.refs_1_ = s32[32,384]{1,0:T(8,128)S(1)} collective-permute-done((s32[32,384]{1,0:T(8,128)S(1)}, s32[32,384]{1,0:T(8,128)S(1)}, u32[]{:S(2)}, u32[]{:S(2)}) %collective-permute-start.3) | collective-permute-done | bytes 49184 | tf_op jit(solution)/shard_map/ppermute | solution.py:399
  14.9 4.4 %backward_block.1.block_ref = bf16[1024,2048]{1,0:T(8,128)(2,1)S(1)} custom-call(s32[1]{0:T(128)} %bitcast.me_ref, s32[32,384]{1,0:T(8,128)S(1)} %get-tuple-element.28.refs_0_, s32[32,384]{1,0:T(8,128)S(1)} %collective-permute-done.3.refs_1_), custom_call_target="tpu_custom_call" | custom-call | flops 65536 | bytes 65536 | tf_op jit(solution)/shard_map/backward_block/pallas_call | solution.py:407
  19.3 2.0 %copy-done = bf16[1024,2048]{1,0:T(8,128)(2,1)} copy-done((bf16[1024,2048]{1,0:T(8,128)(2,1)}, bf16[1024,2048]{1,0:T(8,128)(2,1)S(1)}, u32[]{:S(2)}) %copy-start) | copy-done | bytes 4194328
  21.4 6.0 %all-to-all-start = ((s32[32,1,1536]{2,1,0:T(1,128)}), s32[32,1,1536]{2,1,0:T(1,128)S(1)}, u32[]{:S(2)}, u32[]{:S(2)}) async-start(s32[32,1,1536]{2,1,0:T(1,128)} %get-tuple-element.29), calls=%async_computation | async-start | bytes 393216 | tf_op jit(solution)/shard_map/all_to_all | solution.py:418
  28.5 7.8 %all-to-all-done.edges_ref = s32[32,1,1536]{2,1,0:T(1,128)S(1)} async-done(((s32[32,1,1536]{2,1,0:T(1,128)}), s32[32,1,1536]{2,1,0:T(1,128)S(1)}, u32[]{:S(2)}, u32[]{:S(2)}) %all-to-all-start) | async-done | bytes 196640 | tf_op jit(solution)/shard_map/all_to_all | solution.py:418
  36.9 3.4 %all-to-all-start.1 = ((f32[8,1,256]{2,1,0:T(1,128)}), f32[8,1,256]{2,1,0:T(1,128)S(1)}, u32[]{:S(2)}, u32[]{:S(2)}) async-start(f32[8,1,256]{2,1,0:T(1,128)} %roots.1.roots_ref), calls=%async_computation.1 | async-start | bytes 16384 | tf_op jit(solution)/shard_map/all_to_all | solution.py:429
  40.3 5.6 %all-to-all-done.1.roots_ref = f32[8,1,256]{2,1,0:T(1,128)S(1)} async-done(((f32[8,1,256]{2,1,0:T(1,128)}), f32[8,1,256]{2,1,0:T(1,128)S(1)}, u32[]{:S(2)}, u32[]{:S(2)}) %all-to-all-start.1) | async-done | bytes 8224 | tf_op jit(solution)/shard_map/all_to_all | solution.py:429
  45.8 6.2 %forward.1 = (f32[256,128]{1,0:T(8,128)S(1)}, f32[256,128]{1,0:T(8,128)S(1)}, f32[256,128]{1,0:T(8,128)S(1)}, f32[256,128]{1,0:T(8,128)S(1)}) custom-call(s32[1]{0:T(128)} %bitcast.me_ref, f32[8,1,256]{2,1,0:T(1,128)S(1)} %all-to-all-done.1.roots_ref, s32[32,1,1536]{2,1,0:T(1,128)S(1)} %all-to-all-done.edges_ref, f32[256,128]{1,0:T(8,128)S(1)} %copy-done.4, ...), custom_call_target="tpu_custom_call" | custom-call | flops 2147483648 | bytes 1048576 | tf_op jit(solution)/shard_map/forward/pallas_call | solution.py:444
  54.1 1.5 %collective-permute-start.10 = (f32[256,128]{1,0:T(8,128)S(1)}, f32[256,128]{1,0:T(8,128)S(1)}, u32[]{:S(2)}, u32[]{:S(2)}) collective-permute-start(f32[256,128]{1,0:T(8,128)S(1)} %get-tuple-element.37), channel_id=1, source_target_pairs={{0,18},{1,19},{2,16},{3,17},{4,22},{5,23},{6,20},{7,21},{8,26},{9,... | collective-permute-start | bytes 393224 | tf_op jit(solution)/shard_map/ppermute | solution.py:370
  55.6 2.7 %collective-permute-done.8.refs_1_ = f32[256,128]{1,0:T(8,128)S(1)} collective-permute-done((f32[256,128]{1,0:T(8,128)S(1)}, f32[256,128]{1,0:T(8,128)S(1)}, u32[]{:S(2)}, u32[]{:S(2)}) %collective-permute-start.8) | collective-permute-done | bytes 131104 | tf_op jit(solution)/shard_map/ppermute | solution.py:370
  59.4 1.6 %collective-permute-done.10.refs_3_ = f32[256,128]{1,0:T(8,128)S(1)} collective-permute-done((f32[256,128]{1,0:T(8,128)S(1)}, f32[256,128]{1,0:T(8,128)S(1)}, u32[]{:S(2)}, u32[]{:S(2)}) %collective-permute-start.10) | collective-permute-done | bytes 131104 | tf_op jit(solution)/shard_map/ppermute | solution.py:370
  61.0 2.4 %middle.1 = (f32[256,256]{1,0:T(8,128)}, f32[256,128]{1,0:T(8,128)S(1)}, f32[320,128]{1,0:T(8,128)S(1)}, f32[320,128]{1,0:T(8,128)S(1)}, f32[320,128]{1,0:T(8,128)S(1)}, /*index=5*/f32[320,128]{1,0:T(8,128)S(1)}) custom-call(s32[1]{0:T(128)} %bitcast.me_ref, f32[8,1,256]{2,1,0:T(1,128)} %roots.1.roots_ref, f32[256,128]{1,0:T(8,128)S(1)} %copy-done.4, ...), custom_call_target="tpu_custom_call" | custom-call | flops 301989888 | bytes 1048576 | tf_op jit(solution)/shard_map/middle/pallas_call | solution.py:462
  64.8 3.0 %collective-permute-start.16 = (f32[320,128]{1,0:T(8,128)S(1)}, f32[320,128]{1,0:T(8,128)S(1)}, u32[]{:S(2)}, u32[]{:S(2)}) collective-permute-start(f32[320,128]{1,0:T(8,128)S(1)} %get-tuple-element.44), channel_id=1, source_target_pairs={{0,12},{1,13},{2,14},{3,15},{4,8},{5,9},{6,10},{7,11},{8,4},{9,5},... | collective-permute-start | bytes 491528 | tf_op jit(solution)/shard_map/ppermute | solution.py:346
  67.8 3.0 %collective-permute-done.12.refs_2_ = f32[320,128]{1,0:T(8,128)S(1)} collective-permute-done((f32[320,128]{1,0:T(8,128)S(1)}, f32[320,128]{1,0:T(8,128)S(1)}, u32[]{:S(2)}, u32[]{:S(2)}) %collective-permute-start.12) | collective-permute-done | bytes 163872 | tf_op jit(solution)/shard_map/ppermute | solution.py:346
  70.7 7.6 %collective-permute-done.14.refs_4_ = f32[320,128]{1,0:T(8,128)S(1)} collective-permute-done((f32[320,128]{1,0:T(8,128)S(1)}, f32[320,128]{1,0:T(8,128)S(1)}, u32[]{:S(2)}, u32[]{:S(2)}) %collective-permute-start.14) | collective-permute-done | bytes 163872 | tf_op jit(solution)/shard_map/ppermute | solution.py:346
  79.9 2.2 %backward_sum.1 = (f32[320,128]{1,0:T(8,128)S(1)}, f32[320,128]{1,0:T(8,128)S(1)}, f32[320,128]{1,0:T(8,128)S(1)}, f32[320,128]{1,0:T(8,128)S(1)}) custom-call(s32[1]{0:T(128)} %bitcast.me_ref, bf16[1024,2048]{1,0:T(8,128)(2,1)S(1)} %copy-done.1, f32[320,128]{1,0:T(8,128)S(1)} %get-tuple-element.40.refs_0_.sent_ref, ...), custom_call_target="tpu_custom_call" | custom-call | flops 1073741824 | bytes 4194304 | tf_op jit(solution)/shard_map/backward_sum/pallas_call | solution.py:479
  84.1 1.5 %collective-permute-start.20 = (f32[320,128]{1,0:T(8,128)S(1)}, f32[320,128]{1,0:T(8,128)S(1)}, u32[]{:S(2)}, u32[]{:S(2)}) collective-permute-start(f32[320,128]{1,0:T(8,128)S(1)} %get-tuple-element.48), channel_id=1, source_target_pairs={{0,18},{1,19},{2,16},{3,17},{4,22},{5,23},{6,20},{7,21},{8,26},{9,... | collective-permute-start | bytes 491528 | tf_op jit(solution)/shard_map/ppermute | solution.py:370
  85.6 3.5 %collective-permute-done.18.refs_1_ = f32[320,128]{1,0:T(8,128)S(1)} collective-permute-done((f32[320,128]{1,0:T(8,128)S(1)}, f32[320,128]{1,0:T(8,128)S(1)}, u32[]{:S(2)}, u32[]{:S(2)}) %collective-permute-start.18) | collective-permute-done | bytes 163872 | tf_op jit(solution)/shard_map/ppermute | solution.py:370
  89.2 3.1 %collective-permute-done.20.refs_3_ = f32[320,128]{1,0:T(8,128)S(1)} collective-permute-done((f32[320,128]{1,0:T(8,128)S(1)}, f32[320,128]{1,0:T(8,128)S(1)}, u32[]{:S(2)}, u32[]{:S(2)}) %collective-permute-start.20) | collective-permute-done | bytes 163872 | tf_op jit(solution)/shard_map/ppermute | solution.py:370
  93.1 1.6 %collective-permute-start.23 = (f32[64,128]{1,0:T(8,128)S(1)}, f32[64,128]{1,0:T(8,128)S(1)}, u32[]{:S(2)}, u32[]{:S(2)}) collective-permute-start(f32[64,128]{1,0:T(8,128)S(1)} %get-tuple-element.50.refs_0_), channel_id=1, source_target_pairs={{0,12},{1,13},{2,14},{3,15},{4,8},{5,9},{6,10},{7,11},{8,4},{9,5},... | collective-permute-start | bytes 98312 | tf_op jit(solution)/shard_map/ppermute | solution.py:346
  94.6 1.9 %collective-permute-start.22 = (f32[64,128]{1,0:T(8,128)S(1)}, f32[64,128]{1,0:T(8,128)S(1)}, u32[]{:S(2)}, u32[]{:S(2)}) collective-permute-start(f32[64,128]{1,0:T(8,128)S(1)} %get-tuple-element.50.refs_0_), channel_id=1, source_target_pairs={{0,8},{1,9},{2,10},{3,11},{4,12},{5,13},{6,14},{7,15},{8,0},{9,1},... | collective-permute-start | bytes 98312 | tf_op jit(solution)/shard_map/ppermute | solution.py:346
  97.4 1.6 %collective-permute-done.23.refs_3_ = f32[64,128]{1,0:T(8,128)S(1)} collective-permute-done((f32[64,128]{1,0:T(8,128)S(1)}, f32[64,128]{1,0:T(8,128)S(1)}, u32[]{:S(2)}, u32[]{:S(2)}) %collective-permute-start.23) | collective-permute-done | bytes 32800 | tf_op jit(solution)/shard_map/ppermute | solution.py:346
  (58 shorter events, 18.7 us)
Async XLA Ops:
  0.6 20.7 %collective-permute-start.2 = (f32[256,128]{1,0:T(8,128)}, f32[256,128]{1,0:T(8,128)S(1)}, u32[]{:S(2)}, u32[]{:S(2)}) collective-permute-start(f32[256,128]{1,0:T(8,128)} %features_ref.1), channel_id=1, source_target_pairs={{0,12},{1,13},{2,14},{3,15},{4,8},{5,9},{6,10},{7,11},{8,4},{9,5},... | collective-permute-start | bytes 393224 | tf_op jit(solution)/shard_map/ppermute | solution.py:346
  5.7 15.6 %collective-permute-start.1 = (f32[256,128]{1,0:T(8,128)}, f32[256,128]{1,0:T(8,128)S(1)}, u32[]{:S(2)}, u32[]{:S(2)}) collective-permute-start(f32[256,128]{1,0:T(8,128)} %features_ref.1), channel_id=1, source_target_pairs={{0,8},{1,9},{2,10},{3,11},{4,12},{5,13},{6,14},{7,15},{8,0},{9,1},... | collective-permute-start | bytes 393224 | tf_op jit(solution)/shard_map/ppermute | solution.py:346
  5.7 15.6 %collective-permute-start = (f32[256,128]{1,0:T(8,128)}, f32[256,128]{1,0:T(8,128)S(1)}, u32[]{:S(2)}, u32[]{:S(2)}) collective-permute-start(f32[256,128]{1,0:T(8,128)} %features_ref.1), channel_id=1, source_target_pairs={{0,4},{1,5},{2,6},{3,7},{4,0},{5,1},{6,2},{7,3},{8,12},{9,13},{10,... | collective-permute-start | bytes 393224 | tf_op jit(solution)/shard_map/ppermute | solution.py:346
  10.8 4.1 %collective-permute-start.3 = (s32[32,384]{1,0:T(8,128)S(1)}, s32[32,384]{1,0:T(8,128)S(1)}, u32[]{:S(2)}, u32[]{:S(2)}) collective-permute-start(s32[32,384]{1,0:T(8,128)S(1)} %get-tuple-element.28.refs_0_), channel_id=1, source_target_pairs={{0,2},{1,3},{2,0},{3,1},{4,6},{5,7},{6,4},{7,5},{8,10},{9,11},{10,... | collective-permute-start | bytes 147464 | tf_op jit(solution)/shard_map/ppermute | solution.py:399
  21.4 14.9 %all-to-all-start = ((s32[32,1,1536]{2,1,0:T(1,128)}), s32[32,1,1536]{2,1,0:T(1,128)S(1)}, u32[]{:S(2)}, u32[]{:S(2)}) async-start(s32[32,1,1536]{2,1,0:T(1,128)} %get-tuple-element.29), calls=%async_computation | async-start | bytes 393216 | tf_op jit(solution)/shard_map/all_to_all | solution.py:418
  27.4 12.8 %collective-permute-start.4 = (f32[256,128]{1,0:T(8,128)S(1)}, f32[256,128]{1,0:T(8,128)S(1)}, u32[]{:S(2)}, u32[]{:S(2)}) collective-permute-start(f32[256,128]{1,0:T(8,128)S(1)} %copy-done.4), channel_id=1, source_target_pairs={{0,1},{1,0},{2,3},{3,2},{4,5},{5,4},{6,7},{7,6},{8,9},{9,8},{10,11... | collective-permute-start | bytes 393224 | tf_op jit(solution)/shard_map/ppermute | solution.py:354
  27.7 12.5 %collective-permute-start.5 = (f32[256,128]{1,0:T(8,128)S(1)}, f32[256,128]{1,0:T(8,128)S(1)}, u32[]{:S(2)}, u32[]{:S(2)}) collective-permute-start(f32[256,128]{1,0:T(8,128)S(1)} %collective-permute-done.refs_2_), channel_id=1, source_target_pairs={{0,1},{1,0},{2,3},{3,2},{4,5},{5,4},{6,7},{7,6},{8,9},{9,8},{10,11... | collective-permute-start | bytes 393224 | tf_op jit(solution)/shard_map/ppermute | solution.py:354
  28.0 12.3 %collective-permute-start.6 = (f32[256,128]{1,0:T(8,128)S(1)}, f32[256,128]{1,0:T(8,128)S(1)}, u32[]{:S(2)}, u32[]{:S(2)}) collective-permute-start(f32[256,128]{1,0:T(8,128)S(1)} %collective-permute-done.1.refs_4_), channel_id=1, source_target_pairs={{0,1},{1,0},{2,3},{3,2},{4,5},{5,4},{6,7},{7,6},{8,9},{9,8},{10,11... | collective-permute-start | bytes 393224 | tf_op jit(solution)/shard_map/ppermute | solution.py:354
  28.2 12.0 %collective-permute-start.7 = (f32[256,128]{1,0:T(8,128)S(1)}, f32[256,128]{1,0:T(8,128)S(1)}, u32[]{:S(2)}, u32[]{:S(2)}) collective-permute-start(f32[256,128]{1,0:T(8,128)S(1)} %collective-permute-done.2.refs_6_), channel_id=1, source_target_pairs={{0,1},{1,0},{2,3},{3,2},{4,5},{5,4},{6,7},{7,6},{8,9},{9,8},{10,11... | collective-permute-start | bytes 393224 | tf_op jit(solution)/shard_map/ppermute | solution.py:354
  36.9 9.0 %all-to-all-start.1 = ((f32[8,1,256]{2,1,0:T(1,128)}), f32[8,1,256]{2,1,0:T(1,128)S(1)}, u32[]{:S(2)}, u32[]{:S(2)}) async-start(f32[8,1,256]{2,1,0:T(1,128)} %roots.1.roots_ref), calls=%async_computation.1 | async-start | bytes 16384 | tf_op jit(solution)/shard_map/all_to_all | solution.py:429
  52.0 6.2 %collective-permute-start.8 = (f32[256,128]{1,0:T(8,128)S(1)}, f32[256,128]{1,0:T(8,128)S(1)}, u32[]{:S(2)}, u32[]{:S(2)}) collective-permute-start(f32[256,128]{1,0:T(8,128)S(1)} %get-tuple-element.35), channel_id=1, source_target_pairs={{0,16},{1,17},{2,18},{3,19},{4,20},{5,21},{6,22},{7,23},{8,24},{9,... | collective-permute-start | bytes 393224 | tf_op jit(solution)/shard_map/ppermute | solution.py:370
  53.1 6.3 %collective-permute-start.9 = (f32[256,128]{1,0:T(8,128)S(1)}, f32[256,128]{1,0:T(8,128)S(1)}, u32[]{:S(2)}, u32[]{:S(2)}) collective-permute-start(f32[256,128]{1,0:T(8,128)S(1)} %get-tuple-element.36), channel_id=1, source_target_pairs={{0,2},{1,3},{2,0},{3,1},{4,6},{5,7},{6,4},{7,5},{8,10},{9,11},{10,... | collective-permute-start | bytes 393224 | tf_op jit(solution)/shard_map/ppermute | solution.py:370
  54.1 6.9 %collective-permute-start.10 = (f32[256,128]{1,0:T(8,128)S(1)}, f32[256,128]{1,0:T(8,128)S(1)}, u32[]{:S(2)}, u32[]{:S(2)}) collective-permute-start(f32[256,128]{1,0:T(8,128)S(1)} %get-tuple-element.37), channel_id=1, source_target_pairs={{0,18},{1,19},{2,16},{3,17},{4,22},{5,23},{6,20},{7,21},{8,26},{9,... | collective-permute-start | bytes 393224 | tf_op jit(solution)/shard_map/ppermute | solution.py:370
  63.4 7.4 %collective-permute-start.12 = (f32[320,128]{1,0:T(8,128)S(1)}, f32[320,128]{1,0:T(8,128)S(1)}, u32[]{:S(2)}, u32[]{:S(2)}) collective-permute-start(f32[320,128]{1,0:T(8,128)S(1)} %get-tuple-element.42), channel_id=1, source_target_pairs={{0,4},{1,5},{2,6},{3,7},{4,0},{5,1},{6,2},{7,3},{8,12},{9,13},{10,... | collective-permute-start | bytes 491528 | tf_op jit(solution)/shard_map/ppermute | solution.py:346
  64.0 14.3 %collective-permute-start.14 = (f32[320,128]{1,0:T(8,128)S(1)}, f32[320,128]{1,0:T(8,128)S(1)}, u32[]{:S(2)}, u32[]{:S(2)}) collective-permute-start(f32[320,128]{1,0:T(8,128)S(1)} %get-tuple-element.43), channel_id=1, source_target_pairs={{0,8},{1,9},{2,10},{3,11},{4,12},{5,13},{6,14},{7,15},{8,0},{9,1},... | collective-permute-start | bytes 491528 | tf_op jit(solution)/shard_map/ppermute | solution.py:346
  64.8 13.5 %collective-permute-start.16 = (f32[320,128]{1,0:T(8,128)S(1)}, f32[320,128]{1,0:T(8,128)S(1)}, u32[]{:S(2)}, u32[]{:S(2)}) collective-permute-start(f32[320,128]{1,0:T(8,128)S(1)} %get-tuple-element.44), channel_id=1, source_target_pairs={{0,12},{1,13},{2,14},{3,15},{4,8},{5,9},{6,10},{7,11},{8,4},{9,5},... | collective-permute-start | bytes 491528 | tf_op jit(solution)/shard_map/ppermute | solution.py:346
  67.7 11.1 %collective-permute-start.11 = (f32[320,128]{1,0:T(8,128)S(1)}, f32[320,128]{1,0:T(8,128)S(1)}, u32[]{:S(2)}, u32[]{:S(2)}) collective-permute-start(f32[320,128]{1,0:T(8,128)S(1)} %get-tuple-element.40.refs_0_.sent_ref), channel_id=1, source_target_pairs={{0,1},{1,0},{2,3},{3,2},{4,5},{5,4},{6,7},{7,6},{8,9},{9,8},{10,11... | collective-permute-start | bytes 491528 | tf_op jit(solution)/shard_map/ppermute | solution.py:354
  70.7 8.1 %collective-permute-start.13 = (f32[320,128]{1,0:T(8,128)S(1)}, f32[320,128]{1,0:T(8,128)S(1)}, u32[]{:S(2)}, u32[]{:S(2)}) collective-permute-start(f32[320,128]{1,0:T(8,128)S(1)} %collective-permute-done.12.refs_2_), channel_id=1, source_target_pairs={{0,1},{1,0},{2,3},{3,2},{4,5},{5,4},{6,7},{7,6},{8,9},{9,8},{10,11... | collective-permute-start | bytes 491528 | tf_op jit(solution)/shard_map/ppermute | solution.py:354
  82.1 7.1 %collective-permute-start.18 = (f32[320,128]{1,0:T(8,128)S(1)}, f32[320,128]{1,0:T(8,128)S(1)}, u32[]{:S(2)}, u32[]{:S(2)}) collective-permute-start(f32[320,128]{1,0:T(8,128)S(1)} %get-tuple-element.46), channel_id=1, source_target_pairs={{0,16},{1,17},{2,18},{3,19},{4,20},{5,21},{6,22},{7,23},{8,24},{9,... | collective-permute-start | bytes 491528 | tf_op jit(solution)/shard_map/ppermute | solution.py:370
  82.6 6.6 %collective-permute-start.19 = (f32[320,128]{1,0:T(8,128)S(1)}, f32[320,128]{1,0:T(8,128)S(1)}, u32[]{:S(2)}, u32[]{:S(2)}) collective-permute-start(f32[320,128]{1,0:T(8,128)S(1)} %get-tuple-element.47), channel_id=1, source_target_pairs={{0,2},{1,3},{2,0},{3,1},{4,6},{5,7},{6,4},{7,5},{8,10},{9,11},{10,... | collective-permute-start | bytes 491528 | tf_op jit(solution)/shard_map/ppermute | solution.py:370
  84.1 8.2 %collective-permute-start.20 = (f32[320,128]{1,0:T(8,128)S(1)}, f32[320,128]{1,0:T(8,128)S(1)}, u32[]{:S(2)}, u32[]{:S(2)}) collective-permute-start(f32[320,128]{1,0:T(8,128)S(1)} %get-tuple-element.48), channel_id=1, source_target_pairs={{0,18},{1,19},{2,16},{3,17},{4,22},{5,23},{6,20},{7,21},{8,26},{9,... | collective-permute-start | bytes 491528 | tf_op jit(solution)/shard_map/ppermute | solution.py:370
  93.1 6.0 %collective-permute-start.23 = (f32[64,128]{1,0:T(8,128)S(1)}, f32[64,128]{1,0:T(8,128)S(1)}, u32[]{:S(2)}, u32[]{:S(2)}) collective-permute-start(f32[64,128]{1,0:T(8,128)S(1)} %get-tuple-element.50.refs_0_), channel_id=1, source_target_pairs={{0,12},{1,13},{2,14},{3,15},{4,8},{5,9},{6,10},{7,11},{8,4},{9,5},... | collective-permute-start | bytes 98312 | tf_op jit(solution)/shard_map/ppermute | solution.py:346
  94.6 4.8 %collective-permute-start.22 = (f32[64,128]{1,0:T(8,128)S(1)}, f32[64,128]{1,0:T(8,128)S(1)}, u32[]{:S(2)}, u32[]{:S(2)}) collective-permute-start(f32[64,128]{1,0:T(8,128)S(1)} %get-tuple-element.50.refs_0_), channel_id=1, source_target_pairs={{0,8},{1,9},{2,10},{3,11},{4,12},{5,13},{6,14},{7,15},{8,0},{9,1},... | collective-permute-start | bytes 98312 | tf_op jit(solution)/shard_map/ppermute | solution.py:346
  96.6 3.9 %collective-permute-start.21 = (f32[64,128]{1,0:T(8,128)S(1)}, f32[64,128]{1,0:T(8,128)S(1)}, u32[]{:S(2)}, u32[]{:S(2)}) collective-permute-start(f32[64,128]{1,0:T(8,128)S(1)} %get-tuple-element.50.refs_0_), channel_id=1, source_target_pairs={{0,4},{1,5},{2,6},{3,7},{4,0},{5,1},{6,2},{7,3},{8,12},{9,13},{10,... | collective-permute-start | bytes 98312 | tf_op jit(solution)/shard_map/ppermute | solution.py:346
  (13 other events, 217.0 us)

commit v4 on v3

--- a/solution.py
+++ b/solution.py
@@ -79,55 +79,59 @@
     ).astype(i32)
 
 
-def pack_kernel(grid, cols_ref, counts_ref, pos_ref, keep_ref, lists_ref, pieces_ref):
+def pack_kernel(grid, me_ref, *refs):
+    hbm_refs, lists_ref, sent_refs, refs = refs[:4], refs[4], refs[5 : 5 + DEPTH], refs[5 + DEPTH :]
+    counts_ref, vmem_refs, sem = refs[0], refs[1:5], refs[5]
+    copies = [
+        pltpu.make_async_copy(a, b, sem.at[n]) for n, (a, b) in enumerate(zip(hbm_refs, vmem_refs))
+    ]
+    for copy in copies:
+        copy.start()
+    for copy in copies:
+        copy.wait()
+    cols_ref, tile_counts_ref, pos_ref, keep_ref = vmem_refs
     rows, slots = pos_ref.shape
     slot = lax.broadcasted_iota(i32, (rows, slots), 1)
     tile_of = lax.broadcasted_iota(i32, (TPR, slots), 1) // EPT
     spread = jnp.where(tile_of == lax.broadcasted_iota(i32, (TPR, slots), 0), 1.0, 0.0)
-    count = turned_times(counts_ref[...], spread.astype(bf16))
+    count = turned_times(tile_counts_ref[...], spread.astype(bf16))
     live = ((slot & (EPT - 1)) < count) & (keep_ref[...] == 1)
     pos = jnp.where(live, pos_ref[...], -1)
     lists_ref[:, :slots] = pos
     lane = lax.broadcasted_iota(i32, (TPR, TILE_SIDE), 1)
     k = lax.broadcasted_iota(i32, (TPR, TILE_SIDE), 0)
-    placed = [
-        turned_times(cols_ref[...], jnp.where(lane == u * TPR + k, 1.0, 0.0).astype(bf16))
-        for u in range(grid.per)
-    ]
-    lists_ref[:, slots:] = placed[0]
+    lists_ref[:, slots:] = turned_times(cols_ref[...], jnp.where(lane == k, 1.0, 0.0).astype(bf16))
     target = lax.shift_right_arithmetic(pos, 7)
     ones = jnp.ones((8, slots), bf16)
-    degrees = []
     for t in range(rows):
         hot = one_hot(target[t : t + 1, :], TILE_SIDE)
         sums = lax.dot_general(ones, hot, NT, preferred_element_type=f32)
-        degrees.append(sums[0:1, :].astype(i32))
-    at_cols = grid.wide * grid.per * slots
-    at_degrees = at_cols + grid.wide * TILE_SIDE
-    for z in range(DEPTH):
-        for core in range(CORES):
-            parts, columns = [], []
-            for y in range(grid.wide):
-                t = grid.col(z, y, core) * grid.per
-                parts += [pos[t + s : t + s + 1, :] for s in range(grid.per)]
-                columns.append(sum(placed[s][t + s : t + s + 1, :] for s in range(grid.per)))
-            shared = jnp.concatenate(parts + columns, axis=1)
-            for y in range(grid.wide):
-                t = grid.col(z, y, core) * grid.per
-                own = jnp.concatenate(degrees[t : t + grid.per], axis=1)
-                for x in range(grid.rows):
-                    n = grid.number(x, y, z, core)
-                    pieces_ref[n, :, :at_degrees] = shared
-                    pieces_ref[n, :, at_degrees:] = own
-
-
-def roots_kernel(grid, me_ref, edges_ref, roots_ref):
-    x = lax.div(me_ref[0], grid.cols)
-    at = edges_ref.shape[2] - grid.group
-    counts = edges_ref[pl.ds(x * grid.cols, grid.cols), :, at:]
-    root = lax.rsqrt(1.0 + jnp.sum(counts, axis=0).astype(f32))
-    for g in range(grid.gathered):
-        roots_ref[g] = root
+        counts_ref[t : t + 1, :] = sums[0:1, :].astype(i32)
+    _, _, z, _ = grid.place(me_ref[0])
+    plane = rows // DEPTH
+    for dz, sent_ref in enumerate(sent_refs):
+        at = pl.multiple_of((z ^ dz) * plane, 8)
+        sent_ref[:, : slots + TILE_SIDE] = lists_ref[pl.ds(at, plane), :]
+        for q in range(DEPTH):
+            lanes = slice(slots + (q + 1) * TILE_SIDE, slots + (q + 2) * TILE_SIDE)
+            sent_ref[:, lanes] = counts_ref[q * plane : (q + 1) * plane, :]
+
+
+def relay_kernel(wide, *refs):
+    got, (both_ref, lists_ref, counts_ref) = refs[:-3], refs[-3:]
+    plane = got[0].shape[0]
+    for dz, ref in enumerate(got):
+        rows = slice(dz * plane, (dz + 1) * plane)
+        lists_ref[rows, :] = ref[:, :wide]
+        both_ref[rows, :wide] = ref[:, :wide]
+    for q in range(DEPTH):
+        lanes = slice(wide + q * TILE_SIDE, wide + (q + 1) * TILE_SIDE)
+        count = got[0][:, lanes]
+        for ref in got[1:]:
+            count = count + ref[:, lanes]
+        rows = slice(q * plane, (q + 1) * plane)
+        counts_ref[rows, :] = count
+        both_ref[rows, wide:] = count
 
 
 def slot_columns(columns, first, slots):
@@ -143,41 +147,54 @@
     for g, ref in enumerate(values):
         value = ref[: grid.group, :]
         if scale_of is not None:
-            value = value * spread_down(scale_of(g))
+            value = value * scale_of(g)
         high = value.astype(bf16)
         rows = slice(g * grid.group, (g + 1) * grid.group)
         both_ref[rows, :width] = high
         both_ref[rows, width:] = (value - high.astype(f32)).astype(bf16)
 
 
-def forward_kernel(grid, slots, me_ref, roots_ref, edges_ref, *refs):
-    values, outs, both_ref = refs[: grid.gathered], refs[grid.gathered : -1], refs[-1]
+def forward_kernel(grid, slots, me_ref, *refs):
+    core_refs, refs = refs[:CORES], refs[CORES:]
+    list_refs, refs = refs[: CORES * (grid.rows - 1)], refs[CORES * (grid.rows - 1) :]
+    count_refs, refs = refs[: CORES * (grid.wide - 1)], refs[CORES * (grid.wide - 1) :]
+    values, refs = refs[: grid.gathered], refs[grid.gathered :]
+    scale_ref, outs, (lists_ref, root_ref, both_ref) = refs[0], refs[1:-3], refs[-3:]
     width = values[0].shape[1]
     step = pl.program_id(0)
     x, y, z, core = grid.place(me_ref[0])
+    wide = slots + TILE_SIDE
 
     @pl.when(step == 0)
     def _():
-        split_values(
-            grid,
-            values,
-            both_ref,
-            lambda g: roots_ref[(z ^ (g // CORES)) * CORES + (core ^ (g % CORES))],
-        )
-
-    to_x = lax.rem(x + lax.rem(step, grid.rows), grid.rows)
-    to_y = lax.rem(y + lax.div(step, grid.rows), grid.wide)
-    at_cols = grid.wide * grid.per * slots + to_y * TILE_SIDE
+        count = sum(ref[:, wide:] for ref in core_refs)
+        for ref in count_refs:
+            count = count + ref[...]
+        root_ref[...] = lax.rsqrt(1.0 + count.astype(f32))
+        for n, ref in enumerate(core_refs):
+            lists_ref[n] = ref[:, :wide]
+        for n, ref in enumerate(list_refs):
+            lists_ref[CORES + n] = ref[...]
+
+        def scale_of(g):
+            at = grid.col(z ^ (g // CORES), y, core ^ (g % CORES)) * grid.per
+            return spread_down([root_ref[pl.ds(at + s, 1), :] for s in range(grid.per)])
+
+        scale_ref[...] = scale_of(0)
+        split_values(grid, values, both_ref, scale_of)
+
+    dx, dy = lax.rem(step, grid.rows), lax.div(step, grid.rows)
+    to_y = lax.rem(y + dy, grid.wide)
+    plane = grid.wide * CORES * grid.per
     total = jnp.zeros((grid.group, 2 * width), f32)
     for g in range(grid.gathered):
-        n = grid.number(to_x, y, z ^ (g // CORES), core ^ (g % CORES))
-        columns = edges_ref[n, :, pl.ds(pl.multiple_of(at_cols, TILE_SIDE), TILE_SIDE)]
         hots = []
         for s in range(grid.per):
-            at = pl.multiple_of((to_y * grid.per + s) * slots, TILE_SIDE)
-            pos = edges_ref[n, :, pl.ds(at, slots)]
+            at = (g // CORES) * plane + (to_y * CORES + core) * grid.per + s
+            row = lists_ref[dx * CORES + g % CORES, pl.ds(at, 1), :]
+            pos = row[:, :slots]
             target = lax.shift_right_arithmetic(pos, 7)
-            source = slot_columns(columns, s * TPR, slots) * TILE_SIDE + (pos & (TILE_SIDE - 1))
+            source = slot_columns(row[:, slots:], 0, slots) * TILE_SIDE + (pos & (TILE_SIDE - 1))
             hots.append(
                 lax.dot_general(
                     one_hot(target, TILE_SIDE),
@@ -217,13 +234,9 @@
             )
 
 
-def spread_down(row):
+def spread_down(rows):
     return jnp.concatenate(
-        [
-            jnp.broadcast_to(row[:, a : a + TILE_SIDE], (TILE_SIDE, TILE_SIDE)).T
-            for a in range(0, row.shape[1], TILE_SIDE)
-        ],
-        axis=0,
+        [jnp.broadcast_to(row, (TILE_SIDE, TILE_SIDE)).T for row in rows], axis=0
     )
 
 
@@ -283,7 +296,7 @@
 def middle_kernel(
     grid,
     me_ref,
-    roots_ref,
+    scale_ref,
     features_ref,
     weight_ref,
     bias_ref,
@@ -292,10 +305,9 @@
     *refs,
 ):
     sums, refs = refs[: grid.summed], refs[grid.summed :]
-    (hidden_ref, scale_ref), sent_refs, weight_grad_ref = refs[:2], refs[2:-1], refs[-1]
+    hidden_ref, sent_refs, weight_grad_ref = refs[0], refs[1:-1], refs[-1]
     _, _, z, _ = grid.place(me_ref[0])
-    scale = spread_down(roots_ref[0])
-    scale_ref[...] = scale
+    scale = scale_ref[...]
     total = scale * features_ref[...]
     for ref in sums:
         total = total + ref[...]
@@ -382,28 +394,98 @@
             )
         return got
 
-    piece = grid.wide * grid.per * slots + grid.wide * TILE_SIDE + group
-    lists, pieces = pl.pallas_call(
+    wide = slots + TILE_SIDE
+    plane = rows // DEPTH
+    raw = [tile_cols[0, 0].T, tile_edge_counts[0, 0].T, edge_pos[0, 0], edge_keep_bits[0, 0]]
+    lists, *planes = pl.pallas_call(
         functools.partial(pack_kernel, grid),
+        in_specs=[smem] + [pl.BlockSpec(memory_space=pltpu.HBM)] * 4,
+        out_shape=(jax.ShapeDtypeStruct((rows, wide), i32),)
+        + (jax.ShapeDtypeStruct((plane, wide + DEPTH * TILE_SIDE), i32),) * DEPTH,
+        scratch_shapes=[pltpu.VMEM((rows, TILE_SIDE), i32)]
+        + [pltpu.VMEM(a.shape, i32) for a in raw]
+        + [pltpu.SemaphoreType.DMA((4,))],
+        compiler_params=limit,
+        cost_estimate=pl.CostEstimate(flops=2**21, bytes_accessed=2**17, transcendentals=0),
+        name="pack",
+    )(me, *raw)
+
+    def from_peer(value, move):
+        return lax.ppermute(value, both_axes, [(b, a) for a, b in grid.pairs(move)])
+
+    along = along_z([features] * DEPTH)
+    both, plane_lists, counts = pl.pallas_call(
+        functools.partial(relay_kernel, wide),
         out_shape=(
-            jax.ShapeDtypeStruct((rows, slots + TILE_SIDE), i32),
-            jax.ShapeDtypeStruct((grid.count, 1, piece), i32),
-        ),
-        compiler_params=limit,
-        cost_estimate=pl.CostEstimate(flops=2**31, bytes_accessed=2**23, transcendentals=0),
-        name="pack",
-    )(tile_cols[0, 0].T, tile_edge_counts[0, 0].T, edge_pos[0, 0], edge_keep_bits[0, 0])
-
-    along = along_z([features] * DEPTH)
+            jax.ShapeDtypeStruct((rows, wide + TILE_SIDE), i32),
+            jax.ShapeDtypeStruct((rows, wide), i32),
+            jax.ShapeDtypeStruct((rows, TILE_SIDE), i32),
+        ),
+        compiler_params=limit,
+        cost_estimate=pl.CostEstimate(flops=2**14, bytes_accessed=2**18, transcendentals=0),
+        name="relay",
+    )(*along_z(planes))
+    core_lists = [both, from_peer(both, lambda x, y, z, c: (x, y, z, c ^ 1))]
+    row_lists = [
+        from_peer(
+            plane_lists, lambda x, y, z, c, dx=dx, dc=dc: ((x + dx) % grid.rows, y, z, c ^ dc)
+        )
+        for dx in range(1, grid.rows)
+        for dc in range(CORES)
+    ]
+    wide_counts = [
+        from_peer(counts, lambda x, y, z, c, dy=dy, dc=dc: (x, (y + dy) % grid.wide, z, c ^ dc))
+        for dy in range(1, grid.wide)
+        for dc in range(CORES)
+    ]
     peer_lists = [lists] + [
-        lax.ppermute(
-            lists,
-            both_axes,
-            grid.pairs(lambda x, y, z, c, dy=dy: (x, (y - dy) % grid.wide, z, c)),
-        )
+        from_peer(lists, lambda x, y, z, c, dy=dy: (x, (y + dy) % grid.wide, z, c))
         for dy in range(1, grid.wide)
     ]
+    gathered = to_cores(along)
     side, depth = grid.summed * group, grid.gathered * group
+
+    def whole(*shape):
+        return pl.BlockSpec(shape, lambda k: (0,) * len(shape))
+
+    scale, *sums = pl.pallas_call(
+        functools.partial(forward_kernel, grid, slots),
+        grid=(grid.summed,),
+        in_specs=[smem]
+        + [whole(rows, wide + TILE_SIDE)] * CORES
+        + [whole(rows, wide)] * len(row_lists)
+        + [whole(rows, TILE_SIDE)] * len(wide_counts)
+        + [whole(group, width)] * grid.gathered,
+        out_specs=(whole(group, width),) * (1 + grid.summed),
+        out_shape=(jax.ShapeDtypeStruct((group, width), f32),) * (1 + grid.summed),
+        scratch_shapes=[
+            pltpu.VMEM((CORES * grid.rows, rows, wide), i32),
+            pltpu.VMEM((rows, TILE_SIDE), f32),
+            pltpu.VMEM((depth, 2 * width), bf16),
+        ],
+        compiler_params=limit,
+        cost_estimate=pl.CostEstimate(
+            flops=8 * side * depth * width, bytes_accessed=depth * width * 4, transcendentals=0
+        ),
+        name="forward",
+    )(me, *core_lists, *row_lists, *wide_counts, *gathered)
+    sums = to_owners(sums)
+
+    tall = group + hidden // DEPTH
+    tall_shape = jax.ShapeDtypeStruct((tall, width), f32)
+    hidden_out, *sent = pl.pallas_call(
+        functools.partial(middle_kernel, grid),
+        in_specs=[smem] + [vmem] * (6 + grid.summed),
+        out_shape=(jax.ShapeDtypeStruct((group, hidden), f32),) + (tall_shape,) * DEPTH,
+        scratch_shapes=[pltpu.VMEM((width, hidden), f32)],
+        compiler_params=limit,
+        cost_estimate=pl.CostEstimate(
+            flops=36 * group * width * hidden, bytes_accessed=2**20, transcendentals=2**18
+        ),
+        name="middle",
+    )(me, scale, features, weight, out_bias.reshape(1, hidden), cotangent, drop_keep, *sums)
+
+    *peer_lists, sent[0] = lax.optimization_barrier((*peer_lists, sent[0]))
     backward_block = pl.pallas_call(
         functools.partial(backward_block_kernel, grid, slots),
         grid=(grid.gathered,),
@@ -411,71 +493,16 @@
         out_specs=pl.BlockSpec((side, group), lambda g: (0, g)),
         out_shape=jax.ShapeDtypeStruct((side, depth), bf16),
         compiler_params=limit,
-        cost_estimate=pl.CostEstimate(flops=2**16, bytes_accessed=2**16, transcendentals=0),
+        cost_estimate=pl.CostEstimate(
+            flops=2 * rows * slots * TILE_SIDE * grid.rows * group,
+            bytes_accessed=2 * side * depth,
+            transcendentals=0,
+        ),
         name="backward_block",
     )(me, *peer_lists)
-    *along, pieces, backward_block = lax.optimization_barrier((*along, pieces, backward_block))
-    edges = lax.all_to_all(pieces, both_axes, 0, 0, tiled=True)
-    gathered = to_cores(along)
-
-    own_roots = pl.pallas_call(
-        functools.partial(roots_kernel, grid),
-        in_specs=[smem, vmem],
-        out_shape=jax.ShapeDtypeStruct((grid.gathered, 1, group), f32),
-        compiler_params=limit,
-        cost_estimate=pl.CostEstimate(flops=2**14, bytes_accessed=2**16, transcendentals=0),
-        name="roots",
-    )(me, edges)
-    roots = lax.all_to_all(
-        own_roots,
-        "col",
-        0,
-        0,
-        tiled=True,
-        axis_index_groups=[
-            [grid.col(z, y, c) for z in range(DEPTH) for c in range(CORES)]
-            for y in range(grid.wide)
-        ],
-    )
-
-    def whole(*shape):
-        return pl.BlockSpec(shape, lambda k: (0,) * len(shape))
-
-    sums = pl.pallas_call(
-        functools.partial(forward_kernel, grid, slots),
-        grid=(grid.summed,),
-        in_specs=[smem, whole(*roots.shape), whole(*edges.shape)]
-        + [whole(group, width)] * grid.gathered,
-        out_specs=(whole(group, width),) * grid.summed,
-        out_shape=(jax.ShapeDtypeStruct((group, width), f32),) * grid.summed,
-        scratch_shapes=[pltpu.VMEM((depth, 2 * width), bf16)],
-        compiler_params=limit,
-        cost_estimate=pl.CostEstimate(
-            flops=8 * side * depth * width, bytes_accessed=depth * width * 4, transcendentals=0
-        ),
-        name="forward",
-    )(me, roots, edges, *gathered)
-    sums = to_owners(sums)
-
-    tall = group + hidden // DEPTH
-    tall_shape = jax.ShapeDtypeStruct((tall, width), f32)
-    hidden_out, scale, *sent = pl.pallas_call(
-        functools.partial(middle_kernel, grid),
-        in_specs=[smem] + [vmem] * (6 + grid.summed),
-        out_shape=(
-            jax.ShapeDtypeStruct((group, hidden), f32),
-            jax.ShapeDtypeStruct((group, width), f32),
-        )
-        + (tall_shape,) * DEPTH,
-        scratch_shapes=[pltpu.VMEM((width, hidden), f32)],
-        compiler_params=limit,
-        cost_estimate=pl.CostEstimate(
-            flops=36 * group * width * hidden, bytes_accessed=2**20, transcendentals=2**18
-        ),
-        name="middle",
-    )(me, own_roots, features, weight, out_bias.reshape(1, hidden), cotangent, drop_keep, *sums)
-
-    collected = to_cores(along_z(sent))
+    along = along_z(sent)
+    along[-1], backward_block = lax.optimization_barrier((along[-1], backward_block))
+    collected = to_cores(along)
     sums = pl.pallas_call(
         functools.partial(backward_sum_kernel, grid),
         grid_spec=pltpu.PrefetchScalarGridSpec(

time: 102 us -> 92.2 us (0.904)
  waiting for transfers between devices: 42.5 us -> 31.9 us
  starting transfers between devices: 34.3 us -> 38.5 us
  Pallas kernels: 18.7 us -> 16.9 us
  local copies, waits for them, and re-layouts: 4.88 us -> 3.79 us
    all_to_all x2 -> x0, waiting for transfers between devices: 13.4 us -> none  [the longest x1 7.78 us: shards(): edges = lax.all_to_all(pieces, both_axes, 0, 0, tiled=True)]
    all_to_all x2 -> x0, starting transfers between devices: 9.35 us -> none  [the longest x1 6 us: shards(): edges = lax.all_to_all(pieces, both_axes, 0, 0, tiled=True)]
    ppermute x9 -> x12, starting transfers between devices: 14.5 us -> 22.1 us  [along_z(): lax.ppermute(blocks[dz], both_axes, grid.pairs(lambda x, y, z, c, dz=dz:...]
    ppermute x1 -> x6, waiting for transfers between devices: 2.43 us -> 9.37 us  [from_peer(): return lax.ppermute(value, both_axes, [(b, a) for a, b in grid.pairs(move)])]
    ppermute x9 -> x12, waiting for transfers between devices: 13.6 us -> 7.56 us  [along_z(): lax.ppermute(blocks[dz], both_axes, grid.pairs(lambda x, y, z, c, dz=dz:...]
    ppermute x1 -> x6, starting transfers between devices: 1.66 us -> 7.12 us  [from_peer(): return lax.ppermute(value, both_axes, [(b, a) for a, b in grid.pairs(move)])]
    ppermute x6, waiting for transfers between devices: 12.1 us -> 13.9 us  [to_owners(): lax.ppermute(part, both_axes, grid.pairs(lambda x, y, z, c, dx=dx, dy=dy:...]
    pallas_call x2, Pallas kernels: 2.14 us -> 0.97 us  [the longest x1 0.96 us: shards(): pl.pallas_call(functools.partial(pack_kernel, grid), in_specs=[smem] + [p...]
  transfers between devices with their start and end apart: 26 -> 32, of which waited for: 16 -> 17; matrix products, arithmetic and copies ran while one was open for 0% -> 0% of each run, Pallas kernels for 7% -> 6%
where the time goes in v4:
time: 92.2 us; the launch traced here: 91.9 us
  starting transfers between devices  38.5 us (42%)
  waiting for transfers between devices  31.9 us (35%)
  Pallas kernels  16.9 us (18%)
  local copies, waits for them, and re-layouts  3.79 us (4%)
    ppermute x12, starting transfers between devices, along_z(): lax.ppermute(blocks[dz], both_axes, grid.pairs(lambda x, y, z, c, dz=dz:...  22.1 us
    ppermute x6, waiting for transfers between devices, to_owners(): lax.ppermute(part, both_axes, grid.pairs(lambda x, y, z, c, dx=dx, dy=dy:...  13.9 us
    ppermute x6, waiting for transfers between devices, from_peer(): return lax.ppermute(value, both_axes, [(b, a) for a, b in grid.pairs(move)])  9.37 us
    ppermute x12, waiting for transfers between devices, along_z(): lax.ppermute(blocks[dz], both_axes, grid.pairs(lambda x, y, z, c, dz=dz:...  7.56 us
    ppermute x6, starting transfers between devices, from_peer(): return lax.ppermute(value, both_axes, [(b, a) for a, b in grid.pairs(move)])  7.12 us
    ppermute x6, starting transfers between devices, to_owners(): lax.ppermute(part, both_axes, grid.pairs(lambda x, y, z, c, dx=dx, dy=dy:...  7.11 us
    pallas_call x1, Pallas kernels, shards(): pl.pallas_call(functools.partial(forward_kernel, grid, slots), grid=(grid...  6.29 us
    pallas_call x1, Pallas kernels, shards(): pl.pallas_call(functools.partial(backward_block_kernel, grid, slots), gri...  4.45 us
  transfers between devices with their start and end apart: 32, of which 17 were waited for; matrix products, arithmetic and copies ran while one was open for 0% of the time, Pallas kernels for 6%

profile of v4, /device:TPU:0, one launch (start us, length us, event | category | flops | bytes accessed | tf_op | source)
XLA Modules:
  0.0 91.9 jit_solution(11420514529850267475)
XLA Ops:
  0.7 5.1 %collective-permute-start.13 = (f32[256,128]{1,0:T(8,128)}, f32[256,128]{1,0:T(8,128)S(1)}, u32[]{:S(2)}, u32[]{:S(2)}) collective-permute-start(f32[256,128]{1,0:T(8,128)} %features_ref.1), channel_id=1, source_target_pairs={{0,12},{1,13},{2,14},{3,15},{4,8},{5,9},{6,10},{7,11},{8,4},{9,5},... | collective-permute-start | bytes 393224 | tf_op jit(solution)/shard_map/ppermute | solution.py:358
  10.3 1.4 %collective-permute-start = (s32[8,896]{1,0:T(8,128)S(1)}, s32[8,896]{1,0:T(8,128)S(1)}, u32[]{:S(2)}, u32[]{:S(2)}) collective-permute-start(s32[8,896]{1,0:T(8,128)S(1)} %get-tuple-element.33), channel_id=1, source_target_pairs={{0,4},{1,5},{2,6},{3,7},{4,0},{5,1},{6,2},{7,3},{8,12},{9,13},{10,... | collective-permute-start | bytes 86024 | tf_op jit(solution)/shard_map/ppermute | solution.py:358
  11.7 2.9 %collective-permute-start.1 = (s32[8,896]{1,0:T(8,128)S(1)}, s32[8,896]{1,0:T(8,128)S(1)}, u32[]{:S(2)}, u32[]{:S(2)}) collective-permute-start(s32[8,896]{1,0:T(8,128)S(1)} %get-tuple-element.34), channel_id=1, source_target_pairs={{0,8},{1,9},{2,10},{3,11},{4,12},{5,13},{6,14},{7,15},{8,0},{9,1},... | collective-permute-start | bytes 86024 | tf_op jit(solution)/shard_map/ppermute | solution.py:358
  15.3 3.2 %collective-permute-start.2 = (s32[8,896]{1,0:T(8,128)S(1)}, s32[8,896]{1,0:T(8,128)S(1)}, u32[]{:S(2)}, u32[]{:S(2)}) collective-permute-start(s32[8,896]{1,0:T(8,128)S(1)} %get-tuple-element.35), channel_id=1, source_target_pairs={{0,12},{1,13},{2,14},{3,15},{4,8},{5,9},{6,10},{7,11},{8,4},{9,5},... | collective-permute-start | bytes 86024 | tf_op jit(solution)/shard_map/ppermute | solution.py:358
  18.6 2.4 %collective-permute-done.2.refs_3_ = s32[8,896]{1,0:T(8,128)S(1)} collective-permute-done((s32[8,896]{1,0:T(8,128)S(1)}, s32[8,896]{1,0:T(8,128)S(1)}, u32[]{:S(2)}, u32[]{:S(2)}) %collective-permute-start.2) | collective-permute-done | bytes 28704 | tf_op jit(solution)/shard_map/ppermute | solution.py:358
  21.1 2.7 %collective-permute-start.5 = (s32[32,384]{1,0:T(8,128)S(1)}, s32[32,384]{1,0:T(8,128)S(1)}, u32[]{:S(2)}, u32[]{:S(2)}) collective-permute-start(s32[32,384]{1,0:T(8,128)S(1)} %get-tuple-element.37), channel_id=1, source_target_pairs={{17,0},{16,1},{19,2},{18,3},{21,4},{20,5},{23,6},{22,7},{25,8},{24... | collective-permute-start | bytes 147464 | tf_op jit(solution)/shard_map/ppermute | solution.py:414
  24.3 1.4 %collective-permute-start.6 = (s32[32,128]{1,0:T(8,128)S(1)}, s32[32,128]{1,0:T(8,128)S(1)}, u32[]{:S(2)}, u32[]{:S(2)}) collective-permute-start(s32[32,128]{1,0:T(8,128)S(1)} %get-tuple-element.38), channel_id=1, source_target_pairs={{2,0},{3,1},{0,2},{1,3},{6,4},{7,5},{4,6},{5,7},{10,8},{11,9},{8,1... | collective-permute-start | bytes 49160 | tf_op jit(solution)/shard_map/ppermute | solution.py:414
  25.8 2.3 %collective-permute-done.6.refs_4_ = s32[32,128]{1,0:T(8,128)S(1)} collective-permute-done((s32[32,128]{1,0:T(8,128)S(1)}, s32[32,128]{1,0:T(8,128)S(1)}, u32[]{:S(2)}, u32[]{:S(2)}) %collective-permute-start.6) | collective-permute-done | bytes 16416 | tf_op jit(solution)/shard_map/ppermute | solution.py:414
  29.1 1.5 %collective-permute-start.4 = (s32[32,384]{1,0:T(8,128)S(1)}, s32[32,384]{1,0:T(8,128)S(1)}, u32[]{:S(2)}, u32[]{:S(2)}) collective-permute-start(s32[32,384]{1,0:T(8,128)S(1)} %get-tuple-element.37), channel_id=1, source_target_pairs={{16,0},{17,1},{18,2},{19,3},{20,4},{21,5},{22,6},{23,7},{24,8},{25... | collective-permute-start | bytes 147464 | tf_op jit(solution)/shard_map/ppermute | solution.py:414
  30.6 2.6 %collective-permute-done.4.refs_2_ = s32[32,384]{1,0:T(8,128)S(1)} collective-permute-done((s32[32,384]{1,0:T(8,128)S(1)}, s32[32,384]{1,0:T(8,128)S(1)}, u32[]{:S(2)}, u32[]{:S(2)}) %collective-permute-start.4) | collective-permute-done | bytes 49184 | tf_op jit(solution)/shard_map/ppermute | solution.py:414
  35.4 6.3 %forward.1 = (f32[256,128]{1,0:T(8,128)S(1)}, f32[256,128]{1,0:T(8,128)S(1)}, f32[256,128]{1,0:T(8,128)S(1)}, f32[256,128]{1,0:T(8,128)S(1)}, f32[256,128]{1,0:T(8,128)S(1)}) custom-call(s32[1]{0:T(128)} %bitcast.me_ref, s32[32,512]{1,0:T(8,128)S(1)} %get-tuple-element.36.refs_0_, s32[32,512]{1,0:T(8,128)S(1)} %collective-permute-done.3.refs_1_, ...), custom_call_target="tpu_custom_call" | custom-call | flops 2147483648 | bytes 1048576 | tf_op jit(solution)/shard_map/forward/pallas_call | solution.py:451
  41.7 1.6 %collective-permute-start.15 = (f32[256,128]{1,0:T(8,128)S(1)}, f32[256,128]{1,0:T(8,128)S(1)}, u32[]{:S(2)}, u32[]{:S(2)}) collective-permute-start(f32[256,128]{1,0:T(8,128)S(1)} %get-tuple-element.41), channel_id=1, source_target_pairs={{0,16},{1,17},{2,18},{3,19},{4,20},{5,21},{6,22},{7,23},{8,24},{9,... | collective-permute-start | bytes 393224 | tf_op jit(solution)/shard_map/ppermute | solution.py:382
  45.3 2.4 %collective-permute-done.15.refs_1_ = f32[256,128]{1,0:T(8,128)S(1)} collective-permute-done((f32[256,128]{1,0:T(8,128)S(1)}, f32[256,128]{1,0:T(8,128)S(1)}, u32[]{:S(2)}, u32[]{:S(2)}) %collective-permute-start.15) | collective-permute-done | bytes 131104 | tf_op jit(solution)/shard_map/ppermute | solution.py:382
  47.7 3.7 %collective-permute-done.16.refs_2_ = f32[256,128]{1,0:T(8,128)S(1)} collective-permute-done((f32[256,128]{1,0:T(8,128)S(1)}, f32[256,128]{1,0:T(8,128)S(1)}, u32[]{:S(2)}, u32[]{:S(2)}) %collective-permute-start.16) | collective-permute-done | bytes 131104 | tf_op jit(solution)/shard_map/ppermute | solution.py:382
  51.4 1.6 %middle.1 = (f32[256,256]{1,0:T(8,128)}, f32[320,128]{1,0:T(8,128)S(1)}, f32[320,128]{1,0:T(8,128)S(1)}, f32[320,128]{1,0:T(8,128)S(1)}, f32[320,128]{1,0:T(8,128)S(1)}) custom-call(s32[1]{0:T(128)} %bitcast.me_ref, f32[256,128]{1,0:T(8,128)S(1)} %get-tuple-element.39.scale_ref, f32[256,128]{1,0:T(8,128)S(1)} %copy-done.3, f32[128,256]{1,0:T(8,128)S(1)} %copy-done.4, ...), custom_call_target="tpu_custom_call" | custom-call | flops 301989888 | bytes 1048576 | tf_op jit(solution)/shard_map/middle/pallas_call | solution.py:476
  53.0 3.2 %collective-permute-start.19 = (f32[320,128]{1,0:T(8,128)S(1)}, f32[320,128]{1,0:T(8,128)S(1)}, u32[]{:S(2)}, u32[]{:S(2)}) collective-permute-start(f32[320,128]{1,0:T(8,128)S(1)} %get-tuple-element.48), channel_id=1, source_target_pairs={{0,12},{1,13},{2,14},{3,15},{4,8},{5,9},{6,10},{7,11},{8,4},{9,5},... | collective-permute-start | bytes 491528 | tf_op jit(solution)/shard_map/ppermute | solution.py:358
  58.9 2.7 %collective-permute-done.18.refs_1_ = s32[32,384]{1,0:T(8,128)S(1)} collective-permute-done((s32[32,384]{1,0:T(8,128)S(1)}, s32[32,384]{1,0:T(8,128)S(1)}, u32[]{:S(2)}, u32[]{:S(2)}) %collective-permute-start.18) | collective-permute-done | bytes 49184 | tf_op jit(solution)/shard_map/ppermute | solution.py:414
  61.5 4.4 %backward_block.1.block_ref = bf16[1024,2048]{1,0:T(8,128)(2,1)S(1)} custom-call(s32[1]{0:T(128)} %bitcast.me_ref, s32[32,384]{1,0:T(8,128)S(1)} %get-tuple-element.49.refs_0_, s32[32,384]{1,0:T(8,128)S(1)} %collective-permute-done.18.refs_1_), custom_call_target="tpu_custom_call" | custom-call | flops 1073741824 | bytes 4194304 | tf_op jit(solution)/shard_map/backward_block/pallas_call | solution.py:489
  66.6 2.2 %collective-permute-done.23.refs_4_ = f32[320,128]{1,0:T(8,128)S(1)} collective-permute-done((f32[320,128]{1,0:T(8,128)S(1)}, f32[320,128]{1,0:T(8,128)S(1)}, u32[]{:S(2)}, u32[]{:S(2)}) %collective-permute-start.23) | collective-permute-done | bytes 163872 | tf_op jit(solution)/shard_map/ppermute | solution.py:358
  70.4 2.2 %backward_sum.1 = (f32[320,128]{1,0:T(8,128)S(1)}, f32[320,128]{1,0:T(8,128)S(1)}, f32[320,128]{1,0:T(8,128)S(1)}, f32[320,128]{1,0:T(8,128)S(1)}) custom-call(s32[1]{0:T(128)} %bitcast.me_ref, bf16[1024,2048]{1,0:T(8,128)(2,1)S(1)} %backward_block.1.block_ref, f32[320,128]{1,0:T(8,128)S(1)} %get-tuple-element.47.refs_0_.sent_ref, ...), custom_call_target="tpu_custom_call" | custom-call | flops 1073741824 | bytes 4194304 | tf_op jit(solution)/shard_map/backward_sum/pallas_call | solution.py:506
  72.6 1.7 %collective-permute-start.26 = (f32[320,128]{1,0:T(8,128)S(1)}, f32[320,128]{1,0:T(8,128)S(1)}, u32[]{:S(2)}, u32[]{:S(2)}) collective-permute-start(f32[320,128]{1,0:T(8,128)S(1)} %get-tuple-element.56), channel_id=1, source_target_pairs={{0,16},{1,17},{2,18},{3,19},{4,20},{5,21},{6,22},{7,23},{8,24},{9,... | collective-permute-start | bytes 491528 | tf_op jit(solution)/shard_map/ppermute | solution.py:382
  76.1 3.5 %collective-permute-done.26.refs_1_ = f32[320,128]{1,0:T(8,128)S(1)} collective-permute-done((f32[320,128]{1,0:T(8,128)S(1)}, f32[320,128]{1,0:T(8,128)S(1)}, u32[]{:S(2)}, u32[]{:S(2)}) %collective-permute-start.26) | collective-permute-done | bytes 163872 | tf_op jit(solution)/shard_map/ppermute | solution.py:382
  79.6 4.3 %collective-permute-done.27.refs_2_ = f32[320,128]{1,0:T(8,128)S(1)} collective-permute-done((f32[320,128]{1,0:T(8,128)S(1)}, f32[320,128]{1,0:T(8,128)S(1)}, u32[]{:S(2)}, u32[]{:S(2)}) %collective-permute-start.27) | collective-permute-done | bytes 163872 | tf_op jit(solution)/shard_map/ppermute | solution.py:382
  85.9 3.1 %collective-permute-start.29 = (f32[64,128]{1,0:T(8,128)S(1)}, f32[64,128]{1,0:T(8,128)S(1)}, u32[]{:S(2)}, u32[]{:S(2)}) collective-permute-start(f32[64,128]{1,0:T(8,128)S(1)} %get-tuple-element.60.refs_0_), channel_id=1, source_target_pairs={{0,4},{1,5},{2,6},{3,7},{4,0},{5,1},{6,2},{7,3},{8,12},{9,13},{10,... | collective-permute-start | bytes 98312 | tf_op jit(solution)/shard_map/ppermute | solution.py:358
  (68 shorter events, 22.5 us)
Async XLA Ops:
  0.7 27.4 %collective-permute-start.13 = (f32[256,128]{1,0:T(8,128)}, f32[256,128]{1,0:T(8,128)S(1)}, u32[]{:S(2)}, u32[]{:S(2)}) collective-permute-start(f32[256,128]{1,0:T(8,128)} %features_ref.1), channel_id=1, source_target_pairs={{0,12},{1,13},{2,14},{3,15},{4,8},{5,9},{6,10},{7,11},{8,4},{9,5},... | collective-permute-start | bytes 393224 | tf_op jit(solution)/shard_map/ppermute | solution.py:358
  5.8 22.8 %collective-permute-start.11 = (f32[256,128]{1,0:T(8,128)}, f32[256,128]{1,0:T(8,128)S(1)}, u32[]{:S(2)}, u32[]{:S(2)}) collective-permute-start(f32[256,128]{1,0:T(8,128)} %features_ref.1), channel_id=1, source_target_pairs={{0,8},{1,9},{2,10},{3,11},{4,12},{5,13},{6,14},{7,15},{8,0},{9,1},... | collective-permute-start | bytes 393224 | tf_op jit(solution)/shard_map/ppermute | solution.py:358
  5.8 22.9 %collective-permute-start.9 = (f32[256,128]{1,0:T(8,128)}, f32[256,128]{1,0:T(8,128)S(1)}, u32[]{:S(2)}, u32[]{:S(2)}) collective-permute-start(f32[256,128]{1,0:T(8,128)} %features_ref.1), channel_id=1, source_target_pairs={{0,4},{1,5},{2,6},{3,7},{4,0},{5,1},{6,2},{7,3},{8,12},{9,13},{10,... | collective-permute-start | bytes 393224 | tf_op jit(solution)/shard_map/ppermute | solution.py:358
  10.3 5.1 %collective-permute-start = (s32[8,896]{1,0:T(8,128)S(1)}, s32[8,896]{1,0:T(8,128)S(1)}, u32[]{:S(2)}, u32[]{:S(2)}) collective-permute-start(s32[8,896]{1,0:T(8,128)S(1)} %get-tuple-element.33), channel_id=1, source_target_pairs={{0,4},{1,5},{2,6},{3,7},{4,0},{5,1},{6,2},{7,3},{8,12},{9,13},{10,... | collective-permute-start | bytes 86024 | tf_op jit(solution)/shard_map/ppermute | solution.py:358
  11.7 6.9 %collective-permute-start.1 = (s32[8,896]{1,0:T(8,128)S(1)}, s32[8,896]{1,0:T(8,128)S(1)}, u32[]{:S(2)}, u32[]{:S(2)}) collective-permute-start(s32[8,896]{1,0:T(8,128)S(1)} %get-tuple-element.34), channel_id=1, source_target_pairs={{0,8},{1,9},{2,10},{3,11},{4,12},{5,13},{6,14},{7,15},{8,0},{9,1},... | collective-permute-start | bytes 86024 | tf_op jit(solution)/shard_map/ppermute | solution.py:358
  15.3 5.7 %collective-permute-start.2 = (s32[8,896]{1,0:T(8,128)S(1)}, s32[8,896]{1,0:T(8,128)S(1)}, u32[]{:S(2)}, u32[]{:S(2)}) collective-permute-start(s32[8,896]{1,0:T(8,128)S(1)} %get-tuple-element.35), channel_id=1, source_target_pairs={{0,12},{1,13},{2,14},{3,15},{4,8},{5,9},{6,10},{7,11},{8,4},{9,5},... | collective-permute-start | bytes 86024 | tf_op jit(solution)/shard_map/ppermute | solution.py:358
  21.1 8.0 %collective-permute-start.5 = (s32[32,384]{1,0:T(8,128)S(1)}, s32[32,384]{1,0:T(8,128)S(1)}, u32[]{:S(2)}, u32[]{:S(2)}) collective-permute-start(s32[32,384]{1,0:T(8,128)S(1)} %get-tuple-element.37), channel_id=1, source_target_pairs={{17,0},{16,1},{19,2},{18,3},{21,4},{20,5},{23,6},{22,7},{25,8},{24... | collective-permute-start | bytes 147464 | tf_op jit(solution)/shard_map/ppermute | solution.py:414
  28.1 6.4 %collective-permute-start.8 = (f32[256,128]{1,0:T(8,128)}, f32[256,128]{1,0:T(8,128)S(1)}, u32[]{:S(2)}, u32[]{:S(2)}) collective-permute-start(f32[256,128]{1,0:T(8,128)} %features_ref.1), channel_id=1, source_target_pairs={{0,1},{1,0},{2,3},{3,2},{4,5},{5,4},{6,7},{7,6},{8,9},{9,8},{10,11... | collective-permute-start | bytes 393224 | tf_op jit(solution)/shard_map/ppermute | solution.py:366
  28.1 6.4 %collective-permute-start.14 = (f32[256,128]{1,0:T(8,128)S(1)}, f32[256,128]{1,0:T(8,128)S(1)}, u32[]{:S(2)}, u32[]{:S(2)}) collective-permute-start(f32[256,128]{1,0:T(8,128)S(1)} %collective-permute-done.13.refs_12_), channel_id=1, source_target_pairs={{0,1},{1,0},{2,3},{3,2},{4,5},{5,4},{6,7},{7,6},{8,9},{9,8},{10,11... | collective-permute-start | bytes 393224 | tf_op jit(solution)/shard_map/ppermute | solution.py:366
  28.6 5.9 %collective-permute-start.12 = (f32[256,128]{1,0:T(8,128)S(1)}, f32[256,128]{1,0:T(8,128)S(1)}, u32[]{:S(2)}, u32[]{:S(2)}) collective-permute-start(f32[256,128]{1,0:T(8,128)S(1)} %collective-permute-done.11.refs_10_), channel_id=1, source_target_pairs={{0,1},{1,0},{2,3},{3,2},{4,5},{5,4},{6,7},{7,6},{8,9},{9,8},{10,11... | collective-permute-start | bytes 393224 | tf_op jit(solution)/shard_map/ppermute | solution.py:366
  28.7 5.8 %collective-permute-start.10 = (f32[256,128]{1,0:T(8,128)S(1)}, f32[256,128]{1,0:T(8,128)S(1)}, u32[]{:S(2)}, u32[]{:S(2)}) collective-permute-start(f32[256,128]{1,0:T(8,128)S(1)} %collective-permute-done.9.refs_8_), channel_id=1, source_target_pairs={{0,1},{1,0},{2,3},{3,2},{4,5},{5,4},{6,7},{7,6},{8,9},{9,8},{10,11... | collective-permute-start | bytes 393224 | tf_op jit(solution)/shard_map/ppermute | solution.py:366
  41.7 6.0 %collective-permute-start.15 = (f32[256,128]{1,0:T(8,128)S(1)}, f32[256,128]{1,0:T(8,128)S(1)}, u32[]{:S(2)}, u32[]{:S(2)}) collective-permute-start(f32[256,128]{1,0:T(8,128)S(1)} %get-tuple-element.41), channel_id=1, source_target_pairs={{0,16},{1,17},{2,18},{3,19},{4,20},{5,21},{6,22},{7,23},{8,24},{9,... | collective-permute-start | bytes 393224 | tf_op jit(solution)/shard_map/ppermute | solution.py:382
  43.3 8.1 %collective-permute-start.16 = (f32[256,128]{1,0:T(8,128)S(1)}, f32[256,128]{1,0:T(8,128)S(1)}, u32[]{:S(2)}, u32[]{:S(2)}) collective-permute-start(f32[256,128]{1,0:T(8,128)S(1)} %get-tuple-element.42), channel_id=1, source_target_pairs={{0,2},{1,3},{2,0},{3,1},{4,6},{5,7},{6,4},{7,5},{8,10},{9,11},{10,... | collective-permute-start | bytes 393224 | tf_op jit(solution)/shard_map/ppermute | solution.py:382
  44.7 6.7 %collective-permute-start.17 = (f32[256,128]{1,0:T(8,128)S(1)}, f32[256,128]{1,0:T(8,128)S(1)}, u32[]{:S(2)}, u32[]{:S(2)}) collective-permute-start(f32[256,128]{1,0:T(8,128)S(1)} %get-tuple-element.43), channel_id=1, source_target_pairs={{0,18},{1,19},{2,16},{3,17},{4,22},{5,23},{6,20},{7,21},{8,26},{9,... | collective-permute-start | bytes 393224 | tf_op jit(solution)/shard_map/ppermute | solution.py:382
  53.0 12.9 %collective-permute-start.19 = (f32[320,128]{1,0:T(8,128)S(1)}, f32[320,128]{1,0:T(8,128)S(1)}, u32[]{:S(2)}, u32[]{:S(2)}) collective-permute-start(f32[320,128]{1,0:T(8,128)S(1)} %get-tuple-element.48), channel_id=1, source_target_pairs={{0,12},{1,13},{2,14},{3,15},{4,8},{5,9},{6,10},{7,11},{8,4},{9,5},... | collective-permute-start | bytes 491528 | tf_op jit(solution)/shard_map/ppermute | solution.py:358
  56.3 9.7 %collective-permute-start.21 = (f32[320,128]{1,0:T(8,128)S(1)}, f32[320,128]{1,0:T(8,128)S(1)}, u32[]{:S(2)}, u32[]{:S(2)}) collective-permute-start(f32[320,128]{1,0:T(8,128)S(1)} %get-tuple-element.52), channel_id=1, source_target_pairs={{0,4},{1,5},{2,6},{3,7},{4,0},{5,1},{6,2},{7,3},{8,12},{9,13},{10,... | collective-permute-start | bytes 491528 | tf_op jit(solution)/shard_map/ppermute | solution.py:358
  56.3 12.5 %collective-permute-start.23 = (f32[320,128]{1,0:T(8,128)S(1)}, f32[320,128]{1,0:T(8,128)S(1)}, u32[]{:S(2)}, u32[]{:S(2)}) collective-permute-start(f32[320,128]{1,0:T(8,128)S(1)} %get-tuple-element.53), channel_id=1, source_target_pairs={{0,8},{1,9},{2,10},{3,11},{4,12},{5,13},{6,14},{7,15},{8,0},{9,1},... | collective-permute-start | bytes 491528 | tf_op jit(solution)/shard_map/ppermute | solution.py:358
  61.5 7.7 %collective-permute-start.20 = (f32[320,128]{1,0:T(8,128)S(1)}, f32[320,128]{1,0:T(8,128)S(1)}, u32[]{:S(2)}, u32[]{:S(2)}) collective-permute-start(f32[320,128]{1,0:T(8,128)S(1)} %get-tuple-element.47.refs_0_.sent_ref), channel_id=1, source_target_pairs={{0,1},{1,0},{2,3},{3,2},{4,5},{5,4},{6,7},{7,6},{8,9},{9,8},{10,11... | collective-permute-start | bytes 491528 | tf_op jit(solution)/shard_map/ppermute | solution.py:366
  72.6 7.1 %collective-permute-start.26 = (f32[320,128]{1,0:T(8,128)S(1)}, f32[320,128]{1,0:T(8,128)S(1)}, u32[]{:S(2)}, u32[]{:S(2)}) collective-permute-start(f32[320,128]{1,0:T(8,128)S(1)} %get-tuple-element.56), channel_id=1, source_target_pairs={{0,16},{1,17},{2,18},{3,19},{4,20},{5,21},{6,22},{7,23},{8,24},{9,... | collective-permute-start | bytes 491528 | tf_op jit(solution)/shard_map/ppermute | solution.py:382
  74.3 9.6 %collective-permute-start.27 = (f32[320,128]{1,0:T(8,128)S(1)}, f32[320,128]{1,0:T(8,128)S(1)}, u32[]{:S(2)}, u32[]{:S(2)}) collective-permute-start(f32[320,128]{1,0:T(8,128)S(1)} %get-tuple-element.57), channel_id=1, source_target_pairs={{0,2},{1,3},{2,0},{3,1},{4,6},{5,7},{6,4},{7,5},{8,10},{9,11},{10,... | collective-permute-start | bytes 491528 | tf_op jit(solution)/shard_map/ppermute | solution.py:382
  74.9 9.0 %collective-permute-start.28 = (f32[320,128]{1,0:T(8,128)S(1)}, f32[320,128]{1,0:T(8,128)S(1)}, u32[]{:S(2)}, u32[]{:S(2)}) collective-permute-start(f32[320,128]{1,0:T(8,128)S(1)} %get-tuple-element.58), channel_id=1, source_target_pairs={{0,18},{1,19},{2,16},{3,17},{4,22},{5,23},{6,20},{7,21},{8,26},{9,... | collective-permute-start | bytes 491528 | tf_op jit(solution)/shard_map/ppermute | solution.py:382
  84.6 5.7 %collective-permute-start.31 = (f32[64,128]{1,0:T(8,128)S(1)}, f32[64,128]{1,0:T(8,128)S(1)}, u32[]{:S(2)}, u32[]{:S(2)}) collective-permute-start(f32[64,128]{1,0:T(8,128)S(1)} %get-tuple-element.60.refs_0_), channel_id=1, source_target_pairs={{0,12},{1,13},{2,14},{3,15},{4,8},{5,9},{6,10},{7,11},{8,4},{9,5},... | collective-permute-start | bytes 98312 | tf_op jit(solution)/shard_map/ppermute | solution.py:358
  85.9 5.3 %collective-permute-start.30 = (f32[64,128]{1,0:T(8,128)S(1)}, f32[64,128]{1,0:T(8,128)S(1)}, u32[]{:S(2)}, u32[]{:S(2)}) collective-permute-start(f32[64,128]{1,0:T(8,128)S(1)} %get-tuple-element.60.refs_0_), channel_id=1, source_target_pairs={{0,8},{1,9},{2,10},{3,11},{4,12},{5,13},{6,14},{7,15},{8,0},{9,1},... | collective-permute-start | bytes 98312 | tf_op jit(solution)/shard_map/ppermute | solution.py:358
  85.9 5.3 %collective-permute-start.29 = (f32[64,128]{1,0:T(8,128)S(1)}, f32[64,128]{1,0:T(8,128)S(1)}, u32[]{:S(2)}, u32[]{:S(2)}) collective-permute-start(f32[64,128]{1,0:T(8,128)S(1)} %get-tuple-element.60.refs_0_), channel_id=1, source_target_pairs={{0,4},{1,5},{2,6},{3,7},{4,0},{5,1},{6,2},{7,3},{8,12},{9,13},{10,... | collective-permute-start | bytes 98312 | tf_op jit(solution)/shard_map/ppermute | solution.py:358
  (18 other events, 176.0 us)

commit v5 on v4

--- a/solution.py
+++ b/solution.py
@@ -154,15 +154,12 @@
         both_ref[rows, width:] = (value - high.astype(f32)).astype(bf16)
 
 
-def forward_kernel(grid, slots, me_ref, *refs):
+def forward_block_kernel(grid, slots, me_ref, *refs):
     core_refs, refs = refs[:CORES], refs[CORES:]
     list_refs, refs = refs[: CORES * (grid.rows - 1)], refs[CORES * (grid.rows - 1) :]
-    count_refs, refs = refs[: CORES * (grid.wide - 1)], refs[CORES * (grid.wide - 1) :]
-    values, refs = refs[: grid.gathered], refs[grid.gathered :]
-    scale_ref, outs, (lists_ref, root_ref, both_ref) = refs[0], refs[1:-3], refs[-3:]
-    width = values[0].shape[1]
+    count_refs, (block_ref, root_ref, lists_ref) = refs[:-3], refs[-3:]
     step = pl.program_id(0)
-    x, y, z, core = grid.place(me_ref[0])
+    x, y, _, core = grid.place(me_ref[0])
     wide = slots + TILE_SIDE
 
     @pl.when(step == 0)
@@ -176,37 +173,45 @@
         for n, ref in enumerate(list_refs):
             lists_ref[CORES + n] = ref[...]
 
-        def scale_of(g):
-            at = grid.col(z ^ (g // CORES), y, core ^ (g % CORES)) * grid.per
-            return spread_down([root_ref[pl.ds(at + s, 1), :] for s in range(grid.per)])
-
-        scale_ref[...] = scale_of(0)
-        split_values(grid, values, both_ref, scale_of)
-
     dx, dy = lax.rem(step, grid.rows), lax.div(step, grid.rows)
     to_y = lax.rem(y + dy, grid.wide)
     plane = grid.wide * CORES * grid.per
-    total = jnp.zeros((grid.group, 2 * width), f32)
     for g in range(grid.gathered):
-        hots = []
         for s in range(grid.per):
             at = (g // CORES) * plane + (to_y * CORES + core) * grid.per + s
             row = lists_ref[dx * CORES + g % CORES, pl.ds(at, 1), :]
             pos = row[:, :slots]
             target = lax.shift_right_arithmetic(pos, 7)
             source = slot_columns(row[:, slots:], 0, slots) * TILE_SIDE + (pos & (TILE_SIDE - 1))
-            hots.append(
-                lax.dot_general(
-                    one_hot(target, TILE_SIDE),
-                    one_hot(source - x * grid.group, grid.group),
-                    NT,
-                    preferred_element_type=f32,
-                )
+            hot = lax.dot_general(
+                one_hot(target, TILE_SIDE),
+                one_hot(source - x * grid.group, grid.group),
+                NT,
+                preferred_element_type=f32,
             )
-        block = jnp.concatenate(hots, axis=0).astype(bf16)
-        rows = slice(g * grid.group, (g + 1) * grid.group)
-        total = total + jnp.dot(block, both_ref[rows, :], preferred_element_type=f32)
-    total = total[:, :width] + total[:, width:]
+            block_ref[
+                s * TILE_SIDE : (s + 1) * TILE_SIDE, g * grid.group : (g + 1) * grid.group
+            ] = hot.astype(bf16)
+
+
+def forward_sum_kernel(grid, me_ref, root_ref, block_ref, *refs):
+    values, (scale_ref, *outs, both_ref) = refs[: grid.gathered], refs[grid.gathered :]
+    width = values[0].shape[1]
+    step = pl.program_id(0)
+
+    @pl.when(step == 0)
+    def _():
+        _, y, z, core = grid.place(me_ref[0])
+
+        def scale_of(g):
+            at = grid.col(z ^ (g // CORES), y, core ^ (g % CORES)) * grid.per
+            return spread_down([root_ref[pl.ds(at + s, 1), :] for s in range(grid.per)])
+
+        scale_ref[...] = scale_of(0)
+        split_values(grid, values, both_ref, scale_of)
+
+    part = jnp.dot(block_ref[...], both_ref[...], preferred_element_type=f32)
+    total = part[:, :width] + part[:, width:]
     for k, out_ref in enumerate(outs):
 
         @pl.when(step == k)
@@ -353,12 +358,12 @@
     vmem = pl.BlockSpec(memory_space=pltpu.VMEM)
     limit = pltpu.CompilerParams(vmem_limit_bytes=24 * MIB)
 
+    def toward(dz):
+        return grid.pairs(lambda x, y, z, c: (x, y, z ^ dz, c))
+
     def along_z(blocks):
         return [blocks[0]] + [
-            lax.ppermute(
-                blocks[dz], both_axes, grid.pairs(lambda x, y, z, c, dz=dz: (x, y, z ^ dz, c))
-            )
-            for dz in range(1, DEPTH)
+            lax.ppermute(blocks[dz], both_axes, toward(dz)) for dz in range(1, DEPTH)
         ]
 
     def to_cores(blocks):
@@ -413,7 +418,11 @@
     def from_peer(value, move):
         return lax.ppermute(value, both_axes, [(b, a) for a, b in grid.pairs(move)])
 
-    along = along_z([features] * DEPTH)
+    along = [features, lax.ppermute(features, both_axes, toward(1))]
+    *planes, along[1] = lax.optimization_barrier((*planes, along[1]))
+    got_planes = along_z(planes)
+    *got_planes, later = lax.optimization_barrier((*got_planes, features))
+    along += [lax.ppermute(later, both_axes, toward(dz)) for dz in range(2, DEPTH)]
     both, plane_lists, counts = pl.pallas_call(
         functools.partial(relay_kernel, wide),
         out_shape=(
@@ -424,7 +433,7 @@
         compiler_params=limit,
         cost_estimate=pl.CostEstimate(flops=2**14, bytes_accessed=2**18, transcendentals=0),
         name="relay",
-    )(*along_z(planes))
+    )(*got_planes)
     core_lists = [both, from_peer(both, lambda x, y, z, c: (x, y, z, c ^ 1))]
     row_lists = [
         from_peer(
@@ -442,33 +451,52 @@
         from_peer(lists, lambda x, y, z, c, dy=dy: (x, (y + dy) % grid.wide, z, c))
         for dy in range(1, grid.wide)
     ]
-    gathered = to_cores(along)
     side, depth = grid.summed * group, grid.gathered * group
+
+    formation = pl.CostEstimate(
+        flops=2 * rows * slots * TILE_SIDE * grid.rows * group,
+        bytes_accessed=2 * side * depth,
+        transcendentals=0,
+    )
+    product = pl.CostEstimate(
+        flops=4 * side * depth * width, bytes_accessed=2 * side * depth, transcendentals=0
+    )
 
     def whole(*shape):
         return pl.BlockSpec(shape, lambda k: (0,) * len(shape))
 
-    scale, *sums = pl.pallas_call(
-        functools.partial(forward_kernel, grid, slots),
+    core_lists[1], *peer_lists = lax.optimization_barrier((core_lists[1], *peer_lists))
+    forward_block, roots = pl.pallas_call(
+        functools.partial(forward_block_kernel, grid, slots),
         grid=(grid.summed,),
         in_specs=[smem]
         + [whole(rows, wide + TILE_SIDE)] * CORES
         + [whole(rows, wide)] * len(row_lists)
-        + [whole(rows, TILE_SIDE)] * len(wide_counts)
+        + [whole(rows, TILE_SIDE)] * len(wide_counts),
+        out_specs=(pl.BlockSpec((group, depth), lambda k: (k, 0)), whole(rows, TILE_SIDE)),
+        out_shape=(
+            jax.ShapeDtypeStruct((side, depth), bf16),
+            jax.ShapeDtypeStruct((rows, TILE_SIDE), f32),
+        ),
+        scratch_shapes=[pltpu.VMEM((CORES * grid.rows, rows, wide), i32)],
+        compiler_params=limit,
+        cost_estimate=pl.CostEstimate(flops=2**16, bytes_accessed=2**16, transcendentals=0),
+        name="forward_block",
+    )(me, *core_lists, *row_lists, *wide_counts)
+    along[-1], forward_block = lax.optimization_barrier((along[-1], forward_block))
+    gathered = to_cores(along)
+    scale, *sums = pl.pallas_call(
+        functools.partial(forward_sum_kernel, grid),
+        grid=(grid.summed,),
+        in_specs=[smem, whole(rows, TILE_SIDE), pl.BlockSpec((group, depth), lambda k: (k, 0))]
         + [whole(group, width)] * grid.gathered,
         out_specs=(whole(group, width),) * (1 + grid.summed),
         out_shape=(jax.ShapeDtypeStruct((group, width), f32),) * (1 + grid.summed),
-        scratch_shapes=[
-            pltpu.VMEM((CORES * grid.rows, rows, wide), i32),
-            pltpu.VMEM((rows, TILE_SIDE), f32),
-            pltpu.VMEM((depth, 2 * width), bf16),
-        ],
-        compiler_params=limit,
-        cost_estimate=pl.CostEstimate(
-            flops=8 * side * depth * width, bytes_accessed=depth * width * 4, transcendentals=0
-        ),
-        name="forward",
-    )(me, *core_lists, *row_lists, *wide_counts, *gathered)
+        scratch_shapes=[pltpu.VMEM((depth, 2 * width), bf16)],
+        compiler_params=limit,
+        cost_estimate=product,
+        name="forward_sum",
+    )(me, roots, forward_block, *gathered)
     sums = to_owners(sums)
 
     tall = group + hidden // DEPTH
@@ -493,11 +521,7 @@
         out_specs=pl.BlockSpec((side, group), lambda g: (0, g)),
         out_shape=jax.ShapeDtypeStruct((side, depth), bf16),
         compiler_params=limit,
-        cost_estimate=pl.CostEstimate(
-            flops=2 * rows * slots * TILE_SIDE * grid.rows * group,
-            bytes_accessed=2 * side * depth,
-            transcendentals=0,
-        ),
+        cost_estimate=formation,
         name="backward_block",
     )(me, *peer_lists)
     along = along_z(sent)
@@ -518,9 +542,7 @@
         ),
         out_shape=(tall_shape,) * grid.summed,
         compiler_params=limit,
-        cost_estimate=pl.CostEstimate(
-            flops=4 * side * depth * width, bytes_accessed=2 * side * depth, transcendentals=0
-        ),
+        cost_estimate=product,
         name="backward_sum",
     )(me, backward_block, *collected)
     sums = to_owners(sums)

time: 92.2 us -> 89.4 us (0.970)
  starting transfers between devices: 38.5 us -> 31.2 us
  waiting for transfers between devices: 31.9 us -> 36.6 us
    ppermute x12, waiting for transfers between devices: 7.56 us -> 16.8 us  [the longest x9 16.8 us: along_z(): lax.ppermute(blocks[dz], both_axes, toward(dz))]
    ppermute x12, starting transfers between devices: 22.1 us -> 17.8 us  [the longest x9 14.5 us: along_z(): lax.ppermute(blocks[dz], both_axes, toward(dz))]
    ppermute x6, waiting for transfers between devices: 9.37 us -> 5.37 us  [from_peer(): return lax.ppermute(value, both_axes, [(b, a) for a, b in grid.pairs(move)])]
    ppermute x6, starting transfers between devices: 7.12 us -> 4.68 us  [from_peer(): return lax.ppermute(value, both_axes, [(b, a) for a, b in grid.pairs(move)])]
    ppermute x6, waiting for transfers between devices: 13.9 us -> 12.3 us  [to_owners(): lax.ppermute(part, both_axes, grid.pairs(lambda x, y, z, c, dx=dx, dy=dy:...]
    ppermute x8, waiting for transfers between devices: 1.13 us -> 2.14 us  [to_cores(): lax.ppermute(block, both_axes, grid.pairs(lambda x, y, z, c: (x, y, z, c...]
    pallas_call x1 -> x2, Pallas kernels: 6.29 us -> 6.07 us  [the longest x1 3.77 us: shards(): pl.pallas_call(functools.partial(forward_block_kernel, grid, slots), grid...]
    unnamed x20 -> x18, local copies, waits for them, and re-layouts: 3.79 us -> 3.8 us
  transfers between devices with their start and end apart: 32 -> 32, of which waited for: 17 -> 18; matrix products, arithmetic and copies ran while one was open for 0% -> 0% of each run, Pallas kernels for 6% -> 10%
where the time goes in v5:
time: 89.4 us; the launch traced here: 89 us
  waiting for transfers between devices  36.6 us (41%)
  starting transfers between devices  31.2 us (35%)
  Pallas kernels  16.7 us (19%)
  local copies, waits for them, and re-layouts  3.8 us (4%)
    ppermute x9, waiting for transfers between devices, along_z(): lax.ppermute(blocks[dz], both_axes, toward(dz))  16.8 us
    ppermute x9, starting transfers between devices, along_z(): lax.ppermute(blocks[dz], both_axes, toward(dz))  14.5 us
    ppermute x6, waiting for transfers between devices, to_owners(): lax.ppermute(part, both_axes, grid.pairs(lambda x, y, z, c, dx=dx, dy=dy:...  12.3 us
    ppermute x6, starting transfers between devices, to_owners(): lax.ppermute(part, both_axes, grid.pairs(lambda x, y, z, c, dx=dx, dy=dy:...  7.11 us
    ppermute x6, waiting for transfers between devices, from_peer(): return lax.ppermute(value, both_axes, [(b, a) for a, b in grid.pairs(move)])  5.37 us
    ppermute x6, starting transfers between devices, from_peer(): return lax.ppermute(value, both_axes, [(b, a) for a, b in grid.pairs(move)])  4.68 us
    pallas_call x1, Pallas kernels, shards(): pl.pallas_call(functools.partial(backward_block_kernel, grid, slots), gri...  4.44 us
    unnamed x18, local copies, waits for them, and re-layouts  3.8 us
  transfers between devices with their start and end apart: 32, of which 18 were waited for; matrix products, arithmetic and copies ran while one was open for 0% of the time, Pallas kernels for 10%

profile of v5, /device:TPU:0, one launch (start us, length us, event | category | flops | bytes accessed | tf_op | source)
XLA Modules:
  0.0 89.0 jit_solution(15856066135847487468)
XLA Ops:
  0.7 3.1 %collective-permute-start = (f32[256,128]{1,0:T(8,128)}, f32[256,128]{1,0:T(8,128)S(1)}, u32[]{:S(2)}, u32[]{:S(2)}) collective-permute-start(f32[256,128]{1,0:T(8,128)} %features_ref.1), channel_id=1, source_target_pairs={{0,4},{1,5},{2,6},{3,7},{4,0},{5,1},{6,2},{7,3},{8,12},{9,13},{10,... | collective-permute-start | bytes 393224 | tf_op jit(solution)/shard_map/ppermute | solution.py:421
  7.6 1.6 %collective-permute-start.1 = (s32[8,896]{1,0:T(8,128)S(1)}, s32[8,896]{1,0:T(8,128)S(1)}, u32[]{:S(2)}, u32[]{:S(2)}) collective-permute-start(s32[8,896]{1,0:T(8,128)S(1)} %get-tuple-element.54), channel_id=1, source_target_pairs={{0,4},{1,5},{2,6},{3,7},{4,0},{5,1},{6,2},{7,3},{8,12},{9,13},{10,... | collective-permute-start | bytes 86024 | tf_op jit(solution)/shard_map/ppermute | solution.py:366
  9.2 2.6 %collective-permute-start.2 = (s32[8,896]{1,0:T(8,128)S(1)}, s32[8,896]{1,0:T(8,128)S(1)}, u32[]{:S(2)}, u32[]{:S(2)}) collective-permute-start(s32[8,896]{1,0:T(8,128)S(1)} %get-tuple-element.55), channel_id=1, source_target_pairs={{0,8},{1,9},{2,10},{3,11},{4,12},{5,13},{6,14},{7,15},{8,0},{9,1},... | collective-permute-start | bytes 86024 | tf_op jit(solution)/shard_map/ppermute | solution.py:366
  12.1 2.2 %collective-permute-done.2.refs_2_ = s32[8,896]{1,0:T(8,128)S(1)} collective-permute-done((s32[8,896]{1,0:T(8,128)S(1)}, s32[8,896]{1,0:T(8,128)S(1)}, u32[]{:S(2)}, u32[]{:S(2)}) %collective-permute-start.2) | collective-permute-done | bytes 28704 | tf_op jit(solution)/shard_map/ppermute | solution.py:366
  14.2 3.3 %collective-permute-done.3.refs_3_ = s32[8,896]{1,0:T(8,128)S(1)} collective-permute-done((s32[8,896]{1,0:T(8,128)S(1)}, s32[8,896]{1,0:T(8,128)S(1)}, u32[]{:S(2)}, u32[]{:S(2)}) %collective-permute-start.3) | collective-permute-done | bytes 28704 | tf_op jit(solution)/shard_map/ppermute | solution.py:366
  17.8 1.5 %collective-permute-start.5 = (s32[32,384]{1,0:T(8,128)S(1)}, s32[32,384]{1,0:T(8,128)S(1)}, u32[]{:S(2)}, u32[]{:S(2)}) collective-permute-start(s32[32,384]{1,0:T(8,128)S(1)} %get-tuple-element.83.refs_0_), channel_id=1, source_target_pairs={{2,0},{3,1},{0,2},{1,3},{6,4},{7,5},{4,6},{5,7},{10,8},{11,9},{8,1... | collective-permute-start | bytes 147464 | tf_op jit(solution)/shard_map/ppermute | solution.py:419
  20.0 1.9 %collective-permute-done.5.refs_1_ = s32[32,384]{1,0:T(8,128)S(1)} collective-permute-done((s32[32,384]{1,0:T(8,128)S(1)}, s32[32,384]{1,0:T(8,128)S(1)}, u32[]{:S(2)}, u32[]{:S(2)}) %collective-permute-start.5) | collective-permute-done | bytes 49184 | tf_op jit(solution)/shard_map/ppermute | solution.py:419
  25.1 2.8 %collective-permute-done.8.refs_4_ = s32[32,128]{1,0:T(8,128)S(1)} collective-permute-done((s32[32,128]{1,0:T(8,128)S(1)}, s32[32,128]{1,0:T(8,128)S(1)}, u32[]{:S(2)}, u32[]{:S(2)}) %collective-permute-start.8) | collective-permute-done | bytes 16416 | tf_op jit(solution)/shard_map/ppermute | solution.py:419
  28.4 3.8 %forward_block.1 = (bf16[1024,2048]{1,0:T(8,128)(2,1)S(1)}, f32[32,128]{1,0:T(8,128)S(1)}) custom-call(s32[1]{0:T(128)} %bitcast.me_ref, s32[32,512]{1,0:T(8,128)S(1)} %get-tuple-element.61.refs_0_, s32[32,512]{1,0:T(8,128)S(1)} %collective-permute-done.4.refs_1_, s32[32,384]{1,0:T(8,128)S(1)} %collective-permute-done.6.refs_2_, ...), custom_call_target="tpu_custom_call" | custom-call | flops 65536 | bytes 65536 | tf_op jit(solution)/shard_map/forward_block/pallas_call | solution.py:469
  34.7 2.3 %forward_sum.1 = (f32[256,128]{1,0:T(8,128)S(1)}, f32[256,128]{1,0:T(8,128)S(1)}, f32[256,128]{1,0:T(8,128)S(1)}, f32[256,128]{1,0:T(8,128)S(1)}, f32[256,128]{1,0:T(8,128)S(1)}) custom-call(s32[1]{0:T(128)} %bitcast.me_ref, f32[32,128]{1,0:T(8,128)S(1)} %get-tuple-element.66.root_ref, bf16[1024,2048]{1,0:T(8,128)(2,1)S(1)} %get-tuple-element.69.block_ref, ...), custom_call_target="tpu_custom_call" | custom-call | flops 1073741824 | bytes 4194304 | tf_op jit(solution)/shard_map/forward_sum/pallas_call | solution.py:488
  38.7 1.8 %collective-permute-start.18 = (f32[256,128]{1,0:T(8,128)S(1)}, f32[256,128]{1,0:T(8,128)S(1)}, u32[]{:S(2)}, u32[]{:S(2)}) collective-permute-start(f32[256,128]{1,0:T(8,128)S(1)} %get-tuple-element.76), channel_id=1, source_target_pairs={{0,18},{1,19},{2,16},{3,17},{4,22},{5,23},{6,20},{7,21},{8,26},{9,... | collective-permute-start | bytes 393224 | tf_op jit(solution)/shard_map/ppermute | solution.py:387
  40.5 2.8 %collective-permute-done.16.refs_1_ = f32[256,128]{1,0:T(8,128)S(1)} collective-permute-done((f32[256,128]{1,0:T(8,128)S(1)}, f32[256,128]{1,0:T(8,128)S(1)}, u32[]{:S(2)}, u32[]{:S(2)}) %collective-permute-start.16) | collective-permute-done | bytes 131104 | tf_op jit(solution)/shard_map/ppermute | solution.py:387
  43.5 2.5 %collective-permute-done.18.refs_3_ = f32[256,128]{1,0:T(8,128)S(1)} collective-permute-done((f32[256,128]{1,0:T(8,128)S(1)}, f32[256,128]{1,0:T(8,128)S(1)}, u32[]{:S(2)}, u32[]{:S(2)}) %collective-permute-start.18) | collective-permute-done | bytes 131104 | tf_op jit(solution)/shard_map/ppermute | solution.py:387
  46.0 1.6 %middle.1 = (f32[256,256]{1,0:T(8,128)}, f32[320,128]{1,0:T(8,128)S(1)}, f32[320,128]{1,0:T(8,128)S(1)}, f32[320,128]{1,0:T(8,128)S(1)}, f32[320,128]{1,0:T(8,128)S(1)}) custom-call(s32[1]{0:T(128)} %bitcast.me_ref, f32[256,128]{1,0:T(8,128)S(1)} %get-tuple-element.72.scale_ref, f32[256,128]{1,0:T(8,128)S(1)} %copy-done, f32[128,256]{1,0:T(8,128)S(1)} %copy-done.3, ...), custom_call_target="tpu_custom_call" | custom-call | flops 301989888 | bytes 1048576 | tf_op jit(solution)/shard_map/middle/pallas_call | solution.py:504
  47.6 3.6 %collective-permute-start.19 = (f32[320,128]{1,0:T(8,128)S(1)}, f32[320,128]{1,0:T(8,128)S(1)}, u32[]{:S(2)}, u32[]{:S(2)}) collective-permute-start(f32[320,128]{1,0:T(8,128)S(1)} %get-tuple-element.82), channel_id=1, source_target_pairs={{0,12},{1,13},{2,14},{3,15},{4,8},{5,9},{6,10},{7,11},{8,4},{9,5},... | collective-permute-start | bytes 491528 | tf_op jit(solution)/shard_map/ppermute | solution.py:366
  53.3 4.4 %backward_block.1.block_ref = bf16[1024,2048]{1,0:T(8,128)(2,1)S(1)} custom-call(s32[1]{0:T(128)} %bitcast.me_ref, s32[32,384]{1,0:T(8,128)S(1)} %get-tuple-element.83.refs_0_, s32[32,384]{1,0:T(8,128)S(1)} %collective-permute-done.5.refs_1_), custom_call_target="tpu_custom_call" | custom-call | flops 1073741824 | bytes 4194304 | tf_op jit(solution)/shard_map/backward_block/pallas_call | solution.py:517
  57.8 1.7 %collective-permute-done.21.refs_2_ = f32[320,128]{1,0:T(8,128)S(1)} collective-permute-done((f32[320,128]{1,0:T(8,128)S(1)}, f32[320,128]{1,0:T(8,128)S(1)}, u32[]{:S(2)}, u32[]{:S(2)}) %collective-permute-start.21) | collective-permute-done | bytes 163872 | tf_op jit(solution)/shard_map/ppermute | solution.py:366
  59.4 6.2 %collective-permute-done.23.refs_4_ = f32[320,128]{1,0:T(8,128)S(1)} collective-permute-done((f32[320,128]{1,0:T(8,128)S(1)}, f32[320,128]{1,0:T(8,128)S(1)}, u32[]{:S(2)}, u32[]{:S(2)}) %collective-permute-start.23) | collective-permute-done | bytes 163872 | tf_op jit(solution)/shard_map/ppermute | solution.py:366
  67.3 2.2 %backward_sum.1 = (f32[320,128]{1,0:T(8,128)S(1)}, f32[320,128]{1,0:T(8,128)S(1)}, f32[320,128]{1,0:T(8,128)S(1)}, f32[320,128]{1,0:T(8,128)S(1)}) custom-call(s32[1]{0:T(128)} %bitcast.me_ref, bf16[1024,2048]{1,0:T(8,128)(2,1)S(1)} %backward_block.1.block_ref, f32[320,128]{1,0:T(8,128)S(1)} %get-tuple-element.81.refs_0_.sent_ref, ...), custom_call_target="tpu_custom_call" | custom-call | flops 1073741824 | bytes 4194304 | tf_op jit(solution)/shard_map/backward_sum/pallas_call | solution.py:530
  70.9 2.1 %collective-permute-start.28 = (f32[320,128]{1,0:T(8,128)S(1)}, f32[320,128]{1,0:T(8,128)S(1)}, u32[]{:S(2)}, u32[]{:S(2)}) collective-permute-start(f32[320,128]{1,0:T(8,128)S(1)} %get-tuple-element.92), channel_id=1, source_target_pairs={{0,18},{1,19},{2,16},{3,17},{4,22},{5,23},{6,20},{7,21},{8,26},{9,... | collective-permute-start | bytes 491528 | tf_op jit(solution)/shard_map/ppermute | solution.py:387
  73.0 3.5 %collective-permute-done.26.refs_1_ = f32[320,128]{1,0:T(8,128)S(1)} collective-permute-done((f32[320,128]{1,0:T(8,128)S(1)}, f32[320,128]{1,0:T(8,128)S(1)}, u32[]{:S(2)}, u32[]{:S(2)}) %collective-permute-start.26) | collective-permute-done | bytes 163872 | tf_op jit(solution)/shard_map/ppermute | solution.py:387
  76.6 3.3 %collective-permute-done.28.refs_3_ = f32[320,128]{1,0:T(8,128)S(1)} collective-permute-done((f32[320,128]{1,0:T(8,128)S(1)}, f32[320,128]{1,0:T(8,128)S(1)}, u32[]{:S(2)}, u32[]{:S(2)}) %collective-permute-start.28) | collective-permute-done | bytes 163872 | tf_op jit(solution)/shard_map/ppermute | solution.py:387
  80.6 2.9 %collective-permute-start.31 = (f32[64,128]{1,0:T(8,128)S(1)}, f32[64,128]{1,0:T(8,128)S(1)}, u32[]{:S(2)}, u32[]{:S(2)}) collective-permute-start(f32[64,128]{1,0:T(8,128)S(1)} %get-tuple-element.94.refs_0_), channel_id=1, source_target_pairs={{0,12},{1,13},{2,14},{3,15},{4,8},{5,9},{6,10},{7,11},{8,4},{9,5},... | collective-permute-start | bytes 98312 | tf_op jit(solution)/shard_map/ppermute | solution.py:366
  86.3 2.0 %collective-permute-done.30.refs_2_ = f32[64,128]{1,0:T(8,128)S(1)} collective-permute-done((f32[64,128]{1,0:T(8,128)S(1)}, f32[64,128]{1,0:T(8,128)S(1)}, u32[]{:S(2)}, u32[]{:S(2)}) %collective-permute-start.30) | collective-permute-done | bytes 32800 | tf_op jit(solution)/shard_map/ppermute | solution.py:366
  (67 shorter events, 22.5 us)
Async XLA Ops:
  0.7 6.9 %collective-permute-start = (f32[256,128]{1,0:T(8,128)}, f32[256,128]{1,0:T(8,128)S(1)}, u32[]{:S(2)}, u32[]{:S(2)}) collective-permute-start(f32[256,128]{1,0:T(8,128)} %features_ref.1), channel_id=1, source_target_pairs={{0,4},{1,5},{2,6},{3,7},{4,0},{5,1},{6,2},{7,3},{8,12},{9,13},{10,... | collective-permute-start | bytes 393224 | tf_op jit(solution)/shard_map/ppermute | solution.py:421
  9.2 5.0 %collective-permute-start.2 = (s32[8,896]{1,0:T(8,128)S(1)}, s32[8,896]{1,0:T(8,128)S(1)}, u32[]{:S(2)}, u32[]{:S(2)}) collective-permute-start(s32[8,896]{1,0:T(8,128)S(1)} %get-tuple-element.55), channel_id=1, source_target_pairs={{0,8},{1,9},{2,10},{3,11},{4,12},{5,13},{6,14},{7,15},{8,0},{9,1},... | collective-permute-start | bytes 86024 | tf_op jit(solution)/shard_map/ppermute | solution.py:366
  11.8 5.8 %collective-permute-start.3 = (s32[8,896]{1,0:T(8,128)S(1)}, s32[8,896]{1,0:T(8,128)S(1)}, u32[]{:S(2)}, u32[]{:S(2)}) collective-permute-start(s32[8,896]{1,0:T(8,128)S(1)} %get-tuple-element.56), channel_id=1, source_target_pairs={{0,12},{1,13},{2,14},{3,15},{4,8},{5,9},{6,10},{7,11},{8,4},{9,5},... | collective-permute-start | bytes 86024 | tf_op jit(solution)/shard_map/ppermute | solution.py:366
  17.6 14.6 %collective-permute-start.10 = (f32[256,128]{1,0:T(8,128)}, f32[256,128]{1,0:T(8,128)S(1)}, u32[]{:S(2)}, u32[]{:S(2)}) collective-permute-start(f32[256,128]{1,0:T(8,128)} %features_ref.1), channel_id=1, source_target_pairs={{0,12},{1,13},{2,14},{3,15},{4,8},{5,9},{6,10},{7,11},{8,4},{9,5},... | collective-permute-start | bytes 393224 | tf_op jit(solution)/shard_map/ppermute | solution.py:425
  17.8 14.4 %collective-permute-start.13 = (f32[256,128]{1,0:T(8,128)}, f32[256,128]{1,0:T(8,128)S(1)}, u32[]{:S(2)}, u32[]{:S(2)}) collective-permute-start(f32[256,128]{1,0:T(8,128)} %features_ref.1), channel_id=1, source_target_pairs={{0,8},{1,9},{2,10},{3,11},{4,12},{5,13},{6,14},{7,15},{8,0},{9,1},... | collective-permute-start | bytes 393224 | tf_op jit(solution)/shard_map/ppermute | solution.py:425
  19.3 4.8 %collective-permute-start.4 = (s32[32,512]{1,0:T(8,128)S(1)}, s32[32,512]{1,0:T(8,128)S(1)}, u32[]{:S(2)}, u32[]{:S(2)}) collective-permute-start(s32[32,512]{1,0:T(8,128)S(1)} %get-tuple-element.61.refs_0_), channel_id=1, source_target_pairs={{1,0},{0,1},{3,2},{2,3},{5,4},{4,5},{7,6},{6,7},{9,8},{8,9},{11,10... | collective-permute-start | bytes 196616 | tf_op jit(solution)/shard_map/ppermute | solution.py:419
  21.8 6.0 %collective-permute-start.7 = (s32[32,384]{1,0:T(8,128)S(1)}, s32[32,384]{1,0:T(8,128)S(1)}, u32[]{:S(2)}, u32[]{:S(2)}) collective-permute-start(s32[32,384]{1,0:T(8,128)S(1)} %get-tuple-element.64), channel_id=1, source_target_pairs={{17,0},{16,1},{19,2},{18,3},{21,4},{20,5},{23,6},{22,7},{25,8},{24... | collective-permute-start | bytes 147464 | tf_op jit(solution)/shard_map/ppermute | solution.py:419
  22.6 5.8 %collective-permute-start.6 = (s32[32,384]{1,0:T(8,128)S(1)}, s32[32,384]{1,0:T(8,128)S(1)}, u32[]{:S(2)}, u32[]{:S(2)}) collective-permute-start(s32[32,384]{1,0:T(8,128)S(1)} %get-tuple-element.64), channel_id=1, source_target_pairs={{16,0},{17,1},{18,2},{19,3},{20,4},{21,5},{22,6},{23,7},{24,8},{25... | collective-permute-start | bytes 147464 | tf_op jit(solution)/shard_map/ppermute | solution.py:419
  27.8 4.9 %collective-permute-start.11 = (f32[256,128]{1,0:T(8,128)}, f32[256,128]{1,0:T(8,128)S(1)}, u32[]{:S(2)}, u32[]{:S(2)}) collective-permute-start(f32[256,128]{1,0:T(8,128)} %features_ref.1), channel_id=1, source_target_pairs={{0,1},{1,0},{2,3},{3,2},{4,5},{5,4},{6,7},{7,6},{8,9},{9,8},{10,11... | collective-permute-start | bytes 393224 | tf_op jit(solution)/shard_map/ppermute | solution.py:371
  27.8 4.9 %collective-permute-start.12 = (f32[256,128]{1,0:T(8,128)S(1)}, f32[256,128]{1,0:T(8,128)S(1)}, u32[]{:S(2)}, u32[]{:S(2)}) collective-permute-start(f32[256,128]{1,0:T(8,128)S(1)} %collective-permute-done.refs_2_), channel_id=1, source_target_pairs={{0,1},{1,0},{2,3},{3,2},{4,5},{5,4},{6,7},{7,6},{8,9},{9,8},{10,11... | collective-permute-start | bytes 393224 | tf_op jit(solution)/shard_map/ppermute | solution.py:371
  37.0 6.4 %collective-permute-start.16 = (f32[256,128]{1,0:T(8,128)S(1)}, f32[256,128]{1,0:T(8,128)S(1)}, u32[]{:S(2)}, u32[]{:S(2)}) collective-permute-start(f32[256,128]{1,0:T(8,128)S(1)} %get-tuple-element.74), channel_id=1, source_target_pairs={{0,16},{1,17},{2,18},{3,19},{4,20},{5,21},{6,22},{7,23},{8,24},{9,... | collective-permute-start | bytes 393224 | tf_op jit(solution)/shard_map/ppermute | solution.py:387
  37.6 5.9 %collective-permute-start.17 = (f32[256,128]{1,0:T(8,128)S(1)}, f32[256,128]{1,0:T(8,128)S(1)}, u32[]{:S(2)}, u32[]{:S(2)}) collective-permute-start(f32[256,128]{1,0:T(8,128)S(1)} %get-tuple-element.75), channel_id=1, source_target_pairs={{0,2},{1,3},{2,0},{3,1},{4,6},{5,7},{6,4},{7,5},{8,10},{9,11},{10,... | collective-permute-start | bytes 393224 | tf_op jit(solution)/shard_map/ppermute | solution.py:387
  38.7 7.2 %collective-permute-start.18 = (f32[256,128]{1,0:T(8,128)S(1)}, f32[256,128]{1,0:T(8,128)S(1)}, u32[]{:S(2)}, u32[]{:S(2)}) collective-permute-start(f32[256,128]{1,0:T(8,128)S(1)} %get-tuple-element.76), channel_id=1, source_target_pairs={{0,18},{1,19},{2,16},{3,17},{4,22},{5,23},{6,20},{7,21},{8,26},{9,... | collective-permute-start | bytes 393224 | tf_op jit(solution)/shard_map/ppermute | solution.py:387
  47.6 10.1 %collective-permute-start.19 = (f32[320,128]{1,0:T(8,128)S(1)}, f32[320,128]{1,0:T(8,128)S(1)}, u32[]{:S(2)}, u32[]{:S(2)}) collective-permute-start(f32[320,128]{1,0:T(8,128)S(1)} %get-tuple-element.82), channel_id=1, source_target_pairs={{0,12},{1,13},{2,14},{3,15},{4,8},{5,9},{6,10},{7,11},{8,4},{9,5},... | collective-permute-start | bytes 491528 | tf_op jit(solution)/shard_map/ppermute | solution.py:366
  51.3 8.2 %collective-permute-start.21 = (f32[320,128]{1,0:T(8,128)S(1)}, f32[320,128]{1,0:T(8,128)S(1)}, u32[]{:S(2)}, u32[]{:S(2)}) collective-permute-start(f32[320,128]{1,0:T(8,128)S(1)} %get-tuple-element.86), channel_id=1, source_target_pairs={{0,4},{1,5},{2,6},{3,7},{4,0},{5,1},{6,2},{7,3},{8,12},{9,13},{10,... | collective-permute-start | bytes 491528 | tf_op jit(solution)/shard_map/ppermute | solution.py:366
  51.8 13.8 %collective-permute-start.23 = (f32[320,128]{1,0:T(8,128)S(1)}, f32[320,128]{1,0:T(8,128)S(1)}, u32[]{:S(2)}, u32[]{:S(2)}) collective-permute-start(f32[320,128]{1,0:T(8,128)S(1)} %get-tuple-element.87), channel_id=1, source_target_pairs={{0,8},{1,9},{2,10},{3,11},{4,12},{5,13},{6,14},{7,15},{8,0},{9,1},... | collective-permute-start | bytes 491528 | tf_op jit(solution)/shard_map/ppermute | solution.py:366
  53.3 12.9 %collective-permute-start.20 = (f32[320,128]{1,0:T(8,128)S(1)}, f32[320,128]{1,0:T(8,128)S(1)}, u32[]{:S(2)}, u32[]{:S(2)}) collective-permute-start(f32[320,128]{1,0:T(8,128)S(1)} %get-tuple-element.81.refs_0_.sent_ref), channel_id=1, source_target_pairs={{0,1},{1,0},{2,3},{3,2},{4,5},{5,4},{6,7},{7,6},{8,9},{9,8},{10,11... | collective-permute-start | bytes 491528 | tf_op jit(solution)/shard_map/ppermute | solution.py:371
  59.4 6.8 %collective-permute-start.22 = (f32[320,128]{1,0:T(8,128)S(1)}, f32[320,128]{1,0:T(8,128)S(1)}, u32[]{:S(2)}, u32[]{:S(2)}) collective-permute-start(f32[320,128]{1,0:T(8,128)S(1)} %collective-permute-done.21.refs_2_), channel_id=1, source_target_pairs={{0,1},{1,0},{2,3},{3,2},{4,5},{5,4},{6,7},{7,6},{8,9},{9,8},{10,11... | collective-permute-start | bytes 491528 | tf_op jit(solution)/shard_map/ppermute | solution.py:371
  69.5 7.1 %collective-permute-start.26 = (f32[320,128]{1,0:T(8,128)S(1)}, f32[320,128]{1,0:T(8,128)S(1)}, u32[]{:S(2)}, u32[]{:S(2)}) collective-permute-start(f32[320,128]{1,0:T(8,128)S(1)} %get-tuple-element.90), channel_id=1, source_target_pairs={{0,16},{1,17},{2,18},{3,19},{4,20},{5,21},{6,22},{7,23},{8,24},{9,... | collective-permute-start | bytes 491528 | tf_op jit(solution)/shard_map/ppermute | solution.py:387
  70.0 6.6 %collective-permute-start.27 = (f32[320,128]{1,0:T(8,128)S(1)}, f32[320,128]{1,0:T(8,128)S(1)}, u32[]{:S(2)}, u32[]{:S(2)}) collective-permute-start(f32[320,128]{1,0:T(8,128)S(1)} %get-tuple-element.91), channel_id=1, source_target_pairs={{0,2},{1,3},{2,0},{3,1},{4,6},{5,7},{6,4},{7,5},{8,10},{9,11},{10,... | collective-permute-start | bytes 491528 | tf_op jit(solution)/shard_map/ppermute | solution.py:387
  70.9 9.0 %collective-permute-start.28 = (f32[320,128]{1,0:T(8,128)S(1)}, f32[320,128]{1,0:T(8,128)S(1)}, u32[]{:S(2)}, u32[]{:S(2)}) collective-permute-start(f32[320,128]{1,0:T(8,128)S(1)} %get-tuple-element.92), channel_id=1, source_target_pairs={{0,18},{1,19},{2,16},{3,17},{4,22},{5,23},{6,20},{7,21},{8,26},{9,... | collective-permute-start | bytes 491528 | tf_op jit(solution)/shard_map/ppermute | solution.py:387
  80.6 5.7 %collective-permute-start.31 = (f32[64,128]{1,0:T(8,128)S(1)}, f32[64,128]{1,0:T(8,128)S(1)}, u32[]{:S(2)}, u32[]{:S(2)}) collective-permute-start(f32[64,128]{1,0:T(8,128)S(1)} %get-tuple-element.94.refs_0_), channel_id=1, source_target_pairs={{0,12},{1,13},{2,14},{3,15},{4,8},{5,9},{6,10},{7,11},{8,4},{9,5},... | collective-permute-start | bytes 98312 | tf_op jit(solution)/shard_map/ppermute | solution.py:366
  83.5 4.8 %collective-permute-start.30 = (f32[64,128]{1,0:T(8,128)S(1)}, f32[64,128]{1,0:T(8,128)S(1)}, u32[]{:S(2)}, u32[]{:S(2)}) collective-permute-start(f32[64,128]{1,0:T(8,128)S(1)} %get-tuple-element.94.refs_0_), channel_id=1, source_target_pairs={{0,8},{1,9},{2,10},{3,11},{4,12},{5,13},{6,14},{7,15},{8,0},{9,1},... | collective-permute-start | bytes 98312 | tf_op jit(solution)/shard_map/ppermute | solution.py:366
  83.6 4.8 %collective-permute-start.29 = (f32[64,128]{1,0:T(8,128)S(1)}, f32[64,128]{1,0:T(8,128)S(1)}, u32[]{:S(2)}, u32[]{:S(2)}) collective-permute-start(f32[64,128]{1,0:T(8,128)S(1)} %get-tuple-element.94.refs_0_), channel_id=1, source_target_pairs={{0,4},{1,5},{2,6},{3,7},{4,0},{5,1},{6,2},{7,3},{8,12},{9,13},{10,... | collective-permute-start | bytes 98312 | tf_op jit(solution)/shard_map/ppermute | solution.py:366
  (17 other events, 166.7 us)

commit v6 on v5

--- a/solution.py
+++ b/solution.py
@@ -117,21 +117,43 @@
             sent_ref[:, lanes] = counts_ref[q * plane : (q + 1) * plane, :]
 
 
-def relay_kernel(wide, *refs):
-    got, (both_ref, lists_ref, counts_ref) = refs[:-3], refs[-3:]
+def plane_kernel(wide, *refs):
+    got, both_ref = refs[:-1], refs[-1]
     plane = got[0].shape[0]
     for dz, ref in enumerate(got):
-        rows = slice(dz * plane, (dz + 1) * plane)
-        lists_ref[rows, :] = ref[:, :wide]
-        both_ref[rows, :wide] = ref[:, :wide]
+        both_ref[dz * plane : (dz + 1) * plane, :wide] = ref[:, :wide]
     for q in range(DEPTH):
         lanes = slice(wide + q * TILE_SIDE, wide + (q + 1) * TILE_SIDE)
         count = got[0][:, lanes]
         for ref in got[1:]:
             count = count + ref[:, lanes]
-        rows = slice(q * plane, (q + 1) * plane)
-        counts_ref[rows, :] = count
-        both_ref[rows, wide:] = count
+        both_ref[q * plane : (q + 1) * plane, wide:] = count
+
+
+def chip_kernel(wide, lists_ref, own_ref, other_ref, chip_ref, counted_ref):
+    rows = own_ref.shape[0]
+    chip_ref[:rows, :] = own_ref[:, :wide]
+    chip_ref[rows:, :] = other_ref[:, :wide]
+    counted_ref[:, :wide] = lists_ref[...]
+    counted_ref[:, wide:] = own_ref[:, wide:] + other_ref[:, wide:]
+
+
+def add_kernel(*refs):
+    total = refs[0][...]
+    for ref in refs[1:-1]:
+        total = total + ref[...]
+    refs[-1][...] = total
+
+
+def add_along_z_kernel(grid, me_ref, *refs):
+    parts, (out_ref, placed_ref) = refs[:-2], refs[-2:]
+    _, _, z, _ = grid.place(me_ref[0])
+    for dz, ref in enumerate(parts):
+        placed_ref[z ^ dz] = ref[...]
+    total = placed_ref[0]
+    for n in range(1, DEPTH):
+        total = total + placed_ref[n]
+    out_ref[...] = total
 
 
 def slot_columns(columns, first, slots):
@@ -145,7 +167,7 @@
 def split_values(grid, values, both_ref, scale_of=None):
     width = values[0].shape[1]
     for g, ref in enumerate(values):
-        value = ref[: grid.group, :]
+        value = ref[...]
         if scale_of is not None:
             value = value * scale_of(g)
         high = value.astype(bf16)
@@ -155,31 +177,27 @@
 
 
 def forward_block_kernel(grid, slots, me_ref, *refs):
-    core_refs, refs = refs[:CORES], refs[CORES:]
-    list_refs, refs = refs[: CORES * (grid.rows - 1)], refs[CORES * (grid.rows - 1) :]
-    count_refs, (block_ref, root_ref, lists_ref) = refs[:-3], refs[-3:]
+    chip_refs, refs = refs[: grid.rows], refs[grid.rows :]
+    counted_refs, (block_ref, root_ref, lists_ref) = refs[: grid.wide], refs[grid.wide :]
     step = pl.program_id(0)
     x, y, _, core = grid.place(me_ref[0])
     wide = slots + TILE_SIDE
+    rows = counted_refs[0].shape[0]
 
     @pl.when(step == 0)
     def _():
-        count = sum(ref[:, wide:] for ref in core_refs)
-        for ref in count_refs:
-            count = count + ref[...]
+        count = sum(ref[:, wide:] for ref in counted_refs)
         root_ref[...] = lax.rsqrt(1.0 + count.astype(f32))
-        for n, ref in enumerate(core_refs):
-            lists_ref[n] = ref[:, :wide]
-        for n, ref in enumerate(list_refs):
-            lists_ref[CORES + n] = ref[...]
+        for n, ref in enumerate(chip_refs):
+            lists_ref[n] = ref[...]
 
     dx, dy = lax.rem(step, grid.rows), lax.div(step, grid.rows)
     to_y = lax.rem(y + dy, grid.wide)
     plane = grid.wide * CORES * grid.per
     for g in range(grid.gathered):
         for s in range(grid.per):
-            at = (g // CORES) * plane + (to_y * CORES + core) * grid.per + s
-            row = lists_ref[dx * CORES + g % CORES, pl.ds(at, 1), :]
+            at = (g % CORES) * rows + (g // CORES) * plane + (to_y * CORES + core) * grid.per + s
+            row = lists_ref[dx, pl.ds(at, 1), :]
             pos = row[:, :slots]
             target = lax.shift_right_arithmetic(pos, 7)
             source = slot_columns(row[:, slots:], 0, slots) * TILE_SIDE + (pos & (TILE_SIDE - 1))
@@ -246,21 +264,14 @@
 
 
 def backward_sum_kernel(grid, me_ref, block_ref, *refs):
-    values, outs = refs[: grid.gathered], refs[grid.gathered : -2]
-    shares_ref, both_ref = refs[-2:]
+    values, (own_ref, other_ref, *outs, both_ref) = refs[: grid.gathered], refs[grid.gathered :]
     width = values[0].shape[1]
     step = pl.program_id(0)
 
     @pl.when(step == 0)
     def _():
-        x, y, z, core = grid.place(me_ref[0])
         split_values(grid, values, both_ref)
-        for g, ref in enumerate(values):
-            n = (z ^ (g // CORES)) * CORES + (core ^ (g % CORES))
-            shares_ref[n] = ref[grid.group :, :]
-        share = shares_ref[0]
-        for n in range(1, grid.gathered):
-            share = share + shares_ref[n]
+        share = own_ref[...] + other_ref[...]
         for out_ref in outs:
             out_ref[grid.group :, :] = share
 
@@ -274,28 +285,21 @@
 
 
 def finish_kernel(grid, me_ref, scale_ref, sent_ref, *refs):
-    sums, (features_grad_ref, share_ref, shares_ref) = refs[:-3], refs[-3:]
+    sums, (features_grad_ref, weight_grad_ref, parts_ref) = refs[:-3], refs[-3:]
     x, y, z, core = grid.place(me_ref[0])
-    total = sent_ref[: grid.group, :]
+    total = sent_ref[...]
     for k, ref in enumerate(sums):
         total = total + ref[: grid.group, :]
         from_x = lax.rem(x + grid.rows - k % grid.rows, grid.rows)
         from_y = lax.rem(y + grid.wide - k // grid.rows, grid.wide)
-        shares_ref[from_y * grid.rows + from_x] = ref[grid.group :, :]
+        parts_ref[from_y * grid.rows + from_x] = ref[grid.group :, :]
     features_grad_ref[...] = scale_ref[...] * total
-    share = shares_ref[0]
-    for n in range(1, grid.summed):
-        share = share + shares_ref[n]
-    share_ref[...] = share
-
-
-def join_kernel(grid, me_ref, *refs):
-    quarters, out_ref = refs[:-1], refs[-1]
-    _, _, z, _ = grid.place(me_ref[0])
-    half = quarters[0].shape[0] // 2
-    for dz, ref in enumerate(quarters):
-        rows = pl.ds(pl.multiple_of((z ^ dz) * half, 8), half)
-        out_ref[rows, :] = jnp.concatenate([ref[:half, :], ref[half:, :]], axis=1)
+    high = parts_ref.shape[1] // 2
+    for n in range(grid.summed):
+        part = parts_ref[n]
+        weight_grad_ref[n * high : (n + 1) * high, :] = jnp.concatenate(
+            [part[:high, :], part[high:, :]], axis=1
+        )
 
 
 def middle_kernel(
@@ -310,8 +314,8 @@
     *refs,
 ):
     sums, refs = refs[: grid.summed], refs[grid.summed :]
-    hidden_ref, sent_refs, weight_grad_ref = refs[0], refs[1:-1], refs[-1]
-    _, _, z, _ = grid.place(me_ref[0])
+    hidden_ref, sent_ref, *part_refs, parts_ref = refs
+    x, y, _, _ = grid.place(me_ref[0])
     scale = scale_ref[...]
     total = scale * features_ref[...]
     for ref in sums:
@@ -322,19 +326,21 @@
     dropout = drop_ref[...].astype(f32) / KEEP_RATE
     hidden_ref[...] = gelu_exact(pre_act) * dropout
     grad_pre = cotangent_ref[...] * dropout * gelu_slope(pre_act)
-    sent = scale * lax.dot_general(
+    sent_ref[...] = scale * lax.dot_general(
         grad_pre, weight, NT, precision=highest, preferred_element_type=f32
     )
-    weight_grad_ref[...] = lax.dot_general(
+    weight_grad = lax.dot_general(
         mixed, grad_pre, TN, precision=highest, preferred_element_type=f32
     )
     width = features_ref.shape[1]
-    quarter = width // DEPTH
-    for dz, sent_ref in enumerate(sent_refs):
-        share = weight_grad_ref[pl.ds(pl.multiple_of((z ^ dz) * quarter, 8), quarter), :]
-        sent_ref[: grid.group, :] = sent
-        sent_ref[grid.group : grid.group + quarter, :] = share[:, :width]
-        sent_ref[grid.group + quarter :, :] = share[:, width:]
+    high = width // grid.summed
+    for n in range(grid.summed):
+        part = weight_grad[n * high : (n + 1) * high, :]
+        parts_ref[n] = jnp.concatenate([part[:, :width], part[:, width:]], axis=0)
+    for k, part_ref in enumerate(part_refs):
+        to_x = lax.rem(x + k % grid.rows, grid.rows)
+        to_y = lax.rem(y + k // grid.rows, grid.wide)
+        part_ref[...] = parts_ref[to_y * grid.rows + to_x]
 
 
 def shards(
@@ -423,32 +429,30 @@
     got_planes = along_z(planes)
     *got_planes, later = lax.optimization_barrier((*got_planes, features))
     along += [lax.ppermute(later, both_axes, toward(dz)) for dz in range(2, DEPTH)]
-    both, plane_lists, counts = pl.pallas_call(
-        functools.partial(relay_kernel, wide),
+    small = pl.CostEstimate(flops=2**14, bytes_accessed=2**18, transcendentals=0)
+    both = pl.pallas_call(
+        functools.partial(plane_kernel, wide),
+        out_shape=jax.ShapeDtypeStruct((rows, wide + TILE_SIDE), i32),
+        compiler_params=limit,
+        cost_estimate=small,
+        name="plane",
+    )(*got_planes)
+    chip, counted = pl.pallas_call(
+        functools.partial(chip_kernel, wide),
         out_shape=(
+            jax.ShapeDtypeStruct((CORES * rows, wide), i32),
             jax.ShapeDtypeStruct((rows, wide + TILE_SIDE), i32),
-            jax.ShapeDtypeStruct((rows, wide), i32),
-            jax.ShapeDtypeStruct((rows, TILE_SIDE), i32),
         ),
         compiler_params=limit,
-        cost_estimate=pl.CostEstimate(flops=2**14, bytes_accessed=2**18, transcendentals=0),
-        name="relay",
-    )(*got_planes)
-    core_lists = [both, from_peer(both, lambda x, y, z, c: (x, y, z, c ^ 1))]
-    row_lists = [
-        from_peer(
-            plane_lists, lambda x, y, z, c, dx=dx, dc=dc: ((x + dx) % grid.rows, y, z, c ^ dc)
-        )
+        cost_estimate=small,
+        name="chip",
+    )(lists, both, from_peer(both, lambda x, y, z, c: (x, y, z, c ^ 1)))
+    chips = [chip] + [
+        from_peer(chip, lambda x, y, z, c, dx=dx: ((x + dx) % grid.rows, y, z, c))
         for dx in range(1, grid.rows)
-        for dc in range(CORES)
     ]
-    wide_counts = [
-        from_peer(counts, lambda x, y, z, c, dy=dy, dc=dc: (x, (y + dy) % grid.wide, z, c ^ dc))
-        for dy in range(1, grid.wide)
-        for dc in range(CORES)
-    ]
-    peer_lists = [lists] + [
-        from_peer(lists, lambda x, y, z, c, dy=dy: (x, (y + dy) % grid.wide, z, c))
+    peer_lists = [counted] + [
+        from_peer(counted, lambda x, y, z, c, dy=dy: (x, (y + dy) % grid.wide, z, c))
         for dy in range(1, grid.wide)
     ]
     side, depth = grid.summed * group, grid.gathered * group
@@ -465,24 +469,22 @@
     def whole(*shape):
         return pl.BlockSpec(shape, lambda k: (0,) * len(shape))
 
-    core_lists[1], *peer_lists = lax.optimization_barrier((core_lists[1], *peer_lists))
     forward_block, roots = pl.pallas_call(
         functools.partial(forward_block_kernel, grid, slots),
         grid=(grid.summed,),
         in_specs=[smem]
-        + [whole(rows, wide + TILE_SIDE)] * CORES
-        + [whole(rows, wide)] * len(row_lists)
-        + [whole(rows, TILE_SIDE)] * len(wide_counts),
+        + [whole(CORES * rows, wide)] * grid.rows
+        + [whole(rows, wide + TILE_SIDE)] * grid.wide,
         out_specs=(pl.BlockSpec((group, depth), lambda k: (k, 0)), whole(rows, TILE_SIDE)),
         out_shape=(
             jax.ShapeDtypeStruct((side, depth), bf16),
             jax.ShapeDtypeStruct((rows, TILE_SIDE), f32),
         ),
-        scratch_shapes=[pltpu.VMEM((CORES * grid.rows, rows, wide), i32)],
+        scratch_shapes=[pltpu.VMEM((grid.rows, CORES * rows, wide), i32)],
         compiler_params=limit,
         cost_estimate=pl.CostEstimate(flops=2**16, bytes_accessed=2**16, transcendentals=0),
         name="forward_block",
-    )(me, *core_lists, *row_lists, *wide_counts)
+    )(me, *chips, *peer_lists)
     along[-1], forward_block = lax.optimization_barrier((along[-1], forward_block))
     gathered = to_cores(along)
     scale, *sums = pl.pallas_call(
@@ -497,15 +499,32 @@
         cost_estimate=product,
         name="forward_sum",
     )(me, roots, forward_block, *gathered)
+    *peer_lists, sums[0] = lax.optimization_barrier((*peer_lists, sums[0]))
+    backward_block = pl.pallas_call(
+        functools.partial(backward_block_kernel, grid, slots),
+        grid=(grid.gathered,),
+        in_specs=[smem] + [pl.BlockSpec((rows, wide + TILE_SIDE), lambda g: (0, 0))] * grid.wide,
+        out_specs=pl.BlockSpec((side, group), lambda g: (0, g)),
+        out_shape=jax.ShapeDtypeStruct((side, depth), bf16),
+        compiler_params=limit,
+        cost_estimate=formation,
+        name="backward_block",
+    )(me, *peer_lists)
     sums = to_owners(sums)
-
-    tall = group + hidden // DEPTH
+    sums[-1], backward_block = lax.optimization_barrier((sums[-1], backward_block))
+
+    part_shape = jax.ShapeDtypeStruct((width // grid.summed * 2, width), f32)
+    tall = group + part_shape.shape[0]
     tall_shape = jax.ShapeDtypeStruct((tall, width), f32)
-    hidden_out, *sent = pl.pallas_call(
+    hidden_out, sent, *parts = pl.pallas_call(
         functools.partial(middle_kernel, grid),
         in_specs=[smem] + [vmem] * (6 + grid.summed),
-        out_shape=(jax.ShapeDtypeStruct((group, hidden), f32),) + (tall_shape,) * DEPTH,
-        scratch_shapes=[pltpu.VMEM((width, hidden), f32)],
+        out_shape=(
+            jax.ShapeDtypeStruct((group, hidden), f32),
+            jax.ShapeDtypeStruct((group, width), f32),
+        )
+        + (part_shape,) * grid.summed,
+        scratch_shapes=[pltpu.VMEM((grid.summed, *part_shape.shape), f32)],
         compiler_params=limit,
         cost_estimate=pl.CostEstimate(
             flops=36 * group * width * hidden, bytes_accessed=2**20, transcendentals=2**18
@@ -513,19 +532,26 @@
         name="middle",
     )(me, scale, features, weight, out_bias.reshape(1, hidden), cotangent, drop_keep, *sums)
 
-    *peer_lists, sent[0] = lax.optimization_barrier((*peer_lists, sent[0]))
-    backward_block = pl.pallas_call(
-        functools.partial(backward_block_kernel, grid, slots),
-        grid=(grid.gathered,),
-        in_specs=[smem] + [pl.BlockSpec(lists.shape, lambda g: (0, 0))] * grid.wide,
-        out_specs=pl.BlockSpec((side, group), lambda g: (0, g)),
-        out_shape=jax.ShapeDtypeStruct((side, depth), bf16),
-        compiler_params=limit,
-        cost_estimate=formation,
-        name="backward_block",
-    )(me, *peer_lists)
-    along = along_z(sent)
-    along[-1], backward_block = lax.optimization_barrier((along[-1], backward_block))
+    along = along_z([sent] * DEPTH)
+    share = pl.pallas_call(
+        add_kernel,
+        out_shape=part_shape,
+        compiler_params=limit,
+        cost_estimate=small,
+        name="add_parts",
+    )(*to_owners(parts))
+    over_z = along_z([share] * DEPTH)
+    along[-1], *over_z = lax.optimization_barrier((along[-1], *over_z))
+    share = pl.pallas_call(
+        functools.partial(add_along_z_kernel, grid),
+        in_specs=[smem] + [vmem] * DEPTH,
+        out_shape=part_shape,
+        scratch_shapes=[pltpu.VMEM((DEPTH, *part_shape.shape), f32)],
+        compiler_params=limit,
+        cost_estimate=small,
+        name="add_along_z",
+    )(me, *over_z)
+    shares = [share, from_peer(share, lambda x, y, z, c: (x, y, z, c ^ 1))]
     collected = to_cores(along)
     sums = pl.pallas_call(
         functools.partial(backward_sum_kernel, grid),
@@ -533,39 +559,29 @@
             num_scalar_prefetch=1,
             grid=(grid.summed,),
             in_specs=[pl.BlockSpec((group, depth), lambda k, me_ref: (backward_row(k, me_ref), 0))]
-            + [pl.BlockSpec((tall, width), lambda k, me_ref: (0, 0))] * grid.gathered,
+            + [pl.BlockSpec((group, width), lambda k, me_ref: (0, 0))] * grid.gathered
+            + [pl.BlockSpec(part_shape.shape, lambda k, me_ref: (0, 0))] * CORES,
             out_specs=(pl.BlockSpec((tall, width), lambda k, me_ref: (0, 0)),) * grid.summed,
-            scratch_shapes=[
-                pltpu.VMEM((grid.gathered, tall - group, width), f32),
-                pltpu.VMEM((depth, 2 * width), bf16),
-            ],
+            scratch_shapes=[pltpu.VMEM((depth, 2 * width), bf16)],
         ),
         out_shape=(tall_shape,) * grid.summed,
         compiler_params=limit,
         cost_estimate=product,
         name="backward_sum",
-    )(me, backward_block, *collected)
+    )(me, backward_block, *collected, *shares)
     sums = to_owners(sums)
-    grad_features, share = pl.pallas_call(
+    grad_features, grad_weight = pl.pallas_call(
         functools.partial(finish_kernel, grid),
         in_specs=[smem] + [vmem] * (2 + grid.summed),
         out_shape=(
             jax.ShapeDtypeStruct((group, width), f32),
-            jax.ShapeDtypeStruct((tall - group, width), f32),
+            jax.ShapeDtypeStruct((width, hidden), f32),
         ),
-        scratch_shapes=[pltpu.VMEM((grid.summed, tall - group, width), f32)],
+        scratch_shapes=[pltpu.VMEM((grid.summed, *part_shape.shape), f32)],
         compiler_params=limit,
         cost_estimate=pl.CostEstimate(flops=2**18, bytes_accessed=2**19, transcendentals=0),
         name="finish",
-    )(me, scale, sent[0], *sums)
-    grad_weight = pl.pallas_call(
-        functools.partial(join_kernel, grid),
-        in_specs=[smem] + [vmem] * DEPTH,
-        out_shape=jax.ShapeDtypeStruct((width, hidden), f32),
-        compiler_params=limit,
-        cost_estimate=pl.CostEstimate(flops=0, bytes_accessed=2**18, transcendentals=0),
-        name="join",
-    )(me, *along_z([share] * DEPTH))
+    )(me, scale, sent, *sums)
     return (hidden_out, grad_features, grad_weight)
 
 

time: 89.4 us -> 85.8 us (0.960)
  waiting for transfers between devices: 36.6 us -> 33.6 us
    ppermute x2, waiting for transfers between devices: 0.01 us -> 6.49 us  [shards(): lax.ppermute(later, both_axes, toward(dz))]
    ppermute x6 -> x4, waiting for transfers between devices: 5.37 us -> 0.97 us  [from_peer(): return lax.ppermute(value, both_axes, [(b, a) for a, b in grid.pairs(move)])]
    ppermute x9, waiting for transfers between devices: 16.8 us -> 12.4 us  [along_z(): lax.ppermute(blocks[dz], both_axes, toward(dz))]
    ppermute x6 -> x9, starting transfers between devices: 7.11 us -> 10.6 us  [to_owners(): lax.ppermute(part, both_axes, grid.pairs(lambda x, y, z, c, dx=dx, dy=dy:...]
    ppermute x9, starting transfers between devices: 14.5 us -> 11.5 us  [along_z(): lax.ppermute(blocks[dz], both_axes, toward(dz))]
    ppermute x6 -> x4, starting transfers between devices: 4.68 us -> 3.65 us  [from_peer(): return lax.ppermute(value, both_axes, [(b, a) for a, b in grid.pairs(move)])]
    ppermute x2, starting transfers between devices: 0.2 us -> 1.12 us  [shards(): lax.ppermute(later, both_axes, toward(dz))]
    ppermute x6 -> x9, waiting for transfers between devices: 12.3 us -> 12.4 us  [to_owners(): lax.ppermute(part, both_axes, grid.pairs(lambda x, y, z, c, dx=dx, dy=dy:...]
  transfers between devices with their start and end apart: 32 -> 33, of which waited for: 18 -> 14; matrix products, arithmetic and copies ran while one was open for 0% -> 0% of each run, Pallas kernels for 10% -> 11%
where the time goes in v6:
time: 85.8 us; the launch traced here: 85.5 us
  waiting for transfers between devices  33.6 us (39%)
  starting transfers between devices  31.1 us (36%)
  Pallas kernels  16.2 us (19%)
  local copies, waits for them, and re-layouts  3.8 us (4%)
    ppermute x9, waiting for transfers between devices, along_z(): lax.ppermute(blocks[dz], both_axes, toward(dz))  12.4 us
    ppermute x9, waiting for transfers between devices, to_owners(): lax.ppermute(part, both_axes, grid.pairs(lambda x, y, z, c, dx=dx, dy=dy:...  12.4 us
    ppermute x9, starting transfers between devices, along_z(): lax.ppermute(blocks[dz], both_axes, toward(dz))  11.5 us
    ppermute x9, starting transfers between devices, to_owners(): lax.ppermute(part, both_axes, grid.pairs(lambda x, y, z, c, dx=dx, dy=dy:...  10.6 us
    ppermute x2, waiting for transfers between devices, shards(): lax.ppermute(later, both_axes, toward(dz))  6.49 us
    pallas_call x1, Pallas kernels, shards(): pl.pallas_call(functools.partial(backward_block_kernel, grid, slots), gri...  4.44 us
    unnamed x18, local copies, waits for them, and re-layouts  3.8 us
    pallas_call x1, Pallas kernels, shards(): pl.pallas_call(functools.partial(forward_block_kernel, grid, slots), grid...  3.77 us
  transfers between devices with their start and end apart: 33, of which 14 were waited for; matrix products, arithmetic and copies ran while one was open for 0% of the time, Pallas kernels for 11%

profile of v6, /device:TPU:0, one launch (start us, length us, event | category | flops | bytes accessed | tf_op | source)
XLA Modules:
  0.0 85.5 jit_solution(1734580203743046117)
XLA Ops:
  0.6 3.1 %collective-permute-start = (f32[256,128]{1,0:T(8,128)}, f32[256,128]{1,0:T(8,128)S(1)}, u32[]{:S(2)}, u32[]{:S(2)}) collective-permute-start(f32[256,128]{1,0:T(8,128)} %features_ref.1), channel_id=1, source_target_pairs={{0,4},{1,5},{2,6},{3,7},{4,0},{5,1},{6,2},{7,3},{8,12},{9,13},{10,... | collective-permute-start | bytes 393224 | tf_op jit(solution)/shard_map/ppermute | solution.py:427
  7.6 1.6 %collective-permute-start.1 = (s32[8,896]{1,0:T(8,128)S(1)}, s32[8,896]{1,0:T(8,128)S(1)}, u32[]{:S(2)}, u32[]{:S(2)}) collective-permute-start(s32[8,896]{1,0:T(8,128)S(1)} %get-tuple-element.57), channel_id=1, source_target_pairs={{0,4},{1,5},{2,6},{3,7},{4,0},{5,1},{6,2},{7,3},{8,12},{9,13},{10,... | collective-permute-start | bytes 86024 | tf_op jit(solution)/shard_map/ppermute | solution.py:372
  9.2 2.6 %collective-permute-start.2 = (s32[8,896]{1,0:T(8,128)S(1)}, s32[8,896]{1,0:T(8,128)S(1)}, u32[]{:S(2)}, u32[]{:S(2)}) collective-permute-start(s32[8,896]{1,0:T(8,128)S(1)} %get-tuple-element.58), channel_id=1, source_target_pairs={{0,8},{1,9},{2,10},{3,11},{4,12},{5,13},{6,14},{7,15},{8,0},{9,1},... | collective-permute-start | bytes 86024 | tf_op jit(solution)/shard_map/ppermute | solution.py:372
  12.0 2.2 %collective-permute-done.2.refs_2_ = s32[8,896]{1,0:T(8,128)S(1)} collective-permute-done((s32[8,896]{1,0:T(8,128)S(1)}, s32[8,896]{1,0:T(8,128)S(1)}, u32[]{:S(2)}, u32[]{:S(2)}) %collective-permute-start.2) | collective-permute-done | bytes 28704 | tf_op jit(solution)/shard_map/ppermute | solution.py:372
  14.2 3.2 %collective-permute-done.3.refs_3_ = s32[8,896]{1,0:T(8,128)S(1)} collective-permute-done((s32[8,896]{1,0:T(8,128)S(1)}, s32[8,896]{1,0:T(8,128)S(1)}, u32[]{:S(2)}, u32[]{:S(2)}) %collective-permute-start.3) | collective-permute-done | bytes 28704 | tf_op jit(solution)/shard_map/ppermute | solution.py:372
  18.8 1.6 %collective-permute-start.5 = (s32[64,384]{1,0:T(8,128)S(1)}, s32[64,384]{1,0:T(8,128)S(1)}, u32[]{:S(2)}, u32[]{:S(2)}) collective-permute-start(s32[64,384]{1,0:T(8,128)S(1)} %get-tuple-element.64.refs_0_), channel_id=1, source_target_pairs={{16,0},{17,1},{18,2},{19,3},{20,4},{21,5},{22,6},{23,7},{24,8},{25... | collective-permute-start | bytes 294920 | tf_op jit(solution)/shard_map/ppermute | solution.py:425
  21.9 6.5 %collective-permute-done.10.refs_4_ = f32[256,128]{1,0:T(8,128)S(1)} collective-permute-done((f32[256,128]{1,0:T(8,128)}, f32[256,128]{1,0:T(8,128)S(1)}, u32[]{:S(2)}, u32[]{:S(2)}) %collective-permute-start.10) | collective-permute-done | bytes 131104 | tf_op jit(solution)/shard_map/ppermute | solution.py:431
  28.9 3.8 %forward_block.1 = (bf16[1024,2048]{1,0:T(8,128)(2,1)S(1)}, f32[32,128]{1,0:T(8,128)S(1)}) custom-call(s32[1]{0:T(128)} %bitcast.me_ref, s32[64,384]{1,0:T(8,128)S(1)} %get-tuple-element.64.refs_0_, s32[64,384]{1,0:T(8,128)S(1)} %collective-permute-done.5.refs_1_, s32[32,512]{1,0:T(8,128)S(1)} %get-tuple-element.78.refs_2_.refs_0_, ...), custom_call_target="tpu_custom_call" | custom-call | flops 65536 | bytes 65536 | tf_op jit(solution)/shard_map/forward_block/pallas_call | solution.py:472
  35.0 2.3 %forward_sum.1 = (f32[256,128]{1,0:T(8,128)S(1)}, f32[256,128]{1,0:T(8,128)S(1)}, f32[256,128]{1,0:T(8,128)S(1)}, f32[256,128]{1,0:T(8,128)S(1)}, f32[256,128]{1,0:T(8,128)S(1)}) custom-call(s32[1]{0:T(128)} %bitcast.me_ref, f32[32,128]{1,0:T(8,128)S(1)} %get-tuple-element.66.root_ref, bf16[1024,2048]{1,0:T(8,128)(2,1)S(1)} %get-tuple-element.69.block_ref, ...), custom_call_target="tpu_custom_call" | custom-call | flops 1073741824 | bytes 4194304 | tf_op jit(solution)/shard_map/forward_sum/pallas_call | solution.py:490
  37.3 2.5 %collective-permute-start.15 = (f32[256,128]{1,0:T(8,128)S(1)}, f32[256,128]{1,0:T(8,128)S(1)}, u32[]{:S(2)}, u32[]{:S(2)}) collective-permute-start(f32[256,128]{1,0:T(8,128)S(1)} %get-tuple-element.77), channel_id=1, source_target_pairs={{0,18},{1,19},{2,16},{3,17},{4,22},{5,23},{6,20},{7,21},{8,26},{9,... | collective-permute-start | bytes 393224 | tf_op jit(solution)/shard_map/ppermute | solution.py:393
  40.9 4.4 %backward_block.1.block_ref = bf16[1024,2048]{1,0:T(8,128)(2,1)S(1)} custom-call(s32[1]{0:T(128)} %bitcast.me_ref, s32[32,512]{1,0:T(8,128)S(1)} %get-tuple-element.78.refs_2_.refs_0_, s32[32,512]{1,0:T(8,128)S(1)} %collective-permute-done.6.refs_3_.refs_1_), custom_call_target="tpu_custom_call" | custom-call | flops 1073741824 | bytes 4194304 | tf_op jit(solution)/shard_map/backward_block/pallas_call | solution.py:503
  46.7 1.7 %middle.1 = (f32[256,256]{1,0:T(8,128)}, f32[256,128]{1,0:T(8,128)S(1)}, f32[64,128]{1,0:T(8,128)S(1)}, f32[64,128]{1,0:T(8,128)S(1)}, f32[64,128]{1,0:T(8,128)S(1)}, /*index=5*/f32[64,128]{1,0:T(8,128)S(1)}) custom-call(s32[1]{0:T(128)} %bitcast.me_ref, f32[256,128]{1,0:T(8,128)S(1)} %get-tuple-element.72.scale_ref, f32[256,128]{1,0:T(8,128)S(1)} %copy-done, ...), custom_call_target="tpu_custom_call" | custom-call | flops 301989888 | bytes 1048576 | tf_op jit(solution)/shard_map/middle/pallas_call | solution.py:519
  49.9 2.6 %collective-permute-start.21 = (f32[256,128]{1,0:T(8,128)S(1)}, f32[256,128]{1,0:T(8,128)S(1)}, u32[]{:S(2)}, u32[]{:S(2)}) collective-permute-start(f32[256,128]{1,0:T(8,128)S(1)} %get-tuple-element.82.refs_0_.sent_ref), channel_id=1, source_target_pairs={{0,12},{1,13},{2,14},{3,15},{4,8},{5,9},{6,10},{7,11},{8,4},{9,5},... | collective-permute-start | bytes 393224 | tf_op jit(solution)/shard_map/ppermute | solution.py:372
  52.5 1.8 %collective-permute-start.17 = (f32[256,128]{1,0:T(8,128)S(1)}, f32[256,128]{1,0:T(8,128)S(1)}, u32[]{:S(2)}, u32[]{:S(2)}) collective-permute-start(f32[256,128]{1,0:T(8,128)S(1)} %get-tuple-element.82.refs_0_.sent_ref), channel_id=1, source_target_pairs={{0,4},{1,5},{2,6},{3,7},{4,0},{5,1},{6,2},{7,3},{8,12},{9,13},{10,... | collective-permute-start | bytes 393224 | tf_op jit(solution)/shard_map/ppermute | solution.py:372
  56.3 2.3 %collective-permute-done.23.refs_2_ = f32[64,128]{1,0:T(8,128)S(1)} collective-permute-done((f32[64,128]{1,0:T(8,128)S(1)}, f32[64,128]{1,0:T(8,128)S(1)}, u32[]{:S(2)}, u32[]{:S(2)}) %collective-permute-start.23) | collective-permute-done | bytes 32800 | tf_op jit(solution)/shard_map/ppermute | solution.py:393
  58.5 2.0 %collective-permute-done.24.refs_3_ = f32[64,128]{1,0:T(8,128)S(1)} collective-permute-done((f32[64,128]{1,0:T(8,128)S(1)}, f32[64,128]{1,0:T(8,128)S(1)}, u32[]{:S(2)}, u32[]{:S(2)}) %collective-permute-start.24) | collective-permute-done | bytes 32800 | tf_op jit(solution)/shard_map/ppermute | solution.py:393
  60.6 2.6 %collective-permute-start.27 = (f32[64,128]{1,0:T(8,128)S(1)}, f32[64,128]{1,0:T(8,128)S(1)}, u32[]{:S(2)}, u32[]{:S(2)}) collective-permute-start(f32[64,128]{1,0:T(8,128)S(1)} %add_parts.1.refs_0_), channel_id=1, source_target_pairs={{0,12},{1,13},{2,14},{3,15},{4,8},{5,9},{6,10},{7,11},{8,4},{9,5},... | collective-permute-start | bytes 98312 | tf_op jit(solution)/shard_map/ppermute | solution.py:372
  63.2 3.1 %collective-permute-done.27.refs_3_ = f32[64,128]{1,0:T(8,128)S(1)} collective-permute-done((f32[64,128]{1,0:T(8,128)S(1)}, f32[64,128]{1,0:T(8,128)S(1)}, u32[]{:S(2)}, u32[]{:S(2)}) %collective-permute-start.27) | collective-permute-done | bytes 32800 | tf_op jit(solution)/shard_map/ppermute | solution.py:372
  66.3 1.7 %collective-permute-done.26.refs_2_ = f32[64,128]{1,0:T(8,128)S(1)} collective-permute-done((f32[64,128]{1,0:T(8,128)S(1)}, f32[64,128]{1,0:T(8,128)S(1)}, u32[]{:S(2)}, u32[]{:S(2)}) %collective-permute-start.26) | collective-permute-done | bytes 32800 | tf_op jit(solution)/shard_map/ppermute | solution.py:372
  68.0 2.2 %collective-permute-done.25.refs_1_ = f32[64,128]{1,0:T(8,128)S(1)} collective-permute-done((f32[64,128]{1,0:T(8,128)S(1)}, f32[64,128]{1,0:T(8,128)S(1)}, u32[]{:S(2)}, u32[]{:S(2)}) %collective-permute-start.25) | collective-permute-done | bytes 32800 | tf_op jit(solution)/shard_map/ppermute | solution.py:372
  72.3 2.2 %backward_sum.1 = (f32[320,128]{1,0:T(8,128)S(1)}, f32[320,128]{1,0:T(8,128)S(1)}, f32[320,128]{1,0:T(8,128)S(1)}, f32[320,128]{1,0:T(8,128)S(1)}) custom-call(s32[1]{0:T(128)} %bitcast.me_ref, bf16[1024,2048]{1,0:T(8,128)(2,1)S(1)} %backward_block.1.block_ref, f32[256,128]{1,0:T(8,128)S(1)} %get-tuple-element.82.refs_0_.sent_ref, ...), custom_call_target="tpu_custom_call" | custom-call | flops 1073741824 | bytes 4194304 | tf_op jit(solution)/shard_map/backward_sum/pallas_call | solution.py:556
  75.6 2.4 %collective-permute-start.32 = (f32[320,128]{1,0:T(8,128)S(1)}, f32[320,128]{1,0:T(8,128)S(1)}, u32[]{:S(2)}, u32[]{:S(2)}) collective-permute-start(f32[320,128]{1,0:T(8,128)S(1)} %get-tuple-element.96), channel_id=1, source_target_pairs={{0,18},{1,19},{2,16},{3,17},{4,22},{5,23},{6,20},{7,21},{8,26},{9,... | collective-permute-start | bytes 491528 | tf_op jit(solution)/shard_map/ppermute | solution.py:393
  78.0 3.5 %collective-permute-done.30.refs_1_ = f32[320,128]{1,0:T(8,128)S(1)} collective-permute-done((f32[320,128]{1,0:T(8,128)S(1)}, f32[320,128]{1,0:T(8,128)S(1)}, u32[]{:S(2)}, u32[]{:S(2)}) %collective-permute-start.30) | collective-permute-done | bytes 163872 | tf_op jit(solution)/shard_map/ppermute | solution.py:393
  81.5 3.2 %collective-permute-done.31.refs_2_ = f32[320,128]{1,0:T(8,128)S(1)} collective-permute-done((f32[320,128]{1,0:T(8,128)S(1)}, f32[320,128]{1,0:T(8,128)S(1)}, u32[]{:S(2)}, u32[]{:S(2)}) %collective-permute-start.31) | collective-permute-done | bytes 163872 | tf_op jit(solution)/shard_map/ppermute | solution.py:393
  (71 shorter events, 19.6 us)
Async XLA Ops:
  0.6 6.9 %collective-permute-start = (f32[256,128]{1,0:T(8,128)}, f32[256,128]{1,0:T(8,128)S(1)}, u32[]{:S(2)}, u32[]{:S(2)}) collective-permute-start(f32[256,128]{1,0:T(8,128)} %features_ref.1), channel_id=1, source_target_pairs={{0,4},{1,5},{2,6},{3,7},{4,0},{5,1},{6,2},{7,3},{8,12},{9,13},{10,... | collective-permute-start | bytes 393224 | tf_op jit(solution)/shard_map/ppermute | solution.py:427
  7.6 4.5 %collective-permute-start.1 = (s32[8,896]{1,0:T(8,128)S(1)}, s32[8,896]{1,0:T(8,128)S(1)}, u32[]{:S(2)}, u32[]{:S(2)}) collective-permute-start(s32[8,896]{1,0:T(8,128)S(1)} %get-tuple-element.57), channel_id=1, source_target_pairs={{0,4},{1,5},{2,6},{3,7},{4,0},{5,1},{6,2},{7,3},{8,12},{9,13},{10,... | collective-permute-start | bytes 86024 | tf_op jit(solution)/shard_map/ppermute | solution.py:372
  9.2 5.0 %collective-permute-start.2 = (s32[8,896]{1,0:T(8,128)S(1)}, s32[8,896]{1,0:T(8,128)S(1)}, u32[]{:S(2)}, u32[]{:S(2)}) collective-permute-start(s32[8,896]{1,0:T(8,128)S(1)} %get-tuple-element.58), channel_id=1, source_target_pairs={{0,8},{1,9},{2,10},{3,11},{4,12},{5,13},{6,14},{7,15},{8,0},{9,1},... | collective-permute-start | bytes 86024 | tf_op jit(solution)/shard_map/ppermute | solution.py:372
  11.8 5.7 %collective-permute-start.3 = (s32[8,896]{1,0:T(8,128)S(1)}, s32[8,896]{1,0:T(8,128)S(1)}, u32[]{:S(2)}, u32[]{:S(2)}) collective-permute-start(s32[8,896]{1,0:T(8,128)S(1)} %get-tuple-element.59), channel_id=1, source_target_pairs={{0,12},{1,13},{2,14},{3,15},{4,8},{5,9},{6,10},{7,11},{8,4},{9,5},... | collective-permute-start | bytes 86024 | tf_op jit(solution)/shard_map/ppermute | solution.py:372
  17.5 10.8 %collective-permute-start.10 = (f32[256,128]{1,0:T(8,128)}, f32[256,128]{1,0:T(8,128)S(1)}, u32[]{:S(2)}, u32[]{:S(2)}) collective-permute-start(f32[256,128]{1,0:T(8,128)} %features_ref.1), channel_id=1, source_target_pairs={{0,8},{1,9},{2,10},{3,11},{4,12},{5,13},{6,14},{7,15},{8,0},{9,1},... | collective-permute-start | bytes 393224 | tf_op jit(solution)/shard_map/ppermute | solution.py:431
  17.6 15.0 %collective-permute-start.7 = (f32[256,128]{1,0:T(8,128)}, f32[256,128]{1,0:T(8,128)S(1)}, u32[]{:S(2)}, u32[]{:S(2)}) collective-permute-start(f32[256,128]{1,0:T(8,128)} %features_ref.1), channel_id=1, source_target_pairs={{0,12},{1,13},{2,14},{3,15},{4,8},{5,9},{6,10},{7,11},{8,4},{9,5},... | collective-permute-start | bytes 393224 | tf_op jit(solution)/shard_map/ppermute | solution.py:431
  18.8 10.1 %collective-permute-start.5 = (s32[64,384]{1,0:T(8,128)S(1)}, s32[64,384]{1,0:T(8,128)S(1)}, u32[]{:S(2)}, u32[]{:S(2)}) collective-permute-start(s32[64,384]{1,0:T(8,128)S(1)} %get-tuple-element.64.refs_0_), channel_id=1, source_target_pairs={{16,0},{17,1},{18,2},{19,3},{20,4},{21,5},{22,6},{23,7},{24,8},{25... | collective-permute-start | bytes 294920 | tf_op jit(solution)/shard_map/ppermute | solution.py:425
  20.3 8.0 %collective-permute-start.6 = (s32[32,512]{1,0:T(8,128)S(1)}, s32[32,512]{1,0:T(8,128)S(1)}, u32[]{:S(2)}, u32[]{:S(2)}) collective-permute-start(s32[32,512]{1,0:T(8,128)S(1)} %get-tuple-element.78.refs_2_.refs_0_), channel_id=1, source_target_pairs={{2,0},{3,1},{0,2},{1,3},{6,4},{7,5},{4,6},{5,7},{10,8},{11,9},{8,1... | collective-permute-start | bytes 196616 | tf_op jit(solution)/shard_map/ppermute | solution.py:425
  21.9 10.9 %collective-permute-start.8 = (f32[256,128]{1,0:T(8,128)}, f32[256,128]{1,0:T(8,128)S(1)}, u32[]{:S(2)}, u32[]{:S(2)}) collective-permute-start(f32[256,128]{1,0:T(8,128)} %features_ref.1), channel_id=1, source_target_pairs={{0,1},{1,0},{2,3},{3,2},{4,5},{5,4},{6,7},{7,6},{8,9},{9,8},{10,11... | collective-permute-start | bytes 393224 | tf_op jit(solution)/shard_map/ppermute | solution.py:377
  28.3 4.4 %collective-permute-start.9 = (f32[256,128]{1,0:T(8,128)S(1)}, f32[256,128]{1,0:T(8,128)S(1)}, u32[]{:S(2)}, u32[]{:S(2)}) collective-permute-start(f32[256,128]{1,0:T(8,128)S(1)} %collective-permute-done.refs_2_), channel_id=1, source_target_pairs={{0,1},{1,0},{2,3},{3,2},{4,5},{5,4},{6,7},{7,6},{8,9},{9,8},{10,11... | collective-permute-start | bytes 393224 | tf_op jit(solution)/shard_map/ppermute | solution.py:377
  28.4 4.4 %collective-permute-start.11 = (f32[256,128]{1,0:T(8,128)S(1)}, f32[256,128]{1,0:T(8,128)S(1)}, u32[]{:S(2)}, u32[]{:S(2)}) collective-permute-start(f32[256,128]{1,0:T(8,128)S(1)} %collective-permute-done.10.refs_4_), channel_id=1, source_target_pairs={{0,1},{1,0},{2,3},{3,2},{4,5},{5,4},{6,7},{7,6},{8,9},{9,8},{10,11... | collective-permute-start | bytes 393224 | tf_op jit(solution)/shard_map/ppermute | solution.py:377
  37.3 8.0 %collective-permute-start.15 = (f32[256,128]{1,0:T(8,128)S(1)}, f32[256,128]{1,0:T(8,128)S(1)}, u32[]{:S(2)}, u32[]{:S(2)}) collective-permute-start(f32[256,128]{1,0:T(8,128)S(1)} %get-tuple-element.77), channel_id=1, source_target_pairs={{0,18},{1,19},{2,16},{3,17},{4,22},{5,23},{6,20},{7,21},{8,26},{9,... | collective-permute-start | bytes 393224 | tf_op jit(solution)/shard_map/ppermute | solution.py:393
  39.8 6.9 %collective-permute-start.13 = (f32[256,128]{1,0:T(8,128)S(1)}, f32[256,128]{1,0:T(8,128)S(1)}, u32[]{:S(2)}, u32[]{:S(2)}) collective-permute-start(f32[256,128]{1,0:T(8,128)S(1)} %get-tuple-element.75), channel_id=1, source_target_pairs={{0,16},{1,17},{2,18},{3,19},{4,20},{5,21},{6,22},{7,23},{8,24},{9,... | collective-permute-start | bytes 393224 | tf_op jit(solution)/shard_map/ppermute | solution.py:393
  40.4 6.3 %collective-permute-start.14 = (f32[256,128]{1,0:T(8,128)S(1)}, f32[256,128]{1,0:T(8,128)S(1)}, u32[]{:S(2)}, u32[]{:S(2)}) collective-permute-start(f32[256,128]{1,0:T(8,128)S(1)} %get-tuple-element.76), channel_id=1, source_target_pairs={{0,2},{1,3},{2,0},{3,1},{4,6},{5,7},{6,4},{7,5},{8,10},{9,11},{10,... | collective-permute-start | bytes 393224 | tf_op jit(solution)/shard_map/ppermute | solution.py:393
  48.4 7.3 %collective-permute-start.22 = (f32[64,128]{1,0:T(8,128)S(1)}, f32[64,128]{1,0:T(8,128)S(1)}, u32[]{:S(2)}, u32[]{:S(2)}) collective-permute-start(f32[64,128]{1,0:T(8,128)S(1)} %get-tuple-element.85), channel_id=1, source_target_pairs={{0,16},{1,17},{2,18},{3,19},{4,20},{5,21},{6,22},{7,23},{8,24},{9,... | collective-permute-start | bytes 98312 | tf_op jit(solution)/shard_map/ppermute | solution.py:393
  49.9 20.4 %collective-permute-start.21 = (f32[256,128]{1,0:T(8,128)S(1)}, f32[256,128]{1,0:T(8,128)S(1)}, u32[]{:S(2)}, u32[]{:S(2)}) collective-permute-start(f32[256,128]{1,0:T(8,128)S(1)} %get-tuple-element.82.refs_0_.sent_ref), channel_id=1, source_target_pairs={{0,12},{1,13},{2,14},{3,15},{4,8},{5,9},{6,10},{7,11},{8,4},{9,5},... | collective-permute-start | bytes 393224 | tf_op jit(solution)/shard_map/ppermute | solution.py:372
  52.5 17.8 %collective-permute-start.19 = (f32[256,128]{1,0:T(8,128)S(1)}, f32[256,128]{1,0:T(8,128)S(1)}, u32[]{:S(2)}, u32[]{:S(2)}) collective-permute-start(f32[256,128]{1,0:T(8,128)S(1)} %get-tuple-element.82.refs_0_.sent_ref), channel_id=1, source_target_pairs={{0,8},{1,9},{2,10},{3,11},{4,12},{5,13},{6,14},{7,15},{8,0},{9,1},... | collective-permute-start | bytes 393224 | tf_op jit(solution)/shard_map/ppermute | solution.py:372
  52.5 18.3 %collective-permute-start.17 = (f32[256,128]{1,0:T(8,128)S(1)}, f32[256,128]{1,0:T(8,128)S(1)}, u32[]{:S(2)}, u32[]{:S(2)}) collective-permute-start(f32[256,128]{1,0:T(8,128)S(1)} %get-tuple-element.82.refs_0_.sent_ref), channel_id=1, source_target_pairs={{0,4},{1,5},{2,6},{3,7},{4,0},{5,1},{6,2},{7,3},{8,12},{9,13},{10,... | collective-permute-start | bytes 393224 | tf_op jit(solution)/shard_map/ppermute | solution.py:372
  55.7 4.8 %collective-permute-start.24 = (f32[64,128]{1,0:T(8,128)S(1)}, f32[64,128]{1,0:T(8,128)S(1)}, u32[]{:S(2)}, u32[]{:S(2)}) collective-permute-start(f32[64,128]{1,0:T(8,128)S(1)} %get-tuple-element.87), channel_id=1, source_target_pairs={{0,18},{1,19},{2,16},{3,17},{4,22},{5,23},{6,20},{7,21},{8,26},{9,... | collective-permute-start | bytes 98312 | tf_op jit(solution)/shard_map/ppermute | solution.py:393
  60.6 5.8 %collective-permute-start.27 = (f32[64,128]{1,0:T(8,128)S(1)}, f32[64,128]{1,0:T(8,128)S(1)}, u32[]{:S(2)}, u32[]{:S(2)}) collective-permute-start(f32[64,128]{1,0:T(8,128)S(1)} %add_parts.1.refs_0_), channel_id=1, source_target_pairs={{0,12},{1,13},{2,14},{3,15},{4,8},{5,9},{6,10},{7,11},{8,4},{9,5},... | collective-permute-start | bytes 98312 | tf_op jit(solution)/shard_map/ppermute | solution.py:372
  63.2 4.8 %collective-permute-start.26 = (f32[64,128]{1,0:T(8,128)S(1)}, f32[64,128]{1,0:T(8,128)S(1)}, u32[]{:S(2)}, u32[]{:S(2)}) collective-permute-start(f32[64,128]{1,0:T(8,128)S(1)} %add_parts.1.refs_0_), channel_id=1, source_target_pairs={{0,8},{1,9},{2,10},{3,11},{4,12},{5,13},{6,14},{7,15},{8,0},{9,1},... | collective-permute-start | bytes 98312 | tf_op jit(solution)/shard_map/ppermute | solution.py:372
  74.4 7.1 %collective-permute-start.30 = (f32[320,128]{1,0:T(8,128)S(1)}, f32[320,128]{1,0:T(8,128)S(1)}, u32[]{:S(2)}, u32[]{:S(2)}) collective-permute-start(f32[320,128]{1,0:T(8,128)S(1)} %get-tuple-element.94), channel_id=1, source_target_pairs={{0,16},{1,17},{2,18},{3,19},{4,20},{5,21},{6,22},{7,23},{8,24},{9,... | collective-permute-start | bytes 491528 | tf_op jit(solution)/shard_map/ppermute | solution.py:393
  75.0 9.7 %collective-permute-start.31 = (f32[320,128]{1,0:T(8,128)S(1)}, f32[320,128]{1,0:T(8,128)S(1)}, u32[]{:S(2)}, u32[]{:S(2)}) collective-permute-start(f32[320,128]{1,0:T(8,128)S(1)} %get-tuple-element.95), channel_id=1, source_target_pairs={{0,2},{1,3},{2,0},{3,1},{4,6},{5,7},{6,4},{7,5},{8,10},{9,11},{10,... | collective-permute-start | bytes 491528 | tf_op jit(solution)/shard_map/ppermute | solution.py:393
  75.6 9.1 %collective-permute-start.32 = (f32[320,128]{1,0:T(8,128)S(1)}, f32[320,128]{1,0:T(8,128)S(1)}, u32[]{:S(2)}, u32[]{:S(2)}) collective-permute-start(f32[320,128]{1,0:T(8,128)S(1)} %get-tuple-element.96), channel_id=1, source_target_pairs={{0,18},{1,19},{2,16},{3,17},{4,22},{5,23},{6,20},{7,21},{8,26},{9,... | collective-permute-start | bytes 491528 | tf_op jit(solution)/shard_map/ppermute | solution.py:393
  (18 other events, 71.9 us)

commit v7 on v6

--- a/solution.py
+++ b/solution.py
@@ -264,16 +264,13 @@
 
 
 def backward_sum_kernel(grid, me_ref, block_ref, *refs):
-    values, (own_ref, other_ref, *outs, both_ref) = refs[: grid.gathered], refs[grid.gathered :]
+    values, (*outs, both_ref) = refs[: grid.gathered], refs[grid.gathered :]
     width = values[0].shape[1]
     step = pl.program_id(0)
 
     @pl.when(step == 0)
     def _():
         split_values(grid, values, both_ref)
-        share = own_ref[...] + other_ref[...]
-        for out_ref in outs:
-            out_ref[grid.group :, :] = share
 
     part = jnp.dot(block_ref[...], both_ref[...], preferred_element_type=f32)
     total = part[:, :width] + part[:, width:]
@@ -281,19 +278,21 @@
 
         @pl.when(step == k)
         def _(out_ref=out_ref):
-            out_ref[: grid.group, :] = total
+            out_ref[...] = total
 
 
 def finish_kernel(grid, me_ref, scale_ref, sent_ref, *refs):
-    sums, (features_grad_ref, weight_grad_ref, parts_ref) = refs[:-3], refs[-3:]
+    sums, refs = refs[: grid.summed], refs[grid.summed :]
+    parts, (features_grad_ref, weight_grad_ref, parts_ref) = refs[:-3], refs[-3:]
     x, y, z, core = grid.place(me_ref[0])
     total = sent_ref[...]
-    for k, ref in enumerate(sums):
-        total = total + ref[: grid.group, :]
+    for ref in sums:
+        total = total + ref[...]
+    features_grad_ref[...] = scale_ref[...] * total
+    for k, ref in enumerate(parts):
         from_x = lax.rem(x + grid.rows - k % grid.rows, grid.rows)
         from_y = lax.rem(y + grid.wide - k // grid.rows, grid.wide)
-        parts_ref[from_y * grid.rows + from_x] = ref[grid.group :, :]
-    features_grad_ref[...] = scale_ref[...] * total
+        parts_ref[from_y * grid.rows + from_x] = ref[...]
     high = parts_ref.shape[1] // 2
     for n in range(grid.summed):
         part = parts_ref[n]
@@ -416,19 +415,17 @@
         scratch_shapes=[pltpu.VMEM((rows, TILE_SIDE), i32)]
         + [pltpu.VMEM(a.shape, i32) for a in raw]
         + [pltpu.SemaphoreType.DMA((4,))],
-        compiler_params=limit,
-        cost_estimate=pl.CostEstimate(flops=2**21, bytes_accessed=2**17, transcendentals=0),
+        compiler_params=pltpu.CompilerParams(vmem_limit_bytes=60 * MIB),
+        cost_estimate=pl.CostEstimate(flops=2**31, bytes_accessed=2**23, transcendentals=0),
         name="pack",
     )(me, *raw)
 
     def from_peer(value, move):
         return lax.ppermute(value, both_axes, [(b, a) for a, b in grid.pairs(move)])
 
-    along = [features, lax.ppermute(features, both_axes, toward(1))]
-    *planes, along[1] = lax.optimization_barrier((*planes, along[1]))
+    along = along_z([features] * DEPTH)
     got_planes = along_z(planes)
-    *got_planes, later = lax.optimization_barrier((*got_planes, features))
-    along += [lax.ppermute(later, both_axes, toward(dz)) for dz in range(2, DEPTH)]
+    *along, got_planes[0] = lax.optimization_barrier((*along, got_planes[0]))
     small = pl.CostEstimate(flops=2**14, bytes_accessed=2**18, transcendentals=0)
     both = pl.pallas_call(
         functools.partial(plane_kernel, wide),
@@ -514,8 +511,6 @@
     sums[-1], backward_block = lax.optimization_barrier((sums[-1], backward_block))
 
     part_shape = jax.ShapeDtypeStruct((width // grid.summed * 2, width), f32)
-    tall = group + part_shape.shape[0]
-    tall_shape = jax.ShapeDtypeStruct((tall, width), f32)
     hidden_out, sent, *parts = pl.pallas_call(
         functools.partial(middle_kernel, grid),
         in_specs=[smem] + [vmem] * (6 + grid.summed),
@@ -540,18 +535,8 @@
         cost_estimate=small,
         name="add_parts",
     )(*to_owners(parts))
+    along[-1], share = lax.optimization_barrier((along[-1], share))
     over_z = along_z([share] * DEPTH)
-    along[-1], *over_z = lax.optimization_barrier((along[-1], *over_z))
-    share = pl.pallas_call(
-        functools.partial(add_along_z_kernel, grid),
-        in_specs=[smem] + [vmem] * DEPTH,
-        out_shape=part_shape,
-        scratch_shapes=[pltpu.VMEM((DEPTH, *part_shape.shape), f32)],
-        compiler_params=limit,
-        cost_estimate=small,
-        name="add_along_z",
-    )(me, *over_z)
-    shares = [share, from_peer(share, lambda x, y, z, c: (x, y, z, c ^ 1))]
     collected = to_cores(along)
     sums = pl.pallas_call(
         functools.partial(backward_sum_kernel, grid),
@@ -559,20 +544,39 @@
             num_scalar_prefetch=1,
             grid=(grid.summed,),
             in_specs=[pl.BlockSpec((group, depth), lambda k, me_ref: (backward_row(k, me_ref), 0))]
-            + [pl.BlockSpec((group, width), lambda k, me_ref: (0, 0))] * grid.gathered
-            + [pl.BlockSpec(part_shape.shape, lambda k, me_ref: (0, 0))] * CORES,
-            out_specs=(pl.BlockSpec((tall, width), lambda k, me_ref: (0, 0)),) * grid.summed,
+            + [pl.BlockSpec((group, width), lambda k, me_ref: (0, 0))] * grid.gathered,
+            out_specs=(pl.BlockSpec((group, width), lambda k, me_ref: (0, 0)),) * grid.summed,
             scratch_shapes=[pltpu.VMEM((depth, 2 * width), bf16)],
         ),
-        out_shape=(tall_shape,) * grid.summed,
+        out_shape=(jax.ShapeDtypeStruct((group, width), f32),) * grid.summed,
         compiler_params=limit,
         cost_estimate=product,
         name="backward_sum",
-    )(me, backward_block, *collected, *shares)
+    )(me, backward_block, *collected)
+    first, *over_z = lax.optimization_barrier((sums[0], *over_z))
+    sums = [first, *sums[1:]]
+    share = pl.pallas_call(
+        functools.partial(add_along_z_kernel, grid),
+        in_specs=[smem] + [vmem] * DEPTH,
+        out_shape=part_shape,
+        scratch_shapes=[pltpu.VMEM((DEPTH, *part_shape.shape), f32)],
+        compiler_params=limit,
+        cost_estimate=small,
+        name="add_along_z",
+    )(me, *over_z)
+    shares = [share, from_peer(share, lambda x, y, z, c: (x, y, z, c ^ 1))]
+    share = pl.pallas_call(
+        add_kernel,
+        out_shape=part_shape,
+        compiler_params=limit,
+        cost_estimate=small,
+        name="add_cores",
+    )(*shares)
     sums = to_owners(sums)
+    parts = to_owners([share] * grid.summed)
     grad_features, grad_weight = pl.pallas_call(
         functools.partial(finish_kernel, grid),
-        in_specs=[smem] + [vmem] * (2 + grid.summed),
+        in_specs=[smem] + [vmem] * (2 + 2 * grid.summed),
         out_shape=(
             jax.ShapeDtypeStruct((group, width), f32),
             jax.ShapeDtypeStruct((width, hidden), f32),
@@ -581,7 +585,7 @@
         compiler_params=limit,
         cost_estimate=pl.CostEstimate(flops=2**18, bytes_accessed=2**19, transcendentals=0),
         name="finish",
-    )(me, scale, sent, *sums)
+    )(me, scale, sent, *sums, *parts)
     return (hidden_out, grad_features, grad_weight)
 
 

time: 85.8 us -> 83.2 us (0.970)
  waiting for transfers between devices: 33.6 us -> 24.7 us
  starting transfers between devices: 31.1 us -> 38.3 us
  local copies, waits for them, and re-layouts: 3.8 us -> 1.57 us
  Pallas kernels: 16.2 us -> 17.5 us
    ppermute x9 -> x12, starting transfers between devices: 11.5 us -> 18.9 us  [along_z(): lax.ppermute(blocks[dz], both_axes, toward(dz))]
    ppermute x3 -> x0, waiting for transfers between devices: 6.49 us -> none  [the longest x2 6.49 us: shards(): lax.ppermute(later, both_axes, toward(dz))]
    ppermute x9 -> x12, waiting for transfers between devices: 12.4 us -> 7.82 us  [along_z(): lax.ppermute(blocks[dz], both_axes, toward(dz))]
    ppermute x9 -> x12, starting transfers between devices: 10.6 us -> 15 us  [to_owners(): lax.ppermute(part, both_axes, grid.pairs(lambda x, y, z, c, dx=dx, dy=dy:...]
    ppermute x3 -> x0, starting transfers between devices: 4.21 us -> none  [the longest x1 3.09 us: shards(): along = [features, lax.ppermute(features, both_axes, toward(1))]]
    ppermute x4, waiting for transfers between devices: 0.97 us -> 4.67 us  [from_peer(): return lax.ppermute(value, both_axes, [(b, a) for a, b in grid.pairs(move)])]
    unnamed x18 -> x14, local copies, waits for them, and re-layouts: 3.8 us -> 1.57 us
    ppermute x9 -> x12, waiting for transfers between devices: 12.4 us -> 10.9 us  [to_owners(): lax.ppermute(part, both_axes, grid.pairs(lambda x, y, z, c, dx=dx, dy=dy:...]
  transfers between devices with their start and end apart: 33 -> 36, of which waited for: 14 -> 12; matrix products, arithmetic and copies ran while one was open for 0% -> 0% of each run, Pallas kernels for 11% -> 15%
where the time goes in v7:
time: 83.2 us; the launch traced here: 82.9 us
  starting transfers between devices  38.3 us (46%)
  waiting for transfers between devices  24.7 us (30%)
  Pallas kernels  17.5 us (21%)
  local copies, waits for them, and re-layouts  1.57 us (2%)
  between operations  0.84 us (1%)
    ppermute x12, starting transfers between devices, along_z(): lax.ppermute(blocks[dz], both_axes, toward(dz))  18.9 us
    ppermute x12, starting transfers between devices, to_owners(): lax.ppermute(part, both_axes, grid.pairs(lambda x, y, z, c, dx=dx, dy=dy:...  15 us
    ppermute x12, waiting for transfers between devices, to_owners(): lax.ppermute(part, both_axes, grid.pairs(lambda x, y, z, c, dx=dx, dy=dy:...  10.9 us
    ppermute x12, waiting for transfers between devices, along_z(): lax.ppermute(blocks[dz], both_axes, toward(dz))  7.82 us
    ppermute x4, waiting for transfers between devices, from_peer(): return lax.ppermute(value, both_axes, [(b, a) for a, b in grid.pairs(move)])  4.67 us
    pallas_call x1, Pallas kernels, shards(): pl.pallas_call(functools.partial(backward_block_kernel, grid, slots), gri...  4.44 us
    pallas_call x1, Pallas kernels, shards(): pl.pallas_call(functools.partial(forward_block_kernel, grid, slots), grid...  3.77 us
    ppermute x4, starting transfers between devices, from_peer(): return lax.ppermute(value, both_axes, [(b, a) for a, b in grid.pairs(move)])  3.22 us
  transfers between devices with their start and end apart: 36, of which 12 were waited for; matrix products, arithmetic and copies ran while one was open for 0% of the time, Pallas kernels for 15%

profile of v7, /device:TPU:0, one launch (start us, length us, event | category | flops | bytes accessed | tf_op | source)
XLA Modules:
  0.0 82.9 jit_solution(10196893822383552256)
XLA Ops:
  0.6 3.1 %collective-permute-start = (f32[256,128]{1,0:T(8,128)}, f32[256,128]{1,0:T(8,128)S(1)}, u32[]{:S(2)}, u32[]{:S(2)}) collective-permute-start(f32[256,128]{1,0:T(8,128)} %features_ref.1), channel_id=1, source_target_pairs={{0,4},{1,5},{2,6},{3,7},{4,0},{5,1},{6,2},{7,3},{8,12},{9,13},{10,... | collective-permute-start | bytes 393224 | tf_op jit(solution)/shard_map/ppermute | solution.py:371
  3.7 2.6 %collective-permute-start.1 = (f32[256,128]{1,0:T(8,128)}, f32[256,128]{1,0:T(8,128)S(1)}, u32[]{:S(2)}, u32[]{:S(2)}) collective-permute-start(f32[256,128]{1,0:T(8,128)} %features_ref.1), channel_id=1, source_target_pairs={{0,8},{1,9},{2,10},{3,11},{4,12},{5,13},{6,14},{7,15},{8,0},{9,1},... | collective-permute-start | bytes 393224 | tf_op jit(solution)/shard_map/ppermute | solution.py:371
  6.3 2.3 %pack.1 = (s32[32,384]{1,0:T(8,128)}, s32[8,896]{1,0:T(8,128)}, s32[8,896]{1,0:T(8,128)}, s32[8,896]{1,0:T(8,128)}, s32[8,896]{1,0:T(8,128)}) custom-call(s32[1]{0:T(128)} %bitcast.me_ref, s32[4,32]{1,0:T(4,128)} %bitcast.13, s32[4,32]{1,0:T(4,128)} %bitcast.14, s32[32,256]{1,0:T(8,128)} %bitcast.11, s32[32,256]{1,0:T(8,128)} %bitcast.12), custom_call_target="tpu_custom_call" | custom-call | flops 2147483648 | bytes 8388608 | tf_op jit(solution)/shard_map/pack/pallas_call | solution.py:410
  9.6 3.5 %collective-permute-start.4 = (s32[8,896]{1,0:T(8,128)}, s32[8,896]{1,0:T(8,128)S(1)}, u32[]{:S(2)}, u32[]{:S(2)}) collective-permute-start(s32[8,896]{1,0:T(8,128)} %get-tuple-element.52), channel_id=1, source_target_pairs={{0,8},{1,9},{2,10},{3,11},{4,12},{5,13},{6,14},{7,15},{8,0},{9,1},... | collective-permute-start | bytes 86024 | tf_op jit(solution)/shard_map/ppermute | solution.py:371
  13.1 4.7 %collective-permute-done.1.refs_4_ = f32[256,128]{1,0:T(8,128)S(1)} collective-permute-done((f32[256,128]{1,0:T(8,128)}, f32[256,128]{1,0:T(8,128)S(1)}, u32[]{:S(2)}, u32[]{:S(2)}) %collective-permute-start.1) | collective-permute-done | bytes 131104 | tf_op jit(solution)/shard_map/ppermute | solution.py:371
  17.8 2.6 %collective-permute-done.4.refs_2_ = s32[8,896]{1,0:T(8,128)S(1)} collective-permute-done((s32[8,896]{1,0:T(8,128)}, s32[8,896]{1,0:T(8,128)S(1)}, u32[]{:S(2)}, u32[]{:S(2)}) %collective-permute-start.4) | collective-permute-done | bytes 28704 | tf_op jit(solution)/shard_map/ppermute | solution.py:371
  23.3 1.6 %collective-permute-start.7 = (s32[64,384]{1,0:T(8,128)S(1)}, s32[64,384]{1,0:T(8,128)S(1)}, u32[]{:S(2)}, u32[]{:S(2)}) collective-permute-start(s32[64,384]{1,0:T(8,128)S(1)} %get-tuple-element.54.refs_0_), channel_id=1, source_target_pairs={{16,0},{17,1},{18,2},{19,3},{20,4},{21,5},{22,6},{23,7},{24,8},{25... | collective-permute-start | bytes 294920 | tf_op jit(solution)/shard_map/ppermute | solution.py:424
  24.9 1.5 %collective-permute-start.8 = (s32[32,512]{1,0:T(8,128)S(1)}, s32[32,512]{1,0:T(8,128)S(1)}, u32[]{:S(2)}, u32[]{:S(2)}) collective-permute-start(s32[32,512]{1,0:T(8,128)S(1)} %get-tuple-element.70.refs_2_.refs_0_), channel_id=1, source_target_pairs={{2,0},{3,1},{0,2},{1,3},{6,4},{7,5},{4,6},{5,7},{10,8},{11,9},{8,1... | collective-permute-start | bytes 196616 | tf_op jit(solution)/shard_map/ppermute | solution.py:424
  26.9 2.2 %collective-permute-done.8.refs_3_.refs_1_ = s32[32,512]{1,0:T(8,128)S(1)} collective-permute-done((s32[32,512]{1,0:T(8,128)S(1)}, s32[32,512]{1,0:T(8,128)S(1)}, u32[]{:S(2)}, u32[]{:S(2)}) %collective-permute-start.8) | collective-permute-done | bytes 65568 | tf_op jit(solution)/shard_map/ppermute | solution.py:424
  29.2 3.8 %forward_block.1 = (bf16[1024,2048]{1,0:T(8,128)(2,1)S(1)}, f32[32,128]{1,0:T(8,128)S(1)}) custom-call(s32[1]{0:T(128)} %bitcast.me_ref, s32[64,384]{1,0:T(8,128)S(1)} %get-tuple-element.54.refs_0_, s32[64,384]{1,0:T(8,128)S(1)} %collective-permute-done.7.refs_1_, s32[32,512]{1,0:T(8,128)S(1)} %get-tuple-element.70.refs_2_.refs_0_, ...), custom_call_target="tpu_custom_call" | custom-call | flops 65536 | bytes 65536 | tf_op jit(solution)/shard_map/forward_block/pallas_call | solution.py:469
  34.4 2.3 %forward_sum.1 = (f32[256,128]{1,0:T(8,128)S(1)}, f32[256,128]{1,0:T(8,128)S(1)}, f32[256,128]{1,0:T(8,128)S(1)}, f32[256,128]{1,0:T(8,128)S(1)}, f32[256,128]{1,0:T(8,128)S(1)}) custom-call(s32[1]{0:T(128)} %bitcast.me_ref, f32[32,128]{1,0:T(8,128)S(1)} %get-tuple-element.56.root_ref, bf16[1024,2048]{1,0:T(8,128)(2,1)S(1)} %get-tuple-element.59.block_ref, ...), custom_call_target="tpu_custom_call" | custom-call | flops 1073741824 | bytes 4194304 | tf_op jit(solution)/shard_map/forward_sum/pallas_call | solution.py:487
  36.7 1.6 %collective-permute-start.15 = (f32[256,128]{1,0:T(8,128)S(1)}, f32[256,128]{1,0:T(8,128)S(1)}, u32[]{:S(2)}, u32[]{:S(2)}) collective-permute-start(f32[256,128]{1,0:T(8,128)S(1)} %get-tuple-element.69), channel_id=1, source_target_pairs={{0,18},{1,19},{2,16},{3,17},{4,22},{5,23},{6,20},{7,21},{8,26},{9,... | collective-permute-start | bytes 393224 | tf_op jit(solution)/shard_map/ppermute | solution.py:392
  40.3 4.4 %backward_block.1.block_ref = bf16[1024,2048]{1,0:T(8,128)(2,1)S(1)} custom-call(s32[1]{0:T(128)} %bitcast.me_ref, s32[32,512]{1,0:T(8,128)S(1)} %get-tuple-element.70.refs_2_.refs_0_, s32[32,512]{1,0:T(8,128)S(1)} %collective-permute-done.8.refs_3_.refs_1_), custom_call_target="tpu_custom_call" | custom-call | flops 1073741824 | bytes 4194304 | tf_op jit(solution)/shard_map/backward_block/pallas_call | solution.py:500
  46.1 1.7 %middle.1 = (f32[256,256]{1,0:T(8,128)}, f32[256,128]{1,0:T(8,128)S(1)}, f32[64,128]{1,0:T(8,128)S(1)}, f32[64,128]{1,0:T(8,128)S(1)}, f32[64,128]{1,0:T(8,128)S(1)}, /*index=5*/f32[64,128]{1,0:T(8,128)S(1)}) custom-call(s32[1]{0:T(128)} %bitcast.me_ref, f32[256,128]{1,0:T(8,128)S(1)} %get-tuple-element.64.scale_ref, f32[256,128]{1,0:T(8,128)S(1)} %copy-done, ...), custom_call_target="tpu_custom_call" | custom-call | flops 301989888 | bytes 1048576 | tf_op jit(solution)/shard_map/middle/pallas_call | solution.py:514
  47.8 2.5 %collective-permute-start.21 = (f32[256,128]{1,0:T(8,128)S(1)}, f32[256,128]{1,0:T(8,128)S(1)}, u32[]{:S(2)}, u32[]{:S(2)}) collective-permute-start(f32[256,128]{1,0:T(8,128)S(1)} %get-tuple-element.74.refs_0_.sent_ref), channel_id=1, source_target_pairs={{0,12},{1,13},{2,14},{3,15},{4,8},{5,9},{6,10},{7,11},{8,4},{9,5},... | collective-permute-start | bytes 393224 | tf_op jit(solution)/shard_map/ppermute | solution.py:371
  50.2 1.9 %collective-permute-start.19 = (f32[256,128]{1,0:T(8,128)S(1)}, f32[256,128]{1,0:T(8,128)S(1)}, u32[]{:S(2)}, u32[]{:S(2)}) collective-permute-start(f32[256,128]{1,0:T(8,128)S(1)} %get-tuple-element.74.refs_0_.sent_ref), channel_id=1, source_target_pairs={{0,8},{1,9},{2,10},{3,11},{4,12},{5,13},{6,14},{7,15},{8,0},{9,1},... | collective-permute-start | bytes 393224 | tf_op jit(solution)/shard_map/ppermute | solution.py:371
  54.2 1.9 %collective-permute-done.22.refs_1_ = f32[64,128]{1,0:T(8,128)S(1)} collective-permute-done((f32[64,128]{1,0:T(8,128)S(1)}, f32[64,128]{1,0:T(8,128)S(1)}, u32[]{:S(2)}, u32[]{:S(2)}) %collective-permute-start.22) | collective-permute-done | bytes 32800 | tf_op jit(solution)/shard_map/ppermute | solution.py:392
  57.6 3.3 %collective-permute-done.24.refs_3_ = f32[64,128]{1,0:T(8,128)S(1)} collective-permute-done((f32[64,128]{1,0:T(8,128)S(1)}, f32[64,128]{1,0:T(8,128)S(1)}, u32[]{:S(2)}, u32[]{:S(2)}) %collective-permute-start.24) | collective-permute-done | bytes 32800 | tf_op jit(solution)/shard_map/ppermute | solution.py:392
  62.0 3.0 %collective-permute-start.27 = (f32[64,128]{1,0:T(8,128)S(1)}, f32[64,128]{1,0:T(8,128)S(1)}, u32[]{:S(2)}, u32[]{:S(2)}) collective-permute-start(f32[64,128]{1,0:T(8,128)S(1)} %add_parts.1.refs_0_), channel_id=1, source_target_pairs={{0,8},{1,9},{2,10},{3,11},{4,12},{5,13},{6,14},{7,15},{8,0},{9,1},... | collective-permute-start | bytes 98312 | tf_op jit(solution)/shard_map/ppermute | solution.py:371
  66.4 2.1 %backward_sum.1 = (f32[256,128]{1,0:T(8,128)S(1)}, f32[256,128]{1,0:T(8,128)S(1)}, f32[256,128]{1,0:T(8,128)S(1)}, f32[256,128]{1,0:T(8,128)S(1)}) custom-call(s32[1]{0:T(128)} %bitcast.me_ref, bf16[1024,2048]{1,0:T(8,128)(2,1)S(1)} %backward_block.1.block_ref, f32[256,128]{1,0:T(8,128)S(1)} %get-tuple-element.74.refs_0_.sent_ref, ...), custom_call_target="tpu_custom_call" | custom-call | flops 1073741824 | bytes 4194304 | tf_op jit(solution)/shard_map/backward_sum/pallas_call | solution.py:541
  69.2 1.9 %collective-permute-start.30 = (f32[256,128]{1,0:T(8,128)S(1)}, f32[256,128]{1,0:T(8,128)S(1)}, u32[]{:S(2)}, u32[]{:S(2)}) collective-permute-start(f32[256,128]{1,0:T(8,128)S(1)} %get-tuple-element.85), channel_id=1, source_target_pairs={{0,2},{1,3},{2,0},{3,1},{4,6},{5,7},{6,4},{7,5},{8,10},{9,11},{10,... | collective-permute-start | bytes 393224 | tf_op jit(solution)/shard_map/ppermute | solution.py:392
  74.0 1.9 %collective-permute-start.34 = (f32[64,128]{1,0:T(8,128)S(1)}, f32[64,128]{1,0:T(8,128)S(1)}, u32[]{:S(2)}, u32[]{:S(2)}) collective-permute-start(f32[64,128]{1,0:T(8,128)S(1)} %add_cores.1.refs_4_), channel_id=1, source_target_pairs={{0,2},{1,3},{2,0},{3,1},{4,6},{5,7},{6,4},{7,5},{8,10},{9,11},{10,... | collective-permute-start | bytes 98312 | tf_op jit(solution)/shard_map/ppermute | solution.py:392
  77.3 1.9 %collective-permute-start.35 = (f32[64,128]{1,0:T(8,128)S(1)}, f32[64,128]{1,0:T(8,128)S(1)}, u32[]{:S(2)}, u32[]{:S(2)}) collective-permute-start(f32[64,128]{1,0:T(8,128)S(1)} %add_cores.1.refs_4_), channel_id=1, source_target_pairs={{0,18},{1,19},{2,16},{3,17},{4,22},{5,23},{6,20},{7,21},{8,26},{9,... | collective-permute-start | bytes 98312 | tf_op jit(solution)/shard_map/ppermute | solution.py:392
  79.3 2.9 %collective-permute-done.35.refs_7_ = f32[64,128]{1,0:T(8,128)S(1)} collective-permute-done((f32[64,128]{1,0:T(8,128)S(1)}, f32[64,128]{1,0:T(8,128)S(1)}, u32[]{:S(2)}, u32[]{:S(2)}) %collective-permute-start.35) | collective-permute-done | bytes 32800 | tf_op jit(solution)/shard_map/ppermute | solution.py:392
  (74 shorter events, 20.8 us)
Async XLA Ops:
  0.6 12.5 %collective-permute-start = (f32[256,128]{1,0:T(8,128)}, f32[256,128]{1,0:T(8,128)S(1)}, u32[]{:S(2)}, u32[]{:S(2)}) collective-permute-start(f32[256,128]{1,0:T(8,128)} %features_ref.1), channel_id=1, source_target_pairs={{0,4},{1,5},{2,6},{3,7},{4,0},{5,1},{6,2},{7,3},{8,12},{9,13},{10,... | collective-permute-start | bytes 393224 | tf_op jit(solution)/shard_map/ppermute | solution.py:371
  3.7 14.1 %collective-permute-start.1 = (f32[256,128]{1,0:T(8,128)}, f32[256,128]{1,0:T(8,128)S(1)}, u32[]{:S(2)}, u32[]{:S(2)}) collective-permute-start(f32[256,128]{1,0:T(8,128)} %features_ref.1), channel_id=1, source_target_pairs={{0,8},{1,9},{2,10},{3,11},{4,12},{5,13},{6,14},{7,15},{8,0},{9,1},... | collective-permute-start | bytes 393224 | tf_op jit(solution)/shard_map/ppermute | solution.py:371
  6.3 11.5 %collective-permute-start.2 = (f32[256,128]{1,0:T(8,128)}, f32[256,128]{1,0:T(8,128)S(1)}, u32[]{:S(2)}, u32[]{:S(2)}) collective-permute-start(f32[256,128]{1,0:T(8,128)} %features_ref.1), channel_id=1, source_target_pairs={{0,12},{1,13},{2,14},{3,15},{4,8},{5,9},{6,10},{7,11},{8,4},{9,5},... | collective-permute-start | bytes 393224 | tf_op jit(solution)/shard_map/ppermute | solution.py:371
  8.6 9.2 %collective-permute-start.3 = (s32[8,896]{1,0:T(8,128)}, s32[8,896]{1,0:T(8,128)S(1)}, u32[]{:S(2)}, u32[]{:S(2)}) collective-permute-start(s32[8,896]{1,0:T(8,128)} %get-tuple-element.51), channel_id=1, source_target_pairs={{0,4},{1,5},{2,6},{3,7},{4,0},{5,1},{6,2},{7,3},{8,12},{9,13},{10,... | collective-permute-start | bytes 86024 | tf_op jit(solution)/shard_map/ppermute | solution.py:371
  9.6 10.8 %collective-permute-start.4 = (s32[8,896]{1,0:T(8,128)}, s32[8,896]{1,0:T(8,128)S(1)}, u32[]{:S(2)}, u32[]{:S(2)}) collective-permute-start(s32[8,896]{1,0:T(8,128)} %get-tuple-element.52), channel_id=1, source_target_pairs={{0,8},{1,9},{2,10},{3,11},{4,12},{5,13},{6,14},{7,15},{8,0},{9,1},... | collective-permute-start | bytes 86024 | tf_op jit(solution)/shard_map/ppermute | solution.py:371
  13.1 7.3 %collective-permute-start.5 = (s32[8,896]{1,0:T(8,128)}, s32[8,896]{1,0:T(8,128)S(1)}, u32[]{:S(2)}, u32[]{:S(2)}) collective-permute-start(s32[8,896]{1,0:T(8,128)} %get-tuple-element.53), channel_id=1, source_target_pairs={{0,12},{1,13},{2,14},{3,15},{4,8},{5,9},{6,10},{7,11},{8,4},{9,5},... | collective-permute-start | bytes 86024 | tf_op jit(solution)/shard_map/ppermute | solution.py:371
  23.3 5.8 %collective-permute-start.7 = (s32[64,384]{1,0:T(8,128)S(1)}, s32[64,384]{1,0:T(8,128)S(1)}, u32[]{:S(2)}, u32[]{:S(2)}) collective-permute-start(s32[64,384]{1,0:T(8,128)S(1)} %get-tuple-element.54.refs_0_), channel_id=1, source_target_pairs={{16,0},{17,1},{18,2},{19,3},{20,4},{21,5},{22,6},{23,7},{24,8},{25... | collective-permute-start | bytes 294920 | tf_op jit(solution)/shard_map/ppermute | solution.py:424
  26.4 6.6 %collective-permute-start.9 = (f32[256,128]{1,0:T(8,128)S(1)}, f32[256,128]{1,0:T(8,128)S(1)}, u32[]{:S(2)}, u32[]{:S(2)}) collective-permute-start(f32[256,128]{1,0:T(8,128)S(1)} %copy-done), channel_id=1, source_target_pairs={{0,1},{1,0},{2,3},{3,2},{4,5},{5,4},{6,7},{7,6},{8,9},{9,8},{10,11... | collective-permute-start | bytes 393224 | tf_op jit(solution)/shard_map/ppermute | solution.py:376
  26.4 6.6 %collective-permute-start.10 = (f32[256,128]{1,0:T(8,128)S(1)}, f32[256,128]{1,0:T(8,128)S(1)}, u32[]{:S(2)}, u32[]{:S(2)}) collective-permute-start(f32[256,128]{1,0:T(8,128)S(1)} %collective-permute-done.refs_2_), channel_id=1, source_target_pairs={{0,1},{1,0},{2,3},{3,2},{4,5},{5,4},{6,7},{7,6},{8,9},{9,8},{10,11... | collective-permute-start | bytes 393224 | tf_op jit(solution)/shard_map/ppermute | solution.py:376
  26.9 6.1 %collective-permute-start.11 = (f32[256,128]{1,0:T(8,128)S(1)}, f32[256,128]{1,0:T(8,128)S(1)}, u32[]{:S(2)}, u32[]{:S(2)}) collective-permute-start(f32[256,128]{1,0:T(8,128)S(1)} %collective-permute-done.1.refs_4_), channel_id=1, source_target_pairs={{0,1},{1,0},{2,3},{3,2},{4,5},{5,4},{6,7},{7,6},{8,9},{9,8},{10,11... | collective-permute-start | bytes 393224 | tf_op jit(solution)/shard_map/ppermute | solution.py:376
  36.7 8.0 %collective-permute-start.15 = (f32[256,128]{1,0:T(8,128)S(1)}, f32[256,128]{1,0:T(8,128)S(1)}, u32[]{:S(2)}, u32[]{:S(2)}) collective-permute-start(f32[256,128]{1,0:T(8,128)S(1)} %get-tuple-element.69), channel_id=1, source_target_pairs={{0,18},{1,19},{2,16},{3,17},{4,22},{5,23},{6,20},{7,21},{8,26},{9,... | collective-permute-start | bytes 393224 | tf_op jit(solution)/shard_map/ppermute | solution.py:392
  38.3 7.8 %collective-permute-start.13 = (f32[256,128]{1,0:T(8,128)S(1)}, f32[256,128]{1,0:T(8,128)S(1)}, u32[]{:S(2)}, u32[]{:S(2)}) collective-permute-start(f32[256,128]{1,0:T(8,128)S(1)} %get-tuple-element.67), channel_id=1, source_target_pairs={{0,16},{1,17},{2,18},{3,19},{4,20},{5,21},{6,22},{7,23},{8,24},{9,... | collective-permute-start | bytes 393224 | tf_op jit(solution)/shard_map/ppermute | solution.py:392
  39.8 6.3 %collective-permute-start.14 = (f32[256,128]{1,0:T(8,128)S(1)}, f32[256,128]{1,0:T(8,128)S(1)}, u32[]{:S(2)}, u32[]{:S(2)}) collective-permute-start(f32[256,128]{1,0:T(8,128)S(1)} %get-tuple-element.68), channel_id=1, source_target_pairs={{0,2},{1,3},{2,0},{3,1},{4,6},{5,7},{6,4},{7,5},{8,10},{9,11},{10,... | collective-permute-start | bytes 393224 | tf_op jit(solution)/shard_map/ppermute | solution.py:392
  47.8 13.1 %collective-permute-start.21 = (f32[256,128]{1,0:T(8,128)S(1)}, f32[256,128]{1,0:T(8,128)S(1)}, u32[]{:S(2)}, u32[]{:S(2)}) collective-permute-start(f32[256,128]{1,0:T(8,128)S(1)} %get-tuple-element.74.refs_0_.sent_ref), channel_id=1, source_target_pairs={{0,12},{1,13},{2,14},{3,15},{4,8},{5,9},{6,10},{7,11},{8,4},{9,5},... | collective-permute-start | bytes 393224 | tf_op jit(solution)/shard_map/ppermute | solution.py:371
  50.2 10.7 %collective-permute-start.17 = (f32[256,128]{1,0:T(8,128)S(1)}, f32[256,128]{1,0:T(8,128)S(1)}, u32[]{:S(2)}, u32[]{:S(2)}) collective-permute-start(f32[256,128]{1,0:T(8,128)S(1)} %get-tuple-element.74.refs_0_.sent_ref), channel_id=1, source_target_pairs={{0,4},{1,5},{2,6},{3,7},{4,0},{5,1},{6,2},{7,3},{8,12},{9,13},{10,... | collective-permute-start | bytes 393224 | tf_op jit(solution)/shard_map/ppermute | solution.py:371
  50.2 11.2 %collective-permute-start.19 = (f32[256,128]{1,0:T(8,128)S(1)}, f32[256,128]{1,0:T(8,128)S(1)}, u32[]{:S(2)}, u32[]{:S(2)}) collective-permute-start(f32[256,128]{1,0:T(8,128)S(1)} %get-tuple-element.74.refs_0_.sent_ref), channel_id=1, source_target_pairs={{0,8},{1,9},{2,10},{3,11},{4,12},{5,13},{6,14},{7,15},{8,0},{9,1},... | collective-permute-start | bytes 393224 | tf_op jit(solution)/shard_map/ppermute | solution.py:371
  61.5 4.9 %collective-permute-start.20 = (f32[256,128]{1,0:T(8,128)S(1)}, f32[256,128]{1,0:T(8,128)S(1)}, u32[]{:S(2)}, u32[]{:S(2)}) collective-permute-start(f32[256,128]{1,0:T(8,128)S(1)} %collective-permute-done.19.refs_4_), channel_id=1, source_target_pairs={{0,1},{1,0},{2,3},{3,2},{4,5},{5,4},{6,7},{7,6},{8,9},{9,8},{10,11... | collective-permute-start | bytes 393224 | tf_op jit(solution)/shard_map/ppermute | solution.py:376
  62.0 9.1 %collective-permute-start.26 = (f32[64,128]{1,0:T(8,128)S(1)}, f32[64,128]{1,0:T(8,128)S(1)}, u32[]{:S(2)}, u32[]{:S(2)}) collective-permute-start(f32[64,128]{1,0:T(8,128)S(1)} %add_parts.1.refs_0_), channel_id=1, source_target_pairs={{0,4},{1,5},{2,6},{3,7},{4,0},{5,1},{6,2},{7,3},{8,12},{9,13},{10,... | collective-permute-start | bytes 98312 | tf_op jit(solution)/shard_map/ppermute | solution.py:371
  62.0 10.1 %collective-permute-start.27 = (f32[64,128]{1,0:T(8,128)S(1)}, f32[64,128]{1,0:T(8,128)S(1)}, u32[]{:S(2)}, u32[]{:S(2)}) collective-permute-start(f32[64,128]{1,0:T(8,128)S(1)} %add_parts.1.refs_0_), channel_id=1, source_target_pairs={{0,8},{1,9},{2,10},{3,11},{4,12},{5,13},{6,14},{7,15},{8,0},{9,1},... | collective-permute-start | bytes 98312 | tf_op jit(solution)/shard_map/ppermute | solution.py:371
  65.0 7.1 %collective-permute-start.28 = (f32[64,128]{1,0:T(8,128)S(1)}, f32[64,128]{1,0:T(8,128)S(1)}, u32[]{:S(2)}, u32[]{:S(2)}) collective-permute-start(f32[64,128]{1,0:T(8,128)S(1)} %add_parts.1.refs_0_), channel_id=1, source_target_pairs={{0,12},{1,13},{2,14},{3,15},{4,8},{5,9},{6,10},{7,11},{8,4},{9,5},... | collective-permute-start | bytes 98312 | tf_op jit(solution)/shard_map/ppermute | solution.py:371
  68.5 13.6 %collective-permute-start.29 = (f32[256,128]{1,0:T(8,128)S(1)}, f32[256,128]{1,0:T(8,128)S(1)}, u32[]{:S(2)}, u32[]{:S(2)}) collective-permute-start(f32[256,128]{1,0:T(8,128)S(1)} %get-tuple-element.84), channel_id=1, source_target_pairs={{0,16},{1,17},{2,18},{3,19},{4,20},{5,21},{6,22},{7,23},{8,24},{9,... | collective-permute-start | bytes 393224 | tf_op jit(solution)/shard_map/ppermute | solution.py:392
  69.2 13.0 %collective-permute-start.30 = (f32[256,128]{1,0:T(8,128)S(1)}, f32[256,128]{1,0:T(8,128)S(1)}, u32[]{:S(2)}, u32[]{:S(2)}) collective-permute-start(f32[256,128]{1,0:T(8,128)S(1)} %get-tuple-element.85), channel_id=1, source_target_pairs={{0,2},{1,3},{2,0},{3,1},{4,6},{5,7},{6,4},{7,5},{8,10},{9,11},{10,... | collective-permute-start | bytes 393224 | tf_op jit(solution)/shard_map/ppermute | solution.py:392
  71.1 11.1 %collective-permute-start.31 = (f32[256,128]{1,0:T(8,128)S(1)}, f32[256,128]{1,0:T(8,128)S(1)}, u32[]{:S(2)}, u32[]{:S(2)}) collective-permute-start(f32[256,128]{1,0:T(8,128)S(1)} %get-tuple-element.86), channel_id=1, source_target_pairs={{0,18},{1,19},{2,16},{3,17},{4,22},{5,23},{6,20},{7,21},{8,26},{9,... | collective-permute-start | bytes 393224 | tf_op jit(solution)/shard_map/ppermute | solution.py:392
  74.0 5.3 %collective-permute-start.34 = (f32[64,128]{1,0:T(8,128)S(1)}, f32[64,128]{1,0:T(8,128)S(1)}, u32[]{:S(2)}, u32[]{:S(2)}) collective-permute-start(f32[64,128]{1,0:T(8,128)S(1)} %add_cores.1.refs_4_), channel_id=1, source_target_pairs={{0,2},{1,3},{2,0},{3,1},{4,6},{5,7},{6,4},{7,5},{8,10},{9,11},{10,... | collective-permute-start | bytes 98312 | tf_op jit(solution)/shard_map/ppermute | solution.py:392
  (19 other events, 118.2 us)

commit v8 on v7

--- a/solution.py
+++ b/solution.py
@@ -423,9 +423,11 @@
     def from_peer(value, move):
         return lax.ppermute(value, both_axes, [(b, a) for a, b in grid.pairs(move)])
 
-    along = along_z([features] * DEPTH)
+    along = [features] + [lax.ppermute(features, both_axes, toward(dz)) for dz in (1, 2)]
     got_planes = along_z(planes)
     *along, got_planes[0] = lax.optimization_barrier((*along, got_planes[0]))
+    *got_planes, later = lax.optimization_barrier((*got_planes, features))
+    along += [lax.ppermute(later, both_axes, toward(dz)) for dz in range(3, DEPTH)]
     small = pl.CostEstimate(flops=2**14, bytes_accessed=2**18, transcendentals=0)
     both = pl.pallas_call(
         functools.partial(plane_kernel, wide),

time: 83.2 us -> 80.6 us (0.969)
  waiting for transfers between devices: 24.7 us -> 19.1 us
  starting transfers between devices: 38.3 us -> 41.3 us
    ppermute x0 -> x3, starting transfers between devices: none -> 9.26 us  [the longest x2 5.68 us: shards(): lax.ppermute(features, both_axes, toward(dz))]
    ppermute x12 -> x9, starting transfers between devices: 18.9 us -> 13.2 us  [along_z(): lax.ppermute(blocks[dz], both_axes, toward(dz))]
    ppermute x12 -> x9, waiting for transfers between devices: 7.82 us -> 2.37 us  [along_z(): lax.ppermute(blocks[dz], both_axes, toward(dz))]
    ppermute x12, waiting for transfers between devices: 10.9 us -> 12.3 us  [to_owners(): lax.ppermute(part, both_axes, grid.pairs(lambda x, y, z, c, dx=dx, dy=dy:...]
    ppermute x4, waiting for transfers between devices: 4.67 us -> 3.43 us  [from_peer(): return lax.ppermute(value, both_axes, [(b, a) for a, b in grid.pairs(move)])]
    ppermute x12, starting transfers between devices: 15 us -> 13.8 us  [to_owners(): lax.ppermute(part, both_axes, grid.pairs(lambda x, y, z, c, dx=dx, dy=dy:...]
  transfers between devices with their start and end apart: 36 -> 36, of which waited for: 12 -> 10; matrix products, arithmetic and copies ran while one was open for 0% -> 0% of each run, Pallas kernels for 15% -> 16%
where the time goes in v8:
time: 80.6 us; the launch traced here: 80.3 us
  starting transfers between devices  41.3 us (51%)
  waiting for transfers between devices  19.1 us (24%)
  Pallas kernels  17.5 us (22%)
  local copies, waits for them, and re-layouts  1.57 us (2%)
  between operations  0.83 us (1%)
    ppermute x12, starting transfers between devices, to_owners(): lax.ppermute(part, both_axes, grid.pairs(lambda x, y, z, c, dx=dx, dy=dy:...  13.8 us
    ppermute x9, starting transfers between devices, along_z(): lax.ppermute(blocks[dz], both_axes, toward(dz))  13.2 us
    ppermute x12, waiting for transfers between devices, to_owners(): lax.ppermute(part, both_axes, grid.pairs(lambda x, y, z, c, dx=dx, dy=dy:...  12.3 us
    ppermute x2, starting transfers between devices, shards(): lax.ppermute(features, both_axes, toward(dz))  5.68 us
    pallas_call x1, Pallas kernels, shards(): pl.pallas_call(functools.partial(backward_block_kernel, grid, slots), gri...  4.44 us
    pallas_call x1, Pallas kernels, shards(): pl.pallas_call(functools.partial(forward_block_kernel, grid, slots), grid...  3.77 us
    ppermute x1, starting transfers between devices, shards(): lax.ppermute(later, both_axes, toward(dz))  3.58 us
    ppermute x4, waiting for transfers between devices, from_peer(): return lax.ppermute(value, both_axes, [(b, a) for a, b in grid.pairs(move)])  3.43 us
  transfers between devices with their start and end apart: 36, of which 10 were waited for; matrix products, arithmetic and copies ran while one was open for 0% of the time, Pallas kernels for 16%

profile of v8, /device:TPU:0, one launch (start us, length us, event | category | flops | bytes accessed | tf_op | source)
XLA Modules:
  0.0 80.3 jit_solution(2938083281604554032)
XLA Ops:
  0.6 3.1 %collective-permute-start = (f32[256,128]{1,0:T(8,128)}, f32[256,128]{1,0:T(8,128)S(1)}, u32[]{:S(2)}, u32[]{:S(2)}) collective-permute-start(f32[256,128]{1,0:T(8,128)} %features_ref.1), channel_id=1, source_target_pairs={{0,4},{1,5},{2,6},{3,7},{4,0},{5,1},{6,2},{7,3},{8,12},{9,13},{10,... | collective-permute-start | bytes 393224 | tf_op jit(solution)/shard_map/ppermute | solution.py:426
  3.7 2.6 %collective-permute-start.1 = (f32[256,128]{1,0:T(8,128)}, f32[256,128]{1,0:T(8,128)S(1)}, u32[]{:S(2)}, u32[]{:S(2)}) collective-permute-start(f32[256,128]{1,0:T(8,128)} %features_ref.1), channel_id=1, source_target_pairs={{0,8},{1,9},{2,10},{3,11},{4,12},{5,13},{6,14},{7,15},{8,0},{9,1},... | collective-permute-start | bytes 393224 | tf_op jit(solution)/shard_map/ppermute | solution.py:426
  6.3 2.3 %pack.1 = (s32[32,384]{1,0:T(8,128)}, s32[8,896]{1,0:T(8,128)}, s32[8,896]{1,0:T(8,128)}, s32[8,896]{1,0:T(8,128)}, s32[8,896]{1,0:T(8,128)}) custom-call(s32[1]{0:T(128)} %bitcast.me_ref, s32[4,32]{1,0:T(4,128)} %bitcast.13, s32[4,32]{1,0:T(4,128)} %bitcast.14, s32[32,256]{1,0:T(8,128)} %bitcast.11, s32[32,256]{1,0:T(8,128)} %bitcast.12), custom_call_target="tpu_custom_call" | custom-call | flops 2147483648 | bytes 8388608 | tf_op jit(solution)/shard_map/pack/pallas_call | solution.py:410
  9.2 3.9 %collective-permute-start.4 = (s32[8,896]{1,0:T(8,128)}, s32[8,896]{1,0:T(8,128)S(1)}, u32[]{:S(2)}, u32[]{:S(2)}) collective-permute-start(s32[8,896]{1,0:T(8,128)} %get-tuple-element.57), channel_id=1, source_target_pairs={{0,12},{1,13},{2,14},{3,15},{4,8},{5,9},{6,10},{7,11},{8,4},{9,5},... | collective-permute-start | bytes 86024 | tf_op jit(solution)/shard_map/ppermute | solution.py:371
  16.3 3.6 %collective-permute-start.8 = (f32[256,128]{1,0:T(8,128)S(1)}, f32[256,128]{1,0:T(8,128)S(1)}, u32[]{:S(2)}, u32[]{:S(2)}) collective-permute-start(f32[256,128]{1,0:T(8,128)S(1)} %copy-done), channel_id=1, source_target_pairs={{0,12},{1,13},{2,14},{3,15},{4,8},{5,9},{6,10},{7,11},{8,4},{9,5},... | collective-permute-start | bytes 393224 | tf_op jit(solution)/shard_map/ppermute | solution.py:430
  20.7 1.6 %collective-permute-start.6 = (s32[64,384]{1,0:T(8,128)S(1)}, s32[64,384]{1,0:T(8,128)S(1)}, u32[]{:S(2)}, u32[]{:S(2)}) collective-permute-start(s32[64,384]{1,0:T(8,128)S(1)} %get-tuple-element.62.refs_0_), channel_id=1, source_target_pairs={{16,0},{17,1},{18,2},{19,3},{20,4},{21,5},{22,6},{23,7},{24,8},{25... | collective-permute-start | bytes 294920 | tf_op jit(solution)/shard_map/ppermute | solution.py:424
  22.3 1.5 %collective-permute-start.7 = (s32[32,512]{1,0:T(8,128)S(1)}, s32[32,512]{1,0:T(8,128)S(1)}, u32[]{:S(2)}, u32[]{:S(2)}) collective-permute-start(s32[32,512]{1,0:T(8,128)S(1)} %get-tuple-element.78.refs_2_.refs_0_), channel_id=1, source_target_pairs={{2,0},{3,1},{0,2},{1,3},{6,4},{7,5},{4,6},{5,7},{10,8},{11,9},{8,1... | collective-permute-start | bytes 196616 | tf_op jit(solution)/shard_map/ppermute | solution.py:424
  24.3 2.2 %collective-permute-done.7.refs_3_.refs_1_ = s32[32,512]{1,0:T(8,128)S(1)} collective-permute-done((s32[32,512]{1,0:T(8,128)S(1)}, s32[32,512]{1,0:T(8,128)S(1)}, u32[]{:S(2)}, u32[]{:S(2)}) %collective-permute-start.7) | collective-permute-done | bytes 65568 | tf_op jit(solution)/shard_map/ppermute | solution.py:424
  26.5 3.8 %forward_block.1 = (bf16[1024,2048]{1,0:T(8,128)(2,1)S(1)}, f32[32,128]{1,0:T(8,128)S(1)}) custom-call(s32[1]{0:T(128)} %bitcast.me_ref, s32[64,384]{1,0:T(8,128)S(1)} %get-tuple-element.62.refs_0_, s32[64,384]{1,0:T(8,128)S(1)} %collective-permute-done.6.refs_1_, s32[32,512]{1,0:T(8,128)S(1)} %get-tuple-element.78.refs_2_.refs_0_, ...), custom_call_target="tpu_custom_call" | custom-call | flops 65536 | bytes 65536 | tf_op jit(solution)/shard_map/forward_block/pallas_call | solution.py:471
  31.9 2.3 %forward_sum.1 = (f32[256,128]{1,0:T(8,128)S(1)}, f32[256,128]{1,0:T(8,128)S(1)}, f32[256,128]{1,0:T(8,128)S(1)}, f32[256,128]{1,0:T(8,128)S(1)}, f32[256,128]{1,0:T(8,128)S(1)}) custom-call(s32[1]{0:T(128)} %bitcast.me_ref, f32[32,128]{1,0:T(8,128)S(1)} %get-tuple-element.64.root_ref, bf16[1024,2048]{1,0:T(8,128)(2,1)S(1)} %get-tuple-element.67.block_ref, ...), custom_call_target="tpu_custom_call" | custom-call | flops 1073741824 | bytes 4194304 | tf_op jit(solution)/shard_map/forward_sum/pallas_call | solution.py:489
  34.2 1.6 %collective-permute-start.15 = (f32[256,128]{1,0:T(8,128)S(1)}, f32[256,128]{1,0:T(8,128)S(1)}, u32[]{:S(2)}, u32[]{:S(2)}) collective-permute-start(f32[256,128]{1,0:T(8,128)S(1)} %get-tuple-element.77), channel_id=1, source_target_pairs={{0,18},{1,19},{2,16},{3,17},{4,22},{5,23},{6,20},{7,21},{8,26},{9,... | collective-permute-start | bytes 393224 | tf_op jit(solution)/shard_map/ppermute | solution.py:392
  35.8 1.5 %collective-permute-start.13 = (f32[256,128]{1,0:T(8,128)S(1)}, f32[256,128]{1,0:T(8,128)S(1)}, u32[]{:S(2)}, u32[]{:S(2)}) collective-permute-start(f32[256,128]{1,0:T(8,128)S(1)} %get-tuple-element.75), channel_id=1, source_target_pairs={{0,16},{1,17},{2,18},{3,19},{4,20},{5,21},{6,22},{7,23},{8,24},{9,... | collective-permute-start | bytes 393224 | tf_op jit(solution)/shard_map/ppermute | solution.py:392
  37.8 4.4 %backward_block.1.block_ref = bf16[1024,2048]{1,0:T(8,128)(2,1)S(1)} custom-call(s32[1]{0:T(128)} %bitcast.me_ref, s32[32,512]{1,0:T(8,128)S(1)} %get-tuple-element.78.refs_2_.refs_0_, s32[32,512]{1,0:T(8,128)S(1)} %collective-permute-done.7.refs_3_.refs_1_), custom_call_target="tpu_custom_call" | custom-call | flops 1073741824 | bytes 4194304 | tf_op jit(solution)/shard_map/backward_block/pallas_call | solution.py:502
  42.3 1.6 %collective-permute-done.13.refs_1_ = f32[256,128]{1,0:T(8,128)S(1)} collective-permute-done((f32[256,128]{1,0:T(8,128)S(1)}, f32[256,128]{1,0:T(8,128)S(1)}, u32[]{:S(2)}, u32[]{:S(2)}) %collective-permute-start.13) | collective-permute-done | bytes 131104 | tf_op jit(solution)/shard_map/ppermute | solution.py:392
  43.9 1.7 %middle.1 = (f32[256,256]{1,0:T(8,128)}, f32[256,128]{1,0:T(8,128)S(1)}, f32[64,128]{1,0:T(8,128)S(1)}, f32[64,128]{1,0:T(8,128)S(1)}, f32[64,128]{1,0:T(8,128)S(1)}, /*index=5*/f32[64,128]{1,0:T(8,128)S(1)}) custom-call(s32[1]{0:T(128)} %bitcast.me_ref, f32[256,128]{1,0:T(8,128)S(1)} %get-tuple-element.72.scale_ref, f32[256,128]{1,0:T(8,128)S(1)} %copy-done, ...), custom_call_target="tpu_custom_call" | custom-call | flops 301989888 | bytes 1048576 | tf_op jit(solution)/shard_map/middle/pallas_call | solution.py:516
  46.7 3.2 %collective-permute-start.19 = (f32[256,128]{1,0:T(8,128)S(1)}, f32[256,128]{1,0:T(8,128)S(1)}, u32[]{:S(2)}, u32[]{:S(2)}) collective-permute-start(f32[256,128]{1,0:T(8,128)S(1)} %get-tuple-element.82.refs_0_.sent_ref), channel_id=1, source_target_pairs={{0,8},{1,9},{2,10},{3,11},{4,12},{5,13},{6,14},{7,15},{8,0},{9,1},... | collective-permute-start | bytes 393224 | tf_op jit(solution)/shard_map/ppermute | solution.py:371
  51.9 2.0 %collective-permute-done.22.refs_1_ = f32[64,128]{1,0:T(8,128)S(1)} collective-permute-done((f32[64,128]{1,0:T(8,128)S(1)}, f32[64,128]{1,0:T(8,128)S(1)}, u32[]{:S(2)}, u32[]{:S(2)}) %collective-permute-start.22) | collective-permute-done | bytes 32800 | tf_op jit(solution)/shard_map/ppermute | solution.py:392
  55.3 3.4 %collective-permute-done.24.refs_3_ = f32[64,128]{1,0:T(8,128)S(1)} collective-permute-done((f32[64,128]{1,0:T(8,128)S(1)}, f32[64,128]{1,0:T(8,128)S(1)}, u32[]{:S(2)}, u32[]{:S(2)}) %collective-permute-start.24) | collective-permute-done | bytes 32800 | tf_op jit(solution)/shard_map/ppermute | solution.py:392
  59.4 1.7 %collective-permute-start.27 = (f32[64,128]{1,0:T(8,128)S(1)}, f32[64,128]{1,0:T(8,128)S(1)}, u32[]{:S(2)}, u32[]{:S(2)}) collective-permute-start(f32[64,128]{1,0:T(8,128)S(1)} %add_parts.1.refs_0_), channel_id=1, source_target_pairs={{0,8},{1,9},{2,10},{3,11},{4,12},{5,13},{6,14},{7,15},{8,0},{9,1},... | collective-permute-start | bytes 98312 | tf_op jit(solution)/shard_map/ppermute | solution.py:371
  61.1 2.7 %collective-permute-start.28 = (f32[64,128]{1,0:T(8,128)S(1)}, f32[64,128]{1,0:T(8,128)S(1)}, u32[]{:S(2)}, u32[]{:S(2)}) collective-permute-start(f32[64,128]{1,0:T(8,128)S(1)} %add_parts.1.refs_0_), channel_id=1, source_target_pairs={{0,12},{1,13},{2,14},{3,15},{4,8},{5,9},{6,10},{7,11},{8,4},{9,5},... | collective-permute-start | bytes 98312 | tf_op jit(solution)/shard_map/ppermute | solution.py:371
  63.8 2.1 %backward_sum.1 = (f32[256,128]{1,0:T(8,128)S(1)}, f32[256,128]{1,0:T(8,128)S(1)}, f32[256,128]{1,0:T(8,128)S(1)}, f32[256,128]{1,0:T(8,128)S(1)}) custom-call(s32[1]{0:T(128)} %bitcast.me_ref, bf16[1024,2048]{1,0:T(8,128)(2,1)S(1)} %backward_block.1.block_ref, f32[256,128]{1,0:T(8,128)S(1)} %get-tuple-element.82.refs_0_.sent_ref, ...), custom_call_target="tpu_custom_call" | custom-call | flops 1073741824 | bytes 4194304 | tf_op jit(solution)/shard_map/backward_sum/pallas_call | solution.py:543
  67.9 1.5 %collective-permute-start.31 = (f32[256,128]{1,0:T(8,128)S(1)}, f32[256,128]{1,0:T(8,128)S(1)}, u32[]{:S(2)}, u32[]{:S(2)}) collective-permute-start(f32[256,128]{1,0:T(8,128)S(1)} %get-tuple-element.94), channel_id=1, source_target_pairs={{0,18},{1,19},{2,16},{3,17},{4,22},{5,23},{6,20},{7,21},{8,26},{9,... | collective-permute-start | bytes 393224 | tf_op jit(solution)/shard_map/ppermute | solution.py:392
  72.8 2.0 %collective-permute-done.33.refs_5_ = f32[64,128]{1,0:T(8,128)S(1)} collective-permute-done((f32[64,128]{1,0:T(8,128)S(1)}, f32[64,128]{1,0:T(8,128)S(1)}, u32[]{:S(2)}, u32[]{:S(2)}) %collective-permute-start.33) | collective-permute-done | bytes 32800 | tf_op jit(solution)/shard_map/ppermute | solution.py:392
  76.1 3.4 %collective-permute-done.35.refs_7_ = f32[64,128]{1,0:T(8,128)S(1)} collective-permute-done((f32[64,128]{1,0:T(8,128)S(1)}, f32[64,128]{1,0:T(8,128)S(1)}, u32[]{:S(2)}, u32[]{:S(2)}) %collective-permute-start.35) | collective-permute-done | bytes 32800 | tf_op jit(solution)/shard_map/ppermute | solution.py:392
  (74 shorter events, 19.8 us)
Async XLA Ops:
  0.6 12.5 %collective-permute-start = (f32[256,128]{1,0:T(8,128)}, f32[256,128]{1,0:T(8,128)S(1)}, u32[]{:S(2)}, u32[]{:S(2)}) collective-permute-start(f32[256,128]{1,0:T(8,128)} %features_ref.1), channel_id=1, source_target_pairs={{0,4},{1,5},{2,6},{3,7},{4,0},{5,1},{6,2},{7,3},{8,12},{9,13},{10,... | collective-permute-start | bytes 393224 | tf_op jit(solution)/shard_map/ppermute | solution.py:426
  3.7 9.4 %collective-permute-start.1 = (f32[256,128]{1,0:T(8,128)}, f32[256,128]{1,0:T(8,128)S(1)}, u32[]{:S(2)}, u32[]{:S(2)}) collective-permute-start(f32[256,128]{1,0:T(8,128)} %features_ref.1), channel_id=1, source_target_pairs={{0,8},{1,9},{2,10},{3,11},{4,12},{5,13},{6,14},{7,15},{8,0},{9,1},... | collective-permute-start | bytes 393224 | tf_op jit(solution)/shard_map/ppermute | solution.py:426
  9.2 5.1 %collective-permute-start.3 = (s32[8,896]{1,0:T(8,128)}, s32[8,896]{1,0:T(8,128)S(1)}, u32[]{:S(2)}, u32[]{:S(2)}) collective-permute-start(s32[8,896]{1,0:T(8,128)} %get-tuple-element.56), channel_id=1, source_target_pairs={{0,8},{1,9},{2,10},{3,11},{4,12},{5,13},{6,14},{7,15},{8,0},{9,1},... | collective-permute-start | bytes 86024 | tf_op jit(solution)/shard_map/ppermute | solution.py:371
  9.2 6.3 %collective-permute-start.4 = (s32[8,896]{1,0:T(8,128)}, s32[8,896]{1,0:T(8,128)S(1)}, u32[]{:S(2)}, u32[]{:S(2)}) collective-permute-start(s32[8,896]{1,0:T(8,128)} %get-tuple-element.57), channel_id=1, source_target_pairs={{0,12},{1,13},{2,14},{3,15},{4,8},{5,9},{6,10},{7,11},{8,4},{9,5},... | collective-permute-start | bytes 86024 | tf_op jit(solution)/shard_map/ppermute | solution.py:371
  16.3 14.0 %collective-permute-start.8 = (f32[256,128]{1,0:T(8,128)S(1)}, f32[256,128]{1,0:T(8,128)S(1)}, u32[]{:S(2)}, u32[]{:S(2)}) collective-permute-start(f32[256,128]{1,0:T(8,128)S(1)} %copy-done), channel_id=1, source_target_pairs={{0,12},{1,13},{2,14},{3,15},{4,8},{5,9},{6,10},{7,11},{8,4},{9,5},... | collective-permute-start | bytes 393224 | tf_op jit(solution)/shard_map/ppermute | solution.py:430
  20.7 5.8 %collective-permute-start.6 = (s32[64,384]{1,0:T(8,128)S(1)}, s32[64,384]{1,0:T(8,128)S(1)}, u32[]{:S(2)}, u32[]{:S(2)}) collective-permute-start(s32[64,384]{1,0:T(8,128)S(1)} %get-tuple-element.62.refs_0_), channel_id=1, source_target_pairs={{16,0},{17,1},{18,2},{19,3},{20,4},{21,5},{22,6},{23,7},{24,8},{25... | collective-permute-start | bytes 294920 | tf_op jit(solution)/shard_map/ppermute | solution.py:424
  23.8 7.1 %collective-permute-start.9 = (f32[256,128]{1,0:T(8,128)S(1)}, f32[256,128]{1,0:T(8,128)S(1)}, u32[]{:S(2)}, u32[]{:S(2)}) collective-permute-start(f32[256,128]{1,0:T(8,128)S(1)} %copy-done), channel_id=1, source_target_pairs={{0,1},{1,0},{2,3},{3,2},{4,5},{5,4},{6,7},{7,6},{8,9},{9,8},{10,11... | collective-permute-start | bytes 393224 | tf_op jit(solution)/shard_map/ppermute | solution.py:376
  23.8 7.1 %collective-permute-start.10 = (f32[256,128]{1,0:T(8,128)S(1)}, f32[256,128]{1,0:T(8,128)S(1)}, u32[]{:S(2)}, u32[]{:S(2)}) collective-permute-start(f32[256,128]{1,0:T(8,128)S(1)} %collective-permute-done.refs_2_), channel_id=1, source_target_pairs={{0,1},{1,0},{2,3},{3,2},{4,5},{5,4},{6,7},{7,6},{8,9},{9,8},{10,11... | collective-permute-start | bytes 393224 | tf_op jit(solution)/shard_map/ppermute | solution.py:376
  34.2 8.0 %collective-permute-start.15 = (f32[256,128]{1,0:T(8,128)S(1)}, f32[256,128]{1,0:T(8,128)S(1)}, u32[]{:S(2)}, u32[]{:S(2)}) collective-permute-start(f32[256,128]{1,0:T(8,128)S(1)} %get-tuple-element.77), channel_id=1, source_target_pairs={{0,18},{1,19},{2,16},{3,17},{4,22},{5,23},{6,20},{7,21},{8,26},{9,... | collective-permute-start | bytes 393224 | tf_op jit(solution)/shard_map/ppermute | solution.py:392
  35.8 8.1 %collective-permute-start.13 = (f32[256,128]{1,0:T(8,128)S(1)}, f32[256,128]{1,0:T(8,128)S(1)}, u32[]{:S(2)}, u32[]{:S(2)}) collective-permute-start(f32[256,128]{1,0:T(8,128)S(1)} %get-tuple-element.75), channel_id=1, source_target_pairs={{0,16},{1,17},{2,18},{3,19},{4,20},{5,21},{6,22},{7,23},{8,24},{9,... | collective-permute-start | bytes 393224 | tf_op jit(solution)/shard_map/ppermute | solution.py:392
  37.3 6.6 %collective-permute-start.14 = (f32[256,128]{1,0:T(8,128)S(1)}, f32[256,128]{1,0:T(8,128)S(1)}, u32[]{:S(2)}, u32[]{:S(2)}) collective-permute-start(f32[256,128]{1,0:T(8,128)S(1)} %get-tuple-element.76), channel_id=1, source_target_pairs={{0,2},{1,3},{2,0},{3,1},{4,6},{5,7},{6,4},{7,5},{8,10},{9,11},{10,... | collective-permute-start | bytes 393224 | tf_op jit(solution)/shard_map/ppermute | solution.py:392
  45.6 13.1 %collective-permute-start.21 = (f32[256,128]{1,0:T(8,128)S(1)}, f32[256,128]{1,0:T(8,128)S(1)}, u32[]{:S(2)}, u32[]{:S(2)}) collective-permute-start(f32[256,128]{1,0:T(8,128)S(1)} %get-tuple-element.82.refs_0_.sent_ref), channel_id=1, source_target_pairs={{0,12},{1,13},{2,14},{3,15},{4,8},{5,9},{6,10},{7,11},{8,4},{9,5},... | collective-permute-start | bytes 393224 | tf_op jit(solution)/shard_map/ppermute | solution.py:371
  46.7 12.0 %collective-permute-start.17 = (f32[256,128]{1,0:T(8,128)S(1)}, f32[256,128]{1,0:T(8,128)S(1)}, u32[]{:S(2)}, u32[]{:S(2)}) collective-permute-start(f32[256,128]{1,0:T(8,128)S(1)} %get-tuple-element.82.refs_0_.sent_ref), channel_id=1, source_target_pairs={{0,4},{1,5},{2,6},{3,7},{4,0},{5,1},{6,2},{7,3},{8,12},{9,13},{10,... | collective-permute-start | bytes 393224 | tf_op jit(solution)/shard_map/ppermute | solution.py:371
  46.7 12.1 %collective-permute-start.19 = (f32[256,128]{1,0:T(8,128)S(1)}, f32[256,128]{1,0:T(8,128)S(1)}, u32[]{:S(2)}, u32[]{:S(2)}) collective-permute-start(f32[256,128]{1,0:T(8,128)S(1)} %get-tuple-element.82.refs_0_.sent_ref), channel_id=1, source_target_pairs={{0,8},{1,9},{2,10},{3,11},{4,12},{5,13},{6,14},{7,15},{8,0},{9,1},... | collective-permute-start | bytes 393224 | tf_op jit(solution)/shard_map/ppermute | solution.py:371
  50.5 4.8 %collective-permute-start.23 = (f32[64,128]{1,0:T(8,128)S(1)}, f32[64,128]{1,0:T(8,128)S(1)}, u32[]{:S(2)}, u32[]{:S(2)}) collective-permute-start(f32[64,128]{1,0:T(8,128)S(1)} %get-tuple-element.86), channel_id=1, source_target_pairs={{0,2},{1,3},{2,0},{3,1},{4,6},{5,7},{6,4},{7,5},{8,10},{9,11},{10,... | collective-permute-start | bytes 98312 | tf_op jit(solution)/shard_map/ppermute | solution.py:392
  53.9 4.8 %collective-permute-start.24 = (f32[64,128]{1,0:T(8,128)S(1)}, f32[64,128]{1,0:T(8,128)S(1)}, u32[]{:S(2)}, u32[]{:S(2)}) collective-permute-start(f32[64,128]{1,0:T(8,128)S(1)} %get-tuple-element.87), channel_id=1, source_target_pairs={{0,18},{1,19},{2,16},{3,17},{4,22},{5,23},{6,20},{7,21},{8,26},{9,... | collective-permute-start | bytes 98312 | tf_op jit(solution)/shard_map/ppermute | solution.py:392
  58.8 5.0 %collective-permute-start.20 = (f32[256,128]{1,0:T(8,128)S(1)}, f32[256,128]{1,0:T(8,128)S(1)}, u32[]{:S(2)}, u32[]{:S(2)}) collective-permute-start(f32[256,128]{1,0:T(8,128)S(1)} %collective-permute-done.19.refs_4_), channel_id=1, source_target_pairs={{0,1},{1,0},{2,3},{3,2},{4,5},{5,4},{6,7},{7,6},{8,9},{9,8},{10,11... | collective-permute-start | bytes 393224 | tf_op jit(solution)/shard_map/ppermute | solution.py:376
  59.4 8.6 %collective-permute-start.26 = (f32[64,128]{1,0:T(8,128)S(1)}, f32[64,128]{1,0:T(8,128)S(1)}, u32[]{:S(2)}, u32[]{:S(2)}) collective-permute-start(f32[64,128]{1,0:T(8,128)S(1)} %add_parts.1.refs_0_), channel_id=1, source_target_pairs={{0,4},{1,5},{2,6},{3,7},{4,0},{5,1},{6,2},{7,3},{8,12},{9,13},{10,... | collective-permute-start | bytes 98312 | tf_op jit(solution)/shard_map/ppermute | solution.py:371
  59.4 10.1 %collective-permute-start.27 = (f32[64,128]{1,0:T(8,128)S(1)}, f32[64,128]{1,0:T(8,128)S(1)}, u32[]{:S(2)}, u32[]{:S(2)}) collective-permute-start(f32[64,128]{1,0:T(8,128)S(1)} %add_parts.1.refs_0_), channel_id=1, source_target_pairs={{0,8},{1,9},{2,10},{3,11},{4,12},{5,13},{6,14},{7,15},{8,0},{9,1},... | collective-permute-start | bytes 98312 | tf_op jit(solution)/shard_map/ppermute | solution.py:371
  61.1 8.4 %collective-permute-start.28 = (f32[64,128]{1,0:T(8,128)S(1)}, f32[64,128]{1,0:T(8,128)S(1)}, u32[]{:S(2)}, u32[]{:S(2)}) collective-permute-start(f32[64,128]{1,0:T(8,128)S(1)} %add_parts.1.refs_0_), channel_id=1, source_target_pairs={{0,12},{1,13},{2,14},{3,15},{4,8},{5,9},{6,10},{7,11},{8,4},{9,5},... | collective-permute-start | bytes 98312 | tf_op jit(solution)/shard_map/ppermute | solution.py:371
  65.9 13.6 %collective-permute-start.29 = (f32[256,128]{1,0:T(8,128)S(1)}, f32[256,128]{1,0:T(8,128)S(1)}, u32[]{:S(2)}, u32[]{:S(2)}) collective-permute-start(f32[256,128]{1,0:T(8,128)S(1)} %get-tuple-element.92), channel_id=1, source_target_pairs={{0,16},{1,17},{2,18},{3,19},{4,20},{5,21},{6,22},{7,23},{8,24},{9,... | collective-permute-start | bytes 393224 | tf_op jit(solution)/shard_map/ppermute | solution.py:392
  66.5 13.0 %collective-permute-start.30 = (f32[256,128]{1,0:T(8,128)S(1)}, f32[256,128]{1,0:T(8,128)S(1)}, u32[]{:S(2)}, u32[]{:S(2)}) collective-permute-start(f32[256,128]{1,0:T(8,128)S(1)} %get-tuple-element.93), channel_id=1, source_target_pairs={{0,2},{1,3},{2,0},{3,1},{4,6},{5,7},{6,4},{7,5},{8,10},{9,11},{10,... | collective-permute-start | bytes 393224 | tf_op jit(solution)/shard_map/ppermute | solution.py:392
  67.9 11.6 %collective-permute-start.31 = (f32[256,128]{1,0:T(8,128)S(1)}, f32[256,128]{1,0:T(8,128)S(1)}, u32[]{:S(2)}, u32[]{:S(2)}) collective-permute-start(f32[256,128]{1,0:T(8,128)S(1)} %get-tuple-element.94), channel_id=1, source_target_pairs={{0,18},{1,19},{2,16},{3,17},{4,22},{5,23},{6,20},{7,21},{8,26},{9,... | collective-permute-start | bytes 393224 | tf_op jit(solution)/shard_map/ppermute | solution.py:392
  74.7 4.8 %collective-permute-start.35 = (f32[64,128]{1,0:T(8,128)S(1)}, f32[64,128]{1,0:T(8,128)S(1)}, u32[]{:S(2)}, u32[]{:S(2)}) collective-permute-start(f32[64,128]{1,0:T(8,128)S(1)} %add_cores.1.refs_4_), channel_id=1, source_target_pairs={{0,18},{1,19},{2,16},{3,17},{4,22},{5,23},{6,20},{7,21},{8,26},{9,... | collective-permute-start | bytes 98312 | tf_op jit(solution)/shard_map/ppermute | solution.py:392
  (19 other events, 108.4 us)

commit v9 on v8

--- a/solution.py
+++ b/solution.py
@@ -371,12 +371,11 @@
             lax.ppermute(blocks[dz], both_axes, toward(dz)) for dz in range(1, DEPTH)
         ]
 
+    def to_core(block):
+        return lax.ppermute(block, both_axes, grid.pairs(lambda x, y, z, c: (x, y, z, c ^ 1)))
+
     def to_cores(blocks):
-        others = [
-            lax.ppermute(block, both_axes, grid.pairs(lambda x, y, z, c: (x, y, z, c ^ 1)))
-            for block in blocks
-        ]
-        return [block for pair in zip(blocks, others) for block in pair]
+        return [block for own in blocks for block in (own, to_core(own))]
 
     def backward_row(k, me_ref):
         x, _, _, _ = grid.place(me_ref[0])
@@ -424,10 +423,11 @@
         return lax.ppermute(value, both_axes, [(b, a) for a, b in grid.pairs(move)])
 
     along = [features] + [lax.ppermute(features, both_axes, toward(dz)) for dz in (1, 2)]
+    across = [to_core(features)]
+    *planes, across[0] = lax.optimization_barrier((*planes, across[0]))
     got_planes = along_z(planes)
-    *along, got_planes[0] = lax.optimization_barrier((*along, got_planes[0]))
-    *got_planes, later = lax.optimization_barrier((*got_planes, features))
-    along += [lax.ppermute(later, both_axes, toward(dz)) for dz in range(3, DEPTH)]
+    merged = lax.optimization_barrier((*along, *got_planes))
+    along, got_planes = list(merged[: len(along)]), merged[len(along) :]
     small = pl.CostEstimate(flops=2**14, bytes_accessed=2**18, transcendentals=0)
     both = pl.pallas_call(
         functools.partial(plane_kernel, wide),
@@ -446,6 +446,9 @@
         cost_estimate=small,
         name="chip",
     )(lists, both, from_peer(both, lambda x, y, z, c: (x, y, z, c ^ 1)))
+    across.append(to_core(along[1]))
+    chip, later, across[1] = lax.optimization_barrier((chip, features, across[1]))
+    along += [lax.ppermute(later, both_axes, toward(dz)) for dz in range(3, DEPTH)]
     chips = [chip] + [
         from_peer(chip, lambda x, y, z, c, dx=dx: ((x + dx) % grid.rows, y, z, c))
         for dx in range(1, grid.rows)
@@ -485,7 +488,8 @@
         name="forward_block",
     )(me, *chips, *peer_lists)
     along[-1], forward_block = lax.optimization_barrier((along[-1], forward_block))
-    gathered = to_cores(along)
+    across += [to_core(block) for block in along[2:]]
+    gathered = [block for pair in zip(along, across) for block in pair]
     scale, *sums = pl.pallas_call(
         functools.partial(forward_sum_kernel, grid),
         grid=(grid.summed,),

time: 80.6 us -> 81.6 us (1.012)
  waiting for transfers between devices: 19.1 us -> 20.6 us
    ppermute x4, waiting for transfers between devices: 3.43 us -> 4.84 us  [from_peer(): return lax.ppermute(value, both_axes, [(b, a) for a, b in grid.pairs(move)])]
    ppermute x8, starting transfers between devices: 1.73 us -> 0.73 us  [to_core(): lax.ppermute(block, both_axes, grid.pairs(lambda x, y, z, c: (x, y, z, c...]
  transfers between devices with their start and end apart: 36 -> 36, of which waited for: 10 -> 11; matrix products, arithmetic and copies ran while one was open for 0% -> 0% of each run, Pallas kernels for 16% -> 16%
where the time goes in v9:
time: 81.6 us; the launch traced here: 81.2 us
  starting transfers between devices  40.8 us (50%)
  waiting for transfers between devices  20.6 us (25%)
  Pallas kernels  17.5 us (21%)
  local copies, waits for them, and re-layouts  1.57 us (2%)
  between operations  0.85 us (1%)
    ppermute x12, starting transfers between devices, to_owners(): lax.ppermute(part, both_axes, grid.pairs(lambda x, y, z, c, dx=dx, dy=dy:...  13.9 us
    ppermute x9, starting transfers between devices, along_z(): lax.ppermute(blocks[dz], both_axes, toward(dz))  13.2 us
    ppermute x12, waiting for transfers between devices, to_owners(): lax.ppermute(part, both_axes, grid.pairs(lambda x, y, z, c, dx=dx, dy=dy:...  12 us
    ppermute x2, starting transfers between devices, shards(): lax.ppermute(features, both_axes, toward(dz))  5.68 us
    ppermute x4, waiting for transfers between devices, from_peer(): return lax.ppermute(value, both_axes, [(b, a) for a, b in grid.pairs(move)])  4.84 us
    pallas_call x1, Pallas kernels, shards(): pl.pallas_call(functools.partial(backward_block_kernel, grid, slots), gri...  4.44 us
    pallas_call x1, Pallas kernels, shards(): pl.pallas_call(functools.partial(forward_block_kernel, grid, slots), grid...  3.77 us
    ppermute x4, starting transfers between devices, from_peer(): return lax.ppermute(value, both_axes, [(b, a) for a, b in grid.pairs(move)])  3.65 us
  transfers between devices with their start and end apart: 36, of which 11 were waited for; matrix products, arithmetic and copies ran while one was open for 0% of the time, Pallas kernels for 16%

profile of v9, /device:TPU:0, one launch (start us, length us, event | category | flops | bytes accessed | tf_op | source)
XLA Modules:
  0.0 81.2 jit_solution(15846343425479657237)
XLA Ops:
  0.6 3.1 %collective-permute-start = (f32[256,128]{1,0:T(8,128)}, f32[256,128]{1,0:T(8,128)S(1)}, u32[]{:S(2)}, u32[]{:S(2)}) collective-permute-start(f32[256,128]{1,0:T(8,128)} %features_ref.1), channel_id=1, source_target_pairs={{0,4},{1,5},{2,6},{3,7},{4,0},{5,1},{6,2},{7,3},{8,12},{9,13},{10,... | collective-permute-start | bytes 393224 | tf_op jit(solution)/shard_map/ppermute | solution.py:425
  3.7 2.6 %collective-permute-start.1 = (f32[256,128]{1,0:T(8,128)}, f32[256,128]{1,0:T(8,128)S(1)}, u32[]{:S(2)}, u32[]{:S(2)}) collective-permute-start(f32[256,128]{1,0:T(8,128)} %features_ref.1), channel_id=1, source_target_pairs={{0,8},{1,9},{2,10},{3,11},{4,12},{5,13},{6,14},{7,15},{8,0},{9,1},... | collective-permute-start | bytes 393224 | tf_op jit(solution)/shard_map/ppermute | solution.py:425
  6.3 2.3 %pack.1 = (s32[32,384]{1,0:T(8,128)}, s32[8,896]{1,0:T(8,128)}, s32[8,896]{1,0:T(8,128)}, s32[8,896]{1,0:T(8,128)}, s32[8,896]{1,0:T(8,128)}) custom-call(s32[1]{0:T(128)} %bitcast.me_ref, s32[4,32]{1,0:T(4,128)} %bitcast.13, s32[4,32]{1,0:T(4,128)} %bitcast.14, s32[32,256]{1,0:T(8,128)} %bitcast.11, s32[32,256]{1,0:T(8,128)} %bitcast.12), custom_call_target="tpu_custom_call" | custom-call | flops 2147483648 | bytes 8388608 | tf_op jit(solution)/shard_map/pack/pallas_call | solution.py:409
  9.2 3.9 %collective-permute-start.5 = (s32[8,896]{1,0:T(8,128)}, s32[8,896]{1,0:T(8,128)S(1)}, u32[]{:S(2)}, u32[]{:S(2)}) collective-permute-start(s32[8,896]{1,0:T(8,128)} %get-tuple-element.66), channel_id=1, source_target_pairs={{0,12},{1,13},{2,14},{3,15},{4,8},{5,9},{6,10},{7,11},{8,4},{9,5},... | collective-permute-start | bytes 86024 | tf_op jit(solution)/shard_map/ppermute | solution.py:371
  18.6 3.5 %collective-permute-start.10 = (f32[256,128]{1,0:T(8,128)S(1)}, f32[256,128]{1,0:T(8,128)S(1)}, u32[]{:S(2)}, u32[]{:S(2)}) collective-permute-start(f32[256,128]{1,0:T(8,128)S(1)} %copy-done), channel_id=1, source_target_pairs={{0,12},{1,13},{2,14},{3,15},{4,8},{5,9},{6,10},{7,11},{8,4},{9,5},... | collective-permute-start | bytes 393224 | tf_op jit(solution)/shard_map/ppermute | solution.py:451
  22.1 1.5 %collective-permute-start.8 = (s32[64,384]{1,0:T(8,128)S(1)}, s32[64,384]{1,0:T(8,128)S(1)}, u32[]{:S(2)}, u32[]{:S(2)}) collective-permute-start(s32[64,384]{1,0:T(8,128)S(1)} %get-tuple-element.73.refs_0_), channel_id=1, source_target_pairs={{16,0},{17,1},{18,2},{19,3},{20,4},{21,5},{22,6},{23,7},{24,8},{25... | collective-permute-start | bytes 294920 | tf_op jit(solution)/shard_map/ppermute | solution.py:423
  23.6 1.5 %collective-permute-start.9 = (s32[32,512]{1,0:T(8,128)S(1)}, s32[32,512]{1,0:T(8,128)S(1)}, u32[]{:S(2)}, u32[]{:S(2)}) collective-permute-start(s32[32,512]{1,0:T(8,128)S(1)} %get-tuple-element.90.refs_2_.refs_0_), channel_id=1, source_target_pairs={{2,0},{3,1},{0,2},{1,3},{6,4},{7,5},{4,6},{5,7},{10,8},{11,9},{8,1... | collective-permute-start | bytes 196616 | tf_op jit(solution)/shard_map/ppermute | solution.py:423
  25.1 2.7 %collective-permute-done.9.refs_3_.refs_1_ = s32[32,512]{1,0:T(8,128)S(1)} collective-permute-done((s32[32,512]{1,0:T(8,128)S(1)}, s32[32,512]{1,0:T(8,128)S(1)}, u32[]{:S(2)}, u32[]{:S(2)}) %collective-permute-start.9) | collective-permute-done | bytes 65568 | tf_op jit(solution)/shard_map/ppermute | solution.py:423
  27.9 3.8 %forward_block.1 = (bf16[1024,2048]{1,0:T(8,128)(2,1)S(1)}, f32[32,128]{1,0:T(8,128)S(1)}) custom-call(s32[1]{0:T(128)} %bitcast.me_ref, s32[64,384]{1,0:T(8,128)S(1)} %get-tuple-element.73.refs_0_, s32[64,384]{1,0:T(8,128)S(1)} %collective-permute-done.8.refs_1_, s32[32,512]{1,0:T(8,128)S(1)} %get-tuple-element.90.refs_2_.refs_0_, ...), custom_call_target="tpu_custom_call" | custom-call | flops 65536 | bytes 65536 | tf_op jit(solution)/shard_map/forward_block/pallas_call | solution.py:474
  33.1 2.3 %forward_sum.1 = (f32[256,128]{1,0:T(8,128)S(1)}, f32[256,128]{1,0:T(8,128)S(1)}, f32[256,128]{1,0:T(8,128)S(1)}, f32[256,128]{1,0:T(8,128)S(1)}, f32[256,128]{1,0:T(8,128)S(1)}) custom-call(s32[1]{0:T(128)} %bitcast.me_ref, f32[32,128]{1,0:T(8,128)S(1)} %get-tuple-element.75.root_ref, bf16[1024,2048]{1,0:T(8,128)(2,1)S(1)} %get-tuple-element.78.block_ref, ...), custom_call_target="tpu_custom_call" | custom-call | flops 1073741824 | bytes 4194304 | tf_op jit(solution)/shard_map/forward_sum/pallas_call | solution.py:493
  35.5 1.6 %collective-permute-start.15 = (f32[256,128]{1,0:T(8,128)S(1)}, f32[256,128]{1,0:T(8,128)S(1)}, u32[]{:S(2)}, u32[]{:S(2)}) collective-permute-start(f32[256,128]{1,0:T(8,128)S(1)} %get-tuple-element.89), channel_id=1, source_target_pairs={{0,18},{1,19},{2,16},{3,17},{4,22},{5,23},{6,20},{7,21},{8,26},{9,... | collective-permute-start | bytes 393224 | tf_op jit(solution)/shard_map/ppermute | solution.py:391
  37.0 1.5 %collective-permute-start.13 = (f32[256,128]{1,0:T(8,128)S(1)}, f32[256,128]{1,0:T(8,128)S(1)}, u32[]{:S(2)}, u32[]{:S(2)}) collective-permute-start(f32[256,128]{1,0:T(8,128)S(1)} %get-tuple-element.87), channel_id=1, source_target_pairs={{0,16},{1,17},{2,18},{3,19},{4,20},{5,21},{6,22},{7,23},{8,24},{9,... | collective-permute-start | bytes 393224 | tf_op jit(solution)/shard_map/ppermute | solution.py:391
  39.0 4.4 %backward_block.1.block_ref = bf16[1024,2048]{1,0:T(8,128)(2,1)S(1)} custom-call(s32[1]{0:T(128)} %bitcast.me_ref, s32[32,512]{1,0:T(8,128)S(1)} %get-tuple-element.90.refs_2_.refs_0_, s32[32,512]{1,0:T(8,128)S(1)} %collective-permute-done.9.refs_3_.refs_1_), custom_call_target="tpu_custom_call" | custom-call | flops 1073741824 | bytes 4194304 | tf_op jit(solution)/shard_map/backward_block/pallas_call | solution.py:506
  44.9 1.7 %middle.1 = (f32[256,256]{1,0:T(8,128)}, f32[256,128]{1,0:T(8,128)S(1)}, f32[64,128]{1,0:T(8,128)S(1)}, f32[64,128]{1,0:T(8,128)S(1)}, f32[64,128]{1,0:T(8,128)S(1)}, /*index=5*/f32[64,128]{1,0:T(8,128)S(1)}) custom-call(s32[1]{0:T(128)} %bitcast.me_ref, f32[256,128]{1,0:T(8,128)S(1)} %get-tuple-element.84.scale_ref, f32[256,128]{1,0:T(8,128)S(1)} %copy-done, ...), custom_call_target="tpu_custom_call" | custom-call | flops 301989888 | bytes 1048576 | tf_op jit(solution)/shard_map/middle/pallas_call | solution.py:520
  46.9 4.0 %collective-permute-start.19 = (f32[256,128]{1,0:T(8,128)S(1)}, f32[256,128]{1,0:T(8,128)S(1)}, u32[]{:S(2)}, u32[]{:S(2)}) collective-permute-start(f32[256,128]{1,0:T(8,128)S(1)} %get-tuple-element.94.refs_0_.sent_ref), channel_id=1, source_target_pairs={{0,8},{1,9},{2,10},{3,11},{4,12},{5,13},{6,14},{7,15},{8,0},{9,1},... | collective-permute-start | bytes 393224 | tf_op jit(solution)/shard_map/ppermute | solution.py:371
  51.5 1.5 %collective-permute-start.23 = (f32[64,128]{1,0:T(8,128)S(1)}, f32[64,128]{1,0:T(8,128)S(1)}, u32[]{:S(2)}, u32[]{:S(2)}) collective-permute-start(f32[64,128]{1,0:T(8,128)S(1)} %get-tuple-element.98), channel_id=1, source_target_pairs={{0,2},{1,3},{2,0},{3,1},{4,6},{5,7},{6,4},{7,5},{8,10},{9,11},{10,... | collective-permute-start | bytes 98312 | tf_op jit(solution)/shard_map/ppermute | solution.py:391
  52.9 1.9 %collective-permute-done.22.refs_1_ = f32[64,128]{1,0:T(8,128)S(1)} collective-permute-done((f32[64,128]{1,0:T(8,128)S(1)}, f32[64,128]{1,0:T(8,128)S(1)}, u32[]{:S(2)}, u32[]{:S(2)}) %collective-permute-start.22) | collective-permute-done | bytes 32800 | tf_op jit(solution)/shard_map/ppermute | solution.py:391
  56.3 3.4 %collective-permute-done.24.refs_3_ = f32[64,128]{1,0:T(8,128)S(1)} collective-permute-done((f32[64,128]{1,0:T(8,128)S(1)}, f32[64,128]{1,0:T(8,128)S(1)}, u32[]{:S(2)}, u32[]{:S(2)}) %collective-permute-start.24) | collective-permute-done | bytes 32800 | tf_op jit(solution)/shard_map/ppermute | solution.py:391
  61.3 3.5 %collective-permute-start.28 = (f32[64,128]{1,0:T(8,128)S(1)}, f32[64,128]{1,0:T(8,128)S(1)}, u32[]{:S(2)}, u32[]{:S(2)}) collective-permute-start(f32[64,128]{1,0:T(8,128)S(1)} %add_parts.1.refs_0_), channel_id=1, source_target_pairs={{0,12},{1,13},{2,14},{3,15},{4,8},{5,9},{6,10},{7,11},{8,4},{9,5},... | collective-permute-start | bytes 98312 | tf_op jit(solution)/shard_map/ppermute | solution.py:371
  64.7 2.1 %backward_sum.1 = (f32[256,128]{1,0:T(8,128)S(1)}, f32[256,128]{1,0:T(8,128)S(1)}, f32[256,128]{1,0:T(8,128)S(1)}, f32[256,128]{1,0:T(8,128)S(1)}) custom-call(s32[1]{0:T(128)} %bitcast.me_ref, bf16[1024,2048]{1,0:T(8,128)(2,1)S(1)} %backward_block.1.block_ref, f32[256,128]{1,0:T(8,128)S(1)} %get-tuple-element.94.refs_0_.sent_ref, ...), custom_call_target="tpu_custom_call" | custom-call | flops 1073741824 | bytes 4194304 | tf_op jit(solution)/shard_map/backward_sum/pallas_call | solution.py:547
  67.5 1.5 %collective-permute-start.30 = (f32[256,128]{1,0:T(8,128)S(1)}, f32[256,128]{1,0:T(8,128)S(1)}, u32[]{:S(2)}, u32[]{:S(2)}) collective-permute-start(f32[256,128]{1,0:T(8,128)S(1)} %get-tuple-element.105), channel_id=1, source_target_pairs={{0,2},{1,3},{2,0},{3,1},{4,6},{5,7},{6,4},{7,5},{8,10},{9,11},{10,... | collective-permute-start | bytes 393224 | tf_op jit(solution)/shard_map/ppermute | solution.py:391
  68.9 1.5 %collective-permute-start.31 = (f32[256,128]{1,0:T(8,128)S(1)}, f32[256,128]{1,0:T(8,128)S(1)}, u32[]{:S(2)}, u32[]{:S(2)}) collective-permute-start(f32[256,128]{1,0:T(8,128)S(1)} %get-tuple-element.106), channel_id=1, source_target_pairs={{0,18},{1,19},{2,16},{3,17},{4,22},{5,23},{6,20},{7,21},{8,26},{9,... | collective-permute-start | bytes 393224 | tf_op jit(solution)/shard_map/ppermute | solution.py:391
  73.7 1.9 %collective-permute-done.33.refs_5_ = f32[64,128]{1,0:T(8,128)S(1)} collective-permute-done((f32[64,128]{1,0:T(8,128)S(1)}, f32[64,128]{1,0:T(8,128)S(1)}, u32[]{:S(2)}, u32[]{:S(2)}) %collective-permute-start.33) | collective-permute-done | bytes 32800 | tf_op jit(solution)/shard_map/ppermute | solution.py:391
  77.1 3.4 %collective-permute-done.35.refs_7_ = f32[64,128]{1,0:T(8,128)S(1)} collective-permute-done((f32[64,128]{1,0:T(8,128)S(1)}, f32[64,128]{1,0:T(8,128)S(1)}, u32[]{:S(2)}, u32[]{:S(2)}) %collective-permute-start.35) | collective-permute-done | bytes 32800 | tf_op jit(solution)/shard_map/ppermute | solution.py:391
  (74 shorter events, 19.3 us)
Async XLA Ops:
  0.6 12.5 %collective-permute-start = (f32[256,128]{1,0:T(8,128)}, f32[256,128]{1,0:T(8,128)S(1)}, u32[]{:S(2)}, u32[]{:S(2)}) collective-permute-start(f32[256,128]{1,0:T(8,128)} %features_ref.1), channel_id=1, source_target_pairs={{0,4},{1,5},{2,6},{3,7},{4,0},{5,1},{6,2},{7,3},{8,12},{9,13},{10,... | collective-permute-start | bytes 393224 | tf_op jit(solution)/shard_map/ppermute | solution.py:425
  3.7 9.4 %collective-permute-start.1 = (f32[256,128]{1,0:T(8,128)}, f32[256,128]{1,0:T(8,128)S(1)}, u32[]{:S(2)}, u32[]{:S(2)}) collective-permute-start(f32[256,128]{1,0:T(8,128)} %features_ref.1), channel_id=1, source_target_pairs={{0,8},{1,9},{2,10},{3,11},{4,12},{5,13},{6,14},{7,15},{8,0},{9,1},... | collective-permute-start | bytes 393224 | tf_op jit(solution)/shard_map/ppermute | solution.py:425
  9.2 5.0 %collective-permute-start.4 = (s32[8,896]{1,0:T(8,128)}, s32[8,896]{1,0:T(8,128)S(1)}, u32[]{:S(2)}, u32[]{:S(2)}) collective-permute-start(s32[8,896]{1,0:T(8,128)} %get-tuple-element.65), channel_id=1, source_target_pairs={{0,8},{1,9},{2,10},{3,11},{4,12},{5,13},{6,14},{7,15},{8,0},{9,1},... | collective-permute-start | bytes 86024 | tf_op jit(solution)/shard_map/ppermute | solution.py:371
  9.2 6.4 %collective-permute-start.5 = (s32[8,896]{1,0:T(8,128)}, s32[8,896]{1,0:T(8,128)S(1)}, u32[]{:S(2)}, u32[]{:S(2)}) collective-permute-start(s32[8,896]{1,0:T(8,128)} %get-tuple-element.66), channel_id=1, source_target_pairs={{0,12},{1,13},{2,14},{3,15},{4,8},{5,9},{6,10},{7,11},{8,4},{9,5},... | collective-permute-start | bytes 86024 | tf_op jit(solution)/shard_map/ppermute | solution.py:371
  18.6 13.1 %collective-permute-start.10 = (f32[256,128]{1,0:T(8,128)S(1)}, f32[256,128]{1,0:T(8,128)S(1)}, u32[]{:S(2)}, u32[]{:S(2)}) collective-permute-start(f32[256,128]{1,0:T(8,128)S(1)} %copy-done), channel_id=1, source_target_pairs={{0,12},{1,13},{2,14},{3,15},{4,8},{5,9},{6,10},{7,11},{8,4},{9,5},... | collective-permute-start | bytes 393224 | tf_op jit(solution)/shard_map/ppermute | solution.py:451
  22.1 5.8 %collective-permute-start.8 = (s32[64,384]{1,0:T(8,128)S(1)}, s32[64,384]{1,0:T(8,128)S(1)}, u32[]{:S(2)}, u32[]{:S(2)}) collective-permute-start(s32[64,384]{1,0:T(8,128)S(1)} %get-tuple-element.73.refs_0_), channel_id=1, source_target_pairs={{16,0},{17,1},{18,2},{19,3},{20,4},{21,5},{22,6},{23,7},{24,8},{25... | collective-permute-start | bytes 294920 | tf_op jit(solution)/shard_map/ppermute | solution.py:423
  25.1 6.6 %collective-permute-start.11 = (f32[256,128]{1,0:T(8,128)S(1)}, f32[256,128]{1,0:T(8,128)S(1)}, u32[]{:S(2)}, u32[]{:S(2)}) collective-permute-start(f32[256,128]{1,0:T(8,128)S(1)} %collective-permute-done.1.refs_4_), channel_id=1, source_target_pairs={{0,1},{1,0},{2,3},{3,2},{4,5},{5,4},{6,7},{7,6},{8,9},{9,8},{10,11... | collective-permute-start | bytes 393224 | tf_op jit(solution)/shard_map/ppermute | solution.py:375
  35.5 8.0 %collective-permute-start.15 = (f32[256,128]{1,0:T(8,128)S(1)}, f32[256,128]{1,0:T(8,128)S(1)}, u32[]{:S(2)}, u32[]{:S(2)}) collective-permute-start(f32[256,128]{1,0:T(8,128)S(1)} %get-tuple-element.89), channel_id=1, source_target_pairs={{0,18},{1,19},{2,16},{3,17},{4,22},{5,23},{6,20},{7,21},{8,26},{9,... | collective-permute-start | bytes 393224 | tf_op jit(solution)/shard_map/ppermute | solution.py:391
  37.0 7.8 %collective-permute-start.13 = (f32[256,128]{1,0:T(8,128)S(1)}, f32[256,128]{1,0:T(8,128)S(1)}, u32[]{:S(2)}, u32[]{:S(2)}) collective-permute-start(f32[256,128]{1,0:T(8,128)S(1)} %get-tuple-element.87), channel_id=1, source_target_pairs={{0,16},{1,17},{2,18},{3,19},{4,20},{5,21},{6,22},{7,23},{8,24},{9,... | collective-permute-start | bytes 393224 | tf_op jit(solution)/shard_map/ppermute | solution.py:391
  38.5 6.3 %collective-permute-start.14 = (f32[256,128]{1,0:T(8,128)S(1)}, f32[256,128]{1,0:T(8,128)S(1)}, u32[]{:S(2)}, u32[]{:S(2)}) collective-permute-start(f32[256,128]{1,0:T(8,128)S(1)} %get-tuple-element.88), channel_id=1, source_target_pairs={{0,2},{1,3},{2,0},{3,1},{4,6},{5,7},{6,4},{7,5},{8,10},{9,11},{10,... | collective-permute-start | bytes 393224 | tf_op jit(solution)/shard_map/ppermute | solution.py:391
  46.5 13.1 %collective-permute-start.21 = (f32[256,128]{1,0:T(8,128)S(1)}, f32[256,128]{1,0:T(8,128)S(1)}, u32[]{:S(2)}, u32[]{:S(2)}) collective-permute-start(f32[256,128]{1,0:T(8,128)S(1)} %get-tuple-element.94.refs_0_.sent_ref), channel_id=1, source_target_pairs={{0,12},{1,13},{2,14},{3,15},{4,8},{5,9},{6,10},{7,11},{8,4},{9,5},... | collective-permute-start | bytes 393224 | tf_op jit(solution)/shard_map/ppermute | solution.py:371
  46.9 12.8 %collective-permute-start.17 = (f32[256,128]{1,0:T(8,128)S(1)}, f32[256,128]{1,0:T(8,128)S(1)}, u32[]{:S(2)}, u32[]{:S(2)}) collective-permute-start(f32[256,128]{1,0:T(8,128)S(1)} %get-tuple-element.94.refs_0_.sent_ref), channel_id=1, source_target_pairs={{0,4},{1,5},{2,6},{3,7},{4,0},{5,1},{6,2},{7,3},{8,12},{9,13},{10,... | collective-permute-start | bytes 393224 | tf_op jit(solution)/shard_map/ppermute | solution.py:371
  46.9 12.9 %collective-permute-start.19 = (f32[256,128]{1,0:T(8,128)S(1)}, f32[256,128]{1,0:T(8,128)S(1)}, u32[]{:S(2)}, u32[]{:S(2)}) collective-permute-start(f32[256,128]{1,0:T(8,128)S(1)} %get-tuple-element.94.refs_0_.sent_ref), channel_id=1, source_target_pairs={{0,8},{1,9},{2,10},{3,11},{4,12},{5,13},{6,14},{7,15},{8,0},{9,1},... | collective-permute-start | bytes 393224 | tf_op jit(solution)/shard_map/ppermute | solution.py:371
  51.5 4.8 %collective-permute-start.23 = (f32[64,128]{1,0:T(8,128)S(1)}, f32[64,128]{1,0:T(8,128)S(1)}, u32[]{:S(2)}, u32[]{:S(2)}) collective-permute-start(f32[64,128]{1,0:T(8,128)S(1)} %get-tuple-element.98), channel_id=1, source_target_pairs={{0,2},{1,3},{2,0},{3,1},{4,6},{5,7},{6,4},{7,5},{8,10},{9,11},{10,... | collective-permute-start | bytes 98312 | tf_op jit(solution)/shard_map/ppermute | solution.py:391
  54.8 4.8 %collective-permute-start.24 = (f32[64,128]{1,0:T(8,128)S(1)}, f32[64,128]{1,0:T(8,128)S(1)}, u32[]{:S(2)}, u32[]{:S(2)}) collective-permute-start(f32[64,128]{1,0:T(8,128)S(1)} %get-tuple-element.99), channel_id=1, source_target_pairs={{0,18},{1,19},{2,16},{3,17},{4,22},{5,23},{6,20},{7,21},{8,26},{9,... | collective-permute-start | bytes 98312 | tf_op jit(solution)/shard_map/ppermute | solution.py:391
  59.8 5.0 %collective-permute-start.20 = (f32[256,128]{1,0:T(8,128)S(1)}, f32[256,128]{1,0:T(8,128)S(1)}, u32[]{:S(2)}, u32[]{:S(2)}) collective-permute-start(f32[256,128]{1,0:T(8,128)S(1)} %collective-permute-done.19.refs_4_), channel_id=1, source_target_pairs={{0,1},{1,0},{2,3},{3,2},{4,5},{5,4},{6,7},{7,6},{8,9},{9,8},{10,11... | collective-permute-start | bytes 393224 | tf_op jit(solution)/shard_map/ppermute | solution.py:375
  60.3 8.6 %collective-permute-start.26 = (f32[64,128]{1,0:T(8,128)S(1)}, f32[64,128]{1,0:T(8,128)S(1)}, u32[]{:S(2)}, u32[]{:S(2)}) collective-permute-start(f32[64,128]{1,0:T(8,128)S(1)} %add_parts.1.refs_0_), channel_id=1, source_target_pairs={{0,4},{1,5},{2,6},{3,7},{4,0},{5,1},{6,2},{7,3},{8,12},{9,13},{10,... | collective-permute-start | bytes 98312 | tf_op jit(solution)/shard_map/ppermute | solution.py:371
  60.3 10.1 %collective-permute-start.27 = (f32[64,128]{1,0:T(8,128)S(1)}, f32[64,128]{1,0:T(8,128)S(1)}, u32[]{:S(2)}, u32[]{:S(2)}) collective-permute-start(f32[64,128]{1,0:T(8,128)S(1)} %add_parts.1.refs_0_), channel_id=1, source_target_pairs={{0,8},{1,9},{2,10},{3,11},{4,12},{5,13},{6,14},{7,15},{8,0},{9,1},... | collective-permute-start | bytes 98312 | tf_op jit(solution)/shard_map/ppermute | solution.py:371
  61.3 9.2 %collective-permute-start.28 = (f32[64,128]{1,0:T(8,128)S(1)}, f32[64,128]{1,0:T(8,128)S(1)}, u32[]{:S(2)}, u32[]{:S(2)}) collective-permute-start(f32[64,128]{1,0:T(8,128)S(1)} %add_parts.1.refs_0_), channel_id=1, source_target_pairs={{0,12},{1,13},{2,14},{3,15},{4,8},{5,9},{6,10},{7,11},{8,4},{9,5},... | collective-permute-start | bytes 98312 | tf_op jit(solution)/shard_map/ppermute | solution.py:371
  66.9 13.6 %collective-permute-start.29 = (f32[256,128]{1,0:T(8,128)S(1)}, f32[256,128]{1,0:T(8,128)S(1)}, u32[]{:S(2)}, u32[]{:S(2)}) collective-permute-start(f32[256,128]{1,0:T(8,128)S(1)} %get-tuple-element.104), channel_id=1, source_target_pairs={{0,16},{1,17},{2,18},{3,19},{4,20},{5,21},{6,22},{7,23},{8,24},{9,... | collective-permute-start | bytes 393224 | tf_op jit(solution)/shard_map/ppermute | solution.py:391
  67.5 13.0 %collective-permute-start.30 = (f32[256,128]{1,0:T(8,128)S(1)}, f32[256,128]{1,0:T(8,128)S(1)}, u32[]{:S(2)}, u32[]{:S(2)}) collective-permute-start(f32[256,128]{1,0:T(8,128)S(1)} %get-tuple-element.105), channel_id=1, source_target_pairs={{0,2},{1,3},{2,0},{3,1},{4,6},{5,7},{6,4},{7,5},{8,10},{9,11},{10,... | collective-permute-start | bytes 393224 | tf_op jit(solution)/shard_map/ppermute | solution.py:391
  68.9 11.6 %collective-permute-start.31 = (f32[256,128]{1,0:T(8,128)S(1)}, f32[256,128]{1,0:T(8,128)S(1)}, u32[]{:S(2)}, u32[]{:S(2)}) collective-permute-start(f32[256,128]{1,0:T(8,128)S(1)} %get-tuple-element.106), channel_id=1, source_target_pairs={{0,18},{1,19},{2,16},{3,17},{4,22},{5,23},{6,20},{7,21},{8,26},{9,... | collective-permute-start | bytes 393224 | tf_op jit(solution)/shard_map/ppermute | solution.py:391
  72.3 4.8 %collective-permute-start.34 = (f32[64,128]{1,0:T(8,128)S(1)}, f32[64,128]{1,0:T(8,128)S(1)}, u32[]{:S(2)}, u32[]{:S(2)}) collective-permute-start(f32[64,128]{1,0:T(8,128)S(1)} %add_cores.1.refs_4_), channel_id=1, source_target_pairs={{0,2},{1,3},{2,0},{3,1},{4,6},{5,7},{6,4},{7,5},{8,10},{9,11},{10,... | collective-permute-start | bytes 98312 | tf_op jit(solution)/shard_map/ppermute | solution.py:391
  75.7 4.8 %collective-permute-start.35 = (f32[64,128]{1,0:T(8,128)S(1)}, f32[64,128]{1,0:T(8,128)S(1)}, u32[]{:S(2)}, u32[]{:S(2)}) collective-permute-start(f32[64,128]{1,0:T(8,128)S(1)} %add_cores.1.refs_4_), channel_id=1, source_target_pairs={{0,18},{1,19},{2,16},{3,17},{4,22},{5,23},{6,20},{7,21},{8,26},{9,... | collective-permute-start | bytes 98312 | tf_op jit(solution)/shard_map/ppermute | solution.py:391
  (19 other events, 102.8 us)

commit v10 on v8

--- a/solution.py
+++ b/solution.py
@@ -128,6 +128,12 @@
         for ref in got[1:]:
             count = count + ref[:, lanes]
         both_ref[q * plane : (q + 1) * plane, wide:] = count
+
+
+def keep_kernel(*refs):
+    half = len(refs) // 2
+    for ref, kept_ref in zip(refs[:half], refs[half:]):
+        kept_ref[...] = ref[...]
 
 
 def chip_kernel(wide, lists_ref, own_ref, other_ref, chip_ref, counted_ref):
@@ -425,7 +431,14 @@
 
     along = [features] + [lax.ppermute(features, both_axes, toward(dz)) for dz in (1, 2)]
     got_planes = along_z(planes)
-    *along, got_planes[0] = lax.optimization_barrier((*along, got_planes[0]))
+    lists, got_planes[0] = pl.pallas_call(
+        keep_kernel,
+        out_shape=tuple(jax.ShapeDtypeStruct(a.shape, i32) for a in (lists, planes[0])),
+        compiler_params=limit,
+        cost_estimate=pl.CostEstimate(flops=2**21, bytes_accessed=2**20, transcendentals=0),
+        name="keep",
+    )(lists, planes[0])
+    *along, lists, got_planes[0] = lax.optimization_barrier((*along, lists, got_planes[0]))
     *got_planes, later = lax.optimization_barrier((*got_planes, features))
     along += [lax.ppermute(later, both_axes, toward(dz)) for dz in range(3, DEPTH)]
     small = pl.CostEstimate(flops=2**14, bytes_accessed=2**18, transcendentals=0)

time: 80.6 us -> 79.1 us (0.981)
  waiting for transfers between devices: 19.1 us -> 17.6 us
    ppermute x9, waiting for transfers between devices: 2.37 us -> 0.79 us  [along_z(): lax.ppermute(blocks[dz], both_axes, toward(dz))]
  transfers between devices with their start and end apart: 36 -> 36, of which waited for: 10 -> 9; matrix products, arithmetic and copies ran while one was open for 0% -> 0% of each run, Pallas kernels for 16% -> 16%
where the time goes in v10:
time: 79.1 us; the launch traced here: 78.7 us
  starting transfers between devices  41.3 us (52%)
  waiting for transfers between devices  17.6 us (22%)
  Pallas kernels  17.5 us (22%)
  local copies, waits for them, and re-layouts  1.56 us (2%)
  between operations  0.85 us (1%)
    ppermute x12, starting transfers between devices, to_owners(): lax.ppermute(part, both_axes, grid.pairs(lambda x, y, z, c, dx=dx, dy=dy:...  13.8 us
    ppermute x9, starting transfers between devices, along_z(): lax.ppermute(blocks[dz], both_axes, toward(dz))  13.2 us
    ppermute x12, waiting for transfers between devices, to_owners(): lax.ppermute(part, both_axes, grid.pairs(lambda x, y, z, c, dx=dx, dy=dy:...  12.3 us
    ppermute x2, starting transfers between devices, shards(): lax.ppermute(features, both_axes, toward(dz))  5.68 us
    pallas_call x1, Pallas kernels, shards(): pl.pallas_call(functools.partial(backward_block_kernel, grid, slots), gri...  4.44 us
    pallas_call x1, Pallas kernels, shards(): pl.pallas_call(functools.partial(forward_block_kernel, grid, slots), grid...  3.77 us
    ppermute x1, starting transfers between devices, shards(): lax.ppermute(later, both_axes, toward(dz))  3.58 us
    ppermute x4, waiting for transfers between devices, from_peer(): return lax.ppermute(value, both_axes, [(b, a) for a, b in grid.pairs(move)])  3.43 us
  transfers between devices with their start and end apart: 36, of which 9 were waited for; matrix products, arithmetic and copies ran while one was open for 0% of the time, Pallas kernels for 16%

profile of v10, /device:TPU:0, one launch (start us, length us, event | category | flops | bytes accessed | tf_op | source)
XLA Modules:
  0.0 78.7 jit_solution(17001237035995468057)
XLA Ops:
  0.6 3.1 %collective-permute-start = (f32[256,128]{1,0:T(8,128)}, f32[256,128]{1,0:T(8,128)S(1)}, u32[]{:S(2)}, u32[]{:S(2)}) collective-permute-start(f32[256,128]{1,0:T(8,128)} %features_ref.1), channel_id=1, source_target_pairs={{0,4},{1,5},{2,6},{3,7},{4,0},{5,1},{6,2},{7,3},{8,12},{9,13},{10,... | collective-permute-start | bytes 393224 | tf_op jit(solution)/shard_map/ppermute | solution.py:432
  3.7 2.6 %collective-permute-start.1 = (f32[256,128]{1,0:T(8,128)}, f32[256,128]{1,0:T(8,128)S(1)}, u32[]{:S(2)}, u32[]{:S(2)}) collective-permute-start(f32[256,128]{1,0:T(8,128)} %features_ref.1), channel_id=1, source_target_pairs={{0,8},{1,9},{2,10},{3,11},{4,12},{5,13},{6,14},{7,15},{8,0},{9,1},... | collective-permute-start | bytes 393224 | tf_op jit(solution)/shard_map/ppermute | solution.py:432
  6.3 2.3 %pack.1 = (s32[32,384]{1,0:T(8,128)}, s32[8,896]{1,0:T(8,128)}, s32[8,896]{1,0:T(8,128)}, s32[8,896]{1,0:T(8,128)}, s32[8,896]{1,0:T(8,128)}) custom-call(s32[1]{0:T(128)} %bitcast.me_ref, s32[4,32]{1,0:T(4,128)} %bitcast.13, s32[4,32]{1,0:T(4,128)} %bitcast.14, s32[32,256]{1,0:T(8,128)} %bitcast.11, s32[32,256]{1,0:T(8,128)} %bitcast.12), custom_call_target="tpu_custom_call" | custom-call | flops 2147483648 | bytes 8388608 | tf_op jit(solution)/shard_map/pack/pallas_call | solution.py:416
  9.2 3.9 %collective-permute-start.4 = (s32[8,896]{1,0:T(8,128)}, s32[8,896]{1,0:T(8,128)S(1)}, u32[]{:S(2)}, u32[]{:S(2)}) collective-permute-start(s32[8,896]{1,0:T(8,128)} %get-tuple-element.63), channel_id=1, source_target_pairs={{0,12},{1,13},{2,14},{3,15},{4,8},{5,9},{6,10},{7,11},{8,4},{9,5},... | collective-permute-start | bytes 86024 | tf_op jit(solution)/shard_map/ppermute | solution.py:377
  15.6 3.6 %collective-permute-start.8 = (f32[256,128]{1,0:T(8,128)S(1)}, f32[256,128]{1,0:T(8,128)S(1)}, u32[]{:S(2)}, u32[]{:S(2)}) collective-permute-start(f32[256,128]{1,0:T(8,128)S(1)} %copy-done), channel_id=1, source_target_pairs={{0,12},{1,13},{2,14},{3,15},{4,8},{5,9},{6,10},{7,11},{8,4},{9,5},... | collective-permute-start | bytes 393224 | tf_op jit(solution)/shard_map/ppermute | solution.py:443
  19.2 1.6 %collective-permute-start.6 = (s32[64,384]{1,0:T(8,128)S(1)}, s32[64,384]{1,0:T(8,128)S(1)}, u32[]{:S(2)}, u32[]{:S(2)}) collective-permute-start(s32[64,384]{1,0:T(8,128)S(1)} %get-tuple-element.68.refs_0_), channel_id=1, source_target_pairs={{16,0},{17,1},{18,2},{19,3},{20,4},{21,5},{22,6},{23,7},{24,8},{25... | collective-permute-start | bytes 294920 | tf_op jit(solution)/shard_map/ppermute | solution.py:430
  20.7 1.5 %collective-permute-start.7 = (s32[32,512]{1,0:T(8,128)S(1)}, s32[32,512]{1,0:T(8,128)S(1)}, u32[]{:S(2)}, u32[]{:S(2)}) collective-permute-start(s32[32,512]{1,0:T(8,128)S(1)} %get-tuple-element.84.refs_2_.refs_0_), channel_id=1, source_target_pairs={{2,0},{3,1},{0,2},{1,3},{6,4},{7,5},{4,6},{5,7},{10,8},{11,9},{8,1... | collective-permute-start | bytes 196616 | tf_op jit(solution)/shard_map/ppermute | solution.py:430
  22.8 2.2 %collective-permute-done.7.refs_3_.refs_1_ = s32[32,512]{1,0:T(8,128)S(1)} collective-permute-done((s32[32,512]{1,0:T(8,128)S(1)}, s32[32,512]{1,0:T(8,128)S(1)}, u32[]{:S(2)}, u32[]{:S(2)}) %collective-permute-start.7) | collective-permute-done | bytes 65568 | tf_op jit(solution)/shard_map/ppermute | solution.py:430
  25.0 3.8 %forward_block.1 = (bf16[1024,2048]{1,0:T(8,128)(2,1)S(1)}, f32[32,128]{1,0:T(8,128)S(1)}) custom-call(s32[1]{0:T(128)} %bitcast.me_ref, s32[64,384]{1,0:T(8,128)S(1)} %get-tuple-element.68.refs_0_, s32[64,384]{1,0:T(8,128)S(1)} %collective-permute-done.6.refs_1_, s32[32,512]{1,0:T(8,128)S(1)} %get-tuple-element.84.refs_2_.refs_0_, ...), custom_call_target="tpu_custom_call" | custom-call | flops 65536 | bytes 65536 | tf_op jit(solution)/shard_map/forward_block/pallas_call | solution.py:484
  30.4 2.3 %forward_sum.1 = (f32[256,128]{1,0:T(8,128)S(1)}, f32[256,128]{1,0:T(8,128)S(1)}, f32[256,128]{1,0:T(8,128)S(1)}, f32[256,128]{1,0:T(8,128)S(1)}, f32[256,128]{1,0:T(8,128)S(1)}) custom-call(s32[1]{0:T(128)} %bitcast.me_ref, f32[32,128]{1,0:T(8,128)S(1)} %get-tuple-element.70.root_ref, bf16[1024,2048]{1,0:T(8,128)(2,1)S(1)} %get-tuple-element.73.block_ref, ...), custom_call_target="tpu_custom_call" | custom-call | flops 1073741824 | bytes 4194304 | tf_op jit(solution)/shard_map/forward_sum/pallas_call | solution.py:502
  32.7 1.6 %collective-permute-start.15 = (f32[256,128]{1,0:T(8,128)S(1)}, f32[256,128]{1,0:T(8,128)S(1)}, u32[]{:S(2)}, u32[]{:S(2)}) collective-permute-start(f32[256,128]{1,0:T(8,128)S(1)} %get-tuple-element.83), channel_id=1, source_target_pairs={{0,18},{1,19},{2,16},{3,17},{4,22},{5,23},{6,20},{7,21},{8,26},{9,... | collective-permute-start | bytes 393224 | tf_op jit(solution)/shard_map/ppermute | solution.py:398
  34.3 1.5 %collective-permute-start.13 = (f32[256,128]{1,0:T(8,128)S(1)}, f32[256,128]{1,0:T(8,128)S(1)}, u32[]{:S(2)}, u32[]{:S(2)}) collective-permute-start(f32[256,128]{1,0:T(8,128)S(1)} %get-tuple-element.81), channel_id=1, source_target_pairs={{0,16},{1,17},{2,18},{3,19},{4,20},{5,21},{6,22},{7,23},{8,24},{9,... | collective-permute-start | bytes 393224 | tf_op jit(solution)/shard_map/ppermute | solution.py:398
  36.3 4.4 %backward_block.1.block_ref = bf16[1024,2048]{1,0:T(8,128)(2,1)S(1)} custom-call(s32[1]{0:T(128)} %bitcast.me_ref, s32[32,512]{1,0:T(8,128)S(1)} %get-tuple-element.84.refs_2_.refs_0_, s32[32,512]{1,0:T(8,128)S(1)} %collective-permute-done.7.refs_3_.refs_1_), custom_call_target="tpu_custom_call" | custom-call | flops 1073741824 | bytes 4194304 | tf_op jit(solution)/shard_map/backward_block/pallas_call | solution.py:515
  40.7 1.6 %collective-permute-done.13.refs_1_ = f32[256,128]{1,0:T(8,128)S(1)} collective-permute-done((f32[256,128]{1,0:T(8,128)S(1)}, f32[256,128]{1,0:T(8,128)S(1)}, u32[]{:S(2)}, u32[]{:S(2)}) %collective-permute-start.13) | collective-permute-done | bytes 131104 | tf_op jit(solution)/shard_map/ppermute | solution.py:398
  42.4 1.7 %middle.1 = (f32[256,256]{1,0:T(8,128)}, f32[256,128]{1,0:T(8,128)S(1)}, f32[64,128]{1,0:T(8,128)S(1)}, f32[64,128]{1,0:T(8,128)S(1)}, f32[64,128]{1,0:T(8,128)S(1)}, /*index=5*/f32[64,128]{1,0:T(8,128)S(1)}) custom-call(s32[1]{0:T(128)} %bitcast.me_ref, f32[256,128]{1,0:T(8,128)S(1)} %get-tuple-element.78.scale_ref, f32[256,128]{1,0:T(8,128)S(1)} %copy-done, ...), custom_call_target="tpu_custom_call" | custom-call | flops 301989888 | bytes 1048576 | tf_op jit(solution)/shard_map/middle/pallas_call | solution.py:529
  45.2 3.2 %collective-permute-start.19 = (f32[256,128]{1,0:T(8,128)S(1)}, f32[256,128]{1,0:T(8,128)S(1)}, u32[]{:S(2)}, u32[]{:S(2)}) collective-permute-start(f32[256,128]{1,0:T(8,128)S(1)} %get-tuple-element.88.refs_0_.sent_ref), channel_id=1, source_target_pairs={{0,8},{1,9},{2,10},{3,11},{4,12},{5,13},{6,14},{7,15},{8,0},{9,1},... | collective-permute-start | bytes 393224 | tf_op jit(solution)/shard_map/ppermute | solution.py:377
  50.4 2.0 %collective-permute-done.22.refs_1_ = f32[64,128]{1,0:T(8,128)S(1)} collective-permute-done((f32[64,128]{1,0:T(8,128)S(1)}, f32[64,128]{1,0:T(8,128)S(1)}, u32[]{:S(2)}, u32[]{:S(2)}) %collective-permute-start.22) | collective-permute-done | bytes 32800 | tf_op jit(solution)/shard_map/ppermute | solution.py:398
  53.7 3.4 %collective-permute-done.24.refs_3_ = f32[64,128]{1,0:T(8,128)S(1)} collective-permute-done((f32[64,128]{1,0:T(8,128)S(1)}, f32[64,128]{1,0:T(8,128)S(1)}, u32[]{:S(2)}, u32[]{:S(2)}) %collective-permute-start.24) | collective-permute-done | bytes 32800 | tf_op jit(solution)/shard_map/ppermute | solution.py:398
  57.8 1.7 %collective-permute-start.27 = (f32[64,128]{1,0:T(8,128)S(1)}, f32[64,128]{1,0:T(8,128)S(1)}, u32[]{:S(2)}, u32[]{:S(2)}) collective-permute-start(f32[64,128]{1,0:T(8,128)S(1)} %add_parts.1.refs_0_), channel_id=1, source_target_pairs={{0,8},{1,9},{2,10},{3,11},{4,12},{5,13},{6,14},{7,15},{8,0},{9,1},... | collective-permute-start | bytes 98312 | tf_op jit(solution)/shard_map/ppermute | solution.py:377
  59.6 2.7 %collective-permute-start.28 = (f32[64,128]{1,0:T(8,128)S(1)}, f32[64,128]{1,0:T(8,128)S(1)}, u32[]{:S(2)}, u32[]{:S(2)}) collective-permute-start(f32[64,128]{1,0:T(8,128)S(1)} %add_parts.1.refs_0_), channel_id=1, source_target_pairs={{0,12},{1,13},{2,14},{3,15},{4,8},{5,9},{6,10},{7,11},{8,4},{9,5},... | collective-permute-start | bytes 98312 | tf_op jit(solution)/shard_map/ppermute | solution.py:377
  62.2 2.1 %backward_sum.1 = (f32[256,128]{1,0:T(8,128)S(1)}, f32[256,128]{1,0:T(8,128)S(1)}, f32[256,128]{1,0:T(8,128)S(1)}, f32[256,128]{1,0:T(8,128)S(1)}) custom-call(s32[1]{0:T(128)} %bitcast.me_ref, bf16[1024,2048]{1,0:T(8,128)(2,1)S(1)} %backward_block.1.block_ref, f32[256,128]{1,0:T(8,128)S(1)} %get-tuple-element.88.refs_0_.sent_ref, ...), custom_call_target="tpu_custom_call" | custom-call | flops 1073741824 | bytes 4194304 | tf_op jit(solution)/shard_map/backward_sum/pallas_call | solution.py:556
  66.4 1.5 %collective-permute-start.31 = (f32[256,128]{1,0:T(8,128)S(1)}, f32[256,128]{1,0:T(8,128)S(1)}, u32[]{:S(2)}, u32[]{:S(2)}) collective-permute-start(f32[256,128]{1,0:T(8,128)S(1)} %get-tuple-element.100), channel_id=1, source_target_pairs={{0,18},{1,19},{2,16},{3,17},{4,22},{5,23},{6,20},{7,21},{8,26},{9,... | collective-permute-start | bytes 393224 | tf_op jit(solution)/shard_map/ppermute | solution.py:398
  71.2 2.0 %collective-permute-done.33.refs_5_ = f32[64,128]{1,0:T(8,128)S(1)} collective-permute-done((f32[64,128]{1,0:T(8,128)S(1)}, f32[64,128]{1,0:T(8,128)S(1)}, u32[]{:S(2)}, u32[]{:S(2)}) %collective-permute-start.33) | collective-permute-done | bytes 32800 | tf_op jit(solution)/shard_map/ppermute | solution.py:398
  74.6 3.4 %collective-permute-done.35.refs_7_ = f32[64,128]{1,0:T(8,128)S(1)} collective-permute-done((f32[64,128]{1,0:T(8,128)S(1)}, f32[64,128]{1,0:T(8,128)S(1)}, u32[]{:S(2)}, u32[]{:S(2)}) %collective-permute-start.35) | collective-permute-done | bytes 32800 | tf_op jit(solution)/shard_map/ppermute | solution.py:398
  (75 shorter events, 18.2 us)
Async XLA Ops:
  0.6 14.0 %collective-permute-start = (f32[256,128]{1,0:T(8,128)}, f32[256,128]{1,0:T(8,128)S(1)}, u32[]{:S(2)}, u32[]{:S(2)}) collective-permute-start(f32[256,128]{1,0:T(8,128)} %features_ref.1), channel_id=1, source_target_pairs={{0,4},{1,5},{2,6},{3,7},{4,0},{5,1},{6,2},{7,3},{8,12},{9,13},{10,... | collective-permute-start | bytes 393224 | tf_op jit(solution)/shard_map/ppermute | solution.py:432
  3.7 10.9 %collective-permute-start.1 = (f32[256,128]{1,0:T(8,128)}, f32[256,128]{1,0:T(8,128)S(1)}, u32[]{:S(2)}, u32[]{:S(2)}) collective-permute-start(f32[256,128]{1,0:T(8,128)} %features_ref.1), channel_id=1, source_target_pairs={{0,8},{1,9},{2,10},{3,11},{4,12},{5,13},{6,14},{7,15},{8,0},{9,1},... | collective-permute-start | bytes 393224 | tf_op jit(solution)/shard_map/ppermute | solution.py:432
  8.7 6.0 %collective-permute-start.2 = (s32[8,896]{1,0:T(8,128)}, s32[8,896]{1,0:T(8,128)S(1)}, u32[]{:S(2)}, u32[]{:S(2)}) collective-permute-start(s32[8,896]{1,0:T(8,128)} %get-tuple-element.61), channel_id=1, source_target_pairs={{0,4},{1,5},{2,6},{3,7},{4,0},{5,1},{6,2},{7,3},{8,12},{9,13},{10,... | collective-permute-start | bytes 86024 | tf_op jit(solution)/shard_map/ppermute | solution.py:377
  9.2 5.5 %collective-permute-start.3 = (s32[8,896]{1,0:T(8,128)}, s32[8,896]{1,0:T(8,128)S(1)}, u32[]{:S(2)}, u32[]{:S(2)}) collective-permute-start(s32[8,896]{1,0:T(8,128)} %get-tuple-element.62), channel_id=1, source_target_pairs={{0,8},{1,9},{2,10},{3,11},{4,12},{5,13},{6,14},{7,15},{8,0},{9,1},... | collective-permute-start | bytes 86024 | tf_op jit(solution)/shard_map/ppermute | solution.py:377
  9.2 6.3 %collective-permute-start.4 = (s32[8,896]{1,0:T(8,128)}, s32[8,896]{1,0:T(8,128)S(1)}, u32[]{:S(2)}, u32[]{:S(2)}) collective-permute-start(s32[8,896]{1,0:T(8,128)} %get-tuple-element.63), channel_id=1, source_target_pairs={{0,12},{1,13},{2,14},{3,15},{4,8},{5,9},{6,10},{7,11},{8,4},{9,5},... | collective-permute-start | bytes 86024 | tf_op jit(solution)/shard_map/ppermute | solution.py:377
  15.6 13.2 %collective-permute-start.8 = (f32[256,128]{1,0:T(8,128)S(1)}, f32[256,128]{1,0:T(8,128)S(1)}, u32[]{:S(2)}, u32[]{:S(2)}) collective-permute-start(f32[256,128]{1,0:T(8,128)S(1)} %copy-done), channel_id=1, source_target_pairs={{0,12},{1,13},{2,14},{3,15},{4,8},{5,9},{6,10},{7,11},{8,4},{9,5},... | collective-permute-start | bytes 393224 | tf_op jit(solution)/shard_map/ppermute | solution.py:443
  19.2 5.8 %collective-permute-start.6 = (s32[64,384]{1,0:T(8,128)S(1)}, s32[64,384]{1,0:T(8,128)S(1)}, u32[]{:S(2)}, u32[]{:S(2)}) collective-permute-start(s32[64,384]{1,0:T(8,128)S(1)} %get-tuple-element.68.refs_0_), channel_id=1, source_target_pairs={{16,0},{17,1},{18,2},{19,3},{20,4},{21,5},{22,6},{23,7},{24,8},{25... | collective-permute-start | bytes 294920 | tf_op jit(solution)/shard_map/ppermute | solution.py:430
  22.3 7.1 %collective-permute-start.9 = (f32[256,128]{1,0:T(8,128)S(1)}, f32[256,128]{1,0:T(8,128)S(1)}, u32[]{:S(2)}, u32[]{:S(2)}) collective-permute-start(f32[256,128]{1,0:T(8,128)S(1)} %copy-done), channel_id=1, source_target_pairs={{0,1},{1,0},{2,3},{3,2},{4,5},{5,4},{6,7},{7,6},{8,9},{9,8},{10,11... | collective-permute-start | bytes 393224 | tf_op jit(solution)/shard_map/ppermute | solution.py:382
  22.3 7.1 %collective-permute-start.10 = (f32[256,128]{1,0:T(8,128)S(1)}, f32[256,128]{1,0:T(8,128)S(1)}, u32[]{:S(2)}, u32[]{:S(2)}) collective-permute-start(f32[256,128]{1,0:T(8,128)S(1)} %collective-permute-done.refs_2_), channel_id=1, source_target_pairs={{0,1},{1,0},{2,3},{3,2},{4,5},{5,4},{6,7},{7,6},{8,9},{9,8},{10,11... | collective-permute-start | bytes 393224 | tf_op jit(solution)/shard_map/ppermute | solution.py:382
  32.7 8.0 %collective-permute-start.15 = (f32[256,128]{1,0:T(8,128)S(1)}, f32[256,128]{1,0:T(8,128)S(1)}, u32[]{:S(2)}, u32[]{:S(2)}) collective-permute-start(f32[256,128]{1,0:T(8,128)S(1)} %get-tuple-element.83), channel_id=1, source_target_pairs={{0,18},{1,19},{2,16},{3,17},{4,22},{5,23},{6,20},{7,21},{8,26},{9,... | collective-permute-start | bytes 393224 | tf_op jit(solution)/shard_map/ppermute | solution.py:398
  34.3 8.1 %collective-permute-start.13 = (f32[256,128]{1,0:T(8,128)S(1)}, f32[256,128]{1,0:T(8,128)S(1)}, u32[]{:S(2)}, u32[]{:S(2)}) collective-permute-start(f32[256,128]{1,0:T(8,128)S(1)} %get-tuple-element.81), channel_id=1, source_target_pairs={{0,16},{1,17},{2,18},{3,19},{4,20},{5,21},{6,22},{7,23},{8,24},{9,... | collective-permute-start | bytes 393224 | tf_op jit(solution)/shard_map/ppermute | solution.py:398
  35.8 6.6 %collective-permute-start.14 = (f32[256,128]{1,0:T(8,128)S(1)}, f32[256,128]{1,0:T(8,128)S(1)}, u32[]{:S(2)}, u32[]{:S(2)}) collective-permute-start(f32[256,128]{1,0:T(8,128)S(1)} %get-tuple-element.82), channel_id=1, source_target_pairs={{0,2},{1,3},{2,0},{3,1},{4,6},{5,7},{6,4},{7,5},{8,10},{9,11},{10,... | collective-permute-start | bytes 393224 | tf_op jit(solution)/shard_map/ppermute | solution.py:398
  44.0 13.1 %collective-permute-start.21 = (f32[256,128]{1,0:T(8,128)S(1)}, f32[256,128]{1,0:T(8,128)S(1)}, u32[]{:S(2)}, u32[]{:S(2)}) collective-permute-start(f32[256,128]{1,0:T(8,128)S(1)} %get-tuple-element.88.refs_0_.sent_ref), channel_id=1, source_target_pairs={{0,12},{1,13},{2,14},{3,15},{4,8},{5,9},{6,10},{7,11},{8,4},{9,5},... | collective-permute-start | bytes 393224 | tf_op jit(solution)/shard_map/ppermute | solution.py:377
  45.2 12.0 %collective-permute-start.17 = (f32[256,128]{1,0:T(8,128)S(1)}, f32[256,128]{1,0:T(8,128)S(1)}, u32[]{:S(2)}, u32[]{:S(2)}) collective-permute-start(f32[256,128]{1,0:T(8,128)S(1)} %get-tuple-element.88.refs_0_.sent_ref), channel_id=1, source_target_pairs={{0,4},{1,5},{2,6},{3,7},{4,0},{5,1},{6,2},{7,3},{8,12},{9,13},{10,... | collective-permute-start | bytes 393224 | tf_op jit(solution)/shard_map/ppermute | solution.py:377
  45.2 12.1 %collective-permute-start.19 = (f32[256,128]{1,0:T(8,128)S(1)}, f32[256,128]{1,0:T(8,128)S(1)}, u32[]{:S(2)}, u32[]{:S(2)}) collective-permute-start(f32[256,128]{1,0:T(8,128)S(1)} %get-tuple-element.88.refs_0_.sent_ref), channel_id=1, source_target_pairs={{0,8},{1,9},{2,10},{3,11},{4,12},{5,13},{6,14},{7,15},{8,0},{9,1},... | collective-permute-start | bytes 393224 | tf_op jit(solution)/shard_map/ppermute | solution.py:377
  52.3 4.8 %collective-permute-start.24 = (f32[64,128]{1,0:T(8,128)S(1)}, f32[64,128]{1,0:T(8,128)S(1)}, u32[]{:S(2)}, u32[]{:S(2)}) collective-permute-start(f32[64,128]{1,0:T(8,128)S(1)} %get-tuple-element.93), channel_id=1, source_target_pairs={{0,18},{1,19},{2,16},{3,17},{4,22},{5,23},{6,20},{7,21},{8,26},{9,... | collective-permute-start | bytes 98312 | tf_op jit(solution)/shard_map/ppermute | solution.py:398
  57.3 5.0 %collective-permute-start.20 = (f32[256,128]{1,0:T(8,128)S(1)}, f32[256,128]{1,0:T(8,128)S(1)}, u32[]{:S(2)}, u32[]{:S(2)}) collective-permute-start(f32[256,128]{1,0:T(8,128)S(1)} %collective-permute-done.19.refs_4_), channel_id=1, source_target_pairs={{0,1},{1,0},{2,3},{3,2},{4,5},{5,4},{6,7},{7,6},{8,9},{9,8},{10,11... | collective-permute-start | bytes 393224 | tf_op jit(solution)/shard_map/ppermute | solution.py:382
  57.8 8.6 %collective-permute-start.26 = (f32[64,128]{1,0:T(8,128)S(1)}, f32[64,128]{1,0:T(8,128)S(1)}, u32[]{:S(2)}, u32[]{:S(2)}) collective-permute-start(f32[64,128]{1,0:T(8,128)S(1)} %add_parts.1.refs_0_), channel_id=1, source_target_pairs={{0,4},{1,5},{2,6},{3,7},{4,0},{5,1},{6,2},{7,3},{8,12},{9,13},{10,... | collective-permute-start | bytes 98312 | tf_op jit(solution)/shard_map/ppermute | solution.py:377
  57.8 10.1 %collective-permute-start.27 = (f32[64,128]{1,0:T(8,128)S(1)}, f32[64,128]{1,0:T(8,128)S(1)}, u32[]{:S(2)}, u32[]{:S(2)}) collective-permute-start(f32[64,128]{1,0:T(8,128)S(1)} %add_parts.1.refs_0_), channel_id=1, source_target_pairs={{0,8},{1,9},{2,10},{3,11},{4,12},{5,13},{6,14},{7,15},{8,0},{9,1},... | collective-permute-start | bytes 98312 | tf_op jit(solution)/shard_map/ppermute | solution.py:377
  59.6 8.4 %collective-permute-start.28 = (f32[64,128]{1,0:T(8,128)S(1)}, f32[64,128]{1,0:T(8,128)S(1)}, u32[]{:S(2)}, u32[]{:S(2)}) collective-permute-start(f32[64,128]{1,0:T(8,128)S(1)} %add_parts.1.refs_0_), channel_id=1, source_target_pairs={{0,12},{1,13},{2,14},{3,15},{4,8},{5,9},{6,10},{7,11},{8,4},{9,5},... | collective-permute-start | bytes 98312 | tf_op jit(solution)/shard_map/ppermute | solution.py:377
  64.4 13.6 %collective-permute-start.29 = (f32[256,128]{1,0:T(8,128)S(1)}, f32[256,128]{1,0:T(8,128)S(1)}, u32[]{:S(2)}, u32[]{:S(2)}) collective-permute-start(f32[256,128]{1,0:T(8,128)S(1)} %get-tuple-element.98), channel_id=1, source_target_pairs={{0,16},{1,17},{2,18},{3,19},{4,20},{5,21},{6,22},{7,23},{8,24},{9,... | collective-permute-start | bytes 393224 | tf_op jit(solution)/shard_map/ppermute | solution.py:398
  65.0 13.0 %collective-permute-start.30 = (f32[256,128]{1,0:T(8,128)S(1)}, f32[256,128]{1,0:T(8,128)S(1)}, u32[]{:S(2)}, u32[]{:S(2)}) collective-permute-start(f32[256,128]{1,0:T(8,128)S(1)} %get-tuple-element.99), channel_id=1, source_target_pairs={{0,2},{1,3},{2,0},{3,1},{4,6},{5,7},{6,4},{7,5},{8,10},{9,11},{10,... | collective-permute-start | bytes 393224 | tf_op jit(solution)/shard_map/ppermute | solution.py:398
  66.4 11.6 %collective-permute-start.31 = (f32[256,128]{1,0:T(8,128)S(1)}, f32[256,128]{1,0:T(8,128)S(1)}, u32[]{:S(2)}, u32[]{:S(2)}) collective-permute-start(f32[256,128]{1,0:T(8,128)S(1)} %get-tuple-element.100), channel_id=1, source_target_pairs={{0,18},{1,19},{2,16},{3,17},{4,22},{5,23},{6,20},{7,21},{8,26},{9,... | collective-permute-start | bytes 393224 | tf_op jit(solution)/shard_map/ppermute | solution.py:398
  73.2 4.8 %collective-permute-start.35 = (f32[64,128]{1,0:T(8,128)S(1)}, f32[64,128]{1,0:T(8,128)S(1)}, u32[]{:S(2)}, u32[]{:S(2)}) collective-permute-start(f32[64,128]{1,0:T(8,128)S(1)} %add_cores.1.refs_4_), channel_id=1, source_target_pairs={{0,18},{1,19},{2,16},{3,17},{4,22},{5,23},{6,20},{7,21},{8,26},{9,... | collective-permute-start | bytes 98312 | tf_op jit(solution)/shard_map/ppermute | solution.py:398
  (19 other events, 108.0 us)

commit v11 on v10

--- a/solution.py
+++ b/solution.py
@@ -71,6 +71,11 @@
 def one_hot(index_row, size):
     places = lax.broadcasted_iota(i32, (size, index_row.shape[1]), 0)
     return jnp.where(places == index_row, 1.0, 0.0).astype(bf16)
+
+
+def narrow_one_hot(index_row, places):
+    index = index_row.astype(f32).astype(bf16)
+    return jnp.where(places == index, jnp.ones((), bf16), jnp.zeros((), bf16))
 
 
 def turned_times(values, table):
@@ -200,6 +205,7 @@
     dx, dy = lax.rem(step, grid.rows), lax.div(step, grid.rows)
     to_y = lax.rem(y + dy, grid.wide)
     plane = grid.wide * CORES * grid.per
+    places = lax.broadcasted_iota(i32, (grid.group, slots), 0).astype(f32).astype(bf16)
     for g in range(grid.gathered):
         for s in range(grid.per):
             at = (g % CORES) * rows + (g // CORES) * plane + (to_y * CORES + core) * grid.per + s
@@ -208,8 +214,8 @@
             target = lax.shift_right_arithmetic(pos, 7)
             source = slot_columns(row[:, slots:], 0, slots) * TILE_SIDE + (pos & (TILE_SIDE - 1))
             hot = lax.dot_general(
-                one_hot(target, TILE_SIDE),
-                one_hot(source - x * grid.group, grid.group),
+                narrow_one_hot(target, places[:TILE_SIDE]),
+                narrow_one_hot(source - x * grid.group, places),
                 NT,
                 preferred_element_type=f32,
             )

time: 79.1 us -> 79 us (level)
  no operation moved by 1% of the time
where the time goes in v11:
time: 79 us; the launch traced here: 78.7 us
  starting transfers between devices  41.3 us (52%)
  Pallas kernels  17.5 us (22%)
  waiting for transfers between devices  17.5 us (22%)
  local copies, waits for them, and re-layouts  1.56 us (2%)
  between operations  0.85 us (1%)
    ppermute x12, starting transfers between devices, to_owners(): lax.ppermute(part, both_axes, grid.pairs(lambda x, y, z, c, dx=dx, dy=dy:...  13.8 us
    ppermute x9, starting transfers between devices, along_z(): lax.ppermute(blocks[dz], both_axes, toward(dz))  13.2 us
    ppermute x12, waiting for transfers between devices, to_owners(): lax.ppermute(part, both_axes, grid.pairs(lambda x, y, z, c, dx=dx, dy=dy:...  12.3 us
    ppermute x2, starting transfers between devices, shards(): lax.ppermute(features, both_axes, toward(dz))  5.68 us
    pallas_call x1, Pallas kernels, shards(): pl.pallas_call(functools.partial(backward_block_kernel, grid, slots), gri...  4.45 us
    pallas_call x1, Pallas kernels, shards(): pl.pallas_call(functools.partial(forward_block_kernel, grid, slots), grid...  3.75 us
    ppermute x1, starting transfers between devices, shards(): lax.ppermute(later, both_axes, toward(dz))  3.58 us
    ppermute x4, waiting for transfers between devices, from_peer(): return lax.ppermute(value, both_axes, [(b, a) for a, b in grid.pairs(move)])  3.43 us
  transfers between devices with their start and end apart: 36, of which 9 were waited for; matrix products, arithmetic and copies ran while one was open for 0% of the time, Pallas kernels for 16%

profile of v11, /device:TPU:0, one launch (start us, length us, event | category | flops | bytes accessed | tf_op | source)
XLA Modules:
  0.0 78.7 jit_solution(16389174230857406762)
XLA Ops:
  0.6 3.1 %collective-permute-start = (f32[256,128]{1,0:T(8,128)}, f32[256,128]{1,0:T(8,128)S(1)}, u32[]{:S(2)}, u32[]{:S(2)}) collective-permute-start(f32[256,128]{1,0:T(8,128)} %features_ref.1), channel_id=1, source_target_pairs={{0,4},{1,5},{2,6},{3,7},{4,0},{5,1},{6,2},{7,3},{8,12},{9,13},{10,... | collective-permute-start | bytes 393224 | tf_op jit(solution)/shard_map/ppermute | solution.py:438
  3.7 2.6 %collective-permute-start.1 = (f32[256,128]{1,0:T(8,128)}, f32[256,128]{1,0:T(8,128)S(1)}, u32[]{:S(2)}, u32[]{:S(2)}) collective-permute-start(f32[256,128]{1,0:T(8,128)} %features_ref.1), channel_id=1, source_target_pairs={{0,8},{1,9},{2,10},{3,11},{4,12},{5,13},{6,14},{7,15},{8,0},{9,1},... | collective-permute-start | bytes 393224 | tf_op jit(solution)/shard_map/ppermute | solution.py:438
  6.3 2.3 %pack.1 = (s32[32,384]{1,0:T(8,128)}, s32[8,896]{1,0:T(8,128)}, s32[8,896]{1,0:T(8,128)}, s32[8,896]{1,0:T(8,128)}, s32[8,896]{1,0:T(8,128)}) custom-call(s32[1]{0:T(128)} %bitcast.me_ref, s32[4,32]{1,0:T(4,128)} %bitcast.13, s32[4,32]{1,0:T(4,128)} %bitcast.14, s32[32,256]{1,0:T(8,128)} %bitcast.11, s32[32,256]{1,0:T(8,128)} %bitcast.12), custom_call_target="tpu_custom_call" | custom-call | flops 2147483648 | bytes 8388608 | tf_op jit(solution)/shard_map/pack/pallas_call | solution.py:422
  9.2 3.9 %collective-permute-start.4 = (s32[8,896]{1,0:T(8,128)}, s32[8,896]{1,0:T(8,128)S(1)}, u32[]{:S(2)}, u32[]{:S(2)}) collective-permute-start(s32[8,896]{1,0:T(8,128)} %get-tuple-element.63), channel_id=1, source_target_pairs={{0,12},{1,13},{2,14},{3,15},{4,8},{5,9},{6,10},{7,11},{8,4},{9,5},... | collective-permute-start | bytes 86024 | tf_op jit(solution)/shard_map/ppermute | solution.py:383
  15.6 3.6 %collective-permute-start.8 = (f32[256,128]{1,0:T(8,128)S(1)}, f32[256,128]{1,0:T(8,128)S(1)}, u32[]{:S(2)}, u32[]{:S(2)}) collective-permute-start(f32[256,128]{1,0:T(8,128)S(1)} %copy-done), channel_id=1, source_target_pairs={{0,12},{1,13},{2,14},{3,15},{4,8},{5,9},{6,10},{7,11},{8,4},{9,5},... | collective-permute-start | bytes 393224 | tf_op jit(solution)/shard_map/ppermute | solution.py:449
  19.2 1.6 %collective-permute-start.6 = (s32[64,384]{1,0:T(8,128)S(1)}, s32[64,384]{1,0:T(8,128)S(1)}, u32[]{:S(2)}, u32[]{:S(2)}) collective-permute-start(s32[64,384]{1,0:T(8,128)S(1)} %get-tuple-element.68.refs_0_), channel_id=1, source_target_pairs={{16,0},{17,1},{18,2},{19,3},{20,4},{21,5},{22,6},{23,7},{24,8},{25... | collective-permute-start | bytes 294920 | tf_op jit(solution)/shard_map/ppermute | solution.py:436
  20.7 1.5 %collective-permute-start.7 = (s32[32,512]{1,0:T(8,128)S(1)}, s32[32,512]{1,0:T(8,128)S(1)}, u32[]{:S(2)}, u32[]{:S(2)}) collective-permute-start(s32[32,512]{1,0:T(8,128)S(1)} %get-tuple-element.84.refs_2_.refs_0_), channel_id=1, source_target_pairs={{2,0},{3,1},{0,2},{1,3},{6,4},{7,5},{4,6},{5,7},{10,8},{11,9},{8,1... | collective-permute-start | bytes 196616 | tf_op jit(solution)/shard_map/ppermute | solution.py:436
  22.8 2.2 %collective-permute-done.7.refs_3_.refs_1_ = s32[32,512]{1,0:T(8,128)S(1)} collective-permute-done((s32[32,512]{1,0:T(8,128)S(1)}, s32[32,512]{1,0:T(8,128)S(1)}, u32[]{:S(2)}, u32[]{:S(2)}) %collective-permute-start.7) | collective-permute-done | bytes 65568 | tf_op jit(solution)/shard_map/ppermute | solution.py:436
  25.0 3.7 %forward_block.1 = (bf16[1024,2048]{1,0:T(8,128)(2,1)S(1)}, f32[32,128]{1,0:T(8,128)S(1)}) custom-call(s32[1]{0:T(128)} %bitcast.me_ref, s32[64,384]{1,0:T(8,128)S(1)} %get-tuple-element.68.refs_0_, s32[64,384]{1,0:T(8,128)S(1)} %collective-permute-done.6.refs_1_, s32[32,512]{1,0:T(8,128)S(1)} %get-tuple-element.84.refs_2_.refs_0_, ...), custom_call_target="tpu_custom_call" | custom-call | flops 65536 | bytes 65536 | tf_op jit(solution)/shard_map/forward_block/pallas_call | solution.py:490
  30.3 2.3 %forward_sum.1 = (f32[256,128]{1,0:T(8,128)S(1)}, f32[256,128]{1,0:T(8,128)S(1)}, f32[256,128]{1,0:T(8,128)S(1)}, f32[256,128]{1,0:T(8,128)S(1)}, f32[256,128]{1,0:T(8,128)S(1)}) custom-call(s32[1]{0:T(128)} %bitcast.me_ref, f32[32,128]{1,0:T(8,128)S(1)} %get-tuple-element.70.root_ref, bf16[1024,2048]{1,0:T(8,128)(2,1)S(1)} %get-tuple-element.73.block_ref, ...), custom_call_target="tpu_custom_call" | custom-call | flops 1073741824 | bytes 4194304 | tf_op jit(solution)/shard_map/forward_sum/pallas_call | solution.py:508
  32.7 1.6 %collective-permute-start.15 = (f32[256,128]{1,0:T(8,128)S(1)}, f32[256,128]{1,0:T(8,128)S(1)}, u32[]{:S(2)}, u32[]{:S(2)}) collective-permute-start(f32[256,128]{1,0:T(8,128)S(1)} %get-tuple-element.83), channel_id=1, source_target_pairs={{0,18},{1,19},{2,16},{3,17},{4,22},{5,23},{6,20},{7,21},{8,26},{9,... | collective-permute-start | bytes 393224 | tf_op jit(solution)/shard_map/ppermute | solution.py:404
  34.2 1.5 %collective-permute-start.13 = (f32[256,128]{1,0:T(8,128)S(1)}, f32[256,128]{1,0:T(8,128)S(1)}, u32[]{:S(2)}, u32[]{:S(2)}) collective-permute-start(f32[256,128]{1,0:T(8,128)S(1)} %get-tuple-element.81), channel_id=1, source_target_pairs={{0,16},{1,17},{2,18},{3,19},{4,20},{5,21},{6,22},{7,23},{8,24},{9,... | collective-permute-start | bytes 393224 | tf_op jit(solution)/shard_map/ppermute | solution.py:404
  36.3 4.5 %backward_block.1.block_ref = bf16[1024,2048]{1,0:T(8,128)(2,1)S(1)} custom-call(s32[1]{0:T(128)} %bitcast.me_ref, s32[32,512]{1,0:T(8,128)S(1)} %get-tuple-element.84.refs_2_.refs_0_, s32[32,512]{1,0:T(8,128)S(1)} %collective-permute-done.7.refs_3_.refs_1_), custom_call_target="tpu_custom_call" | custom-call | flops 1073741824 | bytes 4194304 | tf_op jit(solution)/shard_map/backward_block/pallas_call | solution.py:521
  40.7 1.6 %collective-permute-done.13.refs_1_ = f32[256,128]{1,0:T(8,128)S(1)} collective-permute-done((f32[256,128]{1,0:T(8,128)S(1)}, f32[256,128]{1,0:T(8,128)S(1)}, u32[]{:S(2)}, u32[]{:S(2)}) %collective-permute-start.13) | collective-permute-done | bytes 131104 | tf_op jit(solution)/shard_map/ppermute | solution.py:404
  42.3 1.7 %middle.1 = (f32[256,256]{1,0:T(8,128)}, f32[256,128]{1,0:T(8,128)S(1)}, f32[64,128]{1,0:T(8,128)S(1)}, f32[64,128]{1,0:T(8,128)S(1)}, f32[64,128]{1,0:T(8,128)S(1)}, /*index=5*/f32[64,128]{1,0:T(8,128)S(1)}) custom-call(s32[1]{0:T(128)} %bitcast.me_ref, f32[256,128]{1,0:T(8,128)S(1)} %get-tuple-element.78.scale_ref, f32[256,128]{1,0:T(8,128)S(1)} %copy-done, ...), custom_call_target="tpu_custom_call" | custom-call | flops 301989888 | bytes 1048576 | tf_op jit(solution)/shard_map/middle/pallas_call | solution.py:535
  45.2 3.2 %collective-permute-start.19 = (f32[256,128]{1,0:T(8,128)S(1)}, f32[256,128]{1,0:T(8,128)S(1)}, u32[]{:S(2)}, u32[]{:S(2)}) collective-permute-start(f32[256,128]{1,0:T(8,128)S(1)} %get-tuple-element.88.refs_0_.sent_ref), channel_id=1, source_target_pairs={{0,8},{1,9},{2,10},{3,11},{4,12},{5,13},{6,14},{7,15},{8,0},{9,1},... | collective-permute-start | bytes 393224 | tf_op jit(solution)/shard_map/ppermute | solution.py:383
  50.3 2.0 %collective-permute-done.22.refs_1_ = f32[64,128]{1,0:T(8,128)S(1)} collective-permute-done((f32[64,128]{1,0:T(8,128)S(1)}, f32[64,128]{1,0:T(8,128)S(1)}, u32[]{:S(2)}, u32[]{:S(2)}) %collective-permute-start.22) | collective-permute-done | bytes 32800 | tf_op jit(solution)/shard_map/ppermute | solution.py:404
  53.7 3.4 %collective-permute-done.24.refs_3_ = f32[64,128]{1,0:T(8,128)S(1)} collective-permute-done((f32[64,128]{1,0:T(8,128)S(1)}, f32[64,128]{1,0:T(8,128)S(1)}, u32[]{:S(2)}, u32[]{:S(2)}) %collective-permute-start.24) | collective-permute-done | bytes 32800 | tf_op jit(solution)/shard_map/ppermute | solution.py:404
  57.8 1.7 %collective-permute-start.27 = (f32[64,128]{1,0:T(8,128)S(1)}, f32[64,128]{1,0:T(8,128)S(1)}, u32[]{:S(2)}, u32[]{:S(2)}) collective-permute-start(f32[64,128]{1,0:T(8,128)S(1)} %add_parts.1.refs_0_), channel_id=1, source_target_pairs={{0,8},{1,9},{2,10},{3,11},{4,12},{5,13},{6,14},{7,15},{8,0},{9,1},... | collective-permute-start | bytes 98312 | tf_op jit(solution)/shard_map/ppermute | solution.py:383
  59.6 2.7 %collective-permute-start.28 = (f32[64,128]{1,0:T(8,128)S(1)}, f32[64,128]{1,0:T(8,128)S(1)}, u32[]{:S(2)}, u32[]{:S(2)}) collective-permute-start(f32[64,128]{1,0:T(8,128)S(1)} %add_parts.1.refs_0_), channel_id=1, source_target_pairs={{0,12},{1,13},{2,14},{3,15},{4,8},{5,9},{6,10},{7,11},{8,4},{9,5},... | collective-permute-start | bytes 98312 | tf_op jit(solution)/shard_map/ppermute | solution.py:383
  62.2 2.1 %backward_sum.1 = (f32[256,128]{1,0:T(8,128)S(1)}, f32[256,128]{1,0:T(8,128)S(1)}, f32[256,128]{1,0:T(8,128)S(1)}, f32[256,128]{1,0:T(8,128)S(1)}) custom-call(s32[1]{0:T(128)} %bitcast.me_ref, bf16[1024,2048]{1,0:T(8,128)(2,1)S(1)} %backward_block.1.block_ref, f32[256,128]{1,0:T(8,128)S(1)} %get-tuple-element.88.refs_0_.sent_ref, ...), custom_call_target="tpu_custom_call" | custom-call | flops 1073741824 | bytes 4194304 | tf_op jit(solution)/shard_map/backward_sum/pallas_call | solution.py:562
  66.4 1.5 %collective-permute-start.31 = (f32[256,128]{1,0:T(8,128)S(1)}, f32[256,128]{1,0:T(8,128)S(1)}, u32[]{:S(2)}, u32[]{:S(2)}) collective-permute-start(f32[256,128]{1,0:T(8,128)S(1)} %get-tuple-element.100), channel_id=1, source_target_pairs={{0,18},{1,19},{2,16},{3,17},{4,22},{5,23},{6,20},{7,21},{8,26},{9,... | collective-permute-start | bytes 393224 | tf_op jit(solution)/shard_map/ppermute | solution.py:404
  71.2 2.0 %collective-permute-done.33.refs_5_ = f32[64,128]{1,0:T(8,128)S(1)} collective-permute-done((f32[64,128]{1,0:T(8,128)S(1)}, f32[64,128]{1,0:T(8,128)S(1)}, u32[]{:S(2)}, u32[]{:S(2)}) %collective-permute-start.33) | collective-permute-done | bytes 32800 | tf_op jit(solution)/shard_map/ppermute | solution.py:404
  74.5 3.4 %collective-permute-done.35.refs_7_ = f32[64,128]{1,0:T(8,128)S(1)} collective-permute-done((f32[64,128]{1,0:T(8,128)S(1)}, f32[64,128]{1,0:T(8,128)S(1)}, u32[]{:S(2)}, u32[]{:S(2)}) %collective-permute-start.35) | collective-permute-done | bytes 32800 | tf_op jit(solution)/shard_map/ppermute | solution.py:404
  (75 shorter events, 18.2 us)
Async XLA Ops:
  0.6 14.0 %collective-permute-start = (f32[256,128]{1,0:T(8,128)}, f32[256,128]{1,0:T(8,128)S(1)}, u32[]{:S(2)}, u32[]{:S(2)}) collective-permute-start(f32[256,128]{1,0:T(8,128)} %features_ref.1), channel_id=1, source_target_pairs={{0,4},{1,5},{2,6},{3,7},{4,0},{5,1},{6,2},{7,3},{8,12},{9,13},{10,... | collective-permute-start | bytes 393224 | tf_op jit(solution)/shard_map/ppermute | solution.py:438
  3.7 10.9 %collective-permute-start.1 = (f32[256,128]{1,0:T(8,128)}, f32[256,128]{1,0:T(8,128)S(1)}, u32[]{:S(2)}, u32[]{:S(2)}) collective-permute-start(f32[256,128]{1,0:T(8,128)} %features_ref.1), channel_id=1, source_target_pairs={{0,8},{1,9},{2,10},{3,11},{4,12},{5,13},{6,14},{7,15},{8,0},{9,1},... | collective-permute-start | bytes 393224 | tf_op jit(solution)/shard_map/ppermute | solution.py:438
  8.7 6.0 %collective-permute-start.2 = (s32[8,896]{1,0:T(8,128)}, s32[8,896]{1,0:T(8,128)S(1)}, u32[]{:S(2)}, u32[]{:S(2)}) collective-permute-start(s32[8,896]{1,0:T(8,128)} %get-tuple-element.61), channel_id=1, source_target_pairs={{0,4},{1,5},{2,6},{3,7},{4,0},{5,1},{6,2},{7,3},{8,12},{9,13},{10,... | collective-permute-start | bytes 86024 | tf_op jit(solution)/shard_map/ppermute | solution.py:383
  9.2 5.5 %collective-permute-start.3 = (s32[8,896]{1,0:T(8,128)}, s32[8,896]{1,0:T(8,128)S(1)}, u32[]{:S(2)}, u32[]{:S(2)}) collective-permute-start(s32[8,896]{1,0:T(8,128)} %get-tuple-element.62), channel_id=1, source_target_pairs={{0,8},{1,9},{2,10},{3,11},{4,12},{5,13},{6,14},{7,15},{8,0},{9,1},... | collective-permute-start | bytes 86024 | tf_op jit(solution)/shard_map/ppermute | solution.py:383
  9.2 6.3 %collective-permute-start.4 = (s32[8,896]{1,0:T(8,128)}, s32[8,896]{1,0:T(8,128)S(1)}, u32[]{:S(2)}, u32[]{:S(2)}) collective-permute-start(s32[8,896]{1,0:T(8,128)} %get-tuple-element.63), channel_id=1, source_target_pairs={{0,12},{1,13},{2,14},{3,15},{4,8},{5,9},{6,10},{7,11},{8,4},{9,5},... | collective-permute-start | bytes 86024 | tf_op jit(solution)/shard_map/ppermute | solution.py:383
  15.6 13.2 %collective-permute-start.8 = (f32[256,128]{1,0:T(8,128)S(1)}, f32[256,128]{1,0:T(8,128)S(1)}, u32[]{:S(2)}, u32[]{:S(2)}) collective-permute-start(f32[256,128]{1,0:T(8,128)S(1)} %copy-done), channel_id=1, source_target_pairs={{0,12},{1,13},{2,14},{3,15},{4,8},{5,9},{6,10},{7,11},{8,4},{9,5},... | collective-permute-start | bytes 393224 | tf_op jit(solution)/shard_map/ppermute | solution.py:449
  19.2 5.8 %collective-permute-start.6 = (s32[64,384]{1,0:T(8,128)S(1)}, s32[64,384]{1,0:T(8,128)S(1)}, u32[]{:S(2)}, u32[]{:S(2)}) collective-permute-start(s32[64,384]{1,0:T(8,128)S(1)} %get-tuple-element.68.refs_0_), channel_id=1, source_target_pairs={{16,0},{17,1},{18,2},{19,3},{20,4},{21,5},{22,6},{23,7},{24,8},{25... | collective-permute-start | bytes 294920 | tf_op jit(solution)/shard_map/ppermute | solution.py:436
  22.3 7.1 %collective-permute-start.9 = (f32[256,128]{1,0:T(8,128)S(1)}, f32[256,128]{1,0:T(8,128)S(1)}, u32[]{:S(2)}, u32[]{:S(2)}) collective-permute-start(f32[256,128]{1,0:T(8,128)S(1)} %copy-done), channel_id=1, source_target_pairs={{0,1},{1,0},{2,3},{3,2},{4,5},{5,4},{6,7},{7,6},{8,9},{9,8},{10,11... | collective-permute-start | bytes 393224 | tf_op jit(solution)/shard_map/ppermute | solution.py:388
  22.3 7.1 %collective-permute-start.10 = (f32[256,128]{1,0:T(8,128)S(1)}, f32[256,128]{1,0:T(8,128)S(1)}, u32[]{:S(2)}, u32[]{:S(2)}) collective-permute-start(f32[256,128]{1,0:T(8,128)S(1)} %collective-permute-done.refs_2_), channel_id=1, source_target_pairs={{0,1},{1,0},{2,3},{3,2},{4,5},{5,4},{6,7},{7,6},{8,9},{9,8},{10,11... | collective-permute-start | bytes 393224 | tf_op jit(solution)/shard_map/ppermute | solution.py:388
  32.7 8.0 %collective-permute-start.15 = (f32[256,128]{1,0:T(8,128)S(1)}, f32[256,128]{1,0:T(8,128)S(1)}, u32[]{:S(2)}, u32[]{:S(2)}) collective-permute-start(f32[256,128]{1,0:T(8,128)S(1)} %get-tuple-element.83), channel_id=1, source_target_pairs={{0,18},{1,19},{2,16},{3,17},{4,22},{5,23},{6,20},{7,21},{8,26},{9,... | collective-permute-start | bytes 393224 | tf_op jit(solution)/shard_map/ppermute | solution.py:404
  34.2 8.1 %collective-permute-start.13 = (f32[256,128]{1,0:T(8,128)S(1)}, f32[256,128]{1,0:T(8,128)S(1)}, u32[]{:S(2)}, u32[]{:S(2)}) collective-permute-start(f32[256,128]{1,0:T(8,128)S(1)} %get-tuple-element.81), channel_id=1, source_target_pairs={{0,16},{1,17},{2,18},{3,19},{4,20},{5,21},{6,22},{7,23},{8,24},{9,... | collective-permute-start | bytes 393224 | tf_op jit(solution)/shard_map/ppermute | solution.py:404
  35.7 6.6 %collective-permute-start.14 = (f32[256,128]{1,0:T(8,128)S(1)}, f32[256,128]{1,0:T(8,128)S(1)}, u32[]{:S(2)}, u32[]{:S(2)}) collective-permute-start(f32[256,128]{1,0:T(8,128)S(1)} %get-tuple-element.82), channel_id=1, source_target_pairs={{0,2},{1,3},{2,0},{3,1},{4,6},{5,7},{6,4},{7,5},{8,10},{9,11},{10,... | collective-permute-start | bytes 393224 | tf_op jit(solution)/shard_map/ppermute | solution.py:404
  44.0 13.1 %collective-permute-start.21 = (f32[256,128]{1,0:T(8,128)S(1)}, f32[256,128]{1,0:T(8,128)S(1)}, u32[]{:S(2)}, u32[]{:S(2)}) collective-permute-start(f32[256,128]{1,0:T(8,128)S(1)} %get-tuple-element.88.refs_0_.sent_ref), channel_id=1, source_target_pairs={{0,12},{1,13},{2,14},{3,15},{4,8},{5,9},{6,10},{7,11},{8,4},{9,5},... | collective-permute-start | bytes 393224 | tf_op jit(solution)/shard_map/ppermute | solution.py:383
  45.2 12.0 %collective-permute-start.17 = (f32[256,128]{1,0:T(8,128)S(1)}, f32[256,128]{1,0:T(8,128)S(1)}, u32[]{:S(2)}, u32[]{:S(2)}) collective-permute-start(f32[256,128]{1,0:T(8,128)S(1)} %get-tuple-element.88.refs_0_.sent_ref), channel_id=1, source_target_pairs={{0,4},{1,5},{2,6},{3,7},{4,0},{5,1},{6,2},{7,3},{8,12},{9,13},{10,... | collective-permute-start | bytes 393224 | tf_op jit(solution)/shard_map/ppermute | solution.py:383
  45.2 12.1 %collective-permute-start.19 = (f32[256,128]{1,0:T(8,128)S(1)}, f32[256,128]{1,0:T(8,128)S(1)}, u32[]{:S(2)}, u32[]{:S(2)}) collective-permute-start(f32[256,128]{1,0:T(8,128)S(1)} %get-tuple-element.88.refs_0_.sent_ref), channel_id=1, source_target_pairs={{0,8},{1,9},{2,10},{3,11},{4,12},{5,13},{6,14},{7,15},{8,0},{9,1},... | collective-permute-start | bytes 393224 | tf_op jit(solution)/shard_map/ppermute | solution.py:383
  52.3 4.8 %collective-permute-start.24 = (f32[64,128]{1,0:T(8,128)S(1)}, f32[64,128]{1,0:T(8,128)S(1)}, u32[]{:S(2)}, u32[]{:S(2)}) collective-permute-start(f32[64,128]{1,0:T(8,128)S(1)} %get-tuple-element.93), channel_id=1, source_target_pairs={{0,18},{1,19},{2,16},{3,17},{4,22},{5,23},{6,20},{7,21},{8,26},{9,... | collective-permute-start | bytes 98312 | tf_op jit(solution)/shard_map/ppermute | solution.py:404
  57.2 5.0 %collective-permute-start.20 = (f32[256,128]{1,0:T(8,128)S(1)}, f32[256,128]{1,0:T(8,128)S(1)}, u32[]{:S(2)}, u32[]{:S(2)}) collective-permute-start(f32[256,128]{1,0:T(8,128)S(1)} %collective-permute-done.19.refs_4_), channel_id=1, source_target_pairs={{0,1},{1,0},{2,3},{3,2},{4,5},{5,4},{6,7},{7,6},{8,9},{9,8},{10,11... | collective-permute-start | bytes 393224 | tf_op jit(solution)/shard_map/ppermute | solution.py:388
  57.8 8.6 %collective-permute-start.26 = (f32[64,128]{1,0:T(8,128)S(1)}, f32[64,128]{1,0:T(8,128)S(1)}, u32[]{:S(2)}, u32[]{:S(2)}) collective-permute-start(f32[64,128]{1,0:T(8,128)S(1)} %add_parts.1.refs_0_), channel_id=1, source_target_pairs={{0,4},{1,5},{2,6},{3,7},{4,0},{5,1},{6,2},{7,3},{8,12},{9,13},{10,... | collective-permute-start | bytes 98312 | tf_op jit(solution)/shard_map/ppermute | solution.py:383
  57.8 10.1 %collective-permute-start.27 = (f32[64,128]{1,0:T(8,128)S(1)}, f32[64,128]{1,0:T(8,128)S(1)}, u32[]{:S(2)}, u32[]{:S(2)}) collective-permute-start(f32[64,128]{1,0:T(8,128)S(1)} %add_parts.1.refs_0_), channel_id=1, source_target_pairs={{0,8},{1,9},{2,10},{3,11},{4,12},{5,13},{6,14},{7,15},{8,0},{9,1},... | collective-permute-start | bytes 98312 | tf_op jit(solution)/shard_map/ppermute | solution.py:383
  59.6 8.4 %collective-permute-start.28 = (f32[64,128]{1,0:T(8,128)S(1)}, f32[64,128]{1,0:T(8,128)S(1)}, u32[]{:S(2)}, u32[]{:S(2)}) collective-permute-start(f32[64,128]{1,0:T(8,128)S(1)} %add_parts.1.refs_0_), channel_id=1, source_target_pairs={{0,12},{1,13},{2,14},{3,15},{4,8},{5,9},{6,10},{7,11},{8,4},{9,5},... | collective-permute-start | bytes 98312 | tf_op jit(solution)/shard_map/ppermute | solution.py:383
  64.3 13.6 %collective-permute-start.29 = (f32[256,128]{1,0:T(8,128)S(1)}, f32[256,128]{1,0:T(8,128)S(1)}, u32[]{:S(2)}, u32[]{:S(2)}) collective-permute-start(f32[256,128]{1,0:T(8,128)S(1)} %get-tuple-element.98), channel_id=1, source_target_pairs={{0,16},{1,17},{2,18},{3,19},{4,20},{5,21},{6,22},{7,23},{8,24},{9,... | collective-permute-start | bytes 393224 | tf_op jit(solution)/shard_map/ppermute | solution.py:404
  64.9 13.0 %collective-permute-start.30 = (f32[256,128]{1,0:T(8,128)S(1)}, f32[256,128]{1,0:T(8,128)S(1)}, u32[]{:S(2)}, u32[]{:S(2)}) collective-permute-start(f32[256,128]{1,0:T(8,128)S(1)} %get-tuple-element.99), channel_id=1, source_target_pairs={{0,2},{1,3},{2,0},{3,1},{4,6},{5,7},{6,4},{7,5},{8,10},{9,11},{10,... | collective-permute-start | bytes 393224 | tf_op jit(solution)/shard_map/ppermute | solution.py:404
  66.4 11.6 %collective-permute-start.31 = (f32[256,128]{1,0:T(8,128)S(1)}, f32[256,128]{1,0:T(8,128)S(1)}, u32[]{:S(2)}, u32[]{:S(2)}) collective-permute-start(f32[256,128]{1,0:T(8,128)S(1)} %get-tuple-element.100), channel_id=1, source_target_pairs={{0,18},{1,19},{2,16},{3,17},{4,22},{5,23},{6,20},{7,21},{8,26},{9,... | collective-permute-start | bytes 393224 | tf_op jit(solution)/shard_map/ppermute | solution.py:404
  73.1 4.8 %collective-permute-start.35 = (f32[64,128]{1,0:T(8,128)S(1)}, f32[64,128]{1,0:T(8,128)S(1)}, u32[]{:S(2)}, u32[]{:S(2)}) collective-permute-start(f32[64,128]{1,0:T(8,128)S(1)} %add_cores.1.refs_4_), channel_id=1, source_target_pairs={{0,18},{1,19},{2,16},{3,17},{4,22},{5,23},{6,20},{7,21},{8,26},{9,... | collective-permute-start | bytes 98312 | tf_op jit(solution)/shard_map/ppermute | solution.py:404
  (19 other events, 107.9 us)

commit v12 on v10

--- a/solution.py
+++ b/solution.py
@@ -497,7 +497,6 @@
         cost_estimate=pl.CostEstimate(flops=2**16, bytes_accessed=2**16, transcendentals=0),
         name="forward_block",
     )(me, *chips, *peer_lists)
-    along[-1], forward_block = lax.optimization_barrier((along[-1], forward_block))
     gathered = to_cores(along)
     scale, *sums = pl.pallas_call(
         functools.partial(forward_sum_kernel, grid),

time: 79.1 us -> 80.4 us (1.016)
  starting transfers between devices: 41.3 us -> 45.5 us
  waiting for transfers between devices: 17.6 us -> 14.6 us
    ppermute x12, waiting for transfers between devices: 12.3 us -> 6.52 us  [to_owners(): lax.ppermute(part, both_axes, grid.pairs(lambda x, y, z, c, dx=dx, dy=dy:...]
    ppermute x12, starting transfers between devices: 13.8 us -> 18.1 us  [to_owners(): lax.ppermute(part, both_axes, grid.pairs(lambda x, y, z, c, dx=dx, dy=dy:...]
    ppermute x4, waiting for transfers between devices: 3.43 us -> 7.28 us  [from_peer(): return lax.ppermute(value, both_axes, [(b, a) for a, b in grid.pairs(move)])]
    ppermute x8, waiting for transfers between devices: 0.99 us -> 0.02 us  [to_cores(): lax.ppermute(block, both_axes, grid.pairs(lambda x, y, z, c: (x, y, z, c...]
where the time goes in v12:
time: 80.4 us; the launch traced here: 80.1 us
  starting transfers between devices  45.5 us (57%)
  Pallas kernels  17.5 us (22%)
  waiting for transfers between devices  14.6 us (18%)
  local copies, waits for them, and re-layouts  1.57 us (2%)
  between operations  0.92 us (1%)
    ppermute x12, starting transfers between devices, to_owners(): lax.ppermute(part, both_axes, grid.pairs(lambda x, y, z, c, dx=dx, dy=dy:...  18.1 us
    ppermute x9, starting transfers between devices, along_z(): lax.ppermute(blocks[dz], both_axes, toward(dz))  13.2 us
    ppermute x4, waiting for transfers between devices, from_peer(): return lax.ppermute(value, both_axes, [(b, a) for a, b in grid.pairs(move)])  7.28 us
    ppermute x12, waiting for transfers between devices, to_owners(): lax.ppermute(part, both_axes, grid.pairs(lambda x, y, z, c, dx=dx, dy=dy:...  6.52 us
    ppermute x2, starting transfers between devices, shards(): lax.ppermute(features, both_axes, toward(dz))  5.68 us
    pallas_call x1, Pallas kernels, shards(): pl.pallas_call(functools.partial(backward_block_kernel, grid, slots), gri...  4.44 us
    pallas_call x1, Pallas kernels, shards(): pl.pallas_call(functools.partial(forward_block_kernel, grid, slots), grid...  3.77 us
    ppermute x1, starting transfers between devices, shards(): lax.ppermute(later, both_axes, toward(dz))  3.63 us
  transfers between devices with their start and end apart: 36, of which 9 were waited for; matrix products, arithmetic and copies ran while one was open for 0% of the time, Pallas kernels for 16%

profile of v12, /device:TPU:0, one launch (start us, length us, event | category | flops | bytes accessed | tf_op | source)
XLA Modules:
  0.0 80.1 jit_solution(6159598139934063930)
XLA Ops:
  0.6 3.1 %collective-permute-start = (f32[256,128]{1,0:T(8,128)}, f32[256,128]{1,0:T(8,128)S(1)}, u32[]{:S(2)}, u32[]{:S(2)}) collective-permute-start(f32[256,128]{1,0:T(8,128)} %features_ref.1), channel_id=1, source_target_pairs={{0,4},{1,5},{2,6},{3,7},{4,0},{5,1},{6,2},{7,3},{8,12},{9,13},{10,... | collective-permute-start | bytes 393224 | tf_op jit(solution)/shard_map/ppermute | solution.py:432
  3.7 2.6 %collective-permute-start.1 = (f32[256,128]{1,0:T(8,128)}, f32[256,128]{1,0:T(8,128)S(1)}, u32[]{:S(2)}, u32[]{:S(2)}) collective-permute-start(f32[256,128]{1,0:T(8,128)} %features_ref.1), channel_id=1, source_target_pairs={{0,8},{1,9},{2,10},{3,11},{4,12},{5,13},{6,14},{7,15},{8,0},{9,1},... | collective-permute-start | bytes 393224 | tf_op jit(solution)/shard_map/ppermute | solution.py:432
  6.3 2.3 %pack.1 = (s32[32,384]{1,0:T(8,128)}, s32[8,896]{1,0:T(8,128)}, s32[8,896]{1,0:T(8,128)}, s32[8,896]{1,0:T(8,128)}, s32[8,896]{1,0:T(8,128)}) custom-call(s32[1]{0:T(128)} %bitcast.me_ref, s32[4,32]{1,0:T(4,128)} %bitcast.13, s32[4,32]{1,0:T(4,128)} %bitcast.14, s32[32,256]{1,0:T(8,128)} %bitcast.11, s32[32,256]{1,0:T(8,128)} %bitcast.12), custom_call_target="tpu_custom_call" | custom-call | flops 2147483648 | bytes 8388608 | tf_op jit(solution)/shard_map/pack/pallas_call | solution.py:416
  9.2 3.9 %collective-permute-start.4 = (s32[8,896]{1,0:T(8,128)}, s32[8,896]{1,0:T(8,128)S(1)}, u32[]{:S(2)}, u32[]{:S(2)}) collective-permute-start(s32[8,896]{1,0:T(8,128)} %get-tuple-element.61), channel_id=1, source_target_pairs={{0,12},{1,13},{2,14},{3,15},{4,8},{5,9},{6,10},{7,11},{8,4},{9,5},... | collective-permute-start | bytes 86024 | tf_op jit(solution)/shard_map/ppermute | solution.py:377
  15.5 3.6 %collective-permute-start.11 = (f32[256,128]{1,0:T(8,128)S(1)}, f32[256,128]{1,0:T(8,128)S(1)}, u32[]{:S(2)}, u32[]{:S(2)}) collective-permute-start(f32[256,128]{1,0:T(8,128)S(1)} %copy-done), channel_id=1, source_target_pairs={{0,12},{1,13},{2,14},{3,15},{4,8},{5,9},{6,10},{7,11},{8,4},{9,5},... | collective-permute-start | bytes 393224 | tf_op jit(solution)/shard_map/ppermute | solution.py:443
  20.5 1.6 %collective-permute-start.7 = (s32[32,512]{1,0:T(8,128)S(1)}, s32[32,512]{1,0:T(8,128)S(1)}, u32[]{:S(2)}, u32[]{:S(2)}) collective-permute-start(s32[32,512]{1,0:T(8,128)S(1)} %get-tuple-element.80.refs_2_.refs_0_), channel_id=1, source_target_pairs={{2,0},{3,1},{0,2},{1,3},{6,4},{7,5},{4,6},{5,7},{10,8},{11,9},{8,1... | collective-permute-start | bytes 196616 | tf_op jit(solution)/shard_map/ppermute | solution.py:430
  23.1 1.7 %collective-permute-done.7.refs_3_.refs_1_ = s32[32,512]{1,0:T(8,128)S(1)} collective-permute-done((s32[32,512]{1,0:T(8,128)S(1)}, s32[32,512]{1,0:T(8,128)S(1)}, u32[]{:S(2)}, u32[]{:S(2)}) %collective-permute-start.7) | collective-permute-done | bytes 65568 | tf_op jit(solution)/shard_map/ppermute | solution.py:430
  26.3 3.1 %collective-permute-done.6.refs_1_ = s32[64,384]{1,0:T(8,128)S(1)} collective-permute-done((s32[64,384]{1,0:T(8,128)S(1)}, s32[64,384]{1,0:T(8,128)S(1)}, u32[]{:S(2)}, u32[]{:S(2)}) %collective-permute-start.6) | collective-permute-done | bytes 98336 | tf_op jit(solution)/shard_map/ppermute | solution.py:430
  29.4 3.8 %forward_block.1 = (bf16[1024,2048]{1,0:T(8,128)(2,1)S(1)}, f32[32,128]{1,0:T(8,128)S(1)}) custom-call(s32[1]{0:T(128)} %bitcast.me_ref, s32[64,384]{1,0:T(8,128)S(1)} %get-tuple-element.66.refs_0_, s32[64,384]{1,0:T(8,128)S(1)} %collective-permute-done.6.refs_1_, s32[32,512]{1,0:T(8,128)S(1)} %get-tuple-element.80.refs_2_.refs_0_, ...), custom_call_target="tpu_custom_call" | custom-call | flops 65536 | bytes 65536 | tf_op jit(solution)/shard_map/forward_block/pallas_call | solution.py:484
  33.3 2.3 %forward_sum.1 = (f32[256,128]{1,0:T(8,128)S(1)}, f32[256,128]{1,0:T(8,128)S(1)}, f32[256,128]{1,0:T(8,128)S(1)}, f32[256,128]{1,0:T(8,128)S(1)}, f32[256,128]{1,0:T(8,128)S(1)}) custom-call(s32[1]{0:T(128)} %bitcast.me_ref, f32[32,128]{1,0:T(8,128)S(1)} %get-tuple-element.68.root_ref, bf16[1024,2048]{1,0:T(8,128)(2,1)S(1)} %get-tuple-element.69.block_ref, ...), custom_call_target="tpu_custom_call" | custom-call | flops 1073741824 | bytes 4194304 | tf_op jit(solution)/shard_map/forward_sum/pallas_call | solution.py:501
  35.6 2.5 %collective-permute-start.15 = (f32[256,128]{1,0:T(8,128)S(1)}, f32[256,128]{1,0:T(8,128)S(1)}, u32[]{:S(2)}, u32[]{:S(2)}) collective-permute-start(f32[256,128]{1,0:T(8,128)S(1)} %get-tuple-element.79), channel_id=1, source_target_pairs={{0,18},{1,19},{2,16},{3,17},{4,22},{5,23},{6,20},{7,21},{8,26},{9,... | collective-permute-start | bytes 393224 | tf_op jit(solution)/shard_map/ppermute | solution.py:398
  39.2 4.4 %backward_block.1.block_ref = bf16[1024,2048]{1,0:T(8,128)(2,1)S(1)} custom-call(s32[1]{0:T(128)} %bitcast.me_ref, s32[32,512]{1,0:T(8,128)S(1)} %get-tuple-element.80.refs_2_.refs_0_, s32[32,512]{1,0:T(8,128)S(1)} %collective-permute-done.7.refs_3_.refs_1_), custom_call_target="tpu_custom_call" | custom-call | flops 1073741824 | bytes 4194304 | tf_op jit(solution)/shard_map/backward_block/pallas_call | solution.py:514
  43.7 1.7 %middle.1 = (f32[256,256]{1,0:T(8,128)}, f32[256,128]{1,0:T(8,128)S(1)}, f32[64,128]{1,0:T(8,128)S(1)}, f32[64,128]{1,0:T(8,128)S(1)}, f32[64,128]{1,0:T(8,128)S(1)}, /*index=5*/f32[64,128]{1,0:T(8,128)S(1)}) custom-call(s32[1]{0:T(128)} %bitcast.me_ref, f32[256,128]{1,0:T(8,128)S(1)} %get-tuple-element.74.scale_ref, f32[256,128]{1,0:T(8,128)S(1)} %copy-done, ...), custom_call_target="tpu_custom_call" | custom-call | flops 301989888 | bytes 1048576 | tf_op jit(solution)/shard_map/middle/pallas_call | solution.py:528
  45.4 2.6 %collective-permute-start.21 = (f32[256,128]{1,0:T(8,128)S(1)}, f32[256,128]{1,0:T(8,128)S(1)}, u32[]{:S(2)}, u32[]{:S(2)}) collective-permute-start(f32[256,128]{1,0:T(8,128)S(1)} %get-tuple-element.84.refs_0_.sent_ref), channel_id=1, source_target_pairs={{0,12},{1,13},{2,14},{3,15},{4,8},{5,9},{6,10},{7,11},{8,4},{9,5},... | collective-permute-start | bytes 393224 | tf_op jit(solution)/shard_map/ppermute | solution.py:377
  48.0 1.8 %collective-permute-start.19 = (f32[256,128]{1,0:T(8,128)S(1)}, f32[256,128]{1,0:T(8,128)S(1)}, u32[]{:S(2)}, u32[]{:S(2)}) collective-permute-start(f32[256,128]{1,0:T(8,128)S(1)} %get-tuple-element.84.refs_0_.sent_ref), channel_id=1, source_target_pairs={{0,8},{1,9},{2,10},{3,11},{4,12},{5,13},{6,14},{7,15},{8,0},{9,1},... | collective-permute-start | bytes 393224 | tf_op jit(solution)/shard_map/ppermute | solution.py:377
  51.2 1.5 %collective-permute-start.23 = (f32[64,128]{1,0:T(8,128)S(1)}, f32[64,128]{1,0:T(8,128)S(1)}, u32[]{:S(2)}, u32[]{:S(2)}) collective-permute-start(f32[64,128]{1,0:T(8,128)S(1)} %get-tuple-element.88), channel_id=1, source_target_pairs={{0,2},{1,3},{2,0},{3,1},{4,6},{5,7},{6,4},{7,5},{8,10},{9,11},{10,... | collective-permute-start | bytes 98312 | tf_op jit(solution)/shard_map/ppermute | solution.py:398
  53.7 2.5 %collective-permute-start.24 = (f32[64,128]{1,0:T(8,128)S(1)}, f32[64,128]{1,0:T(8,128)S(1)}, u32[]{:S(2)}, u32[]{:S(2)}) collective-permute-start(f32[64,128]{1,0:T(8,128)S(1)} %get-tuple-element.89), channel_id=1, source_target_pairs={{0,18},{1,19},{2,16},{3,17},{4,22},{5,23},{6,20},{7,21},{8,26},{9,... | collective-permute-start | bytes 98312 | tf_op jit(solution)/shard_map/ppermute | solution.py:398
  56.1 2.4 %collective-permute-done.24.refs_3_ = f32[64,128]{1,0:T(8,128)S(1)} collective-permute-done((f32[64,128]{1,0:T(8,128)S(1)}, f32[64,128]{1,0:T(8,128)S(1)}, u32[]{:S(2)}, u32[]{:S(2)}) %collective-permute-start.24) | collective-permute-done | bytes 32800 | tf_op jit(solution)/shard_map/ppermute | solution.py:398
  59.4 2.9 %collective-permute-start.27 = (f32[64,128]{1,0:T(8,128)S(1)}, f32[64,128]{1,0:T(8,128)S(1)}, u32[]{:S(2)}, u32[]{:S(2)}) collective-permute-start(f32[64,128]{1,0:T(8,128)S(1)} %add_parts.1.refs_0_), channel_id=1, source_target_pairs={{0,8},{1,9},{2,10},{3,11},{4,12},{5,13},{6,14},{7,15},{8,0},{9,1},... | collective-permute-start | bytes 98312 | tf_op jit(solution)/shard_map/ppermute | solution.py:377
  63.6 2.1 %backward_sum.1 = (f32[256,128]{1,0:T(8,128)S(1)}, f32[256,128]{1,0:T(8,128)S(1)}, f32[256,128]{1,0:T(8,128)S(1)}, f32[256,128]{1,0:T(8,128)S(1)}) custom-call(s32[1]{0:T(128)} %bitcast.me_ref, bf16[1024,2048]{1,0:T(8,128)(2,1)S(1)} %backward_block.1.block_ref, f32[256,128]{1,0:T(8,128)S(1)} %get-tuple-element.84.refs_0_.sent_ref, ...), custom_call_target="tpu_custom_call" | custom-call | flops 1073741824 | bytes 4194304 | tf_op jit(solution)/shard_map/backward_sum/pallas_call | solution.py:555
  65.7 1.6 %collective-permute-start.29 = (f32[256,128]{1,0:T(8,128)S(1)}, f32[256,128]{1,0:T(8,128)S(1)}, u32[]{:S(2)}, u32[]{:S(2)}) collective-permute-start(f32[256,128]{1,0:T(8,128)S(1)} %get-tuple-element.94), channel_id=1, source_target_pairs={{0,16},{1,17},{2,18},{3,19},{4,20},{5,21},{6,22},{7,23},{8,24},{9,... | collective-permute-start | bytes 393224 | tf_op jit(solution)/shard_map/ppermute | solution.py:398
  67.3 1.5 %collective-permute-start.30 = (f32[256,128]{1,0:T(8,128)S(1)}, f32[256,128]{1,0:T(8,128)S(1)}, u32[]{:S(2)}, u32[]{:S(2)}) collective-permute-start(f32[256,128]{1,0:T(8,128)S(1)} %get-tuple-element.95), channel_id=1, source_target_pairs={{0,2},{1,3},{2,0},{3,1},{4,6},{5,7},{6,4},{7,5},{8,10},{9,11},{10,... | collective-permute-start | bytes 393224 | tf_op jit(solution)/shard_map/ppermute | solution.py:398
  74.5 2.5 %collective-permute-start.35 = (f32[64,128]{1,0:T(8,128)S(1)}, f32[64,128]{1,0:T(8,128)S(1)}, u32[]{:S(2)}, u32[]{:S(2)}) collective-permute-start(f32[64,128]{1,0:T(8,128)S(1)} %add_cores.1.refs_4_), channel_id=1, source_target_pairs={{0,18},{1,19},{2,16},{3,17},{4,22},{5,23},{6,20},{7,21},{8,26},{9,... | collective-permute-start | bytes 98312 | tf_op jit(solution)/shard_map/ppermute | solution.py:398
  77.0 2.4 %collective-permute-done.35.refs_7_ = f32[64,128]{1,0:T(8,128)S(1)} collective-permute-done((f32[64,128]{1,0:T(8,128)S(1)}, f32[64,128]{1,0:T(8,128)S(1)}, u32[]{:S(2)}, u32[]{:S(2)}) %collective-permute-start.35) | collective-permute-done | bytes 32800 | tf_op jit(solution)/shard_map/ppermute | solution.py:398
  (75 shorter events, 18.8 us)
Async XLA Ops:
  0.6 14.0 %collective-permute-start = (f32[256,128]{1,0:T(8,128)}, f32[256,128]{1,0:T(8,128)S(1)}, u32[]{:S(2)}, u32[]{:S(2)}) collective-permute-start(f32[256,128]{1,0:T(8,128)} %features_ref.1), channel_id=1, source_target_pairs={{0,4},{1,5},{2,6},{3,7},{4,0},{5,1},{6,2},{7,3},{8,12},{9,13},{10,... | collective-permute-start | bytes 393224 | tf_op jit(solution)/shard_map/ppermute | solution.py:432
  3.7 10.9 %collective-permute-start.1 = (f32[256,128]{1,0:T(8,128)}, f32[256,128]{1,0:T(8,128)S(1)}, u32[]{:S(2)}, u32[]{:S(2)}) collective-permute-start(f32[256,128]{1,0:T(8,128)} %features_ref.1), channel_id=1, source_target_pairs={{0,8},{1,9},{2,10},{3,11},{4,12},{5,13},{6,14},{7,15},{8,0},{9,1},... | collective-permute-start | bytes 393224 | tf_op jit(solution)/shard_map/ppermute | solution.py:432
  8.7 6.0 %collective-permute-start.2 = (s32[8,896]{1,0:T(8,128)}, s32[8,896]{1,0:T(8,128)S(1)}, u32[]{:S(2)}, u32[]{:S(2)}) collective-permute-start(s32[8,896]{1,0:T(8,128)} %get-tuple-element.59), channel_id=1, source_target_pairs={{0,4},{1,5},{2,6},{3,7},{4,0},{5,1},{6,2},{7,3},{8,12},{9,13},{10,... | collective-permute-start | bytes 86024 | tf_op jit(solution)/shard_map/ppermute | solution.py:377
  9.2 5.5 %collective-permute-start.3 = (s32[8,896]{1,0:T(8,128)}, s32[8,896]{1,0:T(8,128)S(1)}, u32[]{:S(2)}, u32[]{:S(2)}) collective-permute-start(s32[8,896]{1,0:T(8,128)} %get-tuple-element.60), channel_id=1, source_target_pairs={{0,8},{1,9},{2,10},{3,11},{4,12},{5,13},{6,14},{7,15},{8,0},{9,1},... | collective-permute-start | bytes 86024 | tf_op jit(solution)/shard_map/ppermute | solution.py:377
  9.2 6.3 %collective-permute-start.4 = (s32[8,896]{1,0:T(8,128)}, s32[8,896]{1,0:T(8,128)S(1)}, u32[]{:S(2)}, u32[]{:S(2)}) collective-permute-start(s32[8,896]{1,0:T(8,128)} %get-tuple-element.61), channel_id=1, source_target_pairs={{0,12},{1,13},{2,14},{3,15},{4,8},{5,9},{6,10},{7,11},{8,4},{9,5},... | collective-permute-start | bytes 86024 | tf_op jit(solution)/shard_map/ppermute | solution.py:377
  15.5 7.1 %collective-permute-start.11 = (f32[256,128]{1,0:T(8,128)S(1)}, f32[256,128]{1,0:T(8,128)S(1)}, u32[]{:S(2)}, u32[]{:S(2)}) collective-permute-start(f32[256,128]{1,0:T(8,128)S(1)} %copy-done), channel_id=1, source_target_pairs={{0,12},{1,13},{2,14},{3,15},{4,8},{5,9},{6,10},{7,11},{8,4},{9,5},... | collective-permute-start | bytes 393224 | tf_op jit(solution)/shard_map/ppermute | solution.py:443
  22.0 11.1 %collective-permute-start.8 = (f32[256,128]{1,0:T(8,128)S(1)}, f32[256,128]{1,0:T(8,128)S(1)}, u32[]{:S(2)}, u32[]{:S(2)}) collective-permute-start(f32[256,128]{1,0:T(8,128)S(1)} %copy-done), channel_id=1, source_target_pairs={{0,1},{1,0},{2,3},{3,2},{4,5},{5,4},{6,7},{7,6},{8,9},{9,8},{10,11... | collective-permute-start | bytes 393224 | tf_op jit(solution)/shard_map/ppermute | solution.py:382
  22.0 11.1 %collective-permute-start.9 = (f32[256,128]{1,0:T(8,128)S(1)}, f32[256,128]{1,0:T(8,128)S(1)}, u32[]{:S(2)}, u32[]{:S(2)}) collective-permute-start(f32[256,128]{1,0:T(8,128)S(1)} %collective-permute-done.refs_2_), channel_id=1, source_target_pairs={{0,1},{1,0},{2,3},{3,2},{4,5},{5,4},{6,7},{7,6},{8,9},{9,8},{10,11... | collective-permute-start | bytes 393224 | tf_op jit(solution)/shard_map/ppermute | solution.py:382
  22.5 10.7 %collective-permute-start.10 = (f32[256,128]{1,0:T(8,128)S(1)}, f32[256,128]{1,0:T(8,128)S(1)}, u32[]{:S(2)}, u32[]{:S(2)}) collective-permute-start(f32[256,128]{1,0:T(8,128)S(1)} %collective-permute-done.1.refs_4_), channel_id=1, source_target_pairs={{0,1},{1,0},{2,3},{3,2},{4,5},{5,4},{6,7},{7,6},{8,9},{9,8},{10,11... | collective-permute-start | bytes 393224 | tf_op jit(solution)/shard_map/ppermute | solution.py:382
  22.6 10.7 %collective-permute-start.12 = (f32[256,128]{1,0:T(8,128)S(1)}, f32[256,128]{1,0:T(8,128)S(1)}, u32[]{:S(2)}, u32[]{:S(2)}) collective-permute-start(f32[256,128]{1,0:T(8,128)S(1)} %collective-permute-done.11.refs_6_), channel_id=1, source_target_pairs={{0,1},{1,0},{2,3},{3,2},{4,5},{5,4},{6,7},{7,6},{8,9},{9,8},{10,11... | collective-permute-start | bytes 393224 | tf_op jit(solution)/shard_map/ppermute | solution.py:382
  35.6 8.0 %collective-permute-start.15 = (f32[256,128]{1,0:T(8,128)S(1)}, f32[256,128]{1,0:T(8,128)S(1)}, u32[]{:S(2)}, u32[]{:S(2)}) collective-permute-start(f32[256,128]{1,0:T(8,128)S(1)} %get-tuple-element.79), channel_id=1, source_target_pairs={{0,18},{1,19},{2,16},{3,17},{4,22},{5,23},{6,20},{7,21},{8,26},{9,... | collective-permute-start | bytes 393224 | tf_op jit(solution)/shard_map/ppermute | solution.py:398
  38.1 5.5 %collective-permute-start.13 = (f32[256,128]{1,0:T(8,128)S(1)}, f32[256,128]{1,0:T(8,128)S(1)}, u32[]{:S(2)}, u32[]{:S(2)}) collective-permute-start(f32[256,128]{1,0:T(8,128)S(1)} %get-tuple-element.77), channel_id=1, source_target_pairs={{0,16},{1,17},{2,18},{3,19},{4,20},{5,21},{6,22},{7,23},{8,24},{9,... | collective-permute-start | bytes 393224 | tf_op jit(solution)/shard_map/ppermute | solution.py:398
  38.7 5.0 %collective-permute-start.14 = (f32[256,128]{1,0:T(8,128)S(1)}, f32[256,128]{1,0:T(8,128)S(1)}, u32[]{:S(2)}, u32[]{:S(2)}) collective-permute-start(f32[256,128]{1,0:T(8,128)S(1)} %get-tuple-element.78), channel_id=1, source_target_pairs={{0,2},{1,3},{2,0},{3,1},{4,6},{5,7},{6,4},{7,5},{8,10},{9,11},{10,... | collective-permute-start | bytes 393224 | tf_op jit(solution)/shard_map/ppermute | solution.py:398
  45.4 13.1 %collective-permute-start.21 = (f32[256,128]{1,0:T(8,128)S(1)}, f32[256,128]{1,0:T(8,128)S(1)}, u32[]{:S(2)}, u32[]{:S(2)}) collective-permute-start(f32[256,128]{1,0:T(8,128)S(1)} %get-tuple-element.84.refs_0_.sent_ref), channel_id=1, source_target_pairs={{0,12},{1,13},{2,14},{3,15},{4,8},{5,9},{6,10},{7,11},{8,4},{9,5},... | collective-permute-start | bytes 393224 | tf_op jit(solution)/shard_map/ppermute | solution.py:377
  47.9 10.5 %collective-permute-start.17 = (f32[256,128]{1,0:T(8,128)S(1)}, f32[256,128]{1,0:T(8,128)S(1)}, u32[]{:S(2)}, u32[]{:S(2)}) collective-permute-start(f32[256,128]{1,0:T(8,128)S(1)} %get-tuple-element.84.refs_0_.sent_ref), channel_id=1, source_target_pairs={{0,4},{1,5},{2,6},{3,7},{4,0},{5,1},{6,2},{7,3},{8,12},{9,13},{10,... | collective-permute-start | bytes 393224 | tf_op jit(solution)/shard_map/ppermute | solution.py:377
  48.0 10.6 %collective-permute-start.19 = (f32[256,128]{1,0:T(8,128)S(1)}, f32[256,128]{1,0:T(8,128)S(1)}, u32[]{:S(2)}, u32[]{:S(2)}) collective-permute-start(f32[256,128]{1,0:T(8,128)S(1)} %get-tuple-element.84.refs_0_.sent_ref), channel_id=1, source_target_pairs={{0,8},{1,9},{2,10},{3,11},{4,12},{5,13},{6,14},{7,15},{8,0},{9,1},... | collective-permute-start | bytes 393224 | tf_op jit(solution)/shard_map/ppermute | solution.py:377
  51.2 4.9 %collective-permute-start.23 = (f32[64,128]{1,0:T(8,128)S(1)}, f32[64,128]{1,0:T(8,128)S(1)}, u32[]{:S(2)}, u32[]{:S(2)}) collective-permute-start(f32[64,128]{1,0:T(8,128)S(1)} %get-tuple-element.88), channel_id=1, source_target_pairs={{0,2},{1,3},{2,0},{3,1},{4,6},{5,7},{6,4},{7,5},{8,10},{9,11},{10,... | collective-permute-start | bytes 98312 | tf_op jit(solution)/shard_map/ppermute | solution.py:398
  58.6 5.0 %collective-permute-start.20 = (f32[256,128]{1,0:T(8,128)S(1)}, f32[256,128]{1,0:T(8,128)S(1)}, u32[]{:S(2)}, u32[]{:S(2)}) collective-permute-start(f32[256,128]{1,0:T(8,128)S(1)} %collective-permute-done.19.refs_4_), channel_id=1, source_target_pairs={{0,1},{1,0},{2,3},{3,2},{4,5},{5,4},{6,7},{7,6},{8,9},{9,8},{10,11... | collective-permute-start | bytes 393224 | tf_op jit(solution)/shard_map/ppermute | solution.py:382
  59.2 9.6 %collective-permute-start.26 = (f32[64,128]{1,0:T(8,128)S(1)}, f32[64,128]{1,0:T(8,128)S(1)}, u32[]{:S(2)}, u32[]{:S(2)}) collective-permute-start(f32[64,128]{1,0:T(8,128)S(1)} %add_parts.1.refs_0_), channel_id=1, source_target_pairs={{0,4},{1,5},{2,6},{3,7},{4,0},{5,1},{6,2},{7,3},{8,12},{9,13},{10,... | collective-permute-start | bytes 98312 | tf_op jit(solution)/shard_map/ppermute | solution.py:377
  59.4 9.9 %collective-permute-start.27 = (f32[64,128]{1,0:T(8,128)S(1)}, f32[64,128]{1,0:T(8,128)S(1)}, u32[]{:S(2)}, u32[]{:S(2)}) collective-permute-start(f32[64,128]{1,0:T(8,128)S(1)} %add_parts.1.refs_0_), channel_id=1, source_target_pairs={{0,8},{1,9},{2,10},{3,11},{4,12},{5,13},{6,14},{7,15},{8,0},{9,1},... | collective-permute-start | bytes 98312 | tf_op jit(solution)/shard_map/ppermute | solution.py:377
  62.3 6.9 %collective-permute-start.28 = (f32[64,128]{1,0:T(8,128)S(1)}, f32[64,128]{1,0:T(8,128)S(1)}, u32[]{:S(2)}, u32[]{:S(2)}) collective-permute-start(f32[64,128]{1,0:T(8,128)S(1)} %add_parts.1.refs_0_), channel_id=1, source_target_pairs={{0,12},{1,13},{2,14},{3,15},{4,8},{5,9},{6,10},{7,11},{8,4},{9,5},... | collective-permute-start | bytes 98312 | tf_op jit(solution)/shard_map/ppermute | solution.py:377
  65.7 13.6 %collective-permute-start.29 = (f32[256,128]{1,0:T(8,128)S(1)}, f32[256,128]{1,0:T(8,128)S(1)}, u32[]{:S(2)}, u32[]{:S(2)}) collective-permute-start(f32[256,128]{1,0:T(8,128)S(1)} %get-tuple-element.94), channel_id=1, source_target_pairs={{0,16},{1,17},{2,18},{3,19},{4,20},{5,21},{6,22},{7,23},{8,24},{9,... | collective-permute-start | bytes 393224 | tf_op jit(solution)/shard_map/ppermute | solution.py:398
  67.3 12.0 %collective-permute-start.30 = (f32[256,128]{1,0:T(8,128)S(1)}, f32[256,128]{1,0:T(8,128)S(1)}, u32[]{:S(2)}, u32[]{:S(2)}) collective-permute-start(f32[256,128]{1,0:T(8,128)S(1)} %get-tuple-element.95), channel_id=1, source_target_pairs={{0,2},{1,3},{2,0},{3,1},{4,6},{5,7},{6,4},{7,5},{8,10},{9,11},{10,... | collective-permute-start | bytes 393224 | tf_op jit(solution)/shard_map/ppermute | solution.py:398
  68.8 10.5 %collective-permute-start.31 = (f32[256,128]{1,0:T(8,128)S(1)}, f32[256,128]{1,0:T(8,128)S(1)}, u32[]{:S(2)}, u32[]{:S(2)}) collective-permute-start(f32[256,128]{1,0:T(8,128)S(1)} %get-tuple-element.96), channel_id=1, source_target_pairs={{0,18},{1,19},{2,16},{3,17},{4,22},{5,23},{6,20},{7,21},{8,26},{9,... | collective-permute-start | bytes 393224 | tf_op jit(solution)/shard_map/ppermute | solution.py:398
  (19 other events, 103.6 us)
